TPU v7x, 32 devices: a whole 2x2x4 slice. The times are simulated.
32 devices in a mesh: group: 2 (over core), tensor: 16 (over z, y, x).
Axes of the slice: x: 2, y: 2, z: 4, core: 2. Of those that a mesh axis runs over, the one named last changes fastest.
Arguments:
- hidden_in: bfloat16 [2048, 2048], P('tensor'), may hold values from -6 to 6
- queries: bfloat16 [2048, 3072], P('tensor', 'group'), may hold values from -10 to 10
- suffix_latent: bfloat16 [2048, 576], P('tensor'), may hold values from -10 to 10
- prefix_latent: bfloat16 [2048, 576], P(('group', 'tensor')), may hold values from -6 to 6
- key_up: bfloat16 [16, 128, 512], P('group'), may hold values from -0.5 to 0.5
- value_up: bfloat16 [16, 512, 128], P('group'), may hold values from -0.25 to 0.25
- output_weight: bfloat16 [2048, 2048], P('group'), may hold values from -0.125 to 0.125
- norm_gain: bfloat16 [2048], replicated, may hold values from 0.5 to 1.5
- router: bfloat16 [2048, 16], replicated, may hold values from -0.125 to 0.125
- expert_gate: bfloat16 [16, 2048, 1408], P('tensor', None, 'group'), may hold values from -0.125 to 0.125
- expert_up: bfloat16 [16, 2048, 1408], P('tensor', None, 'group'), may hold values from -0.125 to 0.125
- expert_down: bfloat16 [16, 1408, 2048], P('tensor', 'group'), may hold values from -0.15625 to 0.15625
- next_gain: bfloat16 [2048], replicated, may hold values from 0.5 to 1.5
- next_query_weight: bfloat16 [2048, 3072], P(None, 'group'), may hold values from -0.125 to 0.125
- next_latent_weight: bfloat16 [2048, 576], P(None, 'group'), may hold values from -0.125 to 0.125
- suffix_lengths: int32 [8], replicated, may hold values from 1 to 513, 2048 in all
- request_tenant: int32 [8], replicated, may hold values from 0 to 3
- tenant_lengths: int32 [4], replicated, may hold values from 1 to 1024, 2048 in all
- page_table: int32 [256], replicated, may hold values from 0 to 255, each once
- routes: int32 [2, 1024, 6], P(None, 'tensor'), may hold values from 0 to 15, all different within a row; in each aligned block of 64 rows (0 to 63, 64 to 127, ..., all dimensions but the last counted through in order) at most 32 rows name the same one
Outputs:
- layer_out: bfloat16 [1024, 2, 2048], P('tensor', 'group')
- next_queries: bfloat16 [2048, 3072], P('tensor', 'group')
- next_latent: bfloat16 [2048, 576], P('tensor', 'group')
Inputs may be any that keep to these rules, and one draw needn't show every extreme that they name: `page_table`: each stored page maps to a different logical page. In each aligned block of 64 rows of routes (in its order g, a) an expert is named by at most 32 rows, and some block reaches 32; the 6 experts of a token differ.
All inputs are finite; a program needn't handle non-finite values.
Results may differ from a plain program's by a relative error of at most 0.018.
Values may be sent and summed in bfloat16 or wider, within the bound.
No kernel may reach another device: no remote copies, remote signals or barrier semaphores. Data moves between devices by JAX's collectives and lax.ppermute only.
A program may use at most 128 MiB of HBM per device.

v0:
```python
import math

import jax
import jax.numpy as jnp
from jax import lax
from jax.sharding import PartitionSpec as P

NOPE = 128
ROPE = 64
LAT = 512
PAGE = 8
REACH = 4


VERY_NEGATIVE = -1e30
ROUTE_SCALING = 2.446
NORM_EPSILON = 1e-06


def shifted(block, axis, distance):
    devices = range(lax.axis_size(axis))
    route = [(i - distance, i) for i in devices if i - distance in devices]
    return lax.ppermute(block, axis, route)


def norm_rows(row_block, gain_vector):
    values = row_block.astype(jnp.float32)
    mean_square = jnp.mean(values * values, axis=-1, keepdims=True)
    return (
        values * lax.rsqrt(mean_square + NORM_EPSILON) * gain_vector.astype(jnp.float32)
    ).astype(jnp.bfloat16)


def attend_block(running, query_rows, key_rows, visible, heads_dev, score_scale):
    best_score, weight_sum, accumulated = running
    token_count = visible.shape[0]
    scores = jnp.einsum("rc,kc->rk", query_rows, key_rows, preferred_element_type=jnp.float32)
    scores = scores.reshape(token_count, heads_dev, -1) * score_scale
    masked = jnp.where(visible[:, None, :], scores, VERY_NEGATIVE)
    new_best = jnp.maximum(best_score, jnp.max(masked, axis=-1))
    weights = jnp.where(visible[:, None, :], jnp.exp(masked - new_best[:, :, None]), 0.0)
    factor = jnp.exp(best_score - new_best)
    weight_sum = weight_sum * factor + jnp.sum(weights, axis=-1)
    rounded = weights.astype(jnp.bfloat16).reshape(token_count * heads_dev, -1)
    update = jnp.dot(rounded, key_rows[:, :LAT], preferred_element_type=jnp.float32)
    accumulated = accumulated * factor[:, :, None] + update.reshape(token_count, heads_dev, -1)
    return (new_best, weight_sum, accumulated)


def route_weights(normed, router, route_ids):
    probs = jax.nn.sigmoid(jnp.dot(normed, router, preferred_element_type=jnp.float32))
    picked = jnp.take_along_axis(probs, route_ids, axis=1)
    return picked / jnp.sum(picked, axis=1, keepdims=True) * ROUTE_SCALING


def slot_targets(route_ids, expert_count, capacity):
    flat_ids = route_ids.reshape(-1)
    hit_table = (flat_ids[:, None] == jnp.arange(expert_count, dtype=jnp.int32)[None, :]).astype(
        jnp.int32
    )
    rank_table = jnp.cumsum(hit_table, axis=0) - hit_table
    slot_index = jnp.sum(rank_table * hit_table, axis=1)
    return (flat_ids * capacity + slot_index).reshape(route_ids.shape)


def pack_rows(normed, targets, slots_total):
    select = jnp.any(
        jnp.arange(slots_total, dtype=jnp.int32)[:, None, None] == targets[None, :, :], axis=2
    )
    return jnp.dot(select.astype(jnp.bfloat16), normed, preferred_element_type=jnp.float32).astype(
        jnp.bfloat16
    )


def expert_apply(row_block, gate_part, up_part, down_part):
    lead_shape = row_block.shape[:-1]
    flat_rows = row_block.reshape(-1, row_block.shape[-1])
    gate_vals = jnp.dot(flat_rows, gate_part, preferred_element_type=jnp.float32)
    up_vals = jnp.dot(flat_rows, up_part, preferred_element_type=jnp.float32)
    hidden_vals = (jax.nn.silu(gate_vals) * up_vals).astype(jnp.bfloat16)
    output_rows = jnp.dot(hidden_vals, down_part, preferred_element_type=jnp.float32).astype(
        jnp.bfloat16
    )
    return output_rows.reshape(lead_shape + (down_part.shape[1],))


def per_device(
    hidden_in,
    queries,
    suffix_latent,
    prefix_latent,
    key_up,
    value_up,
    output_weight,
    norm_gain,
    router,
    expert_gate,
    expert_up,
    expert_down,
    next_gain,
    next_query_weight,
    next_latent_weight,
    suffix_lengths,
    request_tenant,
    tenant_lengths,
    page_table,
    routes,
):
    tok_slice = hidden_in.shape[0]
    width = hidden_in.shape[1]
    heads_dev = key_up.shape[0]
    groups = lax.axis_size("group")
    group_index = lax.axis_index("group")
    tensor_index = lax.axis_index("tensor")
    tok_quarter = tok_slice // groups
    key_width = suffix_latent.shape[1]
    expert_count = router.shape[1]
    top_count = routes.shape[2]
    score_scale = 1.0 / math.sqrt(NOPE + ROPE)
    first_token = tensor_index * tok_slice
    positions = first_token + jnp.arange(tok_slice, dtype=jnp.int32)
    request_ends = jnp.cumsum(suffix_lengths)
    request_starts = request_ends - suffix_lengths
    inside = (positions[:, None] >= request_starts[None, :]) & (
        positions[:, None] < request_ends[None, :]
    )
    token_start = jnp.sum(jnp.where(inside, request_starts[None, :], 0), axis=1)
    token_tenant = jnp.sum(jnp.where(inside, request_tenant[None, :], 0), axis=1)
    tenant_ends = jnp.cumsum(tenant_lengths)
    tenant_starts = tenant_ends - tenant_lengths
    tenant_pick = (
        token_tenant[:, None] == jnp.arange(tenant_lengths.shape[0], dtype=jnp.int32)[None, :]
    )
    range_low = jnp.sum(jnp.where(tenant_pick, tenant_starts[None, :], 0), axis=1)
    range_high = jnp.sum(jnp.where(tenant_pick, tenant_ends[None, :], 0), axis=1)
    page_count = page_table.shape[0]
    query_split = queries.reshape(tok_slice, heads_dev, NOPE + ROPE)
    absorbed = jnp.einsum(
        "thn,hnl->thl", query_split[:, :, :NOPE], key_up, preferred_element_type=jnp.float32
    ).astype(jnp.bfloat16)
    query_rows = jnp.concatenate([absorbed, query_split[:, :, NOPE:]], axis=-1).reshape(
        tok_slice * heads_dev, key_width
    )
    start_state = (
        jnp.full((tok_slice, heads_dev), VERY_NEGATIVE, jnp.float32),
        jnp.zeros((tok_slice, heads_dev), jnp.float32),
        jnp.zeros((tok_slice, heads_dev, LAT), jnp.float32),
    )
    piece_rows = lax.all_gather(prefix_latent, ("group", "tensor"), axis=0, tiled=True)
    prefix_spots = jnp.arange(piece_rows.shape[0], dtype=jnp.int32)
    page_hit = (prefix_spots // PAGE)[:, None] == jnp.arange(page_count, dtype=jnp.int32)[None, :]
    logical = (
        jnp.sum(jnp.where(page_hit, page_table[None, :], 0), axis=1) * PAGE + prefix_spots % PAGE
    )
    visible = (logical[None, :] >= range_low[:, None]) & (logical[None, :] < range_high[:, None])
    running = attend_block(start_state, query_rows, piece_rows, visible, heads_dev, score_scale)

    def suffix_step(running, key_rows, offset):
        key_spots = first_token - offset * tok_slice + jnp.arange(tok_slice, dtype=jnp.int32)
        visible = (key_spots[None, :] >= token_start[:, None]) & (
            key_spots[None, :] <= positions[:, None]
        )
        needed = token_start[0] <= key_spots[-1]

        def attend_here(state):
            return attend_block(state, query_rows, key_rows, visible, heads_dev, score_scale)

        def keep_state(state):
            return state

        return lax.cond(needed, attend_here, keep_state, running)

    running = suffix_step(running, suffix_latent, 0)
    for offset in range(1, REACH + 1):
        earlier = shifted(suffix_latent, "tensor", offset)
        running = suffix_step(running, earlier, offset)
    best_score, weight_sum, accumulated = running
    latent_out = (accumulated / weight_sum[:, :, None]).astype(jnp.bfloat16)
    head_out = (
        jnp.einsum("thl,hlv->thv", latent_out, value_up, preferred_element_type=jnp.float32)
        .astype(jnp.bfloat16)
        .reshape(tok_slice, -1)
    )
    attend_part = jnp.dot(head_out, output_weight, preferred_element_type=jnp.float32)
    gate_part = expert_gate[0]
    up_part = expert_up[0]
    down_part = expert_down[0]
    base_capacity = max(2, 4 * tok_quarter * top_count // (3 * expert_count))
    attend_full = lax.psum(attend_part.astype(jnp.bfloat16), "group").astype(jnp.float32)
    residual = (hidden_in.astype(jnp.float32) + attend_full).astype(jnp.bfloat16)
    normed = norm_rows(residual, norm_gain)
    route_ids = jnp.transpose(routes, (1, 0, 2)).reshape(tok_slice, top_count)
    weights = route_weights(normed, router, route_ids)
    capacity = groups * base_capacity
    targets = slot_targets(route_ids, expert_count, capacity)
    outgoing = pack_rows(normed, targets, expert_count * capacity).reshape(
        expert_count, capacity, width
    )
    partials = expert_apply(
        lax.all_to_all(outgoing, "tensor", split_axis=0, concat_axis=0, tiled=True),
        gate_part,
        up_part,
        down_part,
    )
    returned = lax.all_to_all(partials, "tensor", split_axis=0, concat_axis=0, tiled=True).reshape(
        expert_count * capacity, width
    )
    picked = jnp.take(returned, targets, axis=0)
    moe_part = jnp.sum(weights[:, :, None] * picked.astype(jnp.float32), axis=1)
    moe_share = lax.psum_scatter(
        moe_part.reshape(tok_quarter, groups, width).astype(jnp.bfloat16),
        "group",
        scatter_dimension=1,
        tiled=True,
    ).astype(jnp.float32)
    resid_quarter = lax.dynamic_slice_in_dim(
        residual.reshape(tok_quarter, groups, width), group_index, 1, 1
    )
    layer_rows = (resid_quarter.astype(jnp.float32) + moe_share).astype(jnp.bfloat16)
    normed_next = norm_rows(layer_rows, next_gain)
    query_cols = next_query_weight.shape[1]
    piece_rows = lax.all_gather(normed_next, "group", axis=1, tiled=True)
    query_part = jnp.einsum(
        "tmd,dc->tmc", piece_rows, next_query_weight, preferred_element_type=jnp.float32
    )
    latent_part = jnp.einsum(
        "tmd,dc->tmc", piece_rows, next_latent_weight, preferred_element_type=jnp.float32
    )
    projected = (
        jnp.concatenate([query_part, latent_part], axis=-1)
        .astype(jnp.bfloat16)
        .reshape(tok_slice, -1)
    )
    next_queries = projected[:, :query_cols]
    next_latent = projected[:, query_cols:]
    return (layer_rows, next_queries, next_latent)


def solution(mesh):
    return jax.shard_map(
        per_device,
        mesh=mesh,
        in_specs=(
            P("tensor", None),
            P("tensor", "group"),
            P("tensor", None),
            P(("group", "tensor"), None),
            P("group", None, None),
            P("group", None, None),
            P("group", None),
            P(),
            P(),
            P("tensor", None, "group"),
            P("tensor", None, "group"),
            P("tensor", "group", None),
            P(),
            P(None, "group"),
            P(None, "group"),
            P(),
            P(),
            P(),
            P(),
            P(None, "tensor", None),
        ),
        out_specs=(P("tensor", "group", None), P("tensor", "group"), P("tensor", "group")),
        check_vma=False,
    )
```

profile of v0, /device:TPU:0, one launch (start us, length us, event | category | flops | bytes accessed | tf_op | source)
XLA Modules:
  0.0 445.8 jit_solution(11471403445320315570)
XLA Ops:
  7.2 0.7 all-gather.2.cloned.1.call-update
  8.0 1.8 copy.150
  9.8 5.5 %collective-permute-start = (bf16[128,576]{1,0:T(8,128)(2,1)}, bf16[128,576]{1,0:T(8,128)(2,1)}, u32[]{:S(2)}, u32[]{:S(2)}) collective-permute-start(bf16[128,576]{1,0:T(8,128)(2,1)} %copy.150), channel_id=1, source_target_pairs={{0,1},{1,2},{2,3},{3,4},{4,5},{5,6},{6,7},{7,8},{8,9},{9,10},{10,1... | collective-permute-start | bytes 442376 | tf_op jit(solution)/shard_map/ppermute | solution.py:23
  15.3 3.4 collective-permute-start.1
  18.7 4.4 collective-permute-start.2
  23.1 3.5 collective-permute-start.3
  26.5 0.8 reduce-window.26
  27.4 0.8 reduce-window.27
  28.2 1.2 copy.141
  29.4 1.7 fusion.57
  31.2 1.0 copy-done.4
  32.2 1.1 pad_maximum_fusion
  33.3 2.9 copy.144
  36.2 0.6 slice.61
  37.6 0.6 slice.60
  38.9 0.6 slice.59
  40.2 0.6 slice.58
  41.5 0.6 slice.57
  43.0 3.0 reduce-window.28
  46.1 0.7 select_reduce_fusion
  46.9 0.7 compare_and_fusion.4
  47.9 24.5 %all-gather.2.cloned.1.call-done = bf16[2048,576]{1,0:T(8,128)(2,1)} async-done(((bf16[64,576]{1,0:T(8,128)(2,1)}), bf16[2048,576]{1,0:T(8,128)(2,1)}) %all-gather.2.cloned.1.call-update) | async-done | bytes 2359312 | tf_op jit(solution)/shard_map/all_gather | solution.py:149
  72.4 6.1 %fusion.33 = (f32[128,8]{0,1:T(8,128)S(1)}, f32[128,8,2048]{2,0,1:T(8,128)S(1)}) fusion(pred[128,2048]{1,0:T(8,128)(4,1)S(1)} %compare_and_fusion.2, bf16[2048,576]{1,0:T(8,128)(2,1)} %all-gather.2.cloned.1.call-done, bf16[128,8,64]{0,2,1:T(8,128)(2,1)S(1)} %slice.73, bf16[128,8,512]{0,2,1:T(8,128)(2,1)} %copy-done.4), kind=kOutput, calls=%fused_computation.66 | convolution fusion | flops 2424568832 | bytes 12193792 | tf_op jit(solution)/shard_map/rc,kc->rk/dot_general | solution.py:37
  78.5 2.5 fusion.37
  81.0 3.8 fusion.54
  84.9 15.9 %conditional.5 = (f32[128,8]{1,0:T(8,128)}, f32[128,8]{1,0:T(8,128)S(1)}, f32[128,8,512]{2,0,1:T(8,128)}) conditional(s32[]{:T(128)} %bitcast.21, (f32[128,8]{0,1:T(8,128)S(1)}, f32[128,8]{0,1:T(8,128)S(1)}, f32[128,8,512]{2,0,1:T(8,128)}) %tuple.46, (pred[128,128]{1,0:T(8,128)(4,1)S(1)}, bf16[1024,576]{1,0:T(8,128)(2,1)}, ...), branch_computations={%region_9.10_spmd, %region_10.13_spmd} | conditional | flops 287180800 | bytes 7753836 | solution.py:171
  85.2 1.9 fusion.98
  87.1 0.7 reduce_max.48
  87.8 0.8 copy.148
  88.6 1.5 max.12
  90.1 1.5 sub.91
  91.6 2.2 fusion.3
  93.8 0.8 reduce_sum.89
  94.6 0.8 copy.149
  95.4 0.9 multiply_add_fusion.1
  96.3 1.1 copy.147
  97.3 3.4 multiply_add_fusion
  100.8 0.6 copy-done.14
  101.7 0.6 copy-done.19
  102.3 2.7 convolution_convert_fusion.4
  105.4 1.6 convolution_convert_fusion.2
  107.8 1.2 fusion.41
  109.0 54.1 %all-reduce.2.cloned.1.call-done = bf16[128,2048]{1,0:T(8,128)(2,1)} async-done(((bf16[128,2048]{1,0:T(8,128)(2,1)}), bf16[128,2048]{1,0:T(8,128)(2,1)}) %all-reduce.2.cloned.1.call-update) | async-done | bytes 524304 | tf_op jit(solution)/shard_map/psum | solution.py:189
  163.1 1.5 fusion.66
  164.6 2.2 convolution_convert_fusion.1
  166.8 112.5 %all_to_all.10 = bf16[16,64,2048]{2,1,0:T(8,128)(2,1)S(1)} all-to-all(bf16[16,64,2048]{2,1,0:T(8,128)(2,1)S(1)} %bitcast.181), channel_id=1, replica_groups=mesh['group'=2,'tensor'=16] {'tensor'}, dimensions={0} | all-to-all | bytes 8388608 | tf_op jit(solution)/shard_map/all_to_all | solution.py:200
  279.3 2.0 copy-done.3
  281.3 4.9 %fusion.43 = f32[1024,704]{0,1:T(8,128)} fusion(bf16[1024,2048]{1,0:T(8,128)(2,1)S(1)} %bitcast.183, bf16[1,2048,704]{1,2,0:T(8,128)(2,1)S(1)} %copy-done.23), kind=kOutput, calls=%fused_computation.78 | convolution fusion | flops 2952790016 | bytes 9961472 | tf_op jit(solution)/shard_map/dot_general | solution.py:79
  286.2 11.3 %convolution_convert_fusion = bf16[1024,2048]{1,0:T(8,128)(2,1)} fusion(bf16[1,704,2048]{2,1,0:T(8,128)(2,1)S(1)} %copy-done, f32[1024,704]{0,1:T(8,128)} %fusion.43, bf16[1024,2048]{1,0:T(8,128)(2,1)} %bitcast.184, bf16[1,2048,704]{1,2,0:T(8,128)(2,1)} %param.39), kind=kOutput, calls=%fused_computation.73 | convolution fusion | flops 5912002560 | bytes 17039360 | tf_op jit(solution)/shard_map/dot_general | solution.py:81
  297.5 4.7 %all-to-all-start.1 = ((bf16[16,64,2048]{2,1,0:T(8,128)(2,1)}), bf16[16,64,2048]{2,1,0:T(8,128)(2,1)}, u32[]{:S(2)}, u32[]{:S(2)}) async-start(bf16[16,64,2048]{2,1,0:T(8,128)(2,1)} %bitcast.182), calls=%async_computation.1 | async-start | bytes 8388608 | tf_op jit(solution)/shard_map/all_to_all | solution.py:205
  303.1 5.1 %gather_fusion.1 = f32[768]{0:T(1024)S(1)} fusion(f32[128,16]{0,1:T(8,128)S(1)} %fusion.65, s32[768]{0:T(1024)S(1)} %reshape.508), kind=kCustom, calls=%fused_computation.1 | custom fusion | bytes 12288 | tf_op jit(solution)/shard_map/jit(take_along_axis)/gather | solution.py:52
  308.9 71.8 %all-to-all-done.1 = bf16[16,64,2048]{2,1,0:T(8,128)(2,1)} async-done(((bf16[16,64,2048]{2,1,0:T(8,128)(2,1)}), bf16[16,64,2048]{2,1,0:T(8,128)(2,1)}, u32[]{:S(2)}, u32[]{:S(2)}) %all-to-all-start.1) | async-done | bytes 4194336 | tf_op jit(solution)/shard_map/all_to_all | solution.py:205
  380.7 9.8 %gather_fusion = bf16[768,2048]{1,0:T(8,128)(2,1)} fusion(bf16[1024,2048]{1,0:T(8,128)(2,1)} %bitcast.43, s32[1024]{0:T(1024)S(1)} %pad_clamp_fusion), kind=kCustom, calls=%fused_computation | custom fusion | bytes 6294528 | tf_op jit(solution)/shard_map/jit(_take)/gather | solution.py:208
  390.5 6.3 %reshape.501 = bf16[128,6,2048]{2,1,0:T(8,128)(2,1)} reshape(bf16[768,2048]{1,0:T(8,128)(2,1)} %gather_fusion) | data formatting | bytes 6291456 | tf_op jit(solution)/shard_map/jit(_take)/gather | solution.py:208
  396.8 6.0 %multiply_reduce_fusion = bf16[128,2048]{1,0:T(8,128)(2,1)S(1)} fusion(bf16[128,6,2048]{2,1,0:T(8,128)(2,1)} %reshape.501, f32[128,6]{1,0:T(8,128)S(1)} %divide_multiply_fusion, pred[128,6]{1,0:T(8,128)(4,1)S(1)} %get-tuple-element.270), kind=kLoop, calls=%fused_computation.63 | loop fusion | flops 6029312 | bytes 3673856 | tf_op jit(solution)/shard_map/reduce_sum | solution.py:209
  403.2 0.9 copy.160
  405.1 20.1 %reduce-scatter.2.cloned.1.call-done = bf16[64,1,2048]{2,0,1:T(8,128)(2,1)} async-done(((bf16[64,2,2048]{2,0,1:T(8,128)(2,1)}), bf16[64,1,2048]{2,0,1:T(8,128)(2,1)}) %reduce-scatter.2.cloned.1.call-update) | async-done | bytes 262160 | tf_op jit(solution)/shard_map/reduce_scatter | solution.py:210
  425.2 1.2 fusion.71
  427.1 2.2 all_gather.7
  429.3 3.9 fusion.49
  433.2 1.1 copy.161
  434.4 1.9 concatenate.11
  436.3 1.9 fusion.60
  438.3 0.7 copy.163
  (114 shorter events, 6.1 us)
Async XLA Ops:
  7.2 279.1 %copy-start = (bf16[1,704,2048]{2,1,0:T(8,128)(2,1)S(1)}, bf16[1,704,2048]{2,1,0:T(8,128)(2,1)}, u32[]{:S(2)}) copy-start(bf16[1,704,2048]{2,1,0:T(8,128)(2,1)} %param.41) | copy-start | bytes 8650756
  7.2 65.2 %all-gather.2.cloned.1.call-start = ((), (), s32[]{:S(2)}) async-start(), calls=%async_computation.3 | async-start | bytes 2703360 | tf_op jit(solution)/shard_map/all_gather | solution.py:149
  7.9 155.2 %all-reduce.2.cloned.1.call-start = ((), (), s32[]{:S(2)}) async-start(), calls=%async_computation.4 | async-start | bytes 1048576 | tf_op jit(solution)/shard_map/psum | solution.py:189
  9.8 91.0 %collective-permute-start = (bf16[128,576]{1,0:T(8,128)(2,1)}, bf16[128,576]{1,0:T(8,128)(2,1)}, u32[]{:S(2)}, u32[]{:S(2)}) collective-permute-start(bf16[128,576]{1,0:T(8,128)(2,1)} %copy.150), channel_id=1, source_target_pairs={{0,1},{1,2},{2,3},{3,4},{4,5},{5,6},{6,7},{7,8},{8,9},{9,10},{10,1... | collective-permute-start | bytes 442376 | tf_op jit(solution)/shard_map/ppermute | solution.py:23
  15.3 85.5 %collective-permute-start.1 = (bf16[128,576]{1,0:T(8,128)(2,1)}, bf16[128,576]{1,0:T(8,128)(2,1)}, u32[]{:S(2)}, u32[]{:S(2)}) collective-permute-start(bf16[128,576]{1,0:T(8,128)(2,1)} %copy.150), channel_id=1, source_target_pairs={{0,2},{1,3},{2,4},{3,5},{4,6},{5,7},{6,8},{7,9},{8,10},{9,11},{10,... | collective-permute-start | bytes 442376 | tf_op jit(solution)/shard_map/ppermute | solution.py:23
  18.7 82.2 %collective-permute-start.2 = (bf16[128,576]{1,0:T(8,128)(2,1)}, bf16[128,576]{1,0:T(8,128)(2,1)}, u32[]{:S(2)}, u32[]{:S(2)}) collective-permute-start(bf16[128,576]{1,0:T(8,128)(2,1)} %copy.150), channel_id=1, source_target_pairs={{0,3},{1,4},{2,5},{3,6},{4,7},{5,8},{6,9},{7,10},{8,11},{9,12},{10... | collective-permute-start | bytes 442376 | tf_op jit(solution)/shard_map/ppermute | solution.py:23
  23.1 78.6 %collective-permute-start.3 = (bf16[128,576]{1,0:T(8,128)(2,1)}, bf16[128,576]{1,0:T(8,128)(2,1)}, u32[]{:S(2)}, u32[]{:S(2)}) collective-permute-start(bf16[128,576]{1,0:T(8,128)(2,1)} %copy.150), channel_id=1, source_target_pairs={{0,4},{1,5},{2,6},{3,7},{4,8},{5,9},{6,10},{7,11},{8,12},{9,13},{1... | collective-permute-start | bytes 442376 | tf_op jit(solution)/shard_map/ppermute | solution.py:23
  31.2 1.0 copy-start.4
  32.1 4.6 %copy-start.26 = (s32[8]{0:T(128)S(1)}, s32[8]{0:T(128)}, u32[]{:S(2)}) copy-start(s32[8]{0:T(128)} %param.45) | copy-start | bytes 100
  32.2 4.6 %copy-start.22 = (s32[8]{0:T(128)S(1)}, s32[8]{0:T(128)}, u32[]{:S(2)}) copy-start(s32[8]{0:T(128)} %param.46) | copy-start | bytes 100
  32.2 10.6 %copy-start.12 = (s32[2,64,6]{1,0,2:T(2,128)S(1)}, s32[2,64,6]{1,0,2:T(2,128)}, u32[]{:S(2)}) copy-start(s32[2,64,6]{1,0,2:T(2,128)} %param.49) | copy-start | bytes 9220
  32.2 13.8 %copy-start.27 = (s32[4]{0:T(128)S(1)}, s32[4]{0:T(128)}, u32[]{:S(2)}) copy-start(s32[4]{0:T(128)} %param.47) | copy-start | bytes 52
  32.2 13.9 %copy-start.17 = (s32[256]{0:T(256)S(1)}, s32[256]{0:T(256)}, u32[]{:S(2)}) copy-start(s32[256]{0:T(256)} %param.48) | copy-start | bytes 3076
  36.2 42.3 %copy-start.10 = (s32[128]{0:T(128)}, s32[128]{0:T(128)S(1)}, u32[]{:S(2)}) copy-start(s32[128]{0:T(128)S(1)} %iota_add_fusion.4) | copy-start | bytes 1540
  36.9 11.0 %copy-start.13 = (s32[128]{0:T(128)}, s32[128]{0:T(128)S(1)}, u32[]{:S(2)}) copy-start(s32[128]{0:T(128)S(1)} %get-tuple-element.255) | copy-start | bytes 1540
  40.1 1.3 copy-start.20
  41.5 4.6 %copy-start.18 = (s32[128]{0:T(128)}, s32[128]{0:T(128)S(1)}, u32[]{:S(2)}) copy-start(s32[128]{0:T(128)S(1)} %iota_add_fusion.3) | copy-start | bytes 1540
  78.5 2.6 copy-start.24
  85.1 2.7 copy-start.7
  85.1 2.7 copy-start.8
  85.1 2.7 copy-start.9
  100.8 0.7 copy-start.14
  100.8 0.7 copy-start.11
  100.8 0.8 copy-start.21
  101.6 0.6 copy-start.19
  102.3 3.2 copy-start.2
  105.4 1.6 copy-start.6
  105.4 2.0 copy-start.15
  166.8 114.5 %copy-start.23 = (bf16[1,2048,704]{1,2,0:T(8,128)(2,1)S(1)}, bf16[1,2048,704]{1,2,0:T(8,128)(2,1)}, u32[]{:S(2)}) copy-start(bf16[1,2048,704]{1,2,0:T(8,128)(2,1)} %param.40) | copy-start | bytes 8650756
  279.3 2.0 copy-start.3
  297.5 5.2 %copy-start.25 = (bf16[2048,16]{0,1:T(8,128)(2,1)S(1)}, bf16[2048,16]{0,1:T(8,128)(2,1)}, u32[]{:S(2)}) copy-start(bf16[2048,16]{0,1:T(8,128)(2,1)} %param.38) | copy-start | bytes 196612
  297.5 83.2 %all-to-all-start.1 = ((bf16[16,64,2048]{2,1,0:T(8,128)(2,1)}), bf16[16,64,2048]{2,1,0:T(8,128)(2,1)}, u32[]{:S(2)}, u32[]{:S(2)}) async-start(bf16[16,64,2048]{2,1,0:T(8,128)(2,1)} %bitcast.182), calls=%async_computation.1 | async-start | bytes 8388608 | tf_op jit(solution)/shard_map/all_to_all | solution.py:205
  302.2 123.0 %reduce-scatter.2.cloned.1.call-start = ((), (), s32[]{:S(2)}) async-start(), calls=%async_computation.5 | async-start | bytes 786432 | tf_op jit(solution)/shard_map/reduce_scatter | solution.py:210
  396.8 7.3 %copy-start.16 = (bf16[2048]{0:T(1024)(128)(2,1)S(1)}, bf16[2048]{0:T(1024)(128)(2,1)}, u32[]{:S(2)}) copy-start(bf16[2048]{0:T(1024)(128)(2,1)} %param.42) | copy-start | bytes 12292
  426.4 0.7 copy-start.5
  429.3 9.8 %copy-start.1 = (bf16[1,704,2048]{2,1,0:T(8,128)(2,1)S(1)}, bf16[1,704,2048]{2,1,0:T(8,128)(2,1)}, u32[]{:S(2)}) copy-start(bf16[1,704,2048]{2,1,0:T(8,128)(2,1)} %param.41) | copy-start | bytes 8650756
Sparse Core Ops, SparseCore 0:
  10.9 61.4 all-gather.1
  107.2 55.9 all-reduce.1
  404.2 20.8 reduce-scatter.1
where the time goes:
time: 450 us; the launch traced here: 446 us
  waiting for transfers between devices  171 us (38%)
  blocking collectives  115 us (26%)
  local copies, waits for them, and re-layouts  49 us (11%)
  matrix products  45.8 us (10%)
  other arithmetic  25.3 us (6%)
  starting transfers between devices  21.6 us (5%)
  between operations  18 us (4%)
    all_to_all x1, blocking collectives, per_device(): lax.all_to_all(outgoing, 'tensor', split_axis=0, concat_axis=0, tiled=True)  113 us
    all_to_all x1, waiting for transfers between devices, per_device(): lax.all_to_all(partials, 'tensor', split_axis=0, concat_axis=0, tiled=True)  71.8 us
    psum x1, waiting for transfers between devices, per_device(): lax.psum(attend_part.astype(jnp.bfloat16), 'group').astype(jnp.float32)  54.1 us
    all_gather x1, waiting for transfers between devices, per_device(): lax.all_gather(prefix_latent, ('group', 'tensor'), axis=0, tiled=True)  24.5 us
    reduce_scatter x1, waiting for transfers between devices, per_device(): lax.psum_scatter(moe_part.reshape(tok_quarter, groups, width).astype(jnp....  20.1 us
    ppermute x4, starting transfers between devices, shifted(): return lax.ppermute(block, axis, route)  16.8 us
    gather x2, local copies, waits for them, and re-layouts, per_device(): picked = jnp.take(returned, targets, axis=0)  16.1 us
    dot_general x1, matrix products, expert_apply(): jnp.dot(hidden_vals, down_part, preferred_element_type=jnp.float32)  11.3 us
  transfers between devices with their start and end apart: 8, of which 4 were waited for; matrix products, arithmetic and copies ran while one was open for 13% of the time, Pallas kernels for 0%

commit v1 on v0

v1 whole, which is shorter than its diff:
```python
import functools
import math

import jax
import jax.numpy as jnp
from jax import lax
from jax.experimental import pallas as pl
from jax.experimental.pallas import tpu as pltpu
from jax.sharding import PartitionSpec as P

NOPE = 128
ROPE = 64
LAT = 512
PAGE = 8
REACH = 4
PLANE = 4

VERY_NEGATIVE = -1e30
ROUTE_SCALING = 2.446
NORM_EPSILON = 1e-06


def ring_order(count):
    odd = list(range(1, count, 2))
    even = list(range(2, count, 2))
    return [0] + odd + even[::-1]


def send_ring(block, count):
    order = ring_order(count)
    after = {order[i]: order[(i + 1) % count] for i in range(count)}
    route = [
        (z * PLANE + p, after[z] * PLANE + p) for z in range(count) for p in range(PLANE)
    ]
    return lax.ppermute(block, "tensor", route)


def send_plane(block, distance):
    devices = range(lax.axis_size("tensor"))
    return lax.ppermute(block, "tensor", [(i, i ^ distance) for i in devices])


def send_group(block, distance):
    devices = range(lax.axis_size("group"))
    return lax.ppermute(block, "group", [(i, i ^ distance) for i in devices])


def send_later(block, distance):
    devices = range(lax.axis_size("tensor"))
    route = [(i - distance, i) for i in devices if i - distance in devices]
    return lax.ppermute(block, "tensor", route)


def norm_rows(row_block, gain_vector):
    values = row_block.astype(jnp.float32)
    mean_square = jnp.mean(values * values, axis=-1, keepdims=True)
    return (
        values * lax.rsqrt(mean_square + NORM_EPSILON) * gain_vector.astype(jnp.float32)
    ).astype(jnp.bfloat16)


def dot_t(left, right):
    return lax.dot_general(
        left, right, (((1,), (1,)), ((), ())), preferred_element_type=jnp.float32
    )


def dot_f(left, right):
    return jnp.dot(left, right, preferred_element_type=jnp.float32)


def attend_kernel(
    prefix_count,
    block_count,
    tok_quarter,
    token_ref,
    spot_ref,
    order_ref,
    query_ref,
    key_up_ref,
    value_up_ref,
    output_ref,
    *refs,
):
    key_refs = refs[:block_count]
    own_ref, other_ref, keys, bias, total = refs[block_count:]
    step = pl.program_id(0)
    tokens = query_ref.shape[0]
    pair = key_up_ref.shape[0]

    @pl.when(step == 0)
    def prepare():
        at = 0
        for ref in key_refs:
            rows = ref.shape[0]
            keys[at : at + rows, :] = ref[...]
            at += rows
        columns = token_ref[...]
        spots = spot_ref[...]
        low, high, start, here = (columns[:, i : i + 1] for i in range(4))
        far = spots[:, :prefix_count]
        near = spots[:, prefix_count:]
        bias[:, :prefix_count] = jnp.where((far >= low) & (far < high), 0.0, VERY_NEGATIVE)
        bias[:, prefix_count:] = jnp.where((near >= start) & (near <= here), 0.0, VERY_NEGATIVE)
        total[...] = jnp.zeros_like(total)

    queries = dot_f(order_ref[...], query_ref[...]).astype(jnp.bfloat16)
    size = NOPE + ROPE
    content = []
    rotated = []
    for h in range(pair):
        part = queries[:, h * size : (h + 1) * size]
        content.append(dot_f(part[:, :NOPE], key_up_ref[h]).astype(jnp.bfloat16))
        rotated.append(part[:, NOPE:])
    content = jnp.concatenate(content, axis=0)
    rotated = jnp.concatenate(rotated, axis=0)
    scores = dot_t(content, keys[:, :LAT]) + dot_t(rotated, keys[:, LAT:])
    masked = (scores.reshape(pair, tokens, -1) + bias[...][None]).reshape(pair * tokens, -1)
    best = jnp.max(masked, axis=-1, keepdims=True)
    factor = math.log2(math.e) / math.sqrt(NOPE + ROPE)
    weights = jnp.exp2((masked - best) * factor)
    weight_sum = jnp.sum(weights, axis=-1, keepdims=True)
    attended = dot_f(weights.astype(jnp.bfloat16), keys[:, :LAT]) / weight_sum
    attended = attended.astype(jnp.bfloat16)
    heads = [
        dot_f(attended[h * tokens : (h + 1) * tokens], value_up_ref[h]).astype(jnp.bfloat16)
        for h in range(pair)
    ]
    total[...] += dot_f(jnp.concatenate(heads, axis=1), output_ref[...])

    @pl.when(step == pl.num_programs(0) - 1)
    def finish():
        own_ref[...] = total[:tok_quarter, :]
        other_ref[...] = total[tok_quarter:, :].astype(jnp.bfloat16)


def attend(tokens_info, spots, order, queries, key_up, value_up, output_weight, blocks, tok_quarter):
    tokens = queries.shape[0]
    heads = key_up.shape[0]
    width = output_weight.shape[1]
    pair = 2
    key_count = sum(block.shape[0] for block in blocks)
    prefix_count = key_count - (REACH + 1) * tokens
    size = NOPE + ROPE

    def whole(array):
        return pl.BlockSpec(array.shape, lambda i: (0,) * array.ndim)

    flops = 2 * heads * tokens * key_count * (LAT + ROPE + LAT)
    return pl.pallas_call(
        functools.partial(attend_kernel, prefix_count, len(blocks), tok_quarter),
        grid=(heads // pair,),
        in_specs=[
            whole(tokens_info),
            whole(spots),
            whole(order),
            pl.BlockSpec((tokens, pair * size), lambda i: (0, i)),
            pl.BlockSpec((pair, NOPE, LAT), lambda i: (i, 0, 0)),
            pl.BlockSpec((pair, LAT, value_up.shape[2]), lambda i: (i, 0, 0)),
            pl.BlockSpec((pair * value_up.shape[2], width), lambda i: (i, 0)),
        ]
        + [whole(block) for block in blocks],
        out_specs=[
            pl.BlockSpec((tok_quarter, width), lambda i: (0, 0)),
            pl.BlockSpec((tokens - tok_quarter, width), lambda i: (0, 0)),
        ],
        out_shape=[
            jax.ShapeDtypeStruct((tok_quarter, width), jnp.float32),
            jax.ShapeDtypeStruct((tokens - tok_quarter, width), jnp.bfloat16),
        ],
        scratch_shapes=[
            pltpu.VMEM((key_count, LAT + ROPE), jnp.bfloat16),
            pltpu.VMEM((tokens, key_count), jnp.float32),
            pltpu.VMEM((tokens, width), jnp.float32),
        ],
        compiler_params=pltpu.CompilerParams(vmem_limit_bytes=40 * 1024 * 1024),
        cost_estimate=pl.CostEstimate(
            flops=flops, bytes_accessed=12_000_000, transcendentals=heads * tokens * key_count
        ),
        name="attend",
    )(tokens_info, spots, order, queries, key_up, value_up, output_weight, *blocks)


def expert_apply(rows, gate_part, up_part, down_part):
    gate_vals = dot_f(rows, gate_part)
    up_vals = dot_f(rows, up_part)
    hidden_vals = (jax.nn.silu(gate_vals) * up_vals).astype(jnp.bfloat16)
    return dot_f(hidden_vals, down_part)


def per_device(
    hidden_in,
    queries,
    suffix_latent,
    prefix_latent,
    key_up,
    value_up,
    output_weight,
    norm_gain,
    router,
    expert_gate,
    expert_up,
    expert_down,
    next_gain,
    next_query_weight,
    next_latent_weight,
    suffix_lengths,
    request_tenant,
    tenant_lengths,
    page_table,
    routes,
):
    tok_slice = hidden_in.shape[0]
    groups = lax.axis_size("group")
    ring = lax.axis_size("tensor") // PLANE
    group_index = lax.axis_index("group")
    tensor_index = lax.axis_index("tensor")
    ring_index = tensor_index // PLANE
    plane_index = tensor_index % PLANE
    tok_quarter = tok_slice // groups
    expert_count = router.shape[1]
    top_count = routes.shape[2]
    capacity = max(2, 4 * tok_quarter * top_count // (3 * expert_count))
    int32 = jnp.int32

    prefix_ring = [prefix_latent]
    routes_own = lax.dynamic_index_in_dim(routes, group_index, 0, keepdims=False)
    routes_ring = [routes_own]
    for _ in range(ring - 1):
        prefix_ring.append(send_ring(prefix_ring[-1], ring))
        routes_ring.append(send_ring(routes_ring[-1], ring))
    suffix_part = lax.dynamic_slice_in_dim(suffix_latent, group_index * tok_quarter, tok_quarter, 0)
    suffix_column = jnp.concatenate(
        [send_later(suffix_part, offset) for offset in range(1, REACH + 1)], axis=0
    )
    prefix_column = jnp.concatenate(prefix_ring, axis=0)
    prefix_plane = [prefix_column] + [send_plane(prefix_column, d) for d in range(1, PLANE)]
    blocks = []
    for j in range(groups):
        blocks += [send_group(block, j) if j else block for block in prefix_plane]
    for j in range(groups):
        blocks.append(send_group(suffix_column, j) if j else suffix_column)
    blocks.append(suffix_latent)

    order = ring_order(ring)
    place = sum(jnp.where(ring_index == z, i, 0) for i, z in enumerate(order))
    piece_rows = prefix_latent.shape[0]
    shape = (groups, PLANE, ring, piece_rows)
    j, d, k, r = (lax.broadcasted_iota(int32, shape, axis) for axis in range(4))
    turn = (place - k + ring) % ring
    source = sum(jnp.where(turn == i, z, 0) for i, z in enumerate(order))
    piece = ((group_index ^ j) * ring + source) * PLANE + (plane_index ^ d)
    spot = (piece * piece_rows + r).reshape(-1)
    page_hit = (spot // PAGE)[:, None] == jnp.arange(page_table.shape[0], dtype=int32)[None, :]
    logical = jnp.sum(jnp.where(page_hit, page_table[None, :], 0), axis=1) * PAGE + spot % PAGE
    shape = (groups, REACH, tok_quarter)
    j, o, r = (lax.broadcasted_iota(int32, shape, axis) for axis in range(3))
    earlier = (tensor_index - 1 - o) * tok_slice + (group_index ^ j) * tok_quarter + r
    first_token = tensor_index * tok_slice
    own_spots = first_token + jnp.arange(tok_slice, dtype=int32)
    spots = jnp.concatenate([logical, earlier.reshape(-1), own_spots])[None, :]

    row = jnp.arange(tok_slice, dtype=int32)
    local = (row % tok_quarter) * groups + (group_index ^ (row // tok_quarter))
    permutation = (local[:, None] == jnp.arange(tok_slice, dtype=int32)[None, :]).astype(
        jnp.bfloat16
    )
    positions = first_token + local
    requests = suffix_lengths.shape[0]
    tenants = tenant_lengths.shape[0]
    upto = jnp.arange(requests)[None, :] <= jnp.arange(requests)[:, None]
    request_ends = jnp.sum(jnp.where(upto, suffix_lengths[None, :], 0), axis=1)
    request_starts = request_ends - suffix_lengths
    inside = (positions[:, None] >= request_starts[None, :]) & (
        positions[:, None] < request_ends[None, :]
    )
    token_start = jnp.sum(jnp.where(inside, request_starts[None, :], 0), axis=1)
    token_tenant = jnp.sum(jnp.where(inside, request_tenant[None, :], 0), axis=1)
    upto = jnp.arange(tenants)[None, :] <= jnp.arange(tenants)[:, None]
    tenant_ends = jnp.sum(jnp.where(upto, tenant_lengths[None, :], 0), axis=1)
    tenant_starts = tenant_ends - tenant_lengths
    tenant_pick = token_tenant[:, None] == jnp.arange(tenants, dtype=int32)[None, :]
    range_low = jnp.sum(jnp.where(tenant_pick, tenant_starts[None, :], 0), axis=1)
    range_high = jnp.sum(jnp.where(tenant_pick, tenant_ends[None, :], 0), axis=1)
    tokens_info = jnp.stack([range_low, range_high, token_start, positions], axis=1)

    attend_own, attend_other = attend(
        tokens_info,
        spots,
        permutation,
        queries,
        key_up,
        value_up,
        output_weight,
        blocks,
        tok_quarter,
    )

    routes_all = jnp.stack(routes_ring)
    target = ring_index * PLANE + (plane_index ^ jnp.arange(PLANE, dtype=int32))
    hits = jnp.any(routes_all[:, :, :, None] == target[None, None, None, :], axis=2)
    below = (
        jnp.arange(tok_quarter)[None, :] < jnp.arange(tok_quarter)[:, None]
    ).astype(jnp.bfloat16)
    rank = jnp.einsum(
        "ij,kjd->kid", below, hits.astype(jnp.bfloat16), preferred_element_type=jnp.float32
    ).astype(int32)
    slots = jnp.arange(capacity, dtype=int32)
    taken = hits[:, :, :, None] & (rank[:, :, :, None] == slots)
    spread = taken.reshape(ring, tok_quarter, PLANE * capacity).astype(jnp.bfloat16)
    named = jnp.any(
        routes_all[:, :, :, None] == jnp.arange(expert_count, dtype=int32), axis=2
    ).astype(jnp.float32)
    aimed = (jnp.arange(expert_count, dtype=int32)[:, None] == target[None, :]).astype(jnp.float32)

    hidden_own = dot_f(permutation[:tok_quarter], hidden_in)
    attend_full = attend_own
    for j in range(1, groups):
        part = attend_other[(j - 1) * tok_quarter : j * tok_quarter]
        attend_full = attend_full + send_group(part, j).astype(jnp.float32)
    residual = (hidden_own + attend_full).astype(jnp.bfloat16)
    normed = norm_rows(residual, norm_gain)

    gate_part = expert_gate[0]
    up_part = expert_up[0]
    down_part = expert_down[0]
    rows_plane = PLANE * capacity
    block = normed
    sums = []
    for k in range(ring):
        if k:
            block = send_ring(block, ring)
        chosen = lax.dot_general(
            spread[k], block, (((0,), (0,)), ((), ())), preferred_element_type=jnp.float32
        ).astype(jnp.bfloat16)
        arrived = [
            send_plane(chosen[d * capacity : (d + 1) * capacity], d)
            if d
            else chosen[:capacity]
            for d in range(PLANE)
        ]
        rows = jnp.concatenate(arrived, axis=0)
        rows = jnp.concatenate(
            [send_group(rows, j) if j else rows for j in range(groups)], axis=0
        )
        partial = expert_apply(rows, gate_part, up_part, down_part)
        combined = partial[:rows_plane]
        for j in range(1, groups):
            part = partial[j * rows_plane : (j + 1) * rows_plane].astype(jnp.bfloat16)
            combined = combined + send_group(part, j).astype(jnp.float32)
        combined = combined.astype(jnp.bfloat16)
        returned = [
            send_plane(combined[d * capacity : (d + 1) * capacity], d)
            if d
            else combined[:capacity]
            for d in range(PLANE)
        ]
        returned = jnp.concatenate(returned, axis=0)
        probs = jax.nn.sigmoid(dot_f(block, router))
        picked = probs * named[k]
        gates = picked / jnp.sum(picked, axis=1, keepdims=True) * ROUTE_SCALING
        gates = jnp.sum(gates[:, :, None] * aimed[None, :, :], axis=1)
        scaled = spread[k].reshape(tok_quarter, PLANE, capacity) * gates[:, :, None].astype(
            jnp.bfloat16
        )
        sums.append(dot_f(scaled.reshape(tok_quarter, rows_plane), returned))
    running = None
    for k in range(1, ring):
        total = sums[k] if running is None else sums[k] + running
        running = send_ring(total.astype(jnp.bfloat16), ring).astype(jnp.float32)
    moe = sums[0] if running is None else sums[0] + running

    layer_rows = (residual.astype(jnp.float32) + moe).astype(jnp.bfloat16)
    normed_next = norm_rows(layer_rows, next_gain)
    shares = [send_group(normed_next, j) if j else normed_next for j in range(groups)]
    gathered = lax.dot_general(
        permutation,
        jnp.concatenate(shares, axis=0),
        (((0,), (0,)), ((), ())),
        preferred_element_type=jnp.float32,
    ).astype(jnp.bfloat16)
    next_queries = dot_f(gathered, next_query_weight).astype(jnp.bfloat16)
    next_latent = dot_f(gathered, next_latent_weight).astype(jnp.bfloat16)
    return (layer_rows[:, None, :], next_queries, next_latent)


def solution(mesh):
    return jax.shard_map(
        per_device,
        mesh=mesh,
        in_specs=(
            P("tensor", None),
            P("tensor", "group"),
            P("tensor", None),
            P(("group", "tensor"), None),
            P("group", None, None),
            P("group", None, None),
            P("group", None),
            P(),
            P(),
            P("tensor", None, "group"),
            P("tensor", None, "group"),
            P("tensor", "group", None),
            P(),
            P(None, "group"),
            P(None, "group"),
            P(),
            P(),
            P(),
            P(),
            P(None, "tensor", None),
        ),
        out_specs=(P("tensor", "group", None), P("tensor", "group"), P("tensor", "group")),
        check_vma=False,
    )
```

time: 450 us -> 228 us (0.51)
  blocking collectives: 115 us -> 0 us
  waiting for transfers between devices: 171 us -> 60.1 us
  starting transfers between devices: 21.6 us -> 57.1 us
  between operations: 18 us -> 1.5 us
  local copies, waits for them, and re-layouts: 49 us -> 32.6 us
  Pallas kernels: 0 us -> 13.8 us
  other arithmetic: 25.3 us -> 14.9 us
    all_to_all x1 -> x0, blocking collectives: 113 us -> none  [per_device(): lax.all_to_all(outgoing, 'tensor', split_axis=0, concat_axis=0, tiled=True)]
    all_to_all x1 -> x0, waiting for transfers between devices: 71.8 us -> none  [per_device(): lax.all_to_all(partials, 'tensor', split_axis=0, concat_axis=0, tiled=True)]
    ppermute x4 -> x58, waiting for transfers between devices: 0.01 us -> 60.1 us  [the longest x12 32.1 us: send_ring(): return lax.ppermute(block, 'tensor', route)]
    psum x1 -> x0, waiting for transfers between devices: 54.1 us -> none  [per_device(): lax.psum(attend_part.astype(jnp.bfloat16), 'group').astype(jnp.float32)]
    ppermute x4 -> x58, starting transfers between devices: 16.8 us -> 57.1 us  [the longest x27 31.8 us: send_plane(): return lax.ppermute(block, 'tensor', [(i, i ^ distance) for i in devices])]
    all_gather x1 -> x0, waiting for transfers between devices: 24.5 us -> none  [per_device(): lax.all_gather(prefix_latent, ('group', 'tensor'), axis=0, tiled=True)]
    gather x6 -> x0, local copies, waits for them, and re-layouts: 21.6 us -> none  [the longest x2 16.1 us: per_device(): picked = jnp.take(returned, targets, axis=0)]
    reduce_scatter x1 -> x0, waiting for transfers between devices: 20.1 us -> none  [per_device(): lax.psum_scatter(moe_part.reshape(tok_quarter, groups, width).astype(jnp....]
  transfers between devices with their start and end apart: 8 -> 58, of which waited for: 4 -> 24; matrix products, arithmetic and copies ran while one was open for 13% -> 35% of each run, Pallas kernels for 0% -> 0%
where the time goes in v1:
time: 228 us; the launch traced here: 227 us
  waiting for transfers between devices  60.1 us (26%)
  starting transfers between devices  57.1 us (25%)
  matrix products  46.8 us (21%)
  local copies, waits for them, and re-layouts  32.6 us (14%)
  other arithmetic  14.9 us (7%)
  Pallas kernels  13.8 us (6%)
    dot_general x19, matrix products, dot_f(): return jnp.dot(left, right, preferred_element_type=jnp.float32)  45.2 us
    ppermute x12, waiting for transfers between devices, send_ring(): return lax.ppermute(block, 'tensor', route)  32.1 us
    ppermute x27, starting transfers between devices, send_plane(): return lax.ppermute(block, 'tensor', [(i, i ^ distance) for i in devices])  31.8 us
    ppermute x27, waiting for transfers between devices, send_plane(): return lax.ppermute(block, 'tensor', [(i, i ^ distance) for i in devices])  24.6 us
    ppermute x4, starting transfers between devices, send_later(): return lax.ppermute(block, 'tensor', route)  16.8 us
    unnamed x78, local copies, waits for them, and re-layouts  16.6 us
    pallas_call x1, Pallas kernels, attend(): pl.pallas_call(functools.partial(attend_kernel, prefix_count, len(blocks)...  13.8 us
    slice x4, local copies, waits for them, and re-layouts, per_device(): part = partial[j * rows_plane:(j + 1) * rows_plane].astype(jnp.bfloat16)  8.19 us
  transfers between devices with their start and end apart: 58, of which 24 were waited for; matrix products, arithmetic and copies ran while one was open for 35% of the time, Pallas kernels for 0%

profile of v1, /device:TPU:0, one launch (start us, length us, event | category | flops | bytes accessed | tf_op | source)
XLA Modules:
  0.0 226.8 jit_solution(13444548235670557099)
XLA Ops:
  0.7 1.2 copy.60.refs_10_
  2.5 5.5 %collective-permute-start.10 = (bf16[64,576]{1,0:T(8,128)(2,1)}, bf16[64,576]{1,0:T(8,128)(2,1)}, u32[]{:S(2)}, u32[]{:S(2)}) collective-permute-start(bf16[64,576]{1,0:T(8,128)(2,1)} %constant_dynamic-slice_fusion.1), channel_id=1, source_target_pairs={{0,1},{1,2},{2,3},{3,4},{4,5},{5,6},{6,7},{7,8},{8,9},{9,10},{10,1... | collective-permute-start | bytes 221192 | tf_op jit(solution)/shard_map/ppermute | solution.py:51
  8.0 3.4 %collective-permute-start.11 = (bf16[64,576]{1,0:T(8,128)(2,1)}, bf16[64,576]{1,0:T(8,128)(2,1)}, u32[]{:S(2)}, u32[]{:S(2)}) collective-permute-start(bf16[64,576]{1,0:T(8,128)(2,1)} %constant_dynamic-slice_fusion.1), channel_id=1, source_target_pairs={{0,2},{1,3},{2,4},{3,5},{4,6},{5,7},{6,8},{7,9},{8,10},{9,11},{10,... | collective-permute-start | bytes 221192 | tf_op jit(solution)/shard_map/ppermute | solution.py:51
  11.4 4.4 %collective-permute-start.12 = (bf16[64,576]{1,0:T(8,128)(2,1)}, bf16[64,576]{1,0:T(8,128)(2,1)}, u32[]{:S(2)}, u32[]{:S(2)}) collective-permute-start(bf16[64,576]{1,0:T(8,128)(2,1)} %constant_dynamic-slice_fusion.1), channel_id=1, source_target_pairs={{0,3},{1,4},{2,5},{3,6},{4,7},{5,8},{6,9},{7,10},{8,11},{9,12},{10... | collective-permute-start | bytes 221192 | tf_op jit(solution)/shard_map/ppermute | solution.py:51
  15.8 3.5 %collective-permute-start.13 = (bf16[64,576]{1,0:T(8,128)(2,1)}, bf16[64,576]{1,0:T(8,128)(2,1)}, u32[]{:S(2)}, u32[]{:S(2)}) collective-permute-start(bf16[64,576]{1,0:T(8,128)(2,1)} %constant_dynamic-slice_fusion.1), channel_id=1, source_target_pairs={{0,4},{1,5},{2,6},{3,7},{4,8},{5,9},{6,10},{7,11},{8,12},{9,13},{1... | collective-permute-start | bytes 221192 | tf_op jit(solution)/shard_map/ppermute | solution.py:51
  25.7 1.4 select_reduce_fusion
  28.0 2.1 fusion.122
  30.2 4.4 %collective-permute-done.17 = s32[64,6]{0,1:T(8,128)S(1)} collective-permute-done((s32[64,6]{0,1:T(8,128)S(1)}, s32[64,6]{0,1:T(8,128)S(1)}, u32[]{:S(2)}, u32[]{:S(2)}) %collective-permute-start.17) | collective-permute-done | bytes 1568 | tf_op jit(solution)/shard_map/ppermute | solution.py:35
  35.5 3.6 %collective-permute-done.18 = s32[64,6]{0,1:T(8,128)S(1)} collective-permute-done((s32[64,6]{0,1:T(8,128)S(1)}, s32[64,6]{0,1:T(8,128)S(1)}, u32[]{:S(2)}, u32[]{:S(2)}) %collective-permute-start.18) | collective-permute-done | bytes 1568 | tf_op jit(solution)/shard_map/ppermute | solution.py:35
  40.2 4.8 %collective-permute-done = bf16[64,576]{1,0:T(8,128)(2,1)S(1)} collective-permute-done((bf16[64,576]{1,0:T(8,128)(2,1)}, bf16[64,576]{1,0:T(8,128)(2,1)S(1)}, u32[]{:S(2)}, u32[]{:S(2)}) %collective-permute-start) | collective-permute-done | bytes 73760 | tf_op jit(solution)/shard_map/ppermute | solution.py:35
  45.0 5.3 %collective-permute-done.1 = bf16[64,576]{1,0:T(8,128)(2,1)S(1)} collective-permute-done((bf16[64,576]{1,0:T(8,128)(2,1)S(1)}, bf16[64,576]{1,0:T(8,128)(2,1)S(1)}, u32[]{:S(2)}, u32[]{:S(2)}) %collective-permute-start.1) | collective-permute-done | bytes 73760 | tf_op jit(solution)/shard_map/ppermute | solution.py:35
  50.3 5.3 %collective-permute-done.2 = bf16[64,576]{1,0:T(8,128)(2,1)S(1)} collective-permute-done((bf16[64,576]{1,0:T(8,128)(2,1)S(1)}, bf16[64,576]{1,0:T(8,128)(2,1)S(1)}, u32[]{:S(2)}, u32[]{:S(2)}) %collective-permute-start.2) | collective-permute-done | bytes 73760 | tf_op jit(solution)/shard_map/ppermute | solution.py:35
  57.1 2.0 collective-permute-start.5
  62.8 4.1 %collective-permute-done.4.refs_2_ = bf16[256,576]{1,0:T(8,128)(2,1)S(1)} collective-permute-done((bf16[256,576]{1,0:T(8,128)(2,1)S(1)}, bf16[256,576]{1,0:T(8,128)(2,1)S(1)}, u32[]{:S(2)}, u32[]{:S(2)}) %collective-permute-start.4) | collective-permute-done | bytes 294944 | tf_op jit(solution)/shard_map/ppermute | solution.py:40
  69.0 2.2 copy-done.1
  71.2 1.2 copy-done.2
  72.4 1.2 copy-done.3
  74.6 13.8 %attend.1 = (f32[64,2048]{1,0:T(8,128)S(1)}, bf16[64,2048]{1,0:T(8,128)(2,1)S(1)}) custom-call(s32[128,4]{1,0:T(8,128)S(1)} %copy.61.token_ref, s32[1,2688]{1,0:T(1,128)S(1)} %broadcast_in_dim.95.spot_ref, bf16[128,128]{1,0:T(8,128)(2,1)S(1)} %get-tuple-element.61.order_ref, bf16[128,1536]{1,0:T(8,128)(2,1)S(1)} %copy-done.4, ...), custom_call_target="tpu_custom_call" | custom-call | flops 5989466112 | bytes 12000000 | tf_op jit(solution)/shard_map/attend/pallas_call | solution.py:150
  90.8 1.5 collective-permute-start.19
  93.1 1.2 collective-permute-start.21
  94.6 2.2 collective-permute-done.19
  96.8 3.6 %collective-permute-done.20 = bf16[32,2048]{1,0:T(8,128)(2,1)S(1)} collective-permute-done((bf16[32,2048]{1,0:T(8,128)(2,1)S(1)}, bf16[32,2048]{1,0:T(8,128)(2,1)S(1)}, u32[]{:S(2)}, u32[]{:S(2)}) %collective-permute-start.20) | collective-permute-done | bytes 131104 | tf_op jit(solution)/shard_map/ppermute | solution.py:40
  102.7 1.8 collective-permute-start.48
  104.5 1.4 collective-permute-start.28
  106.1 1.2 collective-permute-done.46
  107.6 2.4 %collective-permute-done.48 = bf16[32,2048]{1,0:T(8,128)(2,1)S(1)} collective-permute-done((bf16[32,2048]{1,0:T(8,128)(2,1)S(1)}, bf16[32,2048]{1,0:T(8,128)(2,1)S(1)}, u32[]{:S(2)}, u32[]{:S(2)}) %collective-permute-start.48) | collective-permute-done | bytes 131104 | tf_op jit(solution)/shard_map/ppermute | solution.py:40
  110.2 3.1 %collective-permute-done.28 = bf16[64,2048]{1,0:T(8,128)(2,1)S(1)} collective-permute-done((bf16[64,2048]{1,0:T(8,128)(2,1)S(1)}, bf16[64,2048]{1,0:T(8,128)(2,1)S(1)}, u32[]{:S(2)}, u32[]{:S(2)}) %collective-permute-start.28) | collective-permute-done | bytes 262176 | tf_op jit(solution)/shard_map/ppermute | solution.py:35
  115.4 1.7 collective-permute-start.40
  117.4 1.9 collective-permute-done.38
  120.3 1.2 collective-permute-done.39
  122.4 1.8 fusion.14
  124.3 2.3 %collective-permute-done.29 = bf16[64,2048]{1,0:T(8,128)(2,1)S(1)} collective-permute-done((bf16[64,2048]{1,0:T(8,128)(2,1)S(1)}, bf16[64,2048]{1,0:T(8,128)(2,1)S(1)}, u32[]{:S(2)}, u32[]{:S(2)}) %collective-permute-start.29) | collective-permute-done | bytes 262176 | tf_op jit(solution)/shard_map/ppermute | solution.py:35
  127.7 1.2 collective-permute-start.30
  129.9 1.2 collective-permute-start.32
  133.2 1.8 fusion.8
  135.0 6.9 %fusion = f32[256,2048]{1,0:T(8,128)} fusion(bf16[1,704,2048]{2,1,0:T(8,128)(2,1)S(1)} %copy-done, f32[256,704]{0,1:T(8,128)} %fusion.8, bf16[256,2048]{1,0:T(8,128)(2,1)} %copy-done.18, bf16[1,2048,704]{1,2,0:T(8,128)(2,1)} %param.29), kind=kOutput, calls=%fused_computation | convolution fusion | flops 1477476352 | bytes 9633792 | tf_op jit(solution)/shard_map/dot_general | solution.py:69
  141.9 2.2 slice.323
  144.2 1.8 pad_maximum_fusion.1
  147.8 1.6 constant_dynamic-update-slice_fusion.14
  151.4 1.8 fusion.10
  153.2 6.9 %fusion.2 = f32[256,2048]{1,0:T(8,128)} fusion(bf16[1,704,2048]{2,1,0:T(8,128)(2,1)S(1)} %copy-done, f32[256,704]{0,1:T(8,128)} %fusion.10, bf16[256,2048]{1,0:T(8,128)(2,1)} %copy-done.17, bf16[1,2048,704]{1,2,0:T(8,128)(2,1)} %param.29), kind=kOutput, calls=%fused_computation.2 | convolution fusion | flops 1477476352 | bytes 9633792 | tf_op jit(solution)/shard_map/dot_general | solution.py:69
  160.2 2.2 slice.324
  162.4 1.5 fusion.45
  164.6 1.2 collective-permute-start.51
  166.9 1.2 collective-permute-start.53
  170.2 1.9 fusion.12
  172.1 7.2 %fusion.4 = f32[256,2048]{1,0:T(8,128)} fusion(bf16[1,704,2048]{2,1,0:T(8,128)(2,1)S(1)} %copy-done, f32[256,704]{0,1:T(8,128)} %fusion.12, bf16[256,2048]{1,0:T(8,128)(2,1)} %copy-done.14, bf16[1,2048,704]{1,2,0:T(8,128)(2,1)} %param.29), kind=kOutput, calls=%fused_computation.4 | convolution fusion | flops 1477476352 | bytes 9633792 | tf_op jit(solution)/shard_map/dot_general | solution.py:69
  179.3 2.3 slice.325
  181.6 2.0 convolution_convert_fusion.6
  187.7 1.3 collective-permute-start.45
  189.0 6.9 %fusion.6 = f32[256,2048]{1,0:T(8,128)} fusion(bf16[1,704,2048]{2,1,0:T(8,128)(2,1)S(1)} %copy-done, f32[256,704]{0,1:T(8,128)} %fusion.14, bf16[256,2048]{1,0:T(8,128)(2,1)} %copy-done.19, bf16[1,2048,704]{1,2,0:T(8,128)(2,1)} %param.29), kind=kOutput, calls=%fused_computation.6 | convolution fusion | flops 1477476352 | bytes 9633792 | tf_op jit(solution)/shard_map/dot_general | solution.py:69
  196.0 1.4 slice.326
  197.6 1.5 fusion.27
  199.1 1.7 collective-permute-start.55
  202.0 1.3 collective-permute-start.35
  204.4 1.2 collective-permute-start.37
  205.7 3.2 %collective-permute-done.55 = bf16[64,2048]{1,0:T(8,128)(2,1)S(1)} collective-permute-done((bf16[64,2048]{1,0:T(8,128)(2,1)S(1)}, bf16[64,2048]{1,0:T(8,128)(2,1)S(1)}, u32[]{:S(2)}, u32[]{:S(2)}) %collective-permute-start.55) | collective-permute-done | bytes 262176 | tf_op jit(solution)/shard_map/ppermute | solution.py:35
  209.0 2.4 %collective-permute-done.36 = bf16[32,2048]{1,0:T(8,128)(2,1)S(1)} collective-permute-done((bf16[32,2048]{1,0:T(8,128)(2,1)S(1)}, bf16[32,2048]{1,0:T(8,128)(2,1)S(1)}, u32[]{:S(2)}, u32[]{:S(2)}) %collective-permute-start.36) | collective-permute-done | bytes 131104 | tf_op jit(solution)/shard_map/ppermute | solution.py:40
  212.9 1.4 collective-permute-start.24
  215.1 1.3 collective-permute-start.26
  216.5 2.8 %collective-permute-done.24 = bf16[32,2048]{1,0:T(8,128)(2,1)S(1)} collective-permute-done((bf16[32,2048]{1,0:T(8,128)(2,1)S(1)}, bf16[32,2048]{1,0:T(8,128)(2,1)S(1)}, u32[]{:S(2)}, u32[]{:S(2)}) %collective-permute-start.24) | collective-permute-done | bytes 131104 | tf_op jit(solution)/shard_map/ppermute | solution.py:40
  219.2 2.1 collective-permute-done.25
  222.0 1.5 collective-permute-done.57
  224.0 1.7 convolution_convert_fusion.5
  (243 shorter events, 51.8 us)
Async XLA Ops:
  0.6 134.4 %copy-start = (bf16[1,704,2048]{2,1,0:T(8,128)(2,1)S(1)}, bf16[1,704,2048]{2,1,0:T(8,128)(2,1)}, u32[]{:S(2)}) copy-start(bf16[1,704,2048]{2,1,0:T(8,128)(2,1)} %param.31) | copy-start | bytes 8650756
  2.5 36.7 %collective-permute-start.10 = (bf16[64,576]{1,0:T(8,128)(2,1)}, bf16[64,576]{1,0:T(8,128)(2,1)}, u32[]{:S(2)}, u32[]{:S(2)}) collective-permute-start(bf16[64,576]{1,0:T(8,128)(2,1)} %constant_dynamic-slice_fusion.1), channel_id=1, source_target_pairs={{0,1},{1,2},{2,3},{3,4},{4,5},{5,6},{6,7},{7,8},{8,9},{9,10},{10,1... | collective-permute-start | bytes 221192 | tf_op jit(solution)/shard_map/ppermute | solution.py:51
  8.0 49.2 %collective-permute-start.11 = (bf16[64,576]{1,0:T(8,128)(2,1)}, bf16[64,576]{1,0:T(8,128)(2,1)}, u32[]{:S(2)}, u32[]{:S(2)}) collective-permute-start(bf16[64,576]{1,0:T(8,128)(2,1)} %constant_dynamic-slice_fusion.1), channel_id=1, source_target_pairs={{0,2},{1,3},{2,4},{3,5},{4,6},{5,7},{6,8},{7,9},{8,10},{9,11},{10,... | collective-permute-start | bytes 221192 | tf_op jit(solution)/shard_map/ppermute | solution.py:51
  11.4 48.7 %collective-permute-start.12 = (bf16[64,576]{1,0:T(8,128)(2,1)}, bf16[64,576]{1,0:T(8,128)(2,1)}, u32[]{:S(2)}, u32[]{:S(2)}) collective-permute-start(bf16[64,576]{1,0:T(8,128)(2,1)} %constant_dynamic-slice_fusion.1), channel_id=1, source_target_pairs={{0,3},{1,4},{2,5},{3,6},{4,7},{5,8},{6,9},{7,10},{8,11},{9,12},{10... | collective-permute-start | bytes 221192 | tf_op jit(solution)/shard_map/ppermute | solution.py:51
  15.8 45.2 %collective-permute-start.13 = (bf16[64,576]{1,0:T(8,128)(2,1)}, bf16[64,576]{1,0:T(8,128)(2,1)}, u32[]{:S(2)}, u32[]{:S(2)}) collective-permute-start(bf16[64,576]{1,0:T(8,128)(2,1)} %constant_dynamic-slice_fusion.1), channel_id=1, source_target_pairs={{0,4},{1,5},{2,6},{3,7},{4,8},{5,9},{6,10},{7,11},{8,12},{9,13},{1... | collective-permute-start | bytes 221192 | tf_op jit(solution)/shard_map/ppermute | solution.py:51
  20.0 10.1 %collective-permute-start.16 = (s32[64,6]{0,1:T(8,128)S(1)}, s32[64,6]{0,1:T(8,128)S(1)}, u32[]{:S(2)}, u32[]{:S(2)}) collective-permute-start(s32[64,6]{0,1:T(8,128)S(1)} %bitcast.152), channel_id=1, source_target_pairs={{0,4},{1,5},{2,6},{3,7},{4,12},{5,13},{6,14},{7,15},{8,0},{9,1},{1... | collective-permute-start | bytes 4616 | tf_op jit(solution)/shard_map/ppermute | solution.py:35
  21.0 13.7 %copy-start.22 = (s32[128]{0:T(128)}, s32[128]{0:T(128)S(1)}, u32[]{:S(2)}) copy-start(s32[128]{0:T(128)S(1)} %fusion.130) | copy-start | bytes 1540
  30.0 4.6 %collective-permute-start.17 = (s32[64,6]{0,1:T(8,128)S(1)}, s32[64,6]{0,1:T(8,128)S(1)}, u32[]{:S(2)}, u32[]{:S(2)}) collective-permute-start(s32[64,6]{0,1:T(8,128)S(1)} %collective-permute-done.16), channel_id=1, source_target_pairs={{0,4},{1,5},{2,6},{3,7},{4,12},{5,13},{6,14},{7,15},{8,0},{9,1},{1... | collective-permute-start | bytes 4616 | tf_op jit(solution)/shard_map/ppermute | solution.py:35
  34.6 4.5 %collective-permute-start.18 = (s32[64,6]{0,1:T(8,128)S(1)}, s32[64,6]{0,1:T(8,128)S(1)}, u32[]{:S(2)}, u32[]{:S(2)}) collective-permute-start(s32[64,6]{0,1:T(8,128)S(1)} %collective-permute-done.17), channel_id=1, source_target_pairs={{0,4},{1,5},{2,6},{3,7},{4,12},{5,13},{6,14},{7,15},{8,0},{9,1},{1... | collective-permute-start | bytes 4616 | tf_op jit(solution)/shard_map/ppermute | solution.py:35
  39.2 5.8 %collective-permute-start = (bf16[64,576]{1,0:T(8,128)(2,1)}, bf16[64,576]{1,0:T(8,128)(2,1)S(1)}, u32[]{:S(2)}, u32[]{:S(2)}) collective-permute-start(bf16[64,576]{1,0:T(8,128)(2,1)} %param.23), channel_id=1, source_target_pairs={{0,4},{1,5},{2,6},{3,7},{4,12},{5,13},{6,14},{7,15},{8,0},{9,1},{1... | collective-permute-start | bytes 221192 | tf_op jit(solution)/shard_map/ppermute | solution.py:35
  44.9 5.3 %collective-permute-start.1 = (bf16[64,576]{1,0:T(8,128)(2,1)S(1)}, bf16[64,576]{1,0:T(8,128)(2,1)S(1)}, u32[]{:S(2)}, u32[]{:S(2)}) collective-permute-start(bf16[64,576]{1,0:T(8,128)(2,1)S(1)} %collective-permute-done), channel_id=1, source_target_pairs={{0,4},{1,5},{2,6},{3,7},{4,12},{5,13},{6,14},{7,15},{8,0},{9,1},{1... | collective-permute-start | bytes 221192 | tf_op jit(solution)/shard_map/ppermute | solution.py:35
  50.3 5.3 %collective-permute-start.2 = (bf16[64,576]{1,0:T(8,128)(2,1)S(1)}, bf16[64,576]{1,0:T(8,128)(2,1)S(1)}, u32[]{:S(2)}, u32[]{:S(2)}) collective-permute-start(bf16[64,576]{1,0:T(8,128)(2,1)S(1)} %collective-permute-done.1), channel_id=1, source_target_pairs={{0,4},{1,5},{2,6},{3,7},{4,12},{5,13},{6,14},{7,15},{8,0},{9,1},{1... | collective-permute-start | bytes 221192 | tf_op jit(solution)/shard_map/ppermute | solution.py:35
  55.6 7.1 %collective-permute-start.3 = (bf16[256,576]{1,0:T(8,128)(2,1)S(1)}, bf16[256,576]{1,0:T(8,128)(2,1)S(1)}, u32[]{:S(2)}, u32[]{:S(2)}) collective-permute-start(bf16[256,576]{1,0:T(8,128)(2,1)S(1)} %constant_dynamic-update-slice_fusion.refs_0_), channel_id=1, source_target_pairs={{0,1},{1,0},{2,3},{3,2},{4,5},{5,4},{6,7},{7,6},{8,9},{9,8},{10,11... | collective-permute-start | bytes 884744 | tf_op jit(solution)/shard_map/ppermute | solution.py:40
  56.3 10.6 %collective-permute-start.4 = (bf16[256,576]{1,0:T(8,128)(2,1)S(1)}, bf16[256,576]{1,0:T(8,128)(2,1)S(1)}, u32[]{:S(2)}, u32[]{:S(2)}) collective-permute-start(bf16[256,576]{1,0:T(8,128)(2,1)S(1)} %constant_dynamic-update-slice_fusion.refs_0_), channel_id=1, source_target_pairs={{0,2},{1,3},{2,0},{3,1},{4,6},{5,7},{6,4},{7,5},{8,10},{9,11},{10,... | collective-permute-start | bytes 884744 | tf_op jit(solution)/shard_map/ppermute | solution.py:40
  57.1 9.7 %collective-permute-start.5 = (bf16[256,576]{1,0:T(8,128)(2,1)S(1)}, bf16[256,576]{1,0:T(8,128)(2,1)S(1)}, u32[]{:S(2)}, u32[]{:S(2)}) collective-permute-start(bf16[256,576]{1,0:T(8,128)(2,1)S(1)} %constant_dynamic-update-slice_fusion.refs_0_), channel_id=1, source_target_pairs={{0,3},{1,2},{2,1},{3,0},{4,7},{5,6},{6,5},{7,4},{8,11},{9,10},{10,... | collective-permute-start | bytes 884744 | tf_op jit(solution)/shard_map/ppermute | solution.py:40
  61.9 5.7 %collective-permute-start.14 = (bf16[256,576]{1,0:T(8,128)(2,1)S(1)}, bf16[256,576]{1,0:T(8,128)(2,1)S(1)}, u32[]{:S(2)}, u32[]{:S(2)}) collective-permute-start(bf16[256,576]{1,0:T(8,128)(2,1)S(1)} %constant_dynamic-update-slice_fusion.4.refs_8_), channel_id=1, source_target_pairs={{0,16},{16,0},{1,17},{17,1},{2,18},{18,2},{3,19},{19,3},{4,20},{20... | collective-permute-start | bytes 884744 | tf_op jit(solution)/shard_map/ppermute | solution.py:45
  62.0 5.6 %collective-permute-start.6 = (bf16[256,576]{1,0:T(8,128)(2,1)S(1)}, bf16[256,576]{1,0:T(8,128)(2,1)S(1)}, u32[]{:S(2)}, u32[]{:S(2)}) collective-permute-start(bf16[256,576]{1,0:T(8,128)(2,1)S(1)} %constant_dynamic-update-slice_fusion.refs_0_), channel_id=1, source_target_pairs={{0,16},{16,0},{1,17},{17,1},{2,18},{18,2},{3,19},{19,3},{4,20},{20... | collective-permute-start | bytes 884744 | tf_op jit(solution)/shard_map/ppermute | solution.py:45
  62.8 4.8 %collective-permute-start.7 = (bf16[256,576]{1,0:T(8,128)(2,1)S(1)}, bf16[256,576]{1,0:T(8,128)(2,1)S(1)}, u32[]{:S(2)}, u32[]{:S(2)}) collective-permute-start(bf16[256,576]{1,0:T(8,128)(2,1)S(1)} %collective-permute-done.3.refs_1_), channel_id=1, source_target_pairs={{0,16},{16,0},{1,17},{17,1},{2,18},{18,2},{3,19},{19,3},{4,20},{20... | collective-permute-start | bytes 884744 | tf_op jit(solution)/shard_map/ppermute | solution.py:45
  66.9 1.6 collective-permute-start.8
  66.9 2.1 collective-permute-start.9
  74.6 15.4 %copy-start.5 = (f32[64,2048]{1,0:T(8,128)S(1)}, f32[64,2048]{1,0:T(8,128)}, u32[]{:S(2)}) copy-start(f32[64,2048]{1,0:T(8,128)} %fusion.122) | copy-start | bytes 1572868
  88.4 1.6 collective-permute-start.15
  90.4 10.2 %collective-permute-start.27 = (bf16[64,2048]{1,0:T(8,128)(2,1)S(1)}, bf16[64,2048]{1,0:T(8,128)(2,1)S(1)}, u32[]{:S(2)}, u32[]{:S(2)}) collective-permute-start(bf16[64,2048]{1,0:T(8,128)(2,1)S(1)} %fusion.54), channel_id=1, source_target_pairs={{0,4},{1,5},{2,6},{3,7},{4,12},{5,13},{6,14},{7,15},{8,0},{9,1},{1... | collective-permute-start | bytes 786440 | tf_op jit(solution)/shard_map/ppermute | solution.py:35
  90.8 6.0 %collective-permute-start.19 = (bf16[32,2048]{1,0:T(8,128)(2,1)S(1)}, bf16[32,2048]{1,0:T(8,128)(2,1)S(1)}, u32[]{:S(2)}, u32[]{:S(2)}) collective-permute-start(bf16[32,2048]{1,0:T(8,128)(2,1)S(1)} %get-tuple-element.54), channel_id=1, source_target_pairs={{0,1},{1,0},{2,3},{3,2},{4,5},{5,4},{6,7},{7,6},{8,9},{9,8},{10,11... | collective-permute-start | bytes 393224 | tf_op jit(solution)/shard_map/ppermute | solution.py:40
  92.3 8.1 %collective-permute-start.20 = (bf16[32,2048]{1,0:T(8,128)(2,1)S(1)}, bf16[32,2048]{1,0:T(8,128)(2,1)S(1)}, u32[]{:S(2)}, u32[]{:S(2)}) collective-permute-start(bf16[32,2048]{1,0:T(8,128)(2,1)S(1)} %get-tuple-element.53), channel_id=1, source_target_pairs={{0,2},{1,3},{2,0},{3,1},{4,6},{5,7},{6,4},{7,5},{8,10},{9,11},{10,... | collective-permute-start | bytes 393224 | tf_op jit(solution)/shard_map/ppermute | solution.py:40
  93.1 7.2 %collective-permute-start.21 = (bf16[32,2048]{1,0:T(8,128)(2,1)S(1)}, bf16[32,2048]{1,0:T(8,128)(2,1)S(1)}, u32[]{:S(2)}, u32[]{:S(2)}) collective-permute-start(bf16[32,2048]{1,0:T(8,128)(2,1)S(1)} %get-tuple-element.52), channel_id=1, source_target_pairs={{0,3},{1,2},{2,1},{3,0},{4,7},{5,6},{6,5},{7,4},{8,11},{9,10},{10,... | collective-permute-start | bytes 393224 | tf_op jit(solution)/shard_map/ppermute | solution.py:40
  100.4 21.9 %collective-permute-start.22 = (bf16[128,2048]{1,0:T(8,128)(2,1)S(1)}, bf16[128,2048]{1,0:T(8,128)(2,1)S(1)}, u32[]{:S(2)}, u32[]{:S(2)}) collective-permute-start(bf16[128,2048]{1,0:T(8,128)(2,1)S(1)} %pad_maximum_fusion), channel_id=1, source_target_pairs={{0,16},{16,0},{1,17},{17,1},{2,18},{18,2},{3,19},{19,3},{4,20},{20... | collective-permute-start | bytes 1572872 | tf_op jit(solution)/shard_map/ppermute | solution.py:45
  100.9 6.4 %collective-permute-start.46 = (bf16[32,2048]{1,0:T(8,128)(2,1)S(1)}, bf16[32,2048]{1,0:T(8,128)(2,1)S(1)}, u32[]{:S(2)}, u32[]{:S(2)}) collective-permute-start(bf16[32,2048]{1,0:T(8,128)(2,1)S(1)} %get-tuple-element.27), channel_id=1, source_target_pairs={{0,1},{1,0},{2,3},{3,2},{4,5},{5,4},{6,7},{7,6},{8,9},{9,8},{10,11... | collective-permute-start | bytes 393224 | tf_op jit(solution)/shard_map/ppermute | solution.py:40
  101.6 6.0 %collective-permute-start.47 = (bf16[32,2048]{1,0:T(8,128)(2,1)S(1)}, bf16[32,2048]{1,0:T(8,128)(2,1)S(1)}, u32[]{:S(2)}, u32[]{:S(2)}) collective-permute-start(bf16[32,2048]{1,0:T(8,128)(2,1)S(1)} %get-tuple-element.26), channel_id=1, source_target_pairs={{0,2},{1,3},{2,0},{3,1},{4,6},{5,7},{6,4},{7,5},{8,10},{9,11},{10,... | collective-permute-start | bytes 393224 | tf_op jit(solution)/shard_map/ppermute | solution.py:40
  102.7 7.3 %collective-permute-start.48 = (bf16[32,2048]{1,0:T(8,128)(2,1)S(1)}, bf16[32,2048]{1,0:T(8,128)(2,1)S(1)}, u32[]{:S(2)}, u32[]{:S(2)}) collective-permute-start(bf16[32,2048]{1,0:T(8,128)(2,1)S(1)} %get-tuple-element.25), channel_id=1, source_target_pairs={{0,3},{1,2},{2,1},{3,0},{4,7},{5,6},{6,5},{7,4},{8,11},{9,10},{10,... | collective-permute-start | bytes 393224 | tf_op jit(solution)/shard_map/ppermute | solution.py:40
  104.5 8.8 %collective-permute-start.28 = (bf16[64,2048]{1,0:T(8,128)(2,1)S(1)}, bf16[64,2048]{1,0:T(8,128)(2,1)S(1)}, u32[]{:S(2)}, u32[]{:S(2)}) collective-permute-start(bf16[64,2048]{1,0:T(8,128)(2,1)S(1)} %collective-permute-done.27), channel_id=1, source_target_pairs={{0,4},{1,5},{2,6},{3,7},{4,12},{5,13},{6,14},{7,15},{8,0},{9,1},{1... | collective-permute-start | bytes 786440 | tf_op jit(solution)/shard_map/ppermute | solution.py:35
  110.1 22.0 %collective-permute-start.49 = (bf16[128,2048]{1,0:T(8,128)(2,1)S(1)}, bf16[128,2048]{1,0:T(8,128)(2,1)S(1)}, u32[]{:S(2)}, u32[]{:S(2)}) collective-permute-start(bf16[128,2048]{1,0:T(8,128)(2,1)S(1)} %pad_maximum_fusion.3), channel_id=1, source_target_pairs={{0,16},{16,0},{1,17},{17,1},{2,18},{18,2},{3,19},{19,3},{4,20},{20... | collective-permute-start | bytes 1572872 | tf_op jit(solution)/shard_map/ppermute | solution.py:45
  113.6 5.7 %collective-permute-start.38 = (bf16[32,2048]{1,0:T(8,128)(2,1)S(1)}, bf16[32,2048]{1,0:T(8,128)(2,1)S(1)}, u32[]{:S(2)}, u32[]{:S(2)}) collective-permute-start(bf16[32,2048]{1,0:T(8,128)(2,1)S(1)} %get-tuple-element.36), channel_id=1, source_target_pairs={{0,1},{1,0},{2,3},{3,2},{4,5},{5,4},{6,7},{7,6},{8,9},{9,8},{10,11... | collective-permute-start | bytes 393224 | tf_op jit(solution)/shard_map/ppermute | solution.py:40
  114.2 7.3 %collective-permute-start.39 = (bf16[32,2048]{1,0:T(8,128)(2,1)S(1)}, bf16[32,2048]{1,0:T(8,128)(2,1)S(1)}, u32[]{:S(2)}, u32[]{:S(2)}) collective-permute-start(bf16[32,2048]{1,0:T(8,128)(2,1)S(1)} %get-tuple-element.35), channel_id=1, source_target_pairs={{0,2},{1,3},{2,0},{3,1},{4,6},{5,7},{6,4},{7,5},{8,10},{9,11},{10,... | collective-permute-start | bytes 393224 | tf_op jit(solution)/shard_map/ppermute | solution.py:40
  115.4 6.1 %collective-permute-start.40 = (bf16[32,2048]{1,0:T(8,128)(2,1)S(1)}, bf16[32,2048]{1,0:T(8,128)(2,1)S(1)}, u32[]{:S(2)}, u32[]{:S(2)}) collective-permute-start(bf16[32,2048]{1,0:T(8,128)(2,1)S(1)} %get-tuple-element.34), channel_id=1, source_target_pairs={{0,3},{1,2},{2,1},{3,0},{4,7},{5,6},{6,5},{7,4},{8,11},{9,10},{10,... | collective-permute-start | bytes 393224 | tf_op jit(solution)/shard_map/ppermute | solution.py:40
  119.3 7.3 %collective-permute-start.29 = (bf16[64,2048]{1,0:T(8,128)(2,1)S(1)}, bf16[64,2048]{1,0:T(8,128)(2,1)S(1)}, u32[]{:S(2)}, u32[]{:S(2)}) collective-permute-start(bf16[64,2048]{1,0:T(8,128)(2,1)S(1)} %collective-permute-done.28), channel_id=1, source_target_pairs={{0,4},{1,5},{2,6},{3,7},{4,12},{5,13},{6,14},{7,15},{8,0},{9,1},{1... | collective-permute-start | bytes 786440 | tf_op jit(solution)/shard_map/ppermute | solution.py:35
  122.3 27.0 %collective-permute-start.41 = (bf16[128,2048]{1,0:T(8,128)(2,1)}, bf16[128,2048]{1,0:T(8,128)(2,1)}, u32[]{:S(2)}, u32[]{:S(2)}) collective-permute-start(bf16[128,2048]{1,0:T(8,128)(2,1)} %pad_maximum_fusion.2), channel_id=1, source_target_pairs={{0,16},{16,0},{1,17},{17,1},{2,18},{18,2},{3,19},{19,3},{4,20},{20... | collective-permute-start | bytes 1572872 | tf_op jit(solution)/shard_map/ppermute | solution.py:45
  127.7 16.5 %collective-permute-start.30 = (bf16[32,2048]{1,0:T(8,128)(2,1)}, bf16[32,2048]{1,0:T(8,128)(2,1)S(1)}, u32[]{:S(2)}, u32[]{:S(2)}) collective-permute-start(bf16[32,2048]{1,0:T(8,128)(2,1)} %get-tuple-element.45), channel_id=1, source_target_pairs={{0,1},{1,0},{2,3},{3,2},{4,5},{5,4},{6,7},{7,6},{8,9},{9,8},{10,11... | collective-permute-start | bytes 393224 | tf_op jit(solution)/shard_map/ppermute | solution.py:40
  128.8 15.3 %collective-permute-start.31 = (bf16[32,2048]{1,0:T(8,128)(2,1)}, bf16[32,2048]{1,0:T(8,128)(2,1)S(1)}, u32[]{:S(2)}, u32[]{:S(2)}) collective-permute-start(bf16[32,2048]{1,0:T(8,128)(2,1)} %get-tuple-element.44), channel_id=1, source_target_pairs={{0,2},{1,3},{2,0},{3,1},{4,6},{5,7},{6,4},{7,5},{8,10},{9,11},{10,... | collective-permute-start | bytes 393224 | tf_op jit(solution)/shard_map/ppermute | solution.py:40
  129.9 14.2 %collective-permute-start.32 = (bf16[32,2048]{1,0:T(8,128)(2,1)}, bf16[32,2048]{1,0:T(8,128)(2,1)}, u32[]{:S(2)}, u32[]{:S(2)}) collective-permute-start(bf16[32,2048]{1,0:T(8,128)(2,1)} %get-tuple-element.43), channel_id=1, source_target_pairs={{0,3},{1,2},{2,1},{3,0},{4,7},{5,6},{6,5},{7,4},{8,11},{9,10},{10,... | collective-permute-start | bytes 393224 | tf_op jit(solution)/shard_map/ppermute | solution.py:40
  144.2 18.3 %collective-permute-start.50 = (bf16[128,2048]{1,0:T(8,128)(2,1)}, bf16[128,2048]{1,0:T(8,128)(2,1)}, u32[]{:S(2)}, u32[]{:S(2)}) collective-permute-start(bf16[128,2048]{1,0:T(8,128)(2,1)} %slice.323), channel_id=1, source_target_pairs={{0,16},{16,0},{1,17},{17,1},{2,18},{18,2},{3,19},{19,3},{4,20},{20... | collective-permute-start | bytes 1572872 | tf_op jit(solution)/shard_map/ppermute | solution.py:45
  146.0 22.2 %collective-permute-start.33 = (bf16[128,2048]{1,0:T(8,128)(2,1)}, bf16[128,2048]{1,0:T(8,128)(2,1)}, u32[]{:S(2)}, u32[]{:S(2)}) collective-permute-start(bf16[128,2048]{1,0:T(8,128)(2,1)} %pad_maximum_fusion.1), channel_id=1, source_target_pairs={{0,16},{16,0},{1,17},{17,1},{2,18},{18,2},{3,19},{19,3},{4,20},{20... | collective-permute-start | bytes 1572872 | tf_op jit(solution)/shard_map/ppermute | solution.py:45
  162.4 21.2 %collective-permute-start.42 = (bf16[128,2048]{1,0:T(8,128)(2,1)}, bf16[128,2048]{1,0:T(8,128)(2,1)}, u32[]{:S(2)}, u32[]{:S(2)}) collective-permute-start(bf16[128,2048]{1,0:T(8,128)(2,1)} %slice.324), channel_id=1, source_target_pairs={{0,16},{16,0},{1,17},{17,1},{2,18},{18,2},{3,19},{19,3},{4,20},{20... | collective-permute-start | bytes 1572872 | tf_op jit(solution)/shard_map/ppermute | solution.py:45
  164.6 16.9 %collective-permute-start.51 = (bf16[32,2048]{1,0:T(8,128)(2,1)}, bf16[32,2048]{1,0:T(8,128)(2,1)}, u32[]{:S(2)}, u32[]{:S(2)}) collective-permute-start(bf16[32,2048]{1,0:T(8,128)(2,1)} %get-tuple-element.22), channel_id=1, source_target_pairs={{0,1},{1,0},{2,3},{3,2},{4,5},{5,4},{6,7},{7,6},{8,9},{9,8},{10,11... | collective-permute-start | bytes 393224 | tf_op jit(solution)/shard_map/ppermute | solution.py:40
  165.8 15.7 %collective-permute-start.52 = (bf16[32,2048]{1,0:T(8,128)(2,1)}, bf16[32,2048]{1,0:T(8,128)(2,1)}, u32[]{:S(2)}, u32[]{:S(2)}) collective-permute-start(bf16[32,2048]{1,0:T(8,128)(2,1)} %get-tuple-element.21), channel_id=1, source_target_pairs={{0,2},{1,3},{2,0},{3,1},{4,6},{5,7},{6,4},{7,5},{8,10},{9,11},{10,... | collective-permute-start | bytes 393224 | tf_op jit(solution)/shard_map/ppermute | solution.py:40
  166.9 14.6 %collective-permute-start.53 = (bf16[32,2048]{1,0:T(8,128)(2,1)S(1)}, bf16[32,2048]{1,0:T(8,128)(2,1)}, u32[]{:S(2)}, u32[]{:S(2)}) collective-permute-start(bf16[32,2048]{1,0:T(8,128)(2,1)S(1)} %get-tuple-element.20), channel_id=1, source_target_pairs={{0,3},{1,2},{2,1},{3,0},{4,7},{5,6},{6,5},{7,4},{8,11},{9,10},{10,... | collective-permute-start | bytes 393224 | tf_op jit(solution)/shard_map/ppermute | solution.py:40
  181.5 19.3 %collective-permute-start.34 = (bf16[128,2048]{1,0:T(8,128)(2,1)}, bf16[128,2048]{1,0:T(8,128)(2,1)}, u32[]{:S(2)}, u32[]{:S(2)}) collective-permute-start(bf16[128,2048]{1,0:T(8,128)(2,1)} %slice.325), channel_id=1, source_target_pairs={{0,16},{16,0},{1,17},{17,1},{2,18},{18,2},{3,19},{19,3},{4,20},{20... | collective-permute-start | bytes 1572872 | tf_op jit(solution)/shard_map/ppermute | solution.py:45
  183.6 13.8 %collective-permute-start.54 = (bf16[64,2048]{1,0:T(8,128)(2,1)}, bf16[64,2048]{1,0:T(8,128)(2,1)}, u32[]{:S(2)}, u32[]{:S(2)}) collective-permute-start(bf16[64,2048]{1,0:T(8,128)(2,1)} %convolution_convert_fusion.6), channel_id=1, source_target_pairs={{0,4},{1,5},{2,6},{3,7},{4,12},{5,13},{6,14},{7,15},{8,0},{9,1},{1... | collective-permute-start | bytes 786440 | tf_op jit(solution)/shard_map/ppermute | solution.py:35
  185.5 12.0 %collective-permute-start.43 = (bf16[32,2048]{1,0:T(8,128)(2,1)}, bf16[32,2048]{1,0:T(8,128)(2,1)}, u32[]{:S(2)}, u32[]{:S(2)}) collective-permute-start(bf16[32,2048]{1,0:T(8,128)(2,1)} %get-tuple-element.31), channel_id=1, source_target_pairs={{0,1},{1,0},{2,3},{3,2},{4,5},{5,4},{6,7},{7,6},{8,9},{9,8},{10,11... | collective-permute-start | bytes 393224 | tf_op jit(solution)/shard_map/ppermute | solution.py:40
  186.7 10.9 %collective-permute-start.44 = (bf16[32,2048]{1,0:T(8,128)(2,1)}, bf16[32,2048]{1,0:T(8,128)(2,1)}, u32[]{:S(2)}, u32[]{:S(2)}) collective-permute-start(bf16[32,2048]{1,0:T(8,128)(2,1)} %get-tuple-element.30), channel_id=1, source_target_pairs={{0,2},{1,3},{2,0},{3,1},{4,6},{5,7},{6,4},{7,5},{8,10},{9,11},{10,... | collective-permute-start | bytes 393224 | tf_op jit(solution)/shard_map/ppermute | solution.py:40
  187.7 9.8 %collective-permute-start.45 = (bf16[32,2048]{1,0:T(8,128)(2,1)S(1)}, bf16[32,2048]{1,0:T(8,128)(2,1)}, u32[]{:S(2)}, u32[]{:S(2)}) collective-permute-start(bf16[32,2048]{1,0:T(8,128)(2,1)S(1)} %get-tuple-element.29), channel_id=1, source_target_pairs={{0,3},{1,2},{2,1},{3,0},{4,7},{5,6},{6,5},{7,4},{8,11},{9,10},{10,... | collective-permute-start | bytes 393224 | tf_op jit(solution)/shard_map/ppermute | solution.py:40
  197.4 8.2 %collective-permute-start.23 = (bf16[128,2048]{1,0:T(8,128)(2,1)S(1)}, bf16[128,2048]{1,0:T(8,128)(2,1)S(1)}, u32[]{:S(2)}, u32[]{:S(2)}) collective-permute-start(bf16[128,2048]{1,0:T(8,128)(2,1)S(1)} %slice.326), channel_id=1, source_target_pairs={{0,16},{16,0},{1,17},{17,1},{2,18},{18,2},{3,19},{19,3},{4,20},{20... | collective-permute-start | bytes 1572872 | tf_op jit(solution)/shard_map/ppermute | solution.py:45
  197.5 26.4 %slice-start = ((s8[6291456]{0:T(1024)(128)(4,1)}), s8[4194304]{0:T(1024)(128)(4,1)S(1)}, s32[]{:S(2)}) async-start(s8[6291456]{0:T(1024)(128)(4,1)} %bitcast.141), calls=%async_computation | async-start | bytes 8388608
  199.1 9.8 %collective-permute-start.55 = (bf16[64,2048]{1,0:T(8,128)(2,1)S(1)}, bf16[64,2048]{1,0:T(8,128)(2,1)S(1)}, u32[]{:S(2)}, u32[]{:S(2)}) collective-permute-start(bf16[64,2048]{1,0:T(8,128)(2,1)S(1)} %fusion.27), channel_id=1, source_target_pairs={{0,4},{1,5},{2,6},{3,7},{4,12},{5,13},{6,14},{7,15},{8,0},{9,1},{1... | collective-permute-start | bytes 786440 | tf_op jit(solution)/shard_map/ppermute | solution.py:35
  202.0 14.5 %copy-start.20 = (bf16[2048]{0:T(1024)(128)(2,1)S(1)}, bf16[2048]{0:T(1024)(128)(2,1)}, u32[]{:S(2)}) copy-start(bf16[2048]{0:T(1024)(128)(2,1)} %param.32) | copy-start | bytes 12292
  202.0 6.9 %collective-permute-start.35 = (bf16[32,2048]{1,0:T(8,128)(2,1)S(1)}, bf16[32,2048]{1,0:T(8,128)(2,1)S(1)}, u32[]{:S(2)}, u32[]{:S(2)}) collective-permute-start(bf16[32,2048]{1,0:T(8,128)(2,1)S(1)} %get-tuple-element.40), channel_id=1, source_target_pairs={{0,1},{1,0},{2,3},{3,2},{4,5},{5,4},{6,7},{7,6},{8,9},{9,8},{10,11... | collective-permute-start | bytes 393224 | tf_op jit(solution)/shard_map/ppermute | solution.py:40
  203.3 8.1 %collective-permute-start.36 = (bf16[32,2048]{1,0:T(8,128)(2,1)S(1)}, bf16[32,2048]{1,0:T(8,128)(2,1)S(1)}, u32[]{:S(2)}, u32[]{:S(2)}) collective-permute-start(bf16[32,2048]{1,0:T(8,128)(2,1)S(1)} %get-tuple-element.39), channel_id=1, source_target_pairs={{0,2},{1,3},{2,0},{3,1},{4,6},{5,7},{6,4},{7,5},{8,10},{9,11},{10,... | collective-permute-start | bytes 393224 | tf_op jit(solution)/shard_map/ppermute | solution.py:40
  204.4 19.6 %slice-start.1 = ((s8[6291456]{0:T(1024)(128)(4,1)}), s8[2097152]{0:T(1024)(128)(4,1)S(1)}, s32[]{:S(2)}) async-start(s8[6291456]{0:T(1024)(128)(4,1)} %bitcast.141), calls=%async_computation.1 | async-start | bytes 4194304
  204.4 7.0 %collective-permute-start.37 = (bf16[32,2048]{1,0:T(8,128)(2,1)S(1)}, bf16[32,2048]{1,0:T(8,128)(2,1)S(1)}, u32[]{:S(2)}, u32[]{:S(2)}) collective-permute-start(bf16[32,2048]{1,0:T(8,128)(2,1)S(1)} %get-tuple-element.38), channel_id=1, source_target_pairs={{0,3},{1,2},{2,1},{3,0},{4,7},{5,6},{6,5},{7,4},{8,11},{9,10},{10,... | collective-permute-start | bytes 393224 | tf_op jit(solution)/shard_map/ppermute | solution.py:40
  211.7 9.7 %collective-permute-start.56 = (bf16[64,2048]{1,0:T(8,128)(2,1)S(1)}, bf16[64,2048]{1,0:T(8,128)(2,1)S(1)}, u32[]{:S(2)}, u32[]{:S(2)}) collective-permute-start(bf16[64,2048]{1,0:T(8,128)(2,1)S(1)} %fusion.26), channel_id=1, source_target_pairs={{0,4},{1,5},{2,6},{3,7},{4,12},{5,13},{6,14},{7,15},{8,0},{9,1},{1... | collective-permute-start | bytes 786440 | tf_op jit(solution)/shard_map/ppermute | solution.py:35
  212.9 6.3 %collective-permute-start.24 = (bf16[32,2048]{1,0:T(8,128)(2,1)S(1)}, bf16[32,2048]{1,0:T(8,128)(2,1)S(1)}, u32[]{:S(2)}, u32[]{:S(2)}) collective-permute-start(bf16[32,2048]{1,0:T(8,128)(2,1)S(1)} %get-tuple-element.49), channel_id=1, source_target_pairs={{0,1},{1,0},{2,3},{3,2},{4,5},{5,4},{6,7},{7,6},{8,9},{9,8},{10,11... | collective-permute-start | bytes 393224 | tf_op jit(solution)/shard_map/ppermute | solution.py:40
  214.3 7.1 %collective-permute-start.25 = (bf16[32,2048]{1,0:T(8,128)(2,1)S(1)}, bf16[32,2048]{1,0:T(8,128)(2,1)S(1)}, u32[]{:S(2)}, u32[]{:S(2)}) collective-permute-start(bf16[32,2048]{1,0:T(8,128)(2,1)S(1)} %get-tuple-element.48), channel_id=1, source_target_pairs={{0,2},{1,3},{2,0},{3,1},{4,6},{5,7},{6,4},{7,5},{8,10},{9,11},{10,... | collective-permute-start | bytes 393224 | tf_op jit(solution)/shard_map/ppermute | solution.py:40
  215.1 6.2 %collective-permute-start.26 = (bf16[32,2048]{1,0:T(8,128)(2,1)S(1)}, bf16[32,2048]{1,0:T(8,128)(2,1)S(1)}, u32[]{:S(2)}, u32[]{:S(2)}) collective-permute-start(bf16[32,2048]{1,0:T(8,128)(2,1)S(1)} %get-tuple-element.47), channel_id=1, source_target_pairs={{0,3},{1,2},{2,1},{3,0},{4,7},{5,6},{6,5},{7,4},{8,11},{9,10},{10,... | collective-permute-start | bytes 393224 | tf_op jit(solution)/shard_map/ppermute | solution.py:40
  221.9 1.6 collective-permute-start.57
  (23 other events, 127.2 us)

commit v2 on v1

v2 whole, which is shorter than its diff:
```python
import functools
import math

import jax
import jax.numpy as jnp
from jax import lax
from jax.experimental import pallas as pl
from jax.experimental.pallas import tpu as pltpu
from jax.sharding import PartitionSpec as P

NOPE = 128
ROPE = 64
LAT = 512
PAGE = 8
PLANE = 4
ROUTE_ROWS = 16

VERY_NEGATIVE = -1e30
ROUTE_SCALING = 2.446
NORM_EPSILON = 1e-06


def ring_order(count):
    odd = list(range(1, count, 2))
    even = list(range(2, count, 2))
    return [0] + odd + even[::-1]


def send_ring(block, count, steps=1):
    order = ring_order(count)
    after = {order[i]: order[(i + steps) % count] for i in range(count)}
    route = [
        (z * PLANE + p, after[z] * PLANE + p) for z in range(count) for p in range(PLANE)
    ]
    return lax.ppermute(block, "tensor", route)


def send_round(block, distance):
    count = lax.axis_size("tensor")
    return lax.ppermute(block, "tensor", [(i, (i + distance) % count) for i in range(count)])


def send_plane(block, distance):
    devices = range(lax.axis_size("tensor"))
    return lax.ppermute(block, "tensor", [(i, i ^ distance) for i in devices])


def send_group(block, distance):
    devices = range(lax.axis_size("group"))
    return lax.ppermute(block, "group", [(i, i ^ distance) for i in devices])


def norm_rows(row_block, gain_vector):
    values = row_block.astype(jnp.float32)
    mean_square = jnp.mean(values * values, axis=-1, keepdims=True)
    return (
        values * lax.rsqrt(mean_square + NORM_EPSILON) * gain_vector.astype(jnp.float32)
    ).astype(jnp.bfloat16)


def dot_t(left, right):
    return lax.dot_general(
        left, right, (((1,), (1,)), ((), ())), preferred_element_type=jnp.float32
    )


def dot_f(left, right):
    return jnp.dot(left, right, preferred_element_type=jnp.float32)


def whole(array):
    return pl.BlockSpec(array.shape, lambda *i: (0,) * len(array.shape))


def after(kernel, count):
    def inner(*refs):
        kernel(*refs[count:])

    return inner


def unread(arrays):
    return [pl.BlockSpec(memory_space=pl.ANY) for _ in arrays]


def call(kernel, name, inputs, outputs, flops, limit=12, ready=()):
    shapes = [jax.ShapeDtypeStruct(shape, dtype) for shape, dtype in outputs]
    moved = sum(a.size * a.dtype.itemsize for a in list(inputs) + shapes)
    return pl.pallas_call(
        after(kernel, len(ready)),
        grid=(1,),
        in_specs=unread(ready) + [whole(a) for a in inputs],
        out_specs=[whole(s) for s in shapes],
        out_shape=shapes,
        compiler_params=pltpu.CompilerParams(vmem_limit_bytes=limit * 1024 * 1024),
        cost_estimate=pl.CostEstimate(flops=flops, bytes_accessed=moved, transcendentals=0),
        name=name,
    )(*ready, *inputs)


def join_share(piece, suffix_columns, routes_columns, tok_quarter):
    rows = piece.shape[0]
    tokens = suffix_columns.shape[1]
    top, groups, _ = routes_columns.shape

    def kernel(piece_ref, suffix_ref, routes_ref, near_ref, full_ref, lite_ref):
        group_index = lax.axis_index("group")
        shape = (tok_quarter, tokens)
        row = lax.broadcasted_iota(jnp.int32, shape, 0)
        token = lax.broadcasted_iota(jnp.int32, shape, 1)
        select = jnp.where(token == group_index * tok_quarter + row, 1.0, 0.0)
        share = dot_t(select.astype(jnp.bfloat16), suffix_ref[...]).astype(jnp.bfloat16)
        named = jnp.zeros((top, tok_quarter), jnp.float32)
        for j in range(groups):
            part = routes_ref[:, j, :].astype(jnp.float32)
            named = jnp.where(group_index == j, part, named)
        named = jnp.concatenate(
            [named, jnp.zeros((ROUTE_ROWS - top, tok_quarter), jnp.float32)], axis=0
        )
        named = jnp.concatenate(
            [named, jnp.zeros((ROUTE_ROWS, piece_ref.shape[1] - tok_quarter), jnp.float32)], axis=1
        ).astype(jnp.bfloat16)
        piece = piece_ref[...]
        near_ref[:rows, :] = piece
        near_ref[rows:, :] = share
        full_ref[:rows, :] = piece
        full_ref[rows : rows + tok_quarter, :] = share
        full_ref[rows + tok_quarter :, :] = named
        lite_ref[:rows, :] = piece
        lite_ref[rows:, :] = named

    width = piece.shape[1]
    sizes = [rows + tok_quarter, rows + tok_quarter + ROUTE_ROWS, rows + ROUTE_ROWS]
    outputs = [((size, width), piece.dtype) for size in sizes]
    inputs = [piece, suffix_columns, routes_columns]
    return call(kernel, "join_share", inputs, outputs, 10_000_000)


def join_column(full, lites, own, rows):
    share = full.shape[0] - rows - ROUTE_ROWS

    def kernel(*refs):
        full_ref, *lite_refs, own_ref, column_ref, routes_ref = refs
        column_ref[: rows + share, :] = full_ref[: rows + share, :]
        routes_ref[0] = own_ref[rows:, :128]
        routes_ref[1] = full_ref[rows + share :, :128]
        at = rows + share
        for i, ref in enumerate(lite_refs):
            column_ref[at : at + rows, :] = ref[:rows, :]
            routes_ref[i + 2] = ref[rows:, :128]
            at += rows

    count = len(lites)
    outputs = [
        ((rows + share + count * rows, full.shape[1]), full.dtype),
        ((count + 2, ROUTE_ROWS, 128), full.dtype),
    ]
    return call(kernel, "join_column", [full, *lites, own], outputs, 0)


def join_rows(*blocks, ready=()):
    def kernel(*refs):
        out = refs[-1]
        at = 0
        for ref in refs[:-1]:
            out[at : at + ref.shape[0], :] = ref[...]
            at += ref.shape[0]

    rows = sum(block.shape[0] for block in blocks)
    shape = (rows, blocks[0].shape[1])
    return call(kernel, "join_rows", blocks, [(shape, blocks[0].dtype)], 0, ready=ready)[0]


def pass_on(blocks, ready=()):
    def kernel(*refs):
        for ref, out in zip(refs[: len(blocks)], refs[len(blocks) :]):
            out[...] = ref[...]

    outputs = [(block.shape, block.dtype) for block in blocks]
    return call(kernel, "pass_on", blocks, outputs, 0, ready=ready)


def place_keys(key_refs, spot_ref, token_ref, keys, bias):
    at = 0
    for ref in key_refs:
        rows = ref.shape[0]
        keys[at : at + rows, :] = ref[...]
        at += rows
    columns = token_ref[...]
    spots = spot_ref[...]
    low, high, start, here = (columns[:, i : i + 1] for i in range(4))
    seen = ((spots >= low) & (spots < high)) | ((spots >= start) & (spots <= here))
    bias[...] = jnp.where(seen, 0.0, VERY_NEGATIVE)


SCORE_FACTOR = math.log2(math.e) / math.sqrt(NOPE + ROPE)


def score_rows(content, rotated, keys, bias, pair):
    scores = dot_t(content, keys[:, :LAT]) + dot_t(rotated, keys[:, LAT:])
    rows, count = scores.shape
    return (scores.reshape(pair, rows // pair, count) + bias[...][None]).reshape(rows, count)


def near_kernel(
    block_count, token_ref, spot_ref, order_ref, query_ref, key_up_ref, *refs
):
    key_refs = refs[:block_count]
    content_ref, rotated_ref, best_ref, sum_ref, acc_ref, keys, bias = refs[block_count:]
    tokens = query_ref.shape[0]
    pair = key_up_ref.shape[0]

    @pl.when(pl.program_id(0) == 0)
    def prepare():
        place_keys(key_refs, spot_ref, token_ref, keys, bias)

    queries = dot_f(order_ref[...], query_ref[...]).astype(jnp.bfloat16)
    size = NOPE + ROPE
    content = []
    rotated = []
    for h in range(pair):
        part = queries[:, h * size : (h + 1) * size]
        content.append(dot_f(part[:, :NOPE], key_up_ref[h]).astype(jnp.bfloat16))
        rotated.append(part[:, NOPE:])
    content = jnp.concatenate(content, axis=0)
    rotated = jnp.concatenate(rotated, axis=0)
    content_ref[...] = content
    rotated_ref[...] = rotated
    masked = score_rows(content, rotated, keys, bias, pair)
    best = jnp.max(masked, axis=-1, keepdims=True)
    weights = jnp.exp2((masked - best) * SCORE_FACTOR)
    best_ref[...] = best
    sum_ref[...] = jnp.sum(weights, axis=-1, keepdims=True)
    acc_ref[...] = dot_f(weights.astype(jnp.bfloat16), keys[:, :LAT])


def attend_near(tokens_info, spots, order, queries, key_up, blocks, ready):
    tokens = queries.shape[0]
    heads = key_up.shape[0]
    pair = 2
    count = sum(block.shape[0] for block in blocks)
    size = NOPE + ROPE

    def per_step(columns):
        return pl.BlockSpec((pair * tokens, columns), lambda i: (i, 0))

    rows = heads * tokens
    return pl.pallas_call(
        after(functools.partial(near_kernel, len(blocks)), len(ready)),
        grid=(heads // pair,),
        in_specs=unread(ready)
        + [
            whole(tokens_info),
            whole(spots),
            whole(order),
            pl.BlockSpec((tokens, pair * size), lambda i: (0, i)),
            pl.BlockSpec((pair, NOPE, LAT), lambda i: (i, 0, 0)),
        ]
        + [whole(block) for block in blocks],
        out_specs=[per_step(LAT), per_step(ROPE), per_step(1), per_step(1), per_step(LAT)],
        out_shape=[
            jax.ShapeDtypeStruct((rows, LAT), jnp.bfloat16),
            jax.ShapeDtypeStruct((rows, ROPE), jnp.bfloat16),
            jax.ShapeDtypeStruct((rows, 1), jnp.float32),
            jax.ShapeDtypeStruct((rows, 1), jnp.float32),
            jax.ShapeDtypeStruct((rows, LAT), jnp.float32),
        ],
        scratch_shapes=[
            pltpu.VMEM((count, LAT + ROPE), jnp.bfloat16),
            pltpu.VMEM((tokens, count), jnp.float32),
        ],
        compiler_params=pltpu.CompilerParams(vmem_limit_bytes=24 * 1024 * 1024),
        cost_estimate=pl.CostEstimate(
            flops=2 * rows * count * (LAT + ROPE + LAT),
            bytes_accessed=8_000_000,
            transcendentals=rows * count,
        ),
        name="attend_near",
    )(*ready, tokens_info, spots, order, queries, key_up, *blocks)


def far_kernel(
    block_count,
    tok_quarter,
    token_ref,
    spot_ref,
    content_ref,
    rotated_ref,
    best_ref,
    sum_ref,
    acc_ref,
    value_up_ref,
    output_ref,
    *refs,
):
    key_refs = refs[:block_count]
    own_ref, other_ref, keys, bias, total = refs[block_count:]
    step = pl.program_id(0)
    pair = value_up_ref.shape[0]
    tokens = content_ref.shape[0] // pair

    @pl.when(step == 0)
    def prepare():
        place_keys(key_refs, spot_ref, token_ref, keys, bias)
        total[...] = jnp.zeros_like(total)

    masked = score_rows(content_ref[...], rotated_ref[...], keys, bias, pair)
    before = best_ref[...]
    best = jnp.maximum(before, jnp.max(masked, axis=-1, keepdims=True))
    factor = jnp.exp2((before - best) * SCORE_FACTOR)
    weights = jnp.exp2((masked - best) * SCORE_FACTOR)
    weight_sum = sum_ref[...] * factor + jnp.sum(weights, axis=-1, keepdims=True)
    attended = acc_ref[...] * factor + dot_f(weights.astype(jnp.bfloat16), keys[:, :LAT])
    attended = (attended / weight_sum).astype(jnp.bfloat16)
    heads = [
        dot_f(attended[h * tokens : (h + 1) * tokens], value_up_ref[h]).astype(jnp.bfloat16)
        for h in range(pair)
    ]
    total[...] += dot_f(jnp.concatenate(heads, axis=1), output_ref[...])

    @pl.when(step == pl.num_programs(0) - 1)
    def finish():
        own_ref[...] = total[:tok_quarter, :]
        other_ref[...] = total[tok_quarter:, :].astype(jnp.bfloat16)


def attend_far(tokens_info, spots, near, value_up, output_weight, blocks, tok_quarter):
    tokens = tokens_info.shape[0]
    heads = value_up.shape[0]
    width = output_weight.shape[1]
    pair = 2
    count = sum(block.shape[0] for block in blocks)
    rows = heads * tokens

    def per_step(columns):
        return pl.BlockSpec((pair * tokens, columns), lambda i: (i, 0))

    return pl.pallas_call(
        functools.partial(far_kernel, len(blocks), tok_quarter),
        grid=(heads // pair,),
        in_specs=[
            whole(tokens_info),
            whole(spots),
            per_step(LAT),
            per_step(ROPE),
            per_step(1),
            per_step(1),
            per_step(LAT),
            pl.BlockSpec((pair, LAT, value_up.shape[2]), lambda i: (i, 0, 0)),
            pl.BlockSpec((pair * value_up.shape[2], width), lambda i: (i, 0)),
        ]
        + [whole(block) for block in blocks],
        out_specs=[
            pl.BlockSpec((tok_quarter, width), lambda i: (0, 0)),
            pl.BlockSpec((tokens - tok_quarter, width), lambda i: (0, 0)),
        ],
        out_shape=[
            jax.ShapeDtypeStruct((tok_quarter, width), jnp.float32),
            jax.ShapeDtypeStruct((tokens - tok_quarter, width), jnp.bfloat16),
        ],
        scratch_shapes=[
            pltpu.VMEM((count, LAT + ROPE), jnp.bfloat16),
            pltpu.VMEM((tokens, count), jnp.float32),
            pltpu.VMEM((tokens, width), jnp.float32),
        ],
        compiler_params=pltpu.CompilerParams(vmem_limit_bytes=24 * 1024 * 1024),
        cost_estimate=pl.CostEstimate(
            flops=2 * rows * count * (LAT + ROPE + LAT),
            bytes_accessed=12_000_000,
            transcendentals=rows * count,
        ),
        name="attend_far",
    )(tokens_info, spots, *near, value_up, output_weight, *blocks)


def pick_rows(turn, ring, top, block, routes_ref, router_ref, scaled_ref, outs):
    tokens = block.shape[0]
    capacity = outs[0].shape[0]
    tensor_index = lax.axis_index("tensor")
    here = lax.div(tensor_index, PLANE)
    plane_index = lax.rem(tensor_index, PLANE)
    order = ring_order(ring)
    place = sum(jnp.where(here == z, i, 0) for i, z in enumerate(order))
    place = lax.rem(place - turn + ring, ring)
    source = sum(jnp.where(place == i, z, 0) for i, z in enumerate(order))
    routes = routes_ref[lax.rem(here - source + ring, ring)][:, :tokens].astype(jnp.float32)
    targets = [
        (here * PLANE + lax.bitwise_xor(plane_index, d)).astype(jnp.float32)
        for d in range(PLANE)
    ]
    hits = [
        jnp.sum(jnp.where(routes[:top] == target, 1.0, 0.0), axis=0, keepdims=True)
        for target in targets
    ]
    before = lax.broadcasted_iota(jnp.int32, (tokens, tokens), 0)
    after_it = lax.broadcasted_iota(jnp.int32, (tokens, tokens), 1)
    earlier = jnp.where(before < after_it, 1.0, 0.0).astype(jnp.bfloat16)
    ranks = dot_f(jnp.concatenate(hits, axis=0).astype(jnp.bfloat16), earlier)
    count = router_ref.shape[0]
    expert = lax.broadcasted_iota(jnp.int32, (count, tokens), 0).astype(jnp.float32)
    named = jnp.zeros((count, tokens), jnp.float32)
    for i in range(top):
        named = named + jnp.where(expert == routes[i : i + 1], 1.0, 0.0)
    picked = jax.nn.sigmoid(dot_t(router_ref[...], block)) * named
    gates = picked / jnp.sum(picked, axis=0, keepdims=True) * ROUTE_SCALING
    slot = lax.broadcasted_iota(jnp.int32, (capacity, tokens), 0).astype(jnp.float32)
    for d, out in enumerate(outs):
        taken = jnp.where(slot == ranks[d : d + 1], hits[d], 0.0)
        out[...] = dot_f(taken.astype(jnp.bfloat16), block).astype(jnp.bfloat16)
        gate = jnp.sum(jnp.where(expert == targets[d], gates, 0.0), axis=0, keepdims=True)
        scaled_ref[d * capacity : (d + 1) * capacity, :] = (taken * gate).astype(jnp.bfloat16)


def pick_outputs(block, capacity):
    tokens, width = block.shape
    pieces = [((capacity, width), jnp.bfloat16)] * PLANE
    return [((PLANE * capacity, tokens), jnp.bfloat16)] + pieces


def settle(hidden, own, others, gain, routes, router, sizes):
    ring, top, capacity = sizes

    def kernel(*refs):
        hidden_ref, own_ref = refs[:2]
        other_refs = refs[2 : 2 + len(others)]
        gain_ref, routes_ref, router_ref = refs[2 + len(others) : 5 + len(others)]
        residual_ref, normed_ref, scaled_ref, *outs = refs[5 + len(others) :]
        total = own_ref[...]
        for ref in other_refs:
            total = total + ref[...].astype(jnp.float32)
        residual = (hidden_ref[...].astype(jnp.float32) + total).astype(jnp.bfloat16)
        residual_ref[...] = residual
        normed = norm_rows(residual, gain_ref[...])
        normed_ref[...] = normed
        pick_rows(0, ring, top, normed, routes_ref, router_ref, scaled_ref, outs)

    outputs = [(hidden.shape, jnp.bfloat16)] * 2 + pick_outputs(hidden, capacity)
    inputs = [hidden, own, *others, gain, routes, router]
    residual, normed, scaled, *pieces = call(kernel, "settle", inputs, outputs, 70_000_000)
    return residual, normed, scaled, pieces


def choose(turn, block, arrived, routes, router, sizes, ready):
    ring, top, capacity = sizes

    def kernel(block_ref, routes_ref, router_ref, *refs):
        row_refs = refs[:PLANE]
        joined_ref, scaled_ref, *outs = refs[PLANE:]
        pick_rows(turn, ring, top, block_ref[...], routes_ref, router_ref, scaled_ref, outs)
        for d, ref in enumerate(row_refs):
            joined_ref[d * capacity : (d + 1) * capacity, :] = ref[...]

    joined = ((PLANE * capacity, block.shape[1]), jnp.bfloat16)
    outputs = [joined] + pick_outputs(block, capacity)
    inputs = [block, routes, router, *arrived]
    joined, scaled, *pieces = call(kernel, "choose", inputs, outputs, 70_000_000, ready=ready)
    return joined, scaled, pieces


def expert_kernel(count, kept, depth_steps, *refs):
    row_refs = refs[:count]
    gate_ref, up_ref, down_ref, own_ref, other_ref, rows, gate_sum, up_sum, hidden = refs[count:]
    step = pl.program_id(0)
    depth = gate_ref.shape[1]

    @pl.when(step == 0)
    def prepare():
        at = 0
        for ref in row_refs:
            size = ref.shape[0]
            for i in range(depth_steps):
                rows[i, at : at + size, :] = ref[:, i * depth : (i + 1) * depth]
            at += size

    @pl.when(step < depth_steps)
    def widen():
        part = rows[jnp.minimum(step, depth_steps - 1)]
        gate_part = dot_t(part, gate_ref[...])
        up_part = dot_t(part, up_ref[...])

        @pl.when(step == 0)
        def first():
            gate_sum[...] = gate_part
            up_sum[...] = up_part

        @pl.when(step > 0)
        def later():
            gate_sum[...] += gate_part
            up_sum[...] += up_part

    @pl.when(step == depth_steps - 1)
    def activate():
        hidden[...] = (jax.nn.silu(gate_sum[...]) * up_sum[...]).astype(jnp.bfloat16)

    @pl.when(step >= depth_steps)
    def narrow():
        own_ref[...] = dot_f(hidden[:kept, :], down_ref[...])
        other_ref[...] = dot_f(hidden[kept:, :], down_ref[...]).astype(jnp.bfloat16)


def expert_apply(pieces, kept, gate_part, up_part, down_part, ready):
    steps = 2
    total = sum(piece.shape[0] for piece in pieces)
    units, width = gate_part.shape
    depth = width // steps
    return pl.pallas_call(
        after(functools.partial(expert_kernel, len(pieces), kept, steps), len(ready)),
        grid=(2 * steps,),
        in_specs=unread(ready)
        + [whole(piece) for piece in pieces]
        + [
            pl.BlockSpec((units, depth), lambda i: (0, jnp.minimum(i, steps - 1))),
            pl.BlockSpec((units, depth), lambda i: (0, jnp.minimum(i, steps - 1))),
            pl.BlockSpec((units, depth), lambda i: (0, jnp.maximum(i - steps, 0))),
        ],
        out_specs=[
            pl.BlockSpec((kept, depth), lambda i: (0, jnp.maximum(i - steps, 0))),
            pl.BlockSpec((total - kept, depth), lambda i: (0, jnp.maximum(i - steps, 0))),
        ],
        out_shape=[
            jax.ShapeDtypeStruct((kept, width), jnp.float32),
            jax.ShapeDtypeStruct((total - kept, width), jnp.bfloat16),
        ],
        scratch_shapes=[
            pltpu.VMEM((steps, total, depth), jnp.bfloat16),
            pltpu.VMEM((total, units), jnp.float32),
            pltpu.VMEM((total, units), jnp.float32),
            pltpu.VMEM((total, units), jnp.bfloat16),
        ],
        compiler_params=pltpu.CompilerParams(vmem_limit_bytes=24 * 1024 * 1024),
        cost_estimate=pl.CostEstimate(
            flops=6 * total * width * units, bytes_accessed=10_000_000, transcendentals=0
        ),
        name="experts",
    )(*ready, *pieces, gate_part, up_part, down_part)


def blend(own, others, pieces, ready):
    def kernel(own_ref, *refs):
        other_refs = refs[: len(others)]
        outs = refs[len(others) :]
        total = own_ref[...]
        for ref in other_refs:
            total = total + ref[...].astype(jnp.float32)
        total = total.astype(jnp.bfloat16)
        size = outs[0].shape[0]
        for d, out in enumerate(outs):
            out[...] = total[d * size : (d + 1) * size]

    shape = (own.shape[0] // pieces, own.shape[1])
    outputs = [(shape, jnp.bfloat16)] * pieces
    return call(kernel, "blend", [own, *others], outputs, 1_000_000, ready=ready)


def scatter_sum(scaled_ref, piece_refs, running_ref):
    size = piece_refs[0].shape[0]
    returned = jnp.concatenate([ref[...] for ref in piece_refs], axis=0)
    total = lax.dot_general(
        scaled_ref[...], returned, (((0,), (0,)), ((), ())), preferred_element_type=jnp.float32
    )
    if running_ref is not None:
        total = total + running_ref[...].astype(jnp.float32)
    return total


def collect(scaled, pieces, running):
    extra = [] if running is None else [running]

    def kernel(scaled_ref, *refs):
        running_ref = refs[len(pieces)] if extra else None
        total = scatter_sum(scaled_ref, refs[: len(pieces)], running_ref)
        refs[-1][...] = total.astype(jnp.bfloat16)

    shape = (scaled.shape[1], pieces[0].shape[1])
    inputs = [scaled, *pieces, *extra]
    return call(kernel, "collect", inputs, [(shape, jnp.bfloat16)], 35_000_000)[0]


def conclude(scaled, pieces, running, residual, gain):
    extra = [] if running is None else [running]

    def kernel(residual_ref, gain_ref, scaled_ref, *refs):
        running_ref = refs[len(pieces)] if extra else None
        total = scatter_sum(scaled_ref, refs[: len(pieces)], running_ref)
        layer = (residual_ref[...].astype(jnp.float32) + total).astype(jnp.bfloat16)
        refs[-2][...] = layer
        refs[-1][...] = norm_rows(layer, gain_ref[...])

    inputs = [residual, gain, scaled, *pieces, *extra]
    return call(kernel, "conclude", inputs, [(residual.shape, jnp.bfloat16)] * 2, 35_000_000)


def per_device(
    hidden_in,
    queries,
    suffix_latent,
    prefix_latent,
    key_up,
    value_up,
    output_weight,
    norm_gain,
    router,
    expert_gate,
    expert_up,
    expert_down,
    next_gain,
    next_query_weight,
    next_latent_weight,
    suffix_lengths,
    request_tenant,
    tenant_lengths,
    page_table,
    routes,
):
    tok_slice = hidden_in.shape[0]
    groups = lax.axis_size("group")
    ring = lax.axis_size("tensor") // PLANE
    group_index = lax.axis_index("group")
    tensor_index = lax.axis_index("tensor")
    ring_index = tensor_index // PLANE
    plane_index = tensor_index % PLANE
    tok_quarter = tok_slice // groups
    expert_count = router.shape[1]
    top_count = routes.shape[2]
    capacity = max(2, 4 * tok_quarter * top_count // (3 * expert_count))
    capacity = -(-capacity // 16) * 16
    int32 = jnp.int32

    real_rows = prefix_latent.shape[0]
    piece_rows = -(-real_rows // 16) * 16
    piece = prefix_latent
    if piece_rows != real_rows:
        piece = jnp.pad(piece, ((0, piece_rows - real_rows), (0, 0)))
    routes_columns = jnp.transpose(routes, (2, 0, 1))
    both, full, lite = join_share(piece, suffix_latent.T, routes_columns, tok_quarter)
    along = [send_round(full, PLANE)] + [send_round(lite, PLANE * k) for k in range(2, ring)]
    near_plane = [send_plane(both, d) if d else both for d in range(PLANE)]
    near_blocks = [
        send_group(block, j) if j else block for j in range(groups) for block in near_plane
    ]
    column, routes_ring = join_column(along[0], along[1:], lite, piece_rows)
    far_plane = [send_plane(column, d) if d else column for d in range(PLANE)]

    later = 1 << 20
    first_token = tensor_index * tok_slice

    pages = real_rows // PAGE

    def positions_of(steps, with_suffix):
        parts = []
        for k in steps:
            from_ring = (ring_index - k + ring) % ring
            shape = (groups, PLANE, piece_rows)
            j, d, r = (lax.broadcasted_iota(int32, shape, axis) for axis in range(3))
            owner = ((group_index ^ j) * ring + from_ring) * PLANE + (plane_index ^ d)
            spot = owner * real_rows + r
            page = owner[:, :, :pages] * pages + r[:, :, :pages]
            hit = page[..., None] == jnp.arange(page_table.shape[0], dtype=int32)
            page = jnp.sum(jnp.where(hit, page_table, 0), axis=-1)
            page = jnp.repeat(page, PAGE, axis=2)
            page = jnp.pad(page, ((0, 0), (0, 0), (0, piece_rows - real_rows)))
            parts.append(jnp.where(r < real_rows, page * PAGE + spot % PAGE, -1))
            if k in with_suffix:
                shape = (groups, PLANE, tok_quarter)
                j, d, r = (lax.broadcasted_iota(int32, shape, axis) for axis in range(3))
                owner = from_ring * PLANE + (plane_index ^ d)
                token = owner * tok_slice + (group_index ^ j) * tok_quarter + r
                parts.append(token + later)
        return jnp.concatenate(parts, axis=2).reshape(1, -1)

    near_spots = positions_of([0], [0])
    far_spots = positions_of(range(1, ring), [1])

    row = jnp.arange(tok_slice, dtype=int32)
    local = (row % tok_quarter) * groups + (group_index ^ (row // tok_quarter))
    permutation = (local[:, None] == jnp.arange(tok_slice, dtype=int32)[None, :]).astype(
        jnp.bfloat16
    )
    positions = first_token + local
    requests = suffix_lengths.shape[0]
    tenants = tenant_lengths.shape[0]
    upto = jnp.arange(requests)[None, :] <= jnp.arange(requests)[:, None]
    request_ends = jnp.sum(jnp.where(upto, suffix_lengths[None, :], 0), axis=1)
    request_starts = request_ends - suffix_lengths
    inside = (positions[:, None] >= request_starts[None, :]) & (
        positions[:, None] < request_ends[None, :]
    )
    token_start = jnp.sum(jnp.where(inside, request_starts[None, :], 0), axis=1)
    token_tenant = jnp.sum(jnp.where(inside, request_tenant[None, :], 0), axis=1)
    upto = jnp.arange(tenants)[None, :] <= jnp.arange(tenants)[:, None]
    tenant_ends = jnp.sum(jnp.where(upto, tenant_lengths[None, :], 0), axis=1)
    tenant_starts = tenant_ends - tenant_lengths
    tenant_pick = token_tenant[:, None] == jnp.arange(tenants, dtype=int32)[None, :]
    range_low = jnp.sum(jnp.where(tenant_pick, tenant_starts[None, :], 0), axis=1)
    range_high = jnp.sum(jnp.where(tenant_pick, tenant_ends[None, :], 0), axis=1)
    tokens_info = jnp.stack(
        [range_low, range_high, token_start + later, positions + later], axis=1
    )

    near = attend_near(
        tokens_info, near_spots, permutation, queries, key_up, near_blocks, [column]
    )
    far_plane = pass_on(far_plane, ready=[near[4]])
    far_blocks = [
        send_group(block, j) if j else block for j in range(groups) for block in far_plane
    ]
    attend_own, attend_other = attend_far(
        tokens_info, far_spots, near, value_up, output_weight, far_blocks, tok_quarter
    )

    hidden_own = dot_f(permutation[:tok_quarter], hidden_in).astype(jnp.bfloat16)
    others = [
        send_group(attend_other[(j - 1) * tok_quarter : j * tok_quarter], j)
        for j in range(1, groups)
    ]
    sizes = (ring, top_count, capacity)
    experts_columns = router.T
    residual, block, scaled, pieces = settle(
        hidden_own,
        attend_own,
        others,
        norm_gain[None, :],
        routes_ring,
        experts_columns,
        sizes,
    )

    kept = PLANE * capacity
    gate_part = jnp.transpose(expert_gate, (0, 2, 1))[0]
    up_part = jnp.transpose(expert_up, (0, 2, 1))[0]
    down_part = expert_down[0]
    scales = [scaled]
    results = []
    for k in range(ring):
        arrived = [send_plane(piece, d) if d else piece for d, piece in enumerate(pieces)]
        ready = [result[0] for result in results[-1:]]
        if k + 1 < ring:
            block = send_ring(block, ring)
            joined, scaled, pieces = choose(
                k + 1, block, arrived, routes_ring, experts_columns, sizes, ready
            )
            scales.append(scaled)
        else:
            joined = join_rows(*arrived, ready=ready)
        rows = [send_group(joined, j) if j else joined for j in range(groups)]
        results.append(expert_apply(rows, kept, gate_part, up_part, down_part, ready))

    def give_back(k, ready):
        own, other = results[k]
        others = [send_group(other[(j - 1) * kept : j * kept], j) for j in range(1, groups)]
        pieces = blend(own, others, PLANE, ready)
        return [send_plane(piece, d) if d else piece for d, piece in enumerate(pieces)]

    running = None
    total = None
    for k in range(1, ring):
        returned = give_back(k, [])
        total = collect(scales[k], returned, running)
        running = send_ring(total, ring)
    returned = give_back(0, [] if total is None else [total])
    layer_rows, normed_next = conclude(
        scales[0], returned, running, residual, next_gain[None, :]
    )

    shares = [send_group(normed_next, j) if j else normed_next for j in range(groups)]
    gathered = lax.dot_general(
        permutation,
        jnp.concatenate(shares, axis=0),
        (((0,), (0,)), ((), ())),
        preferred_element_type=jnp.float32,
    ).astype(jnp.bfloat16)
    next_queries = dot_f(gathered, next_query_weight).astype(jnp.bfloat16)
    next_latent = dot_f(gathered, next_latent_weight).astype(jnp.bfloat16)
    return (layer_rows[:, None, :], next_queries, next_latent)


def solution(mesh):
    return jax.shard_map(
        per_device,
        mesh=mesh,
        in_specs=(
            P("tensor", None),
            P("tensor", "group"),
            P("tensor", None),
            P(("group", "tensor"), None),
            P("group", None, None),
            P("group", None, None),
            P("group", None),
            P(),
            P(),
            P("tensor", None, "group"),
            P("tensor", None, "group"),
            P("tensor", "group", None),
            P(),
            P(None, "group"),
            P(None, "group"),
            P(),
            P(),
            P(),
            P(),
            P(None, "tensor", None),
        ),
        out_specs=(P("tensor", "group", None), P("tensor", "group"), P("tensor", "group")),
        check_vma=False,
    )
```

time: 228 us -> 165 us (0.72)
  matrix products: 46.8 us -> 3.49 us
  Pallas kernels: 13.8 us -> 42 us
  waiting for transfers between devices: 60.1 us -> 37.1 us
  local copies, waits for them, and re-layouts: 32.6 us -> 22.4 us
  other arithmetic: 14.9 us -> 7.43 us
  starting transfers between devices: 57.1 us -> 50.8 us
    dot_general x19 -> x3, matrix products: 45.2 us -> 3.08 us  [dot_f(): return jnp.dot(left, right, preferred_element_type=jnp.float32)]
    pallas_call x1 -> x22, Pallas kernels: 13.8 us -> 42 us  [the longest x4 18.2 us: expert_apply(): pl.pallas_call(after(functools.partial(expert_kernel, len(pieces), kept,...]
    ppermute x12 -> x6, waiting for transfers between devices: 32.1 us -> 6.11 us  [send_ring(): return lax.ppermute(block, 'tensor', route)]
    slice x13 -> x0, local copies, waits for them, and re-layouts: 10.7 us -> none  [the longest x4 8.19 us: per_device(): part = partial[j * rows_plane:(j + 1) * rows_plane].astype(jnp.bfloat16)]
    ppermute x4 -> x3, starting transfers between devices: 16.8 us -> 6.18 us  [send_round(): lax.ppermute(block, 'tensor', [(i, (i + distance) % count) for i in range...]
    ppermute x4 -> x3, waiting for transfers between devices: 0.01 us -> 7.2 us  [send_round(): lax.ppermute(block, 'tensor', [(i, (i + distance) % count) for i in range...]
    convert_element_type x11 -> x0, other arithmetic: 5.71 us -> none  [the longest x4 3.89 us: per_device(): combined = combined.astype(jnp.bfloat16)]
    ppermute x27 -> x30, waiting for transfers between devices: 24.6 us -> 18.9 us  [send_plane(): return lax.ppermute(block, 'tensor', [(i, i ^ distance) for i in devices])]
  transfers between devices with their start and end apart: 58 -> 57, of which waited for: 24 -> 23; matrix products, arithmetic and copies ran while one was open for 35% -> 5% of each run, Pallas kernels for 0% -> 15%
where the time goes in v2:
time: 165 us
  starting transfers between devices  50.8 us (31%)
  Pallas kernels  42 us (25%)
  waiting for transfers between devices  37.1 us (22%)
  local copies, waits for them, and re-layouts  22.4 us (14%)
  other arithmetic  7.43 us (5%)
  matrix products  3.49 us (2%)
    ppermute x30, starting transfers between devices, send_plane(): return lax.ppermute(block, 'tensor', [(i, i ^ distance) for i in devices])  35.4 us
    unnamed x92, local copies, waits for them, and re-layouts  21.6 us
    ppermute x30, waiting for transfers between devices, send_plane(): return lax.ppermute(block, 'tensor', [(i, i ^ distance) for i in devices])  18.9 us
    pallas_call x4, Pallas kernels, expert_apply(): pl.pallas_call(after(functools.partial(expert_kernel, len(pieces), kept,...  18.2 us
    pallas_call x1, Pallas kernels, attend_far(): pl.pallas_call(functools.partial(far_kernel, len(blocks), tok_quarter), g...  12.5 us
    ppermute x3, waiting for transfers between devices, send_round(): lax.ppermute(block, 'tensor', [(i, (i + distance) % count) for i in range...  7.2 us
    ppermute x3, starting transfers between devices, send_round(): lax.ppermute(block, 'tensor', [(i, (i + distance) % count) for i in range...  6.18 us
    ppermute x6, waiting for transfers between devices, send_ring(): return lax.ppermute(block, 'tensor', route)  6.11 us
  transfers between devices with their start and end apart: 57, of which 23 were waited for; matrix products, arithmetic and copies ran while one was open for 5% of the time, Pallas kernels for 15%

profile of v2, /device:TPU:0, one launch (start us, length us, event | category | flops | bytes accessed | tf_op | source)
XLA Modules:
  0.0 164.6 jit_solution(8294037428499646202)
XLA Ops:
  0.7 1.0 copy-done.5
  3.4 4.1 %collective-permute-start.1 = (bf16[80,576]{1,0:T(8,128)(2,1)S(1)}, bf16[80,576]{1,0:T(8,128)(2,1)S(1)}, u32[]{:S(2)}, u32[]{:S(2)}) collective-permute-start(bf16[80,576]{1,0:T(8,128)(2,1)S(1)} %get-tuple-element.71.refs_3_), channel_id=1, source_target_pairs={{0,8},{1,9},{2,10},{3,11},{4,12},{5,13},{6,14},{7,15},{8,0},{9,1},... | collective-permute-start | bytes 276488 | tf_op jit(solution)/shard_map/ppermute | solution.py:40
  7.5 1.3 collective-permute-start.2
  8.9 1.5 collective-permute-start.3
  10.4 1.5 collective-permute-start.4
  12.5 1.4 select_reduce_fusion
  22.1 7.2 %collective-permute-done.refs_0_ = bf16[144,576]{1,0:T(8,128)(2,1)S(1)} collective-permute-done((bf16[144,576]{1,0:T(8,128)(2,1)S(1)}, bf16[144,576]{1,0:T(8,128)(2,1)S(1)}, u32[]{:S(2)}, u32[]{:S(2)}) %collective-permute-start) | collective-permute-done | bytes 165920 | tf_op jit(solution)/shard_map/ppermute | solution.py:40
  29.3 1.6 collective-permute-start.10
  31.5 1.5 collective-permute-start.11
  35.6 1.2 copy-done.9
  36.9 1.0 copy-done.11
  37.9 0.9 copy-done.13
  38.8 0.9 copy-done.15
  39.7 0.9 copy-done.17
  40.6 0.9 copy-done.19
  41.5 0.9 copy-done.21
  44.3 5.7 %attend_near.1 = (bf16[1024,512]{1,0:T(8,128)(2,1)S(1)}, bf16[1024,64]{1,0:T(8,128)(2,1)S(1)}, f32[1024,1]{1,0:T(8,128)S(1)}, f32[1024,1]{1,0:T(8,128)S(1)}, f32[1024,512]{1,0:T(8,128)S(1)}) custom-call(bf16[256,576]{1,0:T(8,128)(2,1)S(1)} %get-tuple-element.72.refs_0_.refs_1_, s32[128,4]{1,0:T(8,128)S(1)} %copy.29.refs_1_.token_ref, ...), custom_call_target="tpu_custom_call" | custom-call | flops 2281701376 | bytes 8000000 | tf_op jit(solution)/shard_map/attend_near/pallas_call | solution.py:248
  50.1 1.3 pass_on.1
  54.8 2.2 %copy-done.8 = bf16[1024,2048]{1,0:T(8,128)(2,1)S(1)} copy-done((bf16[1024,2048]{1,0:T(8,128)(2,1)S(1)}, bf16[1024,2048]{1,0:T(8,128)(2,1)}, u32[]{:S(2)}) %copy-start.8) | copy-done | bytes 4194328
  56.9 1.2 copy-done.10
  58.2 1.2 copy-done.27
  59.4 1.0 copy-done.29
  60.4 1.0 copy-done.31
  61.5 0.9 copy-done.33
  62.5 12.5 %attend_far.1 = (f32[64,2048]{1,0:T(8,128)S(1)}, bf16[64,2048]{1,0:T(8,128)(2,1)S(1)}) custom-call(s32[128,4]{1,0:T(8,128)S(1)} %copy.29.refs_1_.token_ref, s32[1,2048]{1,0:T(1,128)S(1)} %reshape.113.spot_ref, bf16[1024,512]{1,0:T(8,128)(2,1)S(1)} %copy-done.27, bf16[1024,64]{1,0:T(8,128)(2,1)S(1)} %copy-done.33, f32[1024,1]{1,0:T(8,128)S(1)} %copy-done.29, ...), custom_call_target="tpu_custom_call" | custom-call | flops 4563402752 | bytes 12000000 | tf_op jit(solution)/shard_map/attend_far/pallas_call | solution.py:338
  75.4 1.1 collective-permute-done.17.refs_2_
  77.2 1.6 collective-permute-start.19
  78.7 1.5 collective-permute-start.20
  80.7 2.4 %collective-permute-done.19.refs_4_ = bf16[32,2048]{1,0:T(8,128)(2,1)S(1)} collective-permute-done((bf16[32,2048]{1,0:T(8,128)(2,1)S(1)}, bf16[32,2048]{1,0:T(8,128)(2,1)S(1)}, u32[]{:S(2)}, u32[]{:S(2)}) %collective-permute-start.19) | collective-permute-done | bytes 131104 | tf_op jit(solution)/shard_map/ppermute | solution.py:45
  83.1 3.7 %collective-permute-done.20.refs_5_ = bf16[32,2048]{1,0:T(8,128)(2,1)S(1)} collective-permute-done((bf16[32,2048]{1,0:T(8,128)(2,1)S(1)}, bf16[32,2048]{1,0:T(8,128)(2,1)S(1)}, u32[]{:S(2)}, u32[]{:S(2)}) %collective-permute-start.20) | collective-permute-done | bytes 131104 | tf_op jit(solution)/shard_map/ppermute | solution.py:45
  87.5 1.3 collective-permute-start.24
  88.8 1.4 collective-permute-start.25
  91.1 4.6 %experts.4 = (f32[128,2048]{1,0:T(8,128)S(1)}, bf16[128,2048]{1,0:T(8,128)(2,1)S(1)}) custom-call(bf16[128,2048]{1,0:T(8,128)(2,1)S(1)} %get-tuple-element.93.refs_0_, bf16[128,2048]{1,0:T(8,128)(2,1)S(1)} %collective-permute-done.22.refs_1_, bf16[704,2048]{1,0:T(8,128)(2,1)S(1)} %bitcast.30, bf16[704,2048]{1,0:T(8,128)(2,1)S(1)} %bitcast.34, ...), custom_call_target="tpu_custom_call" | custom-call | flops 2214592512 | bytes 10000000 | tf_op jit(solution)/shard_map/experts/pallas_call | solution.py:506
  96.0 1.1 collective-permute-done.26.refs_7_
  97.6 1.5 collective-permute-start.28
  99.9 1.5 collective-permute-start.30
  101.5 1.2 collective-permute-start.31
  102.6 4.5 %experts.5 = (f32[128,2048]{1,0:T(8,128)S(1)}, bf16[128,2048]{1,0:T(8,128)(2,1)S(1)}) custom-call(f32[128,2048]{1,0:T(8,128)S(1)} %get-tuple-element.94.refs_0_.refs_1_, bf16[128,2048]{1,0:T(8,128)(2,1)S(1)} %get-tuple-element.99.refs_1_, bf16[128,2048]{1,0:T(8,128)(2,1)S(1)} %collective-permute-done.27.refs_2_, bf16[704,2048]{1,0:T(8,128)(2,1)S(1)} %bitcast.31, ...), custom_call_target="tpu_custom_call" | custom-call | flops 2214592512 | bytes 10000000 | tf_op jit(solution)/shard_map/experts/pallas_call | solution.py:506
  108.9 1.2 collective-permute-start.33
  111.0 1.4 collective-permute-start.35
  112.4 4.5 %experts.6 = (f32[128,2048]{1,0:T(8,128)S(1)}, bf16[128,2048]{1,0:T(8,128)(2,1)S(1)}) custom-call(f32[128,2048]{1,0:T(8,128)S(1)} %get-tuple-element.100.refs_0_, bf16[128,2048]{1,0:T(8,128)(2,1)S(1)} %get-tuple-element.106.refs_1_, bf16[128,2048]{1,0:T(8,128)(2,1)S(1)} %collective-permute-done.32.refs_2_, bf16[704,2048]{1,0:T(8,128)(2,1)S(1)} %bitcast.32, ...), custom_call_target="tpu_custom_call" | custom-call | flops 2214592512 | bytes 10000000 | tf_op jit(solution)/shard_map/experts/pallas_call | solution.py:506
  117.0 1.2 collective-permute-done.35.refs_4_
  119.7 1.5 collective-permute-start.47
  121.3 1.2 collective-permute-start.48
  122.4 4.5 %experts.7 = (f32[128,2048]{1,0:T(8,128)S(1)}, bf16[128,2048]{1,0:T(8,128)(2,1)S(1)}) custom-call(f32[128,2048]{1,0:T(8,128)S(1)} %get-tuple-element.107.refs_0_, bf16[128,2048]{1,0:T(8,128)(2,1)S(1)} %join_rows.1.refs_1_, bf16[128,2048]{1,0:T(8,128)(2,1)S(1)} %collective-permute-done.36.refs_2_, bf16[704,2048]{1,0:T(8,128)(2,1)S(1)} %bitcast.33, ...), custom_call_target="tpu_custom_call" | custom-call | flops 2214592512 | bytes 10000000 | tf_op jit(solution)/shard_map/experts/pallas_call | solution.py:506
  128.0 3.1 %collective-permute-start.49 = (bf16[64,2048]{1,0:T(8,128)(2,1)S(1)}, bf16[64,2048]{1,0:T(8,128)(2,1)S(1)}, u32[]{:S(2)}, u32[]{:S(2)}) collective-permute-start(bf16[64,2048]{1,0:T(8,128)(2,1)S(1)} %collect.3), channel_id=1, source_target_pairs={{0,4},{1,5},{2,6},{3,7},{4,12},{5,13},{6,14},{7,15},{8,0},{9,1},{1... | collective-permute-start | bytes 786440 | tf_op jit(solution)/shard_map/ppermute | solution.py:35
  131.2 1.3 collective-permute-start.42
  133.3 1.4 collective-permute-start.44
  134.8 2.2 %collective-permute-done.49.refs_5_ = bf16[64,2048]{1,0:T(8,128)(2,1)S(1)} collective-permute-done((bf16[64,2048]{1,0:T(8,128)(2,1)S(1)}, bf16[64,2048]{1,0:T(8,128)(2,1)S(1)}, u32[]{:S(2)}, u32[]{:S(2)}) %collective-permute-start.49) | collective-permute-done | bytes 262176 | tf_op jit(solution)/shard_map/ppermute | solution.py:35
  137.4 2.9 %collective-permute-done.43.refs_3_ = bf16[32,2048]{1,0:T(8,128)(2,1)S(1)} collective-permute-done((bf16[32,2048]{1,0:T(8,128)(2,1)S(1)}, bf16[32,2048]{1,0:T(8,128)(2,1)S(1)}, u32[]{:S(2)}, u32[]{:S(2)}) %collective-permute-start.43) | collective-permute-done | bytes 131104 | tf_op jit(solution)/shard_map/ppermute | solution.py:45
  141.1 1.2 collective-permute-start.38
  142.2 0.9 collective-permute-start.39
  143.1 1.5 collective-permute-start.40
  144.6 3.8 %collective-permute-done.50.refs_5_ = bf16[64,2048]{1,0:T(8,128)(2,1)S(1)} collective-permute-done((bf16[64,2048]{1,0:T(8,128)(2,1)S(1)}, bf16[64,2048]{1,0:T(8,128)(2,1)S(1)}, u32[]{:S(2)}, u32[]{:S(2)}) %collective-permute-start.50) | collective-permute-done | bytes 262176 | tf_op jit(solution)/shard_map/ppermute | solution.py:35
  148.4 1.2 collective-permute-done.39.refs_3_
  150.8 1.2 collective-permute-start.52
  151.9 1.0 collective-permute-start.53
  153.0 1.4 collective-permute-start.54
  154.3 2.5 %collective-permute-done.52.refs_4_ = bf16[32,2048]{1,0:T(8,128)(2,1)S(1)} collective-permute-done((bf16[32,2048]{1,0:T(8,128)(2,1)S(1)}, bf16[32,2048]{1,0:T(8,128)(2,1)S(1)}, u32[]{:S(2)}, u32[]{:S(2)}) %collective-permute-start.52) | collective-permute-done | bytes 131104 | tf_op jit(solution)/shard_map/ppermute | solution.py:45
  157.2 1.6 collective-permute-done.54.refs_6_
  158.8 1.0 conclude.1
  159.8 1.5 collective-permute-done.56
  161.8 1.7 %convolution_convert_fusion.1 = bf16[128,1536]{1,0:T(8,128)(2,1)} fusion(bf16[128,2048]{1,0:T(8,128)(2,1)S(1)} %convolution_convert_fusion, bf16[2048,1536]{1,0:T(8,128)(2,1)S(1)} %bitcast.50), kind=kOutput, calls=%fused_computation.1 | convolution fusion | flops 805502976 | bytes 7208960 | tf_op jit(solution)/shard_map/dot_general | solution.py:68
  163.5 1.1 convolution_convert_fusion.3
  (210 shorter events, 32.7 us)
Async XLA Ops:
  0.6 162.9 %copy-start = (bf16[2048,288]{0,1:T(8,128)(2,1)S(1)}, bf16[2048,288]{0,1:T(8,128)(2,1)}, u32[]{:S(2)}) copy-start(bf16[2048,288]{0,1:T(8,128)(2,1)} %param.34) | copy-start | bytes 3538948
  3.4 16.9 %collective-permute-start.1 = (bf16[80,576]{1,0:T(8,128)(2,1)S(1)}, bf16[80,576]{1,0:T(8,128)(2,1)S(1)}, u32[]{:S(2)}, u32[]{:S(2)}) collective-permute-start(bf16[80,576]{1,0:T(8,128)(2,1)S(1)} %get-tuple-element.71.refs_3_), channel_id=1, source_target_pairs={{0,8},{1,9},{2,10},{3,11},{4,12},{5,13},{6,14},{7,15},{8,0},{9,1},... | collective-permute-start | bytes 276488 | tf_op jit(solution)/shard_map/ppermute | solution.py:40
  7.5 12.9 %collective-permute-start.2 = (bf16[80,576]{1,0:T(8,128)(2,1)S(1)}, bf16[80,576]{1,0:T(8,128)(2,1)S(1)}, u32[]{:S(2)}, u32[]{:S(2)}) collective-permute-start(bf16[80,576]{1,0:T(8,128)(2,1)S(1)} %get-tuple-element.71.refs_3_), channel_id=1, source_target_pairs={{0,12},{1,13},{2,14},{3,15},{4,0},{5,1},{6,2},{7,3},{8,4},{9,5},{1... | collective-permute-start | bytes 276488 | tf_op jit(solution)/shard_map/ppermute | solution.py:40
  8.9 12.3 %collective-permute-start.3 = (bf16[128,576]{1,0:T(8,128)(2,1)S(1)}, bf16[128,576]{1,0:T(8,128)(2,1)S(1)}, u32[]{:S(2)}, u32[]{:S(2)}) collective-permute-start(bf16[128,576]{1,0:T(8,128)(2,1)S(1)} %get-tuple-element.73.refs_6_), channel_id=1, source_target_pairs={{0,1},{1,0},{2,3},{3,2},{4,5},{5,4},{6,7},{7,6},{8,9},{9,8},{10,11... | collective-permute-start | bytes 442376 | tf_op jit(solution)/shard_map/ppermute | solution.py:45
  10.4 11.0 %collective-permute-start.4 = (bf16[128,576]{1,0:T(8,128)(2,1)S(1)}, bf16[128,576]{1,0:T(8,128)(2,1)S(1)}, u32[]{:S(2)}, u32[]{:S(2)}) collective-permute-start(bf16[128,576]{1,0:T(8,128)(2,1)S(1)} %get-tuple-element.73.refs_6_), channel_id=1, source_target_pairs={{0,2},{1,3},{2,0},{3,1},{4,6},{5,7},{6,4},{7,5},{8,10},{9,11},{10,... | collective-permute-start | bytes 442376 | tf_op jit(solution)/shard_map/ppermute | solution.py:45
  11.9 9.9 %collective-permute-start.5 = (bf16[128,576]{1,0:T(8,128)(2,1)S(1)}, bf16[128,576]{1,0:T(8,128)(2,1)S(1)}, u32[]{:S(2)}, u32[]{:S(2)}) collective-permute-start(bf16[128,576]{1,0:T(8,128)(2,1)S(1)} %get-tuple-element.73.refs_6_), channel_id=1, source_target_pairs={{0,3},{1,2},{2,1},{3,0},{4,7},{5,6},{6,5},{7,4},{8,11},{9,10},{10,... | collective-permute-start | bytes 442376 | tf_op jit(solution)/shard_map/ppermute | solution.py:45
  20.3 10.5 %collective-permute-start.6 = (bf16[128,576]{1,0:T(8,128)(2,1)S(1)}, bf16[128,576]{1,0:T(8,128)(2,1)S(1)}, u32[]{:S(2)}, u32[]{:S(2)}) collective-permute-start(bf16[128,576]{1,0:T(8,128)(2,1)S(1)} %get-tuple-element.73.refs_6_), channel_id=1, source_target_pairs={{0,16},{16,0},{1,17},{17,1},{2,18},{18,2},{3,19},{19,3},{4,20},{20... | collective-permute-start | bytes 442376 | tf_op jit(solution)/shard_map/ppermute | solution.py:50
  20.4 8.8 %collective-permute-start = (bf16[144,576]{1,0:T(8,128)(2,1)S(1)}, bf16[144,576]{1,0:T(8,128)(2,1)S(1)}, u32[]{:S(2)}, u32[]{:S(2)}) collective-permute-start(bf16[144,576]{1,0:T(8,128)(2,1)S(1)} %get-tuple-element.70), channel_id=1, source_target_pairs={{0,4},{1,5},{2,6},{3,7},{4,8},{5,9},{6,10},{7,11},{8,12},{9,13},{1... | collective-permute-start | bytes 497672 | tf_op jit(solution)/shard_map/ppermute | solution.py:40
  21.2 11.9 %collective-permute-start.7 = (bf16[128,576]{1,0:T(8,128)(2,1)S(1)}, bf16[128,576]{1,0:T(8,128)(2,1)S(1)}, u32[]{:S(2)}, u32[]{:S(2)}) collective-permute-start(bf16[128,576]{1,0:T(8,128)(2,1)S(1)} %collective-permute-done.3.refs_7_), channel_id=1, source_target_pairs={{0,16},{16,0},{1,17},{17,1},{2,18},{18,2},{3,19},{19,3},{4,20},{20... | collective-permute-start | bytes 442376 | tf_op jit(solution)/shard_map/ppermute | solution.py:50
  21.4 12.9 %collective-permute-start.8 = (bf16[128,576]{1,0:T(8,128)(2,1)S(1)}, bf16[128,576]{1,0:T(8,128)(2,1)S(1)}, u32[]{:S(2)}, u32[]{:S(2)}) collective-permute-start(bf16[128,576]{1,0:T(8,128)(2,1)S(1)} %collective-permute-done.4.refs_8_), channel_id=1, source_target_pairs={{0,16},{16,0},{1,17},{17,1},{2,18},{18,2},{3,19},{19,3},{4,20},{20... | collective-permute-start | bytes 442376 | tf_op jit(solution)/shard_map/ppermute | solution.py:50
  21.8 13.2 %collective-permute-start.9 = (bf16[128,576]{1,0:T(8,128)(2,1)S(1)}, bf16[128,576]{1,0:T(8,128)(2,1)S(1)}, u32[]{:S(2)}, u32[]{:S(2)}) collective-permute-start(bf16[128,576]{1,0:T(8,128)(2,1)S(1)} %collective-permute-done.5.refs_9_), channel_id=1, source_target_pairs={{0,16},{16,0},{1,17},{17,1},{2,18},{18,2},{3,19},{19,3},{4,20},{20... | collective-permute-start | bytes 442376 | tf_op jit(solution)/shard_map/ppermute | solution.py:50
  29.3 20.7 %collective-permute-start.10 = (bf16[256,576]{1,0:T(8,128)(2,1)S(1)}, bf16[256,576]{1,0:T(8,128)(2,1)S(1)}, u32[]{:S(2)}, u32[]{:S(2)}) collective-permute-start(bf16[256,576]{1,0:T(8,128)(2,1)S(1)} %get-tuple-element.72.refs_0_.refs_1_), channel_id=1, source_target_pairs={{0,1},{1,0},{2,3},{3,2},{4,5},{5,4},{6,7},{7,6},{8,9},{9,8},{10,11... | collective-permute-start | bytes 884744 | tf_op jit(solution)/shard_map/ppermute | solution.py:45
  31.5 18.5 %collective-permute-start.11 = (bf16[256,576]{1,0:T(8,128)(2,1)S(1)}, bf16[256,576]{1,0:T(8,128)(2,1)S(1)}, u32[]{:S(2)}, u32[]{:S(2)}) collective-permute-start(bf16[256,576]{1,0:T(8,128)(2,1)S(1)} %get-tuple-element.72.refs_0_.refs_1_), channel_id=1, source_target_pairs={{0,2},{1,3},{2,0},{3,1},{4,6},{5,7},{6,4},{7,5},{8,10},{9,11},{10,... | collective-permute-start | bytes 884744 | tf_op jit(solution)/shard_map/ppermute | solution.py:45
  33.7 16.3 %collective-permute-start.12 = (bf16[256,576]{1,0:T(8,128)(2,1)S(1)}, bf16[256,576]{1,0:T(8,128)(2,1)S(1)}, u32[]{:S(2)}, u32[]{:S(2)}) collective-permute-start(bf16[256,576]{1,0:T(8,128)(2,1)S(1)} %get-tuple-element.72.refs_0_.refs_1_), channel_id=1, source_target_pairs={{0,3},{1,2},{2,1},{3,0},{4,7},{5,6},{6,5},{7,4},{8,11},{9,10},{10,... | collective-permute-start | bytes 884744 | tf_op jit(solution)/shard_map/ppermute | solution.py:45
  51.4 2.0 %collective-permute-start.13 = (bf16[256,576]{1,0:T(8,128)(2,1)}, bf16[256,576]{1,0:T(8,128)(2,1)}, u32[]{:S(2)}, u32[]{:S(2)}) collective-permute-start(bf16[256,576]{1,0:T(8,128)(2,1)} %get-tuple-element.79.refs_0_), channel_id=1, source_target_pairs={{0,16},{16,0},{1,17},{17,1},{2,18},{18,2},{3,19},{19,3},{4,20},{20... | collective-permute-start | bytes 884744 | tf_op jit(solution)/shard_map/ppermute | solution.py:50
  51.4 2.4 %collective-permute-start.14 = (bf16[256,576]{1,0:T(8,128)(2,1)}, bf16[256,576]{1,0:T(8,128)(2,1)}, u32[]{:S(2)}, u32[]{:S(2)}) collective-permute-start(bf16[256,576]{1,0:T(8,128)(2,1)} %get-tuple-element.80.refs_1_), channel_id=1, source_target_pairs={{0,16},{16,0},{1,17},{17,1},{2,18},{18,2},{3,19},{19,3},{4,20},{20... | collective-permute-start | bytes 884744 | tf_op jit(solution)/shard_map/ppermute | solution.py:50
  51.9 2.4 %collective-permute-start.15 = (bf16[256,576]{1,0:T(8,128)(2,1)}, bf16[256,576]{1,0:T(8,128)(2,1)}, u32[]{:S(2)}, u32[]{:S(2)}) collective-permute-start(bf16[256,576]{1,0:T(8,128)(2,1)} %get-tuple-element.81.refs_2_), channel_id=1, source_target_pairs={{0,16},{16,0},{1,17},{17,1},{2,18},{18,2},{3,19},{19,3},{4,20},{20... | collective-permute-start | bytes 884744 | tf_op jit(solution)/shard_map/ppermute | solution.py:50
  51.9 2.9 %collective-permute-start.16 = (bf16[256,576]{1,0:T(8,128)(2,1)}, bf16[256,576]{1,0:T(8,128)(2,1)}, u32[]{:S(2)}, u32[]{:S(2)}) collective-permute-start(bf16[256,576]{1,0:T(8,128)(2,1)} %get-tuple-element.82.refs_3_), channel_id=1, source_target_pairs={{0,16},{16,0},{1,17},{17,1},{2,18},{18,2},{3,19},{19,3},{4,20},{20... | collective-permute-start | bytes 884744 | tf_op jit(solution)/shard_map/ppermute | solution.py:50
  62.4 28.6 %copy-start.1 = (bf16[1,2048,704]{1,2,0:T(8,128)(2,1)S(1)}, bf16[1,2048,704]{1,2,0:T(8,128)(2,1)}, u32[]{:S(2)}) copy-start(bf16[1,2048,704]{1,2,0:T(8,128)(2,1)} %param.29) | copy-start | bytes 8650756
  62.5 28.6 %copy-start.2 = (bf16[1,2048,704]{1,2,0:T(8,128)(2,1)S(1)}, bf16[1,2048,704]{1,2,0:T(8,128)(2,1)}, u32[]{:S(2)}) copy-start(bf16[1,2048,704]{1,2,0:T(8,128)(2,1)} %param.30) | copy-start | bytes 8650756
  62.5 28.6 %copy-start.3 = (bf16[1,704,2048]{2,1,0:T(8,128)(2,1)S(1)}, bf16[1,704,2048]{2,1,0:T(8,128)(2,1)}, u32[]{:S(2)}) copy-start(bf16[1,704,2048]{2,1,0:T(8,128)(2,1)} %param.31) | copy-start | bytes 8650756
  75.0 1.6 collective-permute-start.17
  77.1 9.7 %collective-permute-start.18 = (bf16[64,2048]{1,0:T(8,128)(2,1)S(1)}, bf16[64,2048]{1,0:T(8,128)(2,1)S(1)}, u32[]{:S(2)}, u32[]{:S(2)}) collective-permute-start(bf16[64,2048]{1,0:T(8,128)(2,1)S(1)} %get-tuple-element.88), channel_id=1, source_target_pairs={{0,4},{1,5},{2,6},{3,7},{4,12},{5,13},{6,14},{7,15},{8,0},{9,1},{1... | collective-permute-start | bytes 786440 | tf_op jit(solution)/shard_map/ppermute | solution.py:35
  77.2 5.9 %collective-permute-start.19 = (bf16[32,2048]{1,0:T(8,128)(2,1)S(1)}, bf16[32,2048]{1,0:T(8,128)(2,1)S(1)}, u32[]{:S(2)}, u32[]{:S(2)}) collective-permute-start(bf16[32,2048]{1,0:T(8,128)(2,1)S(1)} %get-tuple-element.90), channel_id=1, source_target_pairs={{0,1},{1,0},{2,3},{3,2},{4,5},{5,4},{6,7},{7,6},{8,9},{9,8},{10,11... | collective-permute-start | bytes 393224 | tf_op jit(solution)/shard_map/ppermute | solution.py:45
  78.7 8.1 %collective-permute-start.20 = (bf16[32,2048]{1,0:T(8,128)(2,1)S(1)}, bf16[32,2048]{1,0:T(8,128)(2,1)S(1)}, u32[]{:S(2)}, u32[]{:S(2)}) collective-permute-start(bf16[32,2048]{1,0:T(8,128)(2,1)S(1)} %get-tuple-element.91), channel_id=1, source_target_pairs={{0,2},{1,3},{2,0},{3,1},{4,6},{5,7},{6,4},{7,5},{8,10},{9,11},{10,... | collective-permute-start | bytes 393224 | tf_op jit(solution)/shard_map/ppermute | solution.py:45
  80.3 6.6 %collective-permute-start.21 = (bf16[32,2048]{1,0:T(8,128)(2,1)S(1)}, bf16[32,2048]{1,0:T(8,128)(2,1)S(1)}, u32[]{:S(2)}, u32[]{:S(2)}) collective-permute-start(bf16[32,2048]{1,0:T(8,128)(2,1)S(1)} %get-tuple-element.92), channel_id=1, source_target_pairs={{0,3},{1,2},{2,1},{3,0},{4,7},{5,6},{6,5},{7,4},{8,11},{9,10},{10,... | collective-permute-start | bytes 393224 | tf_op jit(solution)/shard_map/ppermute | solution.py:45
  87.3 3.7 %collective-permute-start.22 = (bf16[128,2048]{1,0:T(8,128)(2,1)S(1)}, bf16[128,2048]{1,0:T(8,128)(2,1)S(1)}, u32[]{:S(2)}, u32[]{:S(2)}) collective-permute-start(bf16[128,2048]{1,0:T(8,128)(2,1)S(1)} %get-tuple-element.93.refs_0_), channel_id=1, source_target_pairs={{0,16},{16,0},{1,17},{17,1},{2,18},{18,2},{3,19},{19,3},{4,20},{20... | collective-permute-start | bytes 1572872 | tf_op jit(solution)/shard_map/ppermute | solution.py:50
  87.4 9.7 %collective-permute-start.23 = (bf16[64,2048]{1,0:T(8,128)(2,1)S(1)}, bf16[64,2048]{1,0:T(8,128)(2,1)S(1)}, u32[]{:S(2)}, u32[]{:S(2)}) collective-permute-start(bf16[64,2048]{1,0:T(8,128)(2,1)S(1)} %collective-permute-done.18.refs_0_), channel_id=1, source_target_pairs={{0,4},{1,5},{2,6},{3,7},{4,12},{5,13},{6,14},{7,15},{8,0},{9,1},{1... | collective-permute-start | bytes 786440 | tf_op jit(solution)/shard_map/ppermute | solution.py:35
  87.5 8.2 %collective-permute-start.24 = (bf16[32,2048]{1,0:T(8,128)(2,1)S(1)}, bf16[32,2048]{1,0:T(8,128)(2,1)S(1)}, u32[]{:S(2)}, u32[]{:S(2)}) collective-permute-start(bf16[32,2048]{1,0:T(8,128)(2,1)S(1)} %get-tuple-element.96), channel_id=1, source_target_pairs={{0,1},{1,0},{2,3},{3,2},{4,5},{5,4},{6,7},{7,6},{8,9},{9,8},{10,11... | collective-permute-start | bytes 393224 | tf_op jit(solution)/shard_map/ppermute | solution.py:45
  88.8 7.2 %collective-permute-start.25 = (bf16[32,2048]{1,0:T(8,128)(2,1)S(1)}, bf16[32,2048]{1,0:T(8,128)(2,1)S(1)}, u32[]{:S(2)}, u32[]{:S(2)}) collective-permute-start(bf16[32,2048]{1,0:T(8,128)(2,1)S(1)} %get-tuple-element.97), channel_id=1, source_target_pairs={{0,2},{1,3},{2,0},{3,1},{4,6},{5,7},{6,4},{7,5},{8,10},{9,11},{10,... | collective-permute-start | bytes 393224 | tf_op jit(solution)/shard_map/ppermute | solution.py:45
  90.2 6.9 %collective-permute-start.26 = (bf16[32,2048]{1,0:T(8,128)(2,1)S(1)}, bf16[32,2048]{1,0:T(8,128)(2,1)S(1)}, u32[]{:S(2)}, u32[]{:S(2)}) collective-permute-start(bf16[32,2048]{1,0:T(8,128)(2,1)S(1)} %get-tuple-element.98), channel_id=1, source_target_pairs={{0,3},{1,2},{2,1},{3,0},{4,7},{5,6},{6,5},{7,4},{8,11},{9,10},{10,... | collective-permute-start | bytes 393224 | tf_op jit(solution)/shard_map/ppermute | solution.py:45
  97.6 5.1 %collective-permute-start.27 = (bf16[128,2048]{1,0:T(8,128)(2,1)S(1)}, bf16[128,2048]{1,0:T(8,128)(2,1)S(1)}, u32[]{:S(2)}, u32[]{:S(2)}) collective-permute-start(bf16[128,2048]{1,0:T(8,128)(2,1)S(1)} %get-tuple-element.99.refs_1_), channel_id=1, source_target_pairs={{0,16},{16,0},{1,17},{17,1},{2,18},{18,2},{3,19},{19,3},{4,20},{20... | collective-permute-start | bytes 1572872 | tf_op jit(solution)/shard_map/ppermute | solution.py:50
  97.6 9.6 %collective-permute-start.28 = (bf16[64,2048]{1,0:T(8,128)(2,1)S(1)}, bf16[64,2048]{1,0:T(8,128)(2,1)S(1)}, u32[]{:S(2)}, u32[]{:S(2)}) collective-permute-start(bf16[64,2048]{1,0:T(8,128)(2,1)S(1)} %collective-permute-done.23.refs_1_), channel_id=1, source_target_pairs={{0,4},{1,5},{2,6},{3,7},{4,12},{5,13},{6,14},{7,15},{8,0},{9,1},{1... | collective-permute-start | bytes 786440 | tf_op jit(solution)/shard_map/ppermute | solution.py:35
  99.1 8.1 %collective-permute-start.29 = (bf16[32,2048]{1,0:T(8,128)(2,1)S(1)}, bf16[32,2048]{1,0:T(8,128)(2,1)S(1)}, u32[]{:S(2)}, u32[]{:S(2)}) collective-permute-start(bf16[32,2048]{1,0:T(8,128)(2,1)S(1)} %get-tuple-element.102), channel_id=1, source_target_pairs={{0,1},{1,0},{2,3},{3,2},{4,5},{5,4},{6,7},{7,6},{8,9},{9,8},{10,11... | collective-permute-start | bytes 393224 | tf_op jit(solution)/shard_map/ppermute | solution.py:45
  99.9 7.9 %collective-permute-start.30 = (bf16[32,2048]{1,0:T(8,128)(2,1)S(1)}, bf16[32,2048]{1,0:T(8,128)(2,1)S(1)}, u32[]{:S(2)}, u32[]{:S(2)}) collective-permute-start(bf16[32,2048]{1,0:T(8,128)(2,1)S(1)} %get-tuple-element.103), channel_id=1, source_target_pairs={{0,2},{1,3},{2,0},{3,1},{4,6},{5,7},{6,4},{7,5},{8,10},{9,11},{10,... | collective-permute-start | bytes 393224 | tf_op jit(solution)/shard_map/ppermute | solution.py:45
  101.5 6.4 %collective-permute-start.31 = (bf16[32,2048]{1,0:T(8,128)(2,1)S(1)}, bf16[32,2048]{1,0:T(8,128)(2,1)S(1)}, u32[]{:S(2)}, u32[]{:S(2)}) collective-permute-start(bf16[32,2048]{1,0:T(8,128)(2,1)S(1)} %get-tuple-element.104), channel_id=1, source_target_pairs={{0,3},{1,2},{2,1},{3,0},{4,7},{5,6},{6,5},{7,4},{8,11},{9,10},{10,... | collective-permute-start | bytes 393224 | tf_op jit(solution)/shard_map/ppermute | solution.py:45
  108.3 4.1 %collective-permute-start.32 = (bf16[128,2048]{1,0:T(8,128)(2,1)S(1)}, bf16[128,2048]{1,0:T(8,128)(2,1)S(1)}, u32[]{:S(2)}, u32[]{:S(2)}) collective-permute-start(bf16[128,2048]{1,0:T(8,128)(2,1)S(1)} %get-tuple-element.106.refs_1_), channel_id=1, source_target_pairs={{0,16},{16,0},{1,17},{17,1},{2,18},{18,2},{3,19},{19,3},{4,20},{20... | collective-permute-start | bytes 1572872 | tf_op jit(solution)/shard_map/ppermute | solution.py:50
  108.4 10.4 %collective-permute-start.45 = (bf16[128,2048]{1,0:T(8,128)(2,1)S(1)}, bf16[128,2048]{1,0:T(8,128)(2,1)S(1)}, u32[]{:S(2)}, u32[]{:S(2)}) collective-permute-start(bf16[128,2048]{1,0:T(8,128)(2,1)S(1)} %get-tuple-element.125), channel_id=1, source_target_pairs={{0,16},{16,0},{1,17},{17,1},{2,18},{18,2},{3,19},{19,3},{4,20},{20... | collective-permute-start | bytes 1572872 | tf_op jit(solution)/shard_map/ppermute | solution.py:50
  108.9 8.1 %collective-permute-start.33 = (bf16[32,2048]{1,0:T(8,128)(2,1)S(1)}, bf16[32,2048]{1,0:T(8,128)(2,1)S(1)}, u32[]{:S(2)}, u32[]{:S(2)}) collective-permute-start(bf16[32,2048]{1,0:T(8,128)(2,1)S(1)} %get-tuple-element.109), channel_id=1, source_target_pairs={{0,1},{1,0},{2,3},{3,2},{4,5},{5,4},{6,7},{7,6},{8,9},{9,8},{10,11... | collective-permute-start | bytes 393224 | tf_op jit(solution)/shard_map/ppermute | solution.py:45
  110.1 6.8 %collective-permute-start.34 = (bf16[32,2048]{1,0:T(8,128)(2,1)S(1)}, bf16[32,2048]{1,0:T(8,128)(2,1)S(1)}, u32[]{:S(2)}, u32[]{:S(2)}) collective-permute-start(bf16[32,2048]{1,0:T(8,128)(2,1)S(1)} %get-tuple-element.110), channel_id=1, source_target_pairs={{0,2},{1,3},{2,0},{3,1},{4,6},{5,7},{6,4},{7,5},{8,10},{9,11},{10,... | collective-permute-start | bytes 393224 | tf_op jit(solution)/shard_map/ppermute | solution.py:45
  111.0 7.2 %collective-permute-start.35 = (bf16[32,2048]{1,0:T(8,128)(2,1)S(1)}, bf16[32,2048]{1,0:T(8,128)(2,1)S(1)}, u32[]{:S(2)}, u32[]{:S(2)}) collective-permute-start(bf16[32,2048]{1,0:T(8,128)(2,1)S(1)} %get-tuple-element.111), channel_id=1, source_target_pairs={{0,3},{1,2},{2,1},{3,0},{4,7},{5,6},{6,5},{7,4},{8,11},{9,10},{10,... | collective-permute-start | bytes 393224 | tf_op jit(solution)/shard_map/ppermute | solution.py:45
  118.2 4.2 %collective-permute-start.36 = (bf16[128,2048]{1,0:T(8,128)(2,1)S(1)}, bf16[128,2048]{1,0:T(8,128)(2,1)S(1)}, u32[]{:S(2)}, u32[]{:S(2)}) collective-permute-start(bf16[128,2048]{1,0:T(8,128)(2,1)S(1)} %join_rows.1.refs_1_), channel_id=1, source_target_pairs={{0,16},{16,0},{1,17},{17,1},{2,18},{18,2},{3,19},{19,3},{4,20},{20... | collective-permute-start | bytes 1572872 | tf_op jit(solution)/shard_map/ppermute | solution.py:50
  118.3 12.8 %collective-permute-start.41 = (bf16[128,2048]{1,0:T(8,128)(2,1)S(1)}, bf16[128,2048]{1,0:T(8,128)(2,1)S(1)}, u32[]{:S(2)}, u32[]{:S(2)}) collective-permute-start(bf16[128,2048]{1,0:T(8,128)(2,1)S(1)} %get-tuple-element.119), channel_id=1, source_target_pairs={{0,16},{16,0},{1,17},{17,1},{2,18},{18,2},{3,19},{19,3},{4,20},{20... | collective-permute-start | bytes 1572872 | tf_op jit(solution)/shard_map/ppermute | solution.py:50
  118.8 43.0 %slice-start = ((s8[6291456]{0:T(1024)(128)(4,1)}), s8[4194304]{0:T(1024)(128)(4,1)S(1)}, s32[]{:S(2)}) async-start(s8[6291456]{0:T(1024)(128)(4,1)} %bitcast.49), calls=%async_computation | async-start | bytes 8388608
  118.9 8.2 %collective-permute-start.46 = (bf16[32,2048]{1,0:T(8,128)(2,1)S(1)}, bf16[32,2048]{1,0:T(8,128)(2,1)S(1)}, u32[]{:S(2)}, u32[]{:S(2)}) collective-permute-start(bf16[32,2048]{1,0:T(8,128)(2,1)S(1)} %get-tuple-element.127), channel_id=1, source_target_pairs={{0,1},{1,0},{2,3},{3,2},{4,5},{5,4},{6,7},{7,6},{8,9},{9,8},{10,11... | collective-permute-start | bytes 393224 | tf_op jit(solution)/shard_map/ppermute | solution.py:45
  119.7 8.0 %collective-permute-start.47 = (bf16[32,2048]{1,0:T(8,128)(2,1)S(1)}, bf16[32,2048]{1,0:T(8,128)(2,1)S(1)}, u32[]{:S(2)}, u32[]{:S(2)}) collective-permute-start(bf16[32,2048]{1,0:T(8,128)(2,1)S(1)} %get-tuple-element.128), channel_id=1, source_target_pairs={{0,2},{1,3},{2,0},{3,1},{4,6},{5,7},{6,4},{7,5},{8,10},{9,11},{10,... | collective-permute-start | bytes 393224 | tf_op jit(solution)/shard_map/ppermute | solution.py:45
  121.3 40.5 %slice-start.1 = ((s8[6291456]{0:T(1024)(128)(4,1)}), s8[2097152]{0:T(1024)(128)(4,1)S(1)}, s32[]{:S(2)}) async-start(s8[6291456]{0:T(1024)(128)(4,1)} %bitcast.49), calls=%async_computation.1 | async-start | bytes 4194304
  121.3 6.5 %collective-permute-start.48 = (bf16[32,2048]{1,0:T(8,128)(2,1)S(1)}, bf16[32,2048]{1,0:T(8,128)(2,1)S(1)}, u32[]{:S(2)}, u32[]{:S(2)}) collective-permute-start(bf16[32,2048]{1,0:T(8,128)(2,1)S(1)} %get-tuple-element.129), channel_id=1, source_target_pairs={{0,3},{1,2},{2,1},{3,0},{4,7},{5,6},{6,5},{7,4},{8,11},{9,10},{10,... | collective-permute-start | bytes 393224 | tf_op jit(solution)/shard_map/ppermute | solution.py:45
  127.0 14.0 %collective-permute-start.37 = (bf16[128,2048]{1,0:T(8,128)(2,1)S(1)}, bf16[128,2048]{1,0:T(8,128)(2,1)S(1)}, u32[]{:S(2)}, u32[]{:S(2)}) collective-permute-start(bf16[128,2048]{1,0:T(8,128)(2,1)S(1)} %get-tuple-element.113), channel_id=1, source_target_pairs={{0,16},{16,0},{1,17},{17,1},{2,18},{18,2},{3,19},{19,3},{4,20},{20... | collective-permute-start | bytes 1572872 | tf_op jit(solution)/shard_map/ppermute | solution.py:50
  128.0 9.0 %collective-permute-start.49 = (bf16[64,2048]{1,0:T(8,128)(2,1)S(1)}, bf16[64,2048]{1,0:T(8,128)(2,1)S(1)}, u32[]{:S(2)}, u32[]{:S(2)}) collective-permute-start(bf16[64,2048]{1,0:T(8,128)(2,1)S(1)} %collect.3), channel_id=1, source_target_pairs={{0,4},{1,5},{2,6},{3,7},{4,12},{5,13},{6,14},{7,15},{8,0},{9,1},{1... | collective-permute-start | bytes 786440 | tf_op jit(solution)/shard_map/ppermute | solution.py:35
  131.2 23.1 %copy-start.43 = (bf16[2048]{0:T(1024)(128)(2,1)S(1)}, bf16[2048]{0:T(1024)(128)(2,1)}, u32[]{:S(2)}) copy-start(bf16[2048]{0:T(1024)(128)(2,1)} %param.32) | copy-start | bytes 12292
  131.2 6.2 %collective-permute-start.42 = (bf16[32,2048]{1,0:T(8,128)(2,1)S(1)}, bf16[32,2048]{1,0:T(8,128)(2,1)S(1)}, u32[]{:S(2)}, u32[]{:S(2)}) collective-permute-start(bf16[32,2048]{1,0:T(8,128)(2,1)S(1)} %get-tuple-element.121), channel_id=1, source_target_pairs={{0,1},{1,0},{2,3},{3,2},{4,5},{5,4},{6,7},{7,6},{8,9},{9,8},{10,11... | collective-permute-start | bytes 393224 | tf_op jit(solution)/shard_map/ppermute | solution.py:45
  132.5 7.8 %collective-permute-start.43 = (bf16[32,2048]{1,0:T(8,128)(2,1)S(1)}, bf16[32,2048]{1,0:T(8,128)(2,1)S(1)}, u32[]{:S(2)}, u32[]{:S(2)}) collective-permute-start(bf16[32,2048]{1,0:T(8,128)(2,1)S(1)} %get-tuple-element.122), channel_id=1, source_target_pairs={{0,2},{1,3},{2,0},{3,1},{4,6},{5,7},{6,4},{7,5},{8,10},{9,11},{10,... | collective-permute-start | bytes 393224 | tf_op jit(solution)/shard_map/ppermute | solution.py:45
  133.3 7.0 %collective-permute-start.44 = (bf16[32,2048]{1,0:T(8,128)(2,1)S(1)}, bf16[32,2048]{1,0:T(8,128)(2,1)S(1)}, u32[]{:S(2)}, u32[]{:S(2)}) collective-permute-start(bf16[32,2048]{1,0:T(8,128)(2,1)S(1)} %get-tuple-element.123), channel_id=1, source_target_pairs={{0,3},{1,2},{2,1},{3,0},{4,7},{5,6},{6,5},{7,4},{8,11},{9,10},{10,... | collective-permute-start | bytes 393224 | tf_op jit(solution)/shard_map/ppermute | solution.py:45
  137.0 13.7 %collective-permute-start.51 = (bf16[128,2048]{1,0:T(8,128)(2,1)S(1)}, bf16[128,2048]{1,0:T(8,128)(2,1)S(1)}, u32[]{:S(2)}, u32[]{:S(2)}) collective-permute-start(bf16[128,2048]{1,0:T(8,128)(2,1)S(1)} %get-tuple-element.130), channel_id=1, source_target_pairs={{0,16},{16,0},{1,17},{17,1},{2,18},{18,2},{3,19},{19,3},{4,20},{20... | collective-permute-start | bytes 1572872 | tf_op jit(solution)/shard_map/ppermute | solution.py:50
  140.5 7.9 %collective-permute-start.50 = (bf16[64,2048]{1,0:T(8,128)(2,1)S(1)}, bf16[64,2048]{1,0:T(8,128)(2,1)S(1)}, u32[]{:S(2)}, u32[]{:S(2)}) collective-permute-start(bf16[64,2048]{1,0:T(8,128)(2,1)S(1)} %collect.4), channel_id=1, source_target_pairs={{0,4},{1,5},{2,6},{3,7},{4,12},{5,13},{6,14},{7,15},{8,0},{9,1},{1... | collective-permute-start | bytes 786440 | tf_op jit(solution)/shard_map/ppermute | solution.py:35
  141.1 7.4 %collective-permute-start.38 = (bf16[32,2048]{1,0:T(8,128)(2,1)S(1)}, bf16[32,2048]{1,0:T(8,128)(2,1)S(1)}, u32[]{:S(2)}, u32[]{:S(2)}) collective-permute-start(bf16[32,2048]{1,0:T(8,128)(2,1)S(1)} %get-tuple-element.115), channel_id=1, source_target_pairs={{0,1},{1,0},{2,3},{3,2},{4,5},{5,4},{6,7},{7,6},{8,9},{9,8},{10,11... | collective-permute-start | bytes 393224 | tf_op jit(solution)/shard_map/ppermute | solution.py:45
  142.2 7.4 %collective-permute-start.39 = (bf16[32,2048]{1,0:T(8,128)(2,1)S(1)}, bf16[32,2048]{1,0:T(8,128)(2,1)S(1)}, u32[]{:S(2)}, u32[]{:S(2)}) collective-permute-start(bf16[32,2048]{1,0:T(8,128)(2,1)S(1)} %get-tuple-element.116), channel_id=1, source_target_pairs={{0,2},{1,3},{2,0},{3,1},{4,6},{5,7},{6,4},{7,5},{8,10},{9,11},{10,... | collective-permute-start | bytes 393224 | tf_op jit(solution)/shard_map/ppermute | solution.py:45
  143.1 6.5 %collective-permute-start.40 = (bf16[32,2048]{1,0:T(8,128)(2,1)S(1)}, bf16[32,2048]{1,0:T(8,128)(2,1)S(1)}, u32[]{:S(2)}, u32[]{:S(2)}) collective-permute-start(bf16[32,2048]{1,0:T(8,128)(2,1)S(1)} %get-tuple-element.117), channel_id=1, source_target_pairs={{0,3},{1,2},{2,1},{3,0},{4,7},{5,6},{6,5},{7,4},{8,11},{9,10},{10,... | collective-permute-start | bytes 393224 | tf_op jit(solution)/shard_map/ppermute | solution.py:45
  149.9 9.0 %collective-permute-start.55 = (bf16[64,2048]{1,0:T(8,128)(2,1)S(1)}, bf16[64,2048]{1,0:T(8,128)(2,1)S(1)}, u32[]{:S(2)}, u32[]{:S(2)}) collective-permute-start(bf16[64,2048]{1,0:T(8,128)(2,1)S(1)} %collect.5.refs_0_), channel_id=1, source_target_pairs={{0,4},{1,5},{2,6},{3,7},{4,12},{5,13},{6,14},{7,15},{8,0},{9,1},{1... | collective-permute-start | bytes 786440 | tf_op jit(solution)/shard_map/ppermute | solution.py:35
  150.8 6.1 %collective-permute-start.52 = (bf16[32,2048]{1,0:T(8,128)(2,1)S(1)}, bf16[32,2048]{1,0:T(8,128)(2,1)S(1)}, u32[]{:S(2)}, u32[]{:S(2)}) collective-permute-start(bf16[32,2048]{1,0:T(8,128)(2,1)S(1)} %get-tuple-element.132), channel_id=1, source_target_pairs={{0,1},{1,0},{2,3},{3,2},{4,5},{5,4},{6,7},{7,6},{8,9},{9,8},{10,11... | collective-permute-start | bytes 393224 | tf_op jit(solution)/shard_map/ppermute | solution.py:45
  151.9 5.3 %collective-permute-start.53 = (bf16[32,2048]{1,0:T(8,128)(2,1)S(1)}, bf16[32,2048]{1,0:T(8,128)(2,1)S(1)}, u32[]{:S(2)}, u32[]{:S(2)}) collective-permute-start(bf16[32,2048]{1,0:T(8,128)(2,1)S(1)} %get-tuple-element.133), channel_id=1, source_target_pairs={{0,2},{1,3},{2,0},{3,1},{4,6},{5,7},{6,4},{7,5},{8,10},{9,11},{10,... | collective-permute-start | bytes 393224 | tf_op jit(solution)/shard_map/ppermute | solution.py:45
  153.0 5.9 %collective-permute-start.54 = (bf16[32,2048]{1,0:T(8,128)(2,1)S(1)}, bf16[32,2048]{1,0:T(8,128)(2,1)S(1)}, u32[]{:S(2)}, u32[]{:S(2)}) collective-permute-start(bf16[32,2048]{1,0:T(8,128)(2,1)S(1)} %get-tuple-element.134), channel_id=1, source_target_pairs={{0,3},{1,2},{2,1},{3,0},{4,7},{5,6},{6,5},{7,4},{8,11},{9,10},{10,... | collective-permute-start | bytes 393224 | tf_op jit(solution)/shard_map/ppermute | solution.py:45
  159.8 1.5 collective-permute-start.56
  (39 other events, 162.5 us)

commit v3 on v2

--- a/solution.py
+++ b/solution.py
@@ -3,6 +3,7 @@
 
 import jax
 import jax.numpy as jnp
+import numpy as np
 from jax import lax
 from jax.experimental import pallas as pl
 from jax.experimental.pallas import tpu as pltpu
@@ -14,6 +15,7 @@
 PAGE = 8
 PLANE = 4
 ROUTE_ROWS = 16
+WIDE = 640
 
 VERY_NEGATIVE = -1e30
 ROUTE_SCALING = 2.446
@@ -103,7 +105,7 @@
     tokens = suffix_columns.shape[1]
     top, groups, _ = routes_columns.shape
 
-    def kernel(piece_ref, suffix_ref, routes_ref, near_ref, full_ref, lite_ref):
+    def kernel(piece_ref, suffix_ref, routes_ref, full_ref, lite_ref):
         group_index = lax.axis_index("group")
         shape = (tok_quarter, tokens)
         row = lax.broadcasted_iota(jnp.int32, shape, 0)
@@ -114,70 +116,173 @@
         for j in range(groups):
             part = routes_ref[:, j, :].astype(jnp.float32)
             named = jnp.where(group_index == j, part, named)
-        named = jnp.concatenate(
-            [named, jnp.zeros((ROUTE_ROWS - top, tok_quarter), jnp.float32)], axis=0
-        )
-        named = jnp.concatenate(
-            [named, jnp.zeros((ROUTE_ROWS, piece_ref.shape[1] - tok_quarter), jnp.float32)], axis=1
-        ).astype(jnp.bfloat16)
+        named = jnp.concatenate([named, jnp.zeros((rows - top, tok_quarter), jnp.float32)], axis=0)
+        spare = WIDE - LAT - ROPE - tok_quarter
+        if spare:
+            named = jnp.concatenate([named, jnp.zeros((rows, spare), jnp.float32)], axis=1)
+        named = named.astype(jnp.bfloat16)
         piece = piece_ref[...]
-        near_ref[:rows, :] = piece
-        near_ref[rows:, :] = share
-        full_ref[:rows, :] = piece
-        full_ref[rows : rows + tok_quarter, :] = share
-        full_ref[rows + tok_quarter :, :] = named
-        lite_ref[:rows, :] = piece
-        lite_ref[rows:, :] = named
-
-    width = piece.shape[1]
-    sizes = [rows + tok_quarter, rows + tok_quarter + ROUTE_ROWS, rows + ROUTE_ROWS]
-    outputs = [((size, width), piece.dtype) for size in sizes]
+        last = jnp.concatenate([piece[:, LAT:], named], axis=1)
+        for ref in (full_ref, lite_ref):
+            ref[:rows, :LAT] = piece[:, :LAT]
+            ref[:rows, LAT:] = last
+        empty = jnp.zeros((tok_quarter, WIDE - LAT - ROPE), jnp.bfloat16)
+        full_ref[rows:, :LAT] = share[:, :LAT]
+        full_ref[rows:, LAT:] = jnp.concatenate([share[:, LAT:], empty], axis=1)
+
+    outputs = [((size, WIDE), piece.dtype) for size in (rows + tok_quarter, rows)]
     inputs = [piece, suffix_columns, routes_columns]
-    return call(kernel, "join_share", inputs, outputs, 10_000_000)
-
-
-def join_column(full, lites, own, rows):
-    share = full.shape[0] - rows - ROUTE_ROWS
+    return call(kernel, "join_share", inputs, outputs, 10_000_000, limit=58)
+
+
+def join_column(blocks, rows, share):
+    count = len(blocks)
 
     def kernel(*refs):
-        full_ref, *lite_refs, own_ref, column_ref, routes_ref = refs
-        column_ref[: rows + share, :] = full_ref[: rows + share, :]
-        routes_ref[0] = own_ref[rows:, :128]
-        routes_ref[1] = full_ref[rows + share :, :128]
-        at = rows + share
-        for i, ref in enumerate(lite_refs):
-            column_ref[at : at + rows, :] = ref[:rows, :]
-            routes_ref[i + 2] = ref[rows:, :128]
-            at += rows
-
-    count = len(lites)
-    outputs = [
-        ((rows + share + count * rows, full.shape[1]), full.dtype),
-        ((count + 2, ROUTE_ROWS, 128), full.dtype),
-    ]
-    return call(kernel, "join_column", [full, *lites, own], outputs, 0)
-
-
-def join_rows(*blocks, ready=()):
+        block_refs = refs[:count]
+        near_ref, *far_refs, routes_ref = refs[count:]
+        plane_index = lax.rem(lax.axis_index("tensor"), PLANE)
+        at = 0
+        for i, ref in enumerate(block_refs):
+            near_ref[at : at + ref.shape[0], :] = ref[...]
+            at += ref.shape[0]
+            routes_ref[i] = ref[:ROUTE_ROWS, LAT:]
+        here = block_refs[0][rows:, :].astype(jnp.float32)
+        before = block_refs[1][rows:, :].astype(jnp.float32)
+        for d, far_ref in enumerate(far_refs):
+            for i, ref in enumerate(block_refs):
+                far_ref[i * rows : (i + 1) * rows, :] = ref[:rows, :]
+            later = plane_index < lax.bitwise_xor(plane_index, d + 1)
+            part = jnp.where(later, here, before).astype(jnp.bfloat16)
+            far_ref[count * rows :, :] = part
+
+    dtype = blocks[0].dtype
+    outputs = [((count * rows + 2 * share, WIDE), dtype)]
+    outputs += [((count * rows + share, WIDE), dtype)] * (PLANE - 1)
+    outputs.append(((count, ROUTE_ROWS, WIDE - LAT), dtype))
+    near, *far, routes = call(kernel, "join_column", blocks, outputs, 0)
+    return near, far, routes
+
+
+def pass_on(blocks, ready):
+    first = len(ready)
+
     def kernel(*refs):
-        out = refs[-1]
-        at = 0
-        for ref in refs[:-1]:
-            out[at : at + ref.shape[0], :] = ref[...]
-            at += ref.shape[0]
-
-    rows = sum(block.shape[0] for block in blocks)
-    shape = (rows, blocks[0].shape[1])
-    return call(kernel, "join_rows", blocks, [(shape, blocks[0].dtype)], 0, ready=ready)[0]
-
-
-def pass_on(blocks, ready=()):
-    def kernel(*refs):
-        for ref, out in zip(refs[: len(blocks)], refs[len(blocks) :]):
-            out[...] = ref[...]
-
-    outputs = [(block.shape, block.dtype) for block in blocks]
-    return call(kernel, "pass_on", blocks, outputs, 0, ready=ready)
+        pass
+
+    return pl.pallas_call(
+        kernel,
+        in_specs=unread(ready) + unread(blocks),
+        out_specs=unread(blocks),
+        out_shape=[jax.ShapeDtypeStruct(block.shape, block.dtype) for block in blocks],
+        input_output_aliases={first + i: i for i in range(len(blocks))},
+        compiler_params=pltpu.CompilerParams(vmem_limit_bytes=1024 * 1024),
+        name="pass_on",
+    )(*ready, *blocks)
+
+
+LATER = 1 << 20
+
+
+def key_table(groups, planes, segments):
+    rows = []
+    for j in range(groups):
+        for d in planes:
+            for k, count, real, suffix in segments:
+                rows += [(j, d, k, r, suffix, r < real) for r in range(count)]
+    table = np.zeros((8, len(rows)), np.int32)
+    table[:6] = np.array(rows, np.int32).T
+    table[6] = table[3] // PAGE
+    table[7] = table[3] % PAGE
+    return table
+
+
+def make_plan(tables, lengths, tenants, tenant_lengths, page_table, ring, piece_rows, sizes, ready):
+    tok_slice, tok_quarter, groups = sizes
+    requests = lengths.shape[0]
+    tenant_count = tenant_lengths.shape[0]
+    pages = page_table.shape[1]
+    piece_pages = piece_rows // PAGE
+
+    def spots_of(table, page_row, group_index, ring_index, plane_index):
+        j, d, k, r, suffix, real, page_at, within = (table[i : i + 1, :] for i in range(8))
+        in_plane = lax.bitwise_xor(plane_index, d)
+        k = jnp.where(suffix == 2, jnp.where(in_plane < plane_index, 0, 1), k)
+        from_ring = ring_index - k
+        from_ring = jnp.where(from_ring < 0, from_ring + ring, from_ring)
+        of_group = lax.bitwise_xor(group_index, j)
+        owner = (of_group * ring + from_ring) * PLANE + in_plane
+        index = owner * piece_pages + page_at
+        count = table.shape[1]
+        page = lax.broadcasted_iota(jnp.int32, (pages, count), 0)
+        hit = jnp.where(page == index, 1.0, 0.0).astype(jnp.bfloat16)
+        found = dot_f(page_row, hit)[:1].astype(jnp.int32)
+        logical = jnp.where(real > 0, found * PAGE + within, -1)
+        token = (from_ring * PLANE + in_plane) * tok_slice + of_group * tok_quarter + r
+        return jnp.where(suffix > 0, token + LATER, logical)
+
+    def kernel(lengths_ref, tenants_ref, tenant_lengths_ref, page_ref, *refs):
+        table_refs = refs[: len(tables)]
+        info_ref, order_ref, *spot_refs = refs[len(tables) :]
+        group_index = jnp.full((1, 1), lax.axis_index("group"), jnp.int32)
+        tensor_index = lax.axis_index("tensor")
+        ring_index = jnp.full((1, 1), lax.div(tensor_index, PLANE), jnp.int32)
+        plane_index = jnp.full((1, 1), lax.rem(tensor_index, PLANE), jnp.int32)
+        page_row = page_ref[...].astype(jnp.float32).astype(jnp.bfloat16)
+        page_row = jnp.broadcast_to(page_row, (16, pages))
+        for table_ref, spot_ref in zip(table_refs, spot_refs):
+            spot_ref[...] = spots_of(
+                table_ref[...], page_row, group_index, ring_index, plane_index
+            )
+        row = lax.broadcasted_iota(jnp.int32, (tok_slice, 1), 0)
+        share = jnp.zeros((tok_slice, 1), jnp.int32)
+        for j in range(1, groups):
+            share = share + jnp.where(row >= j * tok_quarter, 1, 0)
+        local = (row - share * tok_quarter) * groups + lax.bitwise_xor(group_index, share)
+        column = lax.broadcasted_iota(jnp.int32, (tok_slice, tok_slice), 1)
+        order_ref[...] = jnp.where(column == local, 1.0, 0.0).astype(jnp.bfloat16)
+        position = local + tensor_index * tok_slice
+        low = jnp.zeros((tok_slice, 1), jnp.int32)
+        high = jnp.zeros((tok_slice, 1), jnp.int32)
+        start = jnp.zeros((tok_slice, 1), jnp.int32)
+        begin = 0
+        for i in range(requests):
+            end = begin + lengths_ref[i]
+            inside = (position >= begin) & (position < end)
+            tenant = tenants_ref[i]
+            first = 0
+            tenant_low = 0
+            tenant_high = 0
+            for t in range(tenant_count):
+                last = first + tenant_lengths_ref[t]
+                tenant_low = jnp.where(tenant == t, first, tenant_low)
+                tenant_high = jnp.where(tenant == t, last, tenant_high)
+                first = last
+            start = jnp.where(inside, begin, start)
+            low = jnp.where(inside, tenant_low, low)
+            high = jnp.where(inside, tenant_high, high)
+            begin = end
+        for i, value in enumerate((low, high, start + LATER, position + LATER)):
+            info_ref[:, i : i + 1] = value
+
+    shapes = [
+        jax.ShapeDtypeStruct((tok_slice, 4), jnp.int32),
+        jax.ShapeDtypeStruct((tok_slice, tok_slice), jnp.bfloat16),
+    ] + [jax.ShapeDtypeStruct((1, table.shape[1]), jnp.int32) for table in tables]
+    scalar = pl.BlockSpec(memory_space=pltpu.SMEM)
+    arrays = [page_table, *tables]
+    return pl.pallas_call(
+        after(kernel, len(ready)),
+        grid=(1,),
+        in_specs=unread(ready) + [scalar, scalar, scalar] + [whole(a) for a in arrays],
+        out_specs=[whole(shape) for shape in shapes],
+        out_shape=shapes,
+        compiler_params=pltpu.CompilerParams(vmem_limit_bytes=58 * 1024 * 1024),
+        cost_estimate=pl.CostEstimate(
+            flops=4_000_000_000, bytes_accessed=1_000_000, transcendentals=0
+        ),
+        name="make_plan",
+    )(*ready, lengths, tenants, tenant_lengths, *arrays)
 
 
 def place_keys(key_refs, spot_ref, token_ref, keys, bias):
@@ -196,8 +301,8 @@
 SCORE_FACTOR = math.log2(math.e) / math.sqrt(NOPE + ROPE)
 
 
-def score_rows(content, rotated, keys, bias, pair):
-    scores = dot_t(content, keys[:, :LAT]) + dot_t(rotated, keys[:, LAT:])
+def score_rows(queries, keys, bias, pair):
+    scores = dot_t(queries, keys[...])
     rows, count = scores.shape
     return (scores.reshape(pair, rows // pair, count) + bias[...][None]).reshape(rows, count)
 
@@ -206,7 +311,8 @@
     block_count, token_ref, spot_ref, order_ref, query_ref, key_up_ref, *refs
 ):
     key_refs = refs[:block_count]
-    content_ref, rotated_ref, best_ref, sum_ref, acc_ref, keys, bias = refs[block_count:]
+    wide_ref, best_ref, sum_ref, acc_ref, flag_ref, keys, bias = refs[block_count:]
+    flag_ref[...] = jnp.zeros_like(flag_ref)
     tokens = query_ref.shape[0]
     pair = key_up_ref.shape[0]
 
@@ -216,17 +322,15 @@
 
     queries = dot_f(order_ref[...], query_ref[...]).astype(jnp.bfloat16)
     size = NOPE + ROPE
-    content = []
-    rotated = []
+    wide = []
+    empty = jnp.zeros((tokens, WIDE - LAT - ROPE), jnp.bfloat16)
     for h in range(pair):
         part = queries[:, h * size : (h + 1) * size]
-        content.append(dot_f(part[:, :NOPE], key_up_ref[h]).astype(jnp.bfloat16))
-        rotated.append(part[:, NOPE:])
-    content = jnp.concatenate(content, axis=0)
-    rotated = jnp.concatenate(rotated, axis=0)
-    content_ref[...] = content
-    rotated_ref[...] = rotated
-    masked = score_rows(content, rotated, keys, bias, pair)
+        content = dot_f(part[:, :NOPE], key_up_ref[h]).astype(jnp.bfloat16)
+        wide.append(jnp.concatenate([content, part[:, NOPE:], empty], axis=1))
+    wide = jnp.concatenate(wide, axis=0)
+    wide_ref[...] = wide
+    masked = score_rows(wide, keys, bias, pair)
     best = jnp.max(masked, axis=-1, keepdims=True)
     weights = jnp.exp2((masked - best) * SCORE_FACTOR)
     best_ref[...] = best
@@ -237,7 +341,7 @@
 def attend_near(tokens_info, spots, order, queries, key_up, blocks, ready):
     tokens = queries.shape[0]
     heads = key_up.shape[0]
-    pair = 2
+    pair = min(4, heads)
     count = sum(block.shape[0] for block in blocks)
     size = NOPE + ROPE
 
@@ -257,19 +361,20 @@
             pl.BlockSpec((pair, NOPE, LAT), lambda i: (i, 0, 0)),
         ]
         + [whole(block) for block in blocks],
-        out_specs=[per_step(LAT), per_step(ROPE), per_step(1), per_step(1), per_step(LAT)],
+        out_specs=[per_step(WIDE), per_step(1), per_step(1), per_step(LAT)]
+        + [pl.BlockSpec((8, 128), lambda i: (0, 0))],
         out_shape=[
-            jax.ShapeDtypeStruct((rows, LAT), jnp.bfloat16),
-            jax.ShapeDtypeStruct((rows, ROPE), jnp.bfloat16),
+            jax.ShapeDtypeStruct((rows, WIDE), jnp.bfloat16),
             jax.ShapeDtypeStruct((rows, 1), jnp.float32),
             jax.ShapeDtypeStruct((rows, 1), jnp.float32),
             jax.ShapeDtypeStruct((rows, LAT), jnp.float32),
+            jax.ShapeDtypeStruct((8, 128), jnp.float32),
         ],
         scratch_shapes=[
-            pltpu.VMEM((count, LAT + ROPE), jnp.bfloat16),
+            pltpu.VMEM((count, WIDE), jnp.bfloat16),
             pltpu.VMEM((tokens, count), jnp.float32),
         ],
-        compiler_params=pltpu.CompilerParams(vmem_limit_bytes=24 * 1024 * 1024),
+        compiler_params=pltpu.CompilerParams(vmem_limit_bytes=58 * 1024 * 1024),
         cost_estimate=pl.CostEstimate(
             flops=2 * rows * count * (LAT + ROPE + LAT),
             bytes_accessed=8_000_000,
@@ -279,13 +384,75 @@
     )(*ready, tokens_info, spots, order, queries, key_up, *blocks)
 
 
+def add_keys(wide_ref, best_ref, sum_ref, acc_ref, keys, bias, pair):
+    masked = score_rows(wide_ref[...], keys, bias, pair)
+    before = best_ref[...]
+    best = jnp.maximum(before, jnp.max(masked, axis=-1, keepdims=True))
+    factor = jnp.exp2((before - best) * SCORE_FACTOR)
+    weights = jnp.exp2((masked - best) * SCORE_FACTOR)
+    weight_sum = sum_ref[...] * factor + jnp.sum(weights, axis=-1, keepdims=True)
+    attended = acc_ref[...] * factor + dot_f(weights.astype(jnp.bfloat16), keys[:, :LAT])
+    return best, weight_sum, attended
+
+
+def mid_kernel(block_count, pair, token_ref, spot_ref, wide_ref, best_ref, sum_ref, acc_ref, *refs):
+    key_refs = refs[:block_count]
+    new_best_ref, new_sum_ref, new_acc_ref, flag_ref, keys, bias = refs[block_count:]
+    flag_ref[...] = jnp.zeros_like(flag_ref)
+
+    @pl.when(pl.program_id(0) == 0)
+    def prepare():
+        place_keys(key_refs, spot_ref, token_ref, keys, bias)
+
+    new_best_ref[...], new_sum_ref[...], new_acc_ref[...] = add_keys(
+        wide_ref, best_ref, sum_ref, acc_ref, keys, bias, pair
+    )
+
+
+def attend_mid(tokens_info, spots, near, blocks):
+    tokens = tokens_info.shape[0]
+    rows = near[0].shape[0]
+    heads = rows // tokens
+    pair = min(4, heads)
+    count = sum(block.shape[0] for block in blocks)
+
+    def per_step(columns):
+        return pl.BlockSpec((pair * tokens, columns), lambda i: (i, 0))
+
+    return pl.pallas_call(
+        functools.partial(mid_kernel, len(blocks), pair),
+        grid=(heads // pair,),
+        in_specs=[whole(tokens_info), whole(spots)]
+        + [per_step(WIDE), per_step(1), per_step(1), per_step(LAT)]
+        + [whole(block) for block in blocks],
+        out_specs=[per_step(1), per_step(1), per_step(LAT)]
+        + [pl.BlockSpec((8, 128), lambda i: (0, 0))],
+        out_shape=[
+            jax.ShapeDtypeStruct((rows, 1), jnp.float32),
+            jax.ShapeDtypeStruct((rows, 1), jnp.float32),
+            jax.ShapeDtypeStruct((rows, LAT), jnp.float32),
+            jax.ShapeDtypeStruct((8, 128), jnp.float32),
+        ],
+        scratch_shapes=[
+            pltpu.VMEM((count, WIDE), jnp.bfloat16),
+            pltpu.VMEM((tokens, count), jnp.float32),
+        ],
+        compiler_params=pltpu.CompilerParams(vmem_limit_bytes=58 * 1024 * 1024),
+        cost_estimate=pl.CostEstimate(
+            flops=2 * rows * count * (LAT + ROPE + LAT),
+            bytes_accessed=8_000_000,
+            transcendentals=rows * count,
+        ),
+        name="attend_mid",
+    )(tokens_info, spots, *near, *blocks)
+
+
 def far_kernel(
     block_count,
     tok_quarter,
     token_ref,
     spot_ref,
-    content_ref,
-    rotated_ref,
+    wide_ref,
     best_ref,
     sum_ref,
     acc_ref,
@@ -297,20 +464,14 @@
     own_ref, other_ref, keys, bias, total = refs[block_count:]
     step = pl.program_id(0)
     pair = value_up_ref.shape[0]
-    tokens = content_ref.shape[0] // pair
+    tokens = wide_ref.shape[0] // pair
 
     @pl.when(step == 0)
     def prepare():
         place_keys(key_refs, spot_ref, token_ref, keys, bias)
         total[...] = jnp.zeros_like(total)
 
-    masked = score_rows(content_ref[...], rotated_ref[...], keys, bias, pair)
-    before = best_ref[...]
-    best = jnp.maximum(before, jnp.max(masked, axis=-1, keepdims=True))
-    factor = jnp.exp2((before - best) * SCORE_FACTOR)
-    weights = jnp.exp2((masked - best) * SCORE_FACTOR)
-    weight_sum = sum_ref[...] * factor + jnp.sum(weights, axis=-1, keepdims=True)
-    attended = acc_ref[...] * factor + dot_f(weights.astype(jnp.bfloat16), keys[:, :LAT])
+    _, weight_sum, attended = add_keys(wide_ref, best_ref, sum_ref, acc_ref, keys, bias, pair)
     attended = (attended / weight_sum).astype(jnp.bfloat16)
     heads = [
         dot_f(attended[h * tokens : (h + 1) * tokens], value_up_ref[h]).astype(jnp.bfloat16)
@@ -328,7 +489,7 @@
     tokens = tokens_info.shape[0]
     heads = value_up.shape[0]
     width = output_weight.shape[1]
-    pair = 2
+    pair = min(4, heads)
     count = sum(block.shape[0] for block in blocks)
     rows = heads * tokens
 
@@ -341,8 +502,7 @@
         in_specs=[
             whole(tokens_info),
             whole(spots),
-            per_step(LAT),
-            per_step(ROPE),
+            per_step(WIDE),
             per_step(1),
             per_step(1),
             per_step(LAT),
@@ -359,11 +519,11 @@
             jax.ShapeDtypeStruct((tokens - tok_quarter, width), jnp.bfloat16),
         ],
         scratch_shapes=[
-            pltpu.VMEM((count, LAT + ROPE), jnp.bfloat16),
+            pltpu.VMEM((count, WIDE), jnp.bfloat16),
             pltpu.VMEM((tokens, count), jnp.float32),
             pltpu.VMEM((tokens, width), jnp.float32),
         ],
-        compiler_params=pltpu.CompilerParams(vmem_limit_bytes=24 * 1024 * 1024),
+        compiler_params=pltpu.CompilerParams(vmem_limit_bytes=58 * 1024 * 1024),
         cost_estimate=pl.CostEstimate(
             flops=2 * rows * count * (LAT + ROPE + LAT),
             bytes_accessed=12_000_000,
@@ -383,7 +543,8 @@
     place = sum(jnp.where(here == z, i, 0) for i, z in enumerate(order))
     place = lax.rem(place - turn + ring, ring)
     source = sum(jnp.where(place == i, z, 0) for i, z in enumerate(order))
-    routes = routes_ref[lax.rem(here - source + ring, ring)][:, :tokens].astype(jnp.float32)
+    routes = routes_ref[lax.rem(here - source + ring, ring)].astype(jnp.float32)
+    routes = routes[:, ROPE : ROPE + tokens]
     targets = [
         (here * PLANE + lax.bitwise_xor(plane_index, d)).astype(jnp.float32)
         for d in range(PLANE)
@@ -436,30 +597,66 @@
 
     outputs = [(hidden.shape, jnp.bfloat16)] * 2 + pick_outputs(hidden, capacity)
     inputs = [hidden, own, *others, gain, routes, router]
-    residual, normed, scaled, *pieces = call(kernel, "settle", inputs, outputs, 70_000_000)
+    residual, normed, scaled, *pieces = call(kernel, "settle", inputs, outputs, 10_000_000_000)
     return residual, normed, scaled, pieces
 
 
-def choose(turn, block, arrived, routes, router, sizes, ready):
+def turn(step, block, arrived, results, routes, router, sizes, ready):
     ring, top, capacity = sizes
-
-    def kernel(block_ref, routes_ref, router_ref, *refs):
-        row_refs = refs[:PLANE]
-        joined_ref, scaled_ref, *outs = refs[PLANE:]
-        pick_rows(turn, ring, top, block_ref[...], routes_ref, router_ref, scaled_ref, outs)
-        for d, ref in enumerate(row_refs):
-            joined_ref[d * capacity : (d + 1) * capacity, :] = ref[...]
-
-    joined = ((PLANE * capacity, block.shape[1]), jnp.bfloat16)
-    outputs = [joined] + pick_outputs(block, capacity)
-    inputs = [block, routes, router, *arrived]
-    joined, scaled, *pieces = call(kernel, "choose", inputs, outputs, 70_000_000, ready=ready)
-    return joined, scaled, pieces
+    inputs = []
+    outputs = []
+    width = arrived[0].shape[1]
+    rows = 0
+    if block is not None:
+        inputs += [block, routes, router]
+        outputs.append(((PLANE * capacity, block.shape[0]), jnp.bfloat16))
+        rows += capacity
+    if results is not None:
+        inputs += results
+        rows += capacity
+    joining = step <= ring
+    if joining:
+        inputs += arrived
+        outputs.append(((PLANE * capacity, width), jnp.bfloat16))
+    count = len(inputs)
+    outputs += [((rows, width), jnp.bfloat16)] * PLANE
+
+    def kernel(*refs):
+        taken = list(refs[:count])
+        given = list(refs[count:])
+        outs = given[-PLANE:]
+        at = 0
+        if block is not None:
+            block_ref, routes_ref, router_ref = taken[:3]
+            taken = taken[3:]
+            parts = [out.at[pl.ds(0, capacity), :] for out in outs]
+            values = block_ref[...]
+            pick_rows(step, ring, top, values, routes_ref, router_ref, given.pop(0), parts)
+            at = capacity
+        if results is not None:
+            total = taken[0][...]
+            for ref in taken[1 : len(results)]:
+                total = total + ref[...].astype(jnp.float32)
+            taken = taken[len(results) :]
+            total = total.astype(jnp.bfloat16)
+            for d, out in enumerate(outs):
+                out[at : at + capacity, :] = total[d * capacity : (d + 1) * capacity]
+        if joining:
+            joined_ref = given.pop(0)
+            for d, ref in enumerate(taken):
+                joined_ref[d * capacity : (d + 1) * capacity, :] = ref[:capacity, :]
+
+    found = list(call(kernel, "turn", inputs, outputs, 70_000_000, ready=ready))
+    scaled = found.pop(0) if block is not None else None
+    joined = found.pop(0) if joining else None
+    return scaled, joined, found
 
 
 def expert_kernel(count, kept, depth_steps, *refs):
     row_refs = refs[:count]
-    gate_ref, up_ref, down_ref, own_ref, other_ref, rows, gate_sum, up_sum, hidden = refs[count:]
+    gate_ref, up_ref, down_ref, own_ref, other_ref, flag_ref, *scratch = refs[count:]
+    rows, gate_sum, up_sum, hidden = scratch
+    flag_ref[...] = jnp.zeros_like(flag_ref)
     step = pl.program_id(0)
     depth = gate_ref.shape[1]
 
@@ -516,10 +713,12 @@
         out_specs=[
             pl.BlockSpec((kept, depth), lambda i: (0, jnp.maximum(i - steps, 0))),
             pl.BlockSpec((total - kept, depth), lambda i: (0, jnp.maximum(i - steps, 0))),
+            pl.BlockSpec((8, 128), lambda i: (0, 0)),
         ],
         out_shape=[
             jax.ShapeDtypeStruct((kept, width), jnp.float32),
             jax.ShapeDtypeStruct((total - kept, width), jnp.bfloat16),
+            jax.ShapeDtypeStruct((8, 128), jnp.float32),
         ],
         scratch_shapes=[
             pltpu.VMEM((steps, total, depth), jnp.bfloat16),
@@ -535,26 +734,10 @@
     )(*ready, *pieces, gate_part, up_part, down_part)
 
 
-def blend(own, others, pieces, ready):
-    def kernel(own_ref, *refs):
-        other_refs = refs[: len(others)]
-        outs = refs[len(others) :]
-        total = own_ref[...]
-        for ref in other_refs:
-            total = total + ref[...].astype(jnp.float32)
-        total = total.astype(jnp.bfloat16)
-        size = outs[0].shape[0]
-        for d, out in enumerate(outs):
-            out[...] = total[d * size : (d + 1) * size]
-
-    shape = (own.shape[0] // pieces, own.shape[1])
-    outputs = [(shape, jnp.bfloat16)] * pieces
-    return call(kernel, "blend", [own, *others], outputs, 1_000_000, ready=ready)
-
-
 def scatter_sum(scaled_ref, piece_refs, running_ref):
-    size = piece_refs[0].shape[0]
-    returned = jnp.concatenate([ref[...] for ref in piece_refs], axis=0)
+    size = scaled_ref.shape[0] // PLANE
+    parts = [ref[ref.shape[0] - size :, :] for ref in piece_refs]
+    returned = jnp.concatenate(parts, axis=0)
     total = lax.dot_general(
         scaled_ref[...], returned, (((0,), (0,)), ((), ())), preferred_element_type=jnp.float32
     )
@@ -615,16 +798,11 @@
     tok_slice = hidden_in.shape[0]
     groups = lax.axis_size("group")
     ring = lax.axis_size("tensor") // PLANE
-    group_index = lax.axis_index("group")
-    tensor_index = lax.axis_index("tensor")
-    ring_index = tensor_index // PLANE
-    plane_index = tensor_index % PLANE
     tok_quarter = tok_slice // groups
     expert_count = router.shape[1]
     top_count = routes.shape[2]
     capacity = max(2, 4 * tok_quarter * top_count // (3 * expert_count))
     capacity = -(-capacity // 16) * 16
-    int32 = jnp.int32
 
     real_rows = prefix_latent.shape[0]
     piece_rows = -(-real_rows // 16) * 16
@@ -632,78 +810,47 @@
     if piece_rows != real_rows:
         piece = jnp.pad(piece, ((0, piece_rows - real_rows), (0, 0)))
     routes_columns = jnp.transpose(routes, (2, 0, 1))
-    both, full, lite = join_share(piece, suffix_latent.T, routes_columns, tok_quarter)
+    full, lite = join_share(piece, suffix_latent.T, routes_columns, tok_quarter)
     along = [send_round(full, PLANE)] + [send_round(lite, PLANE * k) for k in range(2, ring)]
-    near_plane = [send_plane(both, d) if d else both for d in range(PLANE)]
-    near_blocks = [
-        send_group(block, j) if j else block for j in range(groups) for block in near_plane
-    ]
-    column, routes_ring = join_column(along[0], along[1:], lite, piece_rows)
-    far_plane = [send_plane(column, d) if d else column for d in range(PLANE)]
-
-    later = 1 << 20
-    first_token = tensor_index * tok_slice
-
-    pages = real_rows // PAGE
-
-    def positions_of(steps, with_suffix):
-        parts = []
-        for k in steps:
-            from_ring = (ring_index - k + ring) % ring
-            shape = (groups, PLANE, piece_rows)
-            j, d, r = (lax.broadcasted_iota(int32, shape, axis) for axis in range(3))
-            owner = ((group_index ^ j) * ring + from_ring) * PLANE + (plane_index ^ d)
-            spot = owner * real_rows + r
-            page = owner[:, :, :pages] * pages + r[:, :, :pages]
-            hit = page[..., None] == jnp.arange(page_table.shape[0], dtype=int32)
-            page = jnp.sum(jnp.where(hit, page_table, 0), axis=-1)
-            page = jnp.repeat(page, PAGE, axis=2)
-            page = jnp.pad(page, ((0, 0), (0, 0), (0, piece_rows - real_rows)))
-            parts.append(jnp.where(r < real_rows, page * PAGE + spot % PAGE, -1))
-            if k in with_suffix:
-                shape = (groups, PLANE, tok_quarter)
-                j, d, r = (lax.broadcasted_iota(int32, shape, axis) for axis in range(3))
-                owner = from_ring * PLANE + (plane_index ^ d)
-                token = owner * tok_slice + (group_index ^ j) * tok_quarter + r
-                parts.append(token + later)
-        return jnp.concatenate(parts, axis=2).reshape(1, -1)
-
-    near_spots = positions_of([0], [0])
-    far_spots = positions_of(range(1, ring), [1])
-
-    row = jnp.arange(tok_slice, dtype=int32)
-    local = (row % tok_quarter) * groups + (group_index ^ (row // tok_quarter))
-    permutation = (local[:, None] == jnp.arange(tok_slice, dtype=int32)[None, :]).astype(
-        jnp.bfloat16
+    column, plane, routes_ring = join_column([full, *along], piece_rows, tok_quarter)
+    plane = [send_plane(part, d + 1) for d, part in enumerate(plane)]
+    near_blocks = [send_group(column, j) if j else column for j in range(groups)]
+
+    near_segments = []
+    far_segments = []
+    for k in range(ring):
+        near_segments.append((k, piece_rows, real_rows, 0))
+        far_segments.append((k, piece_rows, real_rows, 0))
+        if k < 2:
+            near_segments.append((k, tok_quarter, 0, 1))
+    far_segments.append((0, tok_quarter, 0, 2))
+    sides = (
+        ((0,), near_segments),
+        (range(1, PLANE - 1), far_segments),
+        ((PLANE - 1,), far_segments),
     )
-    positions = first_token + local
-    requests = suffix_lengths.shape[0]
-    tenants = tenant_lengths.shape[0]
-    upto = jnp.arange(requests)[None, :] <= jnp.arange(requests)[:, None]
-    request_ends = jnp.sum(jnp.where(upto, suffix_lengths[None, :], 0), axis=1)
-    request_starts = request_ends - suffix_lengths
-    inside = (positions[:, None] >= request_starts[None, :]) & (
-        positions[:, None] < request_ends[None, :]
+    tables = [jnp.asarray(key_table(groups, side, parts)) for side, parts in sides]
+    tokens_info, permutation, near_spots, mid_spots, far_spots = make_plan(
+        tables,
+        suffix_lengths,
+        request_tenant,
+        tenant_lengths,
+        page_table[None, :],
+        ring,
+        real_rows,
+        (tok_slice, tok_quarter, groups),
+        [full],
     )
-    token_start = jnp.sum(jnp.where(inside, request_starts[None, :], 0), axis=1)
-    token_tenant = jnp.sum(jnp.where(inside, request_tenant[None, :], 0), axis=1)
-    upto = jnp.arange(tenants)[None, :] <= jnp.arange(tenants)[:, None]
-    tenant_ends = jnp.sum(jnp.where(upto, tenant_lengths[None, :], 0), axis=1)
-    tenant_starts = tenant_ends - tenant_lengths
-    tenant_pick = token_tenant[:, None] == jnp.arange(tenants, dtype=int32)[None, :]
-    range_low = jnp.sum(jnp.where(tenant_pick, tenant_starts[None, :], 0), axis=1)
-    range_high = jnp.sum(jnp.where(tenant_pick, tenant_ends[None, :], 0), axis=1)
-    tokens_info = jnp.stack(
-        [range_low, range_high, token_start + later, positions + later], axis=1
-    )
-
-    near = attend_near(
+
+    *near, near_flag = attend_near(
         tokens_info, near_spots, permutation, queries, key_up, near_blocks, [column]
     )
-    far_plane = pass_on(far_plane, ready=[near[4]])
-    far_blocks = [
-        send_group(block, j) if j else block for j in range(groups) for block in far_plane
-    ]
+    beside = pass_on(plane[:-1], [near_flag])
+    mid_blocks = [send_group(block, j) if j else block for j in range(groups) for block in beside]
+    *mid, mid_flag = attend_mid(tokens_info, mid_spots, near, mid_blocks)
+    near = [near[0], *mid]
+    across = pass_on(plane[-1:], [mid_flag])[0]
+    far_blocks = [send_group(across, j) if j else across for j in range(groups)]
     attend_own, attend_other = attend_far(
         tokens_info, far_spots, near, value_up, output_weight, far_blocks, tok_quarter
     )
@@ -731,35 +878,48 @@
     down_part = expert_down[0]
     scales = [scaled]
     results = []
-    for k in range(ring):
-        arrived = [send_plane(piece, d) if d else piece for d, piece in enumerate(pieces)]
-        ready = [result[0] for result in results[-1:]]
-        if k + 1 < ring:
+    running = None
+    payload = pieces
+    for step in range(1, ring + 4):
+        arrived = [send_plane(piece, d) if d else piece for d, piece in enumerate(payload)]
+        if step <= ring - 1:
             block = send_ring(block, ring)
-            joined, scaled, pieces = choose(
-                k + 1, block, arrived, routes_ring, experts_columns, sizes, ready
-            )
+        if 4 <= step:
+            k = step - 3
+            if k < ring:
+                landed = running
+                total = collect(scales[k], arrived, running)
+                running = send_ring(total, ring)
+            else:
+                break
+        back = step - 2 if step - 2 < ring else 0
+        given = None
+        if step >= 3:
+            own, other, _ = results[back]
+            if back:
+                along_z = [block] if step <= ring - 1 else [landed] if step > 4 else []
+                other = pass_on([other], arrived[1:] + along_z)[0]
+            given = [own] + [
+                send_group(other[(j - 1) * kept : j * kept], j) for j in range(1, groups)
+            ]
+        ready = [results[step - 2][2]] if 2 <= step <= ring else []
+        scaled, joined, payload = turn(
+            step,
+            block if step <= ring - 1 else None,
+            arrived,
+            given,
+            routes_ring,
+            experts_columns,
+            sizes,
+            ready if step <= ring else [total],
+        )
+        if scaled is not None:
             scales.append(scaled)
-        else:
-            joined = join_rows(*arrived, ready=ready)
-        rows = [send_group(joined, j) if j else joined for j in range(groups)]
-        results.append(expert_apply(rows, kept, gate_part, up_part, down_part, ready))
-
-    def give_back(k, ready):
-        own, other = results[k]
-        others = [send_group(other[(j - 1) * kept : j * kept], j) for j in range(1, groups)]
-        pieces = blend(own, others, PLANE, ready)
-        return [send_plane(piece, d) if d else piece for d, piece in enumerate(pieces)]
-
-    running = None
-    total = None
-    for k in range(1, ring):
-        returned = give_back(k, [])
-        total = collect(scales[k], returned, running)
-        running = send_ring(total, ring)
-    returned = give_back(0, [] if total is None else [total])
+        if joined is not None:
+            rows = [send_group(joined, j) if j else joined for j in range(groups)]
+            results.append(expert_apply(rows, kept, gate_part, up_part, down_part, []))
     layer_rows, normed_next = conclude(
-        scales[0], returned, running, residual, next_gain[None, :]
+        scales[0], arrived, running, residual, next_gain[None, :]
     )
 
     shares = [send_group(normed_next, j) if j else normed_next for j in range(groups)]

time: 165 us -> 151 us (0.915)
  local copies, waits for them, and re-layouts: 22.4 us -> 5.68 us
  Pallas kernels: 42 us -> 52.2 us
  other arithmetic: 7.43 us -> 0.01 us
  waiting for transfers between devices: 37.1 us -> 41 us
  starting transfers between devices: 50.8 us -> 47.3 us
    unnamed x92 -> x46, local copies, waits for them, and re-layouts: 21.6 us -> 5.67 us
    pallas_call x0 -> x7, Pallas kernels: none -> 10.8 us  [the longest x1 8.85 us: attend_mid(): pl.pallas_call(functools.partial(mid_kernel, len(blocks), pair), grid=(he...]
    ppermute x30 -> x24, starting transfers between devices: 35.4 us -> 29.1 us  [send_plane(): return lax.ppermute(block, 'tensor', [(i, i ^ distance) for i in devices])]
    ppermute x18 -> x14, waiting for transfers between devices: 4.89 us -> 8.78 us  [send_group(): return lax.ppermute(block, 'group', [(i, i ^ distance) for i in devices])]
    reduce_sum x5 -> x0, other arithmetic: 3.75 us -> none  [the longest x1 1.38 us: positions_of(): page = jnp.sum(jnp.where(hit, page_table, 0), axis=-1)]
    ppermute x6, starting transfers between devices: 5.93 us -> 9.42 us  [send_ring(): return lax.ppermute(block, 'tensor', route)]
    pallas_call x1, Pallas kernels: 12.5 us -> 9.41 us  [attend_far(): pl.pallas_call(functools.partial(far_kernel, len(blocks), tok_quarter), g...]
    ppermute x30 -> x24, waiting for transfers between devices: 18.9 us -> 21.4 us  [send_plane(): return lax.ppermute(block, 'tensor', [(i, i ^ distance) for i in devices])]
  transfers between devices with their start and end apart: 57 -> 47, of which waited for: 23 -> 25; matrix products, arithmetic and copies ran while one was open for 5% -> 0% of each run, Pallas kernels for 15% -> 25%
where the time goes in v3:
time: 151 us; the launch traced here: 150 us
  Pallas kernels  52.2 us (35%)
  starting transfers between devices  47.3 us (31%)
  waiting for transfers between devices  41 us (27%)
  local copies, waits for them, and re-layouts  5.68 us (4%)
  matrix products  3.42 us (2%)
    ppermute x24, starting transfers between devices, send_plane(): return lax.ppermute(block, 'tensor', [(i, i ^ distance) for i in devices])  29.1 us
    ppermute x24, waiting for transfers between devices, send_plane(): return lax.ppermute(block, 'tensor', [(i, i ^ distance) for i in devices])  21.4 us
    pallas_call x4, Pallas kernels, expert_apply(): pl.pallas_call(after(functools.partial(expert_kernel, len(pieces), kept,...  18.8 us
    ppermute x6, starting transfers between devices, send_ring(): return lax.ppermute(block, 'tensor', route)  9.42 us
    pallas_call x1, Pallas kernels, attend_far(): pl.pallas_call(functools.partial(far_kernel, len(blocks), tok_quarter), g...  9.41 us
    pallas_call x1, Pallas kernels, attend_mid(): pl.pallas_call(functools.partial(mid_kernel, len(blocks), pair), grid=(he...  8.85 us
    ppermute x14, waiting for transfers between devices, send_group(): return lax.ppermute(block, 'group', [(i, i ^ distance) for i in devices])  8.78 us
    ppermute x3, starting transfers between devices, send_round(): lax.ppermute(block, 'tensor', [(i, (i + distance) % count) for i in range...  6.96 us
  transfers between devices with their start and end apart: 47, of which 25 were waited for; matrix products, arithmetic and copies ran while one was open for 0% of the time, Pallas kernels for 25%

profile of v3, /device:TPU:0, one launch (start us, length us, event | category | flops | bytes accessed | tf_op | source)
XLA Modules:
  0.0 150.5 jit_solution(8346972546075446813)
XLA Ops:
  0.6 1.9 %join_share.1 = (bf16[128,640]{1,0:T(8,128)(2,1)}, bf16[64,640]{1,0:T(8,128)(2,1)}) custom-call(bf16[64,576]{1,0:T(8,128)(2,1)} %refs_0_.1, bf16[576,128]{1,0:T(8,128)(2,1)} %bitcast.36, s32[6,2,64]{2,1,0:T(2,128)} %bitcast.37), custom_call_target="tpu_custom_call" | custom-call | flops 10000000 | bytes 470016 | tf_op jit(solution)/shard_map/join_share/pallas_call | solution.py:91
  2.6 3.0 %collective-permute-start = (bf16[128,640]{1,0:T(8,128)(2,1)}, bf16[128,640]{1,0:T(8,128)(2,1)S(1)}, u32[]{:S(2)}, u32[]{:S(2)}) collective-permute-start(bf16[128,640]{1,0:T(8,128)(2,1)} %get-tuple-element.79.refs_0_), channel_id=1, source_target_pairs={{0,4},{1,5},{2,6},{3,7},{4,8},{5,9},{6,10},{7,11},{8,12},{9,13},{1... | collective-permute-start | bytes 491528 | tf_op jit(solution)/shard_map/ppermute | solution.py:42
  5.6 2.6 %collective-permute-start.1 = (bf16[64,640]{1,0:T(8,128)(2,1)}, bf16[64,640]{1,0:T(8,128)(2,1)S(1)}, u32[]{:S(2)}, u32[]{:S(2)}) collective-permute-start(bf16[64,640]{1,0:T(8,128)(2,1)} %get-tuple-element.83), channel_id=1, source_target_pairs={{0,8},{1,9},{2,10},{3,11},{4,12},{5,13},{6,14},{7,15},{8,0},{9,1},... | collective-permute-start | bytes 245768 | tf_op jit(solution)/shard_map/ppermute | solution.py:42
  8.2 1.3 collective-permute-start.2
  9.5 6.1 %collective-permute-done.1.refs_2_ = bf16[64,640]{1,0:T(8,128)(2,1)S(1)} collective-permute-done((bf16[64,640]{1,0:T(8,128)(2,1)}, bf16[64,640]{1,0:T(8,128)(2,1)S(1)}, u32[]{:S(2)}, u32[]{:S(2)}) %collective-permute-start.1) | collective-permute-done | bytes 81952 | tf_op jit(solution)/shard_map/ppermute | solution.py:42
  15.6 0.9 copy-done.8
  16.8 1.6 %collective-permute-start.4 = (bf16[320,640]{1,0:T(8,128)(2,1)S(1)}, bf16[320,640]{1,0:T(8,128)(2,1)S(1)}, u32[]{:S(2)}, u32[]{:S(2)}) collective-permute-start(bf16[320,640]{1,0:T(8,128)(2,1)S(1)} %get-tuple-element.92), channel_id=1, source_target_pairs={{0,1},{1,0},{2,3},{3,2},{4,5},{5,4},{6,7},{7,6},{8,9},{9,8},{10,11... | collective-permute-start | bytes 1228808 | tf_op jit(solution)/shard_map/ppermute | solution.py:47
  18.3 1.5 %collective-permute-start.5 = (bf16[320,640]{1,0:T(8,128)(2,1)S(1)}, bf16[320,640]{1,0:T(8,128)(2,1)S(1)}, u32[]{:S(2)}, u32[]{:S(2)}) collective-permute-start(bf16[320,640]{1,0:T(8,128)(2,1)S(1)} %get-tuple-element.93), channel_id=1, source_target_pairs={{0,2},{1,3},{2,0},{3,1},{4,6},{5,7},{6,4},{7,5},{8,10},{9,11},{10,... | collective-permute-start | bytes 1228808 | tf_op jit(solution)/shard_map/ppermute | solution.py:47
  19.8 1.9 %make_plan.1 = (s32[128,4]{1,0:T(8,128)}, bf16[128,128]{1,0:T(8,128)(2,1)}, s32[1,768]{1,0:T(1,128)}, s32[1,1280]{1,0:T(1,128)}, s32[1,640]{1,0:T(1,128)}) custom-call(bf16[128,640]{1,0:T(8,128)(2,1)} %get-tuple-element.79.refs_0_, s32[8]{0:T(128)} %refs_1_.1, s32[8]{0:T(128)} %refs_2_.1, s32[4]{0:T(128)} %refs_3_.1, s32[1,256]{1,0:T(1,128)} %bitcast.39, ...), custom_call_target="tpu_custom_call" | custom-call | flops 4000000000 | bytes 1000000 | tf_op jit(solution)/shard_map/make_plan/pallas_call | solution.py:274
  21.8 0.8 copy-done.18
  22.6 6.6 %attend_near.1 = (bf16[1024,640]{1,0:T(8,128)(2,1)}, f32[1024,1]{1,0:T(8,128)}, f32[1024,1]{1,0:T(8,128)}, f32[1024,512]{1,0:T(8,128)}, f32[8,128]{1,0:T(8,128)}) custom-call(bf16[384,640]{1,0:T(8,128)(2,1)} %copy-done.12, s32[128,4]{1,0:T(8,128)} %get-tuple-element.81.refs_1_.token_ref, s32[1,768]{1,0:T(1,128)} %get-tuple-element.85.refs_2_, ...), custom_call_target="tpu_custom_call" | custom-call | flops 1711276032 | bytes 8000000 | tf_op jit(solution)/shard_map/attend_near/pallas_call | solution.py:352
  31.1 1.5 collective-permute-start.8
  33.7 8.8 %attend_mid.1 = (f32[1024,1]{1,0:T(8,128)}, f32[1024,1]{1,0:T(8,128)}, f32[1024,512]{1,0:T(8,128)}, f32[8,128]{1,0:T(8,128)}) custom-call(s32[128,4]{1,0:T(8,128)} %get-tuple-element.81.refs_1_.token_ref, s32[1,1280]{1,0:T(1,128)} %get-tuple-element.87.spot_ref, bf16[1024,640]{1,0:T(8,128)(2,1)} %get-tuple-element.86.wide_ref, ...), custom_call_target="tpu_custom_call" | custom-call | flops 2852126720 | bytes 8000000 | tf_op jit(solution)/shard_map/attend_mid/pallas_call | solution.py:422
  42.5 0.9 collective-permute-done.8.refs_1_
  44.1 1.7 %collective-permute-done.9.refs_1_ = bf16[320,640]{1,0:T(8,128)(2,1)S(1)} collective-permute-done((bf16[320,640]{1,0:T(8,128)(2,1)S(1)}, bf16[320,640]{1,0:T(8,128)(2,1)S(1)}, u32[]{:S(2)}, u32[]{:S(2)}) %collective-permute-start.9) | collective-permute-done | bytes 409632 | tf_op jit(solution)/shard_map/ppermute | solution.py:52
  46.6 9.4 %attend_far.1 = (f32[64,2048]{1,0:T(8,128)}, bf16[64,2048]{1,0:T(8,128)(2,1)}) custom-call(s32[128,4]{1,0:T(8,128)} %get-tuple-element.81.refs_1_.token_ref, s32[1,640]{1,0:T(1,128)} %get-tuple-element.82.spot_ref, bf16[1024,640]{1,0:T(8,128)(2,1)} %get-tuple-element.86.wide_ref, f32[1024,1]{1,0:T(8,128)} %get-tuple-element.96.best_ref, ...), custom_call_target="tpu_custom_call" | custom-call | flops 1426063360 | bytes 12000000 | tf_op jit(solution)/shard_map/attend_far/pallas_call | solution.py:499
  56.4 1.3 collective-permute-done.10.refs_2_
  57.8 1.0 copy-done.11
  59.4 2.3 %collective-permute-start.11 = (bf16[64,2048]{1,0:T(8,128)(2,1)S(1)}, bf16[64,2048]{1,0:T(8,128)(2,1)S(1)}, u32[]{:S(2)}, u32[]{:S(2)}) collective-permute-start(bf16[64,2048]{1,0:T(8,128)(2,1)S(1)} %get-tuple-element.106), channel_id=1, source_target_pairs={{0,4},{1,5},{2,6},{3,7},{4,12},{5,13},{6,14},{7,15},{8,0},{9,1},{1... | collective-permute-start | bytes 786440 | tf_op jit(solution)/shard_map/ppermute | solution.py:37
  62.2 1.5 %collective-permute-start.13 = (bf16[32,2048]{1,0:T(8,128)(2,1)S(1)}, bf16[32,2048]{1,0:T(8,128)(2,1)S(1)}, u32[]{:S(2)}, u32[]{:S(2)}) collective-permute-start(bf16[32,2048]{1,0:T(8,128)(2,1)S(1)} %get-tuple-element.109), channel_id=1, source_target_pairs={{0,2},{1,3},{2,0},{3,1},{4,6},{5,7},{6,4},{7,5},{8,10},{9,11},{10,... | collective-permute-start | bytes 393224 | tf_op jit(solution)/shard_map/ppermute | solution.py:47
  63.7 1.4 collective-permute-start.14
  65.2 2.9 %collective-permute-done.12.refs_4_ = bf16[32,2048]{1,0:T(8,128)(2,1)S(1)} collective-permute-done((bf16[32,2048]{1,0:T(8,128)(2,1)S(1)}, bf16[32,2048]{1,0:T(8,128)(2,1)S(1)}, u32[]{:S(2)}, u32[]{:S(2)}) %collective-permute-start.12) | collective-permute-done | bytes 131104 | tf_op jit(solution)/shard_map/ppermute | solution.py:47
  68.1 1.0 collective-permute-done.13.refs_5_
  69.1 1.6 %collective-permute-done.14.refs_6_ = bf16[32,2048]{1,0:T(8,128)(2,1)S(1)} collective-permute-done((bf16[32,2048]{1,0:T(8,128)(2,1)S(1)}, bf16[32,2048]{1,0:T(8,128)(2,1)S(1)}, u32[]{:S(2)}, u32[]{:S(2)}) %collective-permute-start.14) | collective-permute-done | bytes 131104 | tf_op jit(solution)/shard_map/ppermute | solution.py:47
  71.4 1.9 %collective-permute-start.16 = (bf16[64,2048]{1,0:T(8,128)(2,1)S(1)}, bf16[64,2048]{1,0:T(8,128)(2,1)S(1)}, u32[]{:S(2)}, u32[]{:S(2)}) collective-permute-start(bf16[64,2048]{1,0:T(8,128)(2,1)S(1)} %collective-permute-done.11.refs_0_), channel_id=1, source_target_pairs={{0,4},{1,5},{2,6},{3,7},{4,12},{5,13},{6,14},{7,15},{8,0},{9,1},{1... | collective-permute-start | bytes 786440 | tf_op jit(solution)/shard_map/ppermute | solution.py:37
  73.2 0.8 collective-permute-start.17
  74.0 1.5 %collective-permute-start.18 = (bf16[32,2048]{1,0:T(8,128)(2,1)S(1)}, bf16[32,2048]{1,0:T(8,128)(2,1)S(1)}, u32[]{:S(2)}, u32[]{:S(2)}) collective-permute-start(bf16[32,2048]{1,0:T(8,128)(2,1)S(1)} %get-tuple-element.115), channel_id=1, source_target_pairs={{0,2},{1,3},{2,0},{3,1},{4,6},{5,7},{6,4},{7,5},{8,10},{9,11},{10,... | collective-permute-start | bytes 393224 | tf_op jit(solution)/shard_map/ppermute | solution.py:47
  75.5 1.2 collective-permute-start.19
  76.7 4.6 %experts.4 = (f32[128,2048]{1,0:T(8,128)S(1)}, bf16[128,2048]{1,0:T(8,128)(2,1)S(1)}, f32[8,128]{1,0:T(8,128)S(1)}) custom-call(bf16[128,2048]{1,0:T(8,128)(2,1)S(1)} %get-tuple-element.111.refs_0_, bf16[128,2048]{1,0:T(8,128)(2,1)S(1)} %collective-permute-done.15.refs_1_, bf16[704,2048]{1,0:T(8,128)(2,1)S(1)} %bitcast.18, bf16[704,2048]{1,0:T(8,128)(2,1)S(1)} %bitcast.22, ...), custom_call_target="tpu_custom_call" | custom-call | flops 2214592512 | bytes 10000000 | tf_op jit(solution)/shard_map/experts/pallas_call | solution.py:703
  83.3 0.9 collective-permute-start.22
  84.2 1.4 collective-permute-start.23
  85.6 1.2 collective-permute-start.24
  86.8 4.5 %experts.5 = (f32[128,2048]{1,0:T(8,128)S(1)}, bf16[128,2048]{1,0:T(8,128)(2,1)S(1)}, f32[8,128]{1,0:T(8,128)S(1)}) custom-call(bf16[128,2048]{1,0:T(8,128)(2,1)S(1)} %get-tuple-element.117.refs_0_, bf16[128,2048]{1,0:T(8,128)(2,1)S(1)} %collective-permute-done.20.refs_1_, bf16[704,2048]{1,0:T(8,128)(2,1)S(1)} %bitcast.19, bf16[704,2048]{1,0:T(8,128)(2,1)S(1)} %bitcast.23, ...), custom_call_target="tpu_custom_call" | custom-call | flops 2214592512 | bytes 10000000 | tf_op jit(solution)/shard_map/experts/pallas_call | solution.py:703
  91.3 0.9 collective-permute-done.21.refs_3_.refs_1_
  92.3 1.9 %collective-permute-done.25.refs_5_ = bf16[128,2048]{1,0:T(8,128)(2,1)S(1)} collective-permute-done((bf16[128,2048]{1,0:T(8,128)(2,1)S(1)}, bf16[128,2048]{1,0:T(8,128)(2,1)S(1)}, u32[]{:S(2)}, u32[]{:S(2)}) %collective-permute-start.25) | collective-permute-done | bytes 524320 | tf_op jit(solution)/shard_map/ppermute | solution.py:52
  94.2 0.8 turn.8
  95.2 1.2 collective-permute-start.27
  96.4 1.1 collective-permute-start.28
  97.5 1.2 collective-permute-start.29
  98.7 4.5 %experts.6 = (f32[128,2048]{1,0:T(8,128)S(1)}, bf16[128,2048]{1,0:T(8,128)(2,1)S(1)}, f32[8,128]{1,0:T(8,128)S(1)}) custom-call(bf16[128,2048]{1,0:T(8,128)(2,1)S(1)} %get-tuple-element.127.refs_0_, bf16[128,2048]{1,0:T(8,128)(2,1)S(1)} %collective-permute-done.26.refs_1_, bf16[704,2048]{1,0:T(8,128)(2,1)S(1)} %bitcast.20, bf16[704,2048]{1,0:T(8,128)(2,1)S(1)} %bitcast.24, ...), custom_call_target="tpu_custom_call" | custom-call | flops 2214592512 | bytes 10000000 | tf_op jit(solution)/shard_map/experts/pallas_call | solution.py:703
  103.3 1.1 collective-permute-done.27.refs_0_.refs_4_.refs_2_
  104.3 4.6 %collective-permute-done.28.refs_1_.refs_5_.refs_3_ = bf16[64,2048]{1,0:T(8,128)(2,1)S(1)} collective-permute-done((bf16[64,2048]{1,0:T(8,128)(2,1)S(1)}, bf16[64,2048]{1,0:T(8,128)(2,1)S(1)}, u32[]{:S(2)}, u32[]{:S(2)}) %collective-permute-start.28) | collective-permute-done | bytes 262176 | tf_op jit(solution)/shard_map/ppermute | solution.py:47
  109.0 1.3 collective-permute-done.29.refs_2_.refs_6_.refs_4_
  110.3 1.9 %collective-permute-done.30.refs_2_ = bf16[128,2048]{1,0:T(8,128)(2,1)S(1)} collective-permute-done((bf16[128,2048]{1,0:T(8,128)(2,1)S(1)}, bf16[128,2048]{1,0:T(8,128)(2,1)S(1)}, u32[]{:S(2)}, u32[]{:S(2)}) %collective-permute-start.30) | collective-permute-done | bytes 524320 | tf_op jit(solution)/shard_map/ppermute | solution.py:52
  113.2 1.3 collective-permute-start.31
  114.5 1.0 collective-permute-start.32
  115.5 1.2 collective-permute-start.33
  116.7 5.1 %experts.7 = (f32[128,2048]{1,0:T(8,128)S(1)}, bf16[128,2048]{1,0:T(8,128)(2,1)S(1)}, f32[8,128]{1,0:T(8,128)}) custom-call(bf16[128,2048]{1,0:T(8,128)(2,1)S(1)} %get-tuple-element.140.refs_0_, bf16[128,2048]{1,0:T(8,128)(2,1)S(1)} %collective-permute-done.35.refs_1_, bf16[704,2048]{1,0:T(8,128)(2,1)S(1)} %bitcast.21, bf16[704,2048]{1,0:T(8,128)(2,1)S(1)} %bitcast.25, ...), custom_call_target="tpu_custom_call" | custom-call | flops 2214592512 | bytes 10000000 | tf_op jit(solution)/shard_map/experts/pallas_call | solution.py:703
  123.3 2.5 %collective-permute-start.40 = (bf16[64,2048]{1,0:T(8,128)(2,1)S(1)}, bf16[64,2048]{1,0:T(8,128)(2,1)S(1)}, u32[]{:S(2)}, u32[]{:S(2)}) collective-permute-start(bf16[64,2048]{1,0:T(8,128)(2,1)S(1)} %collect.4.refs_0_), channel_id=1, source_target_pairs={{0,4},{1,5},{2,6},{3,7},{4,12},{5,13},{6,14},{7,15},{8,0},{9,1},{1... | collective-permute-start | bytes 786440 | tf_op jit(solution)/shard_map/ppermute | solution.py:37
  125.9 0.9 collective-permute-start.37
  126.7 1.5 %collective-permute-start.38 = (bf16[32,2048]{1,0:T(8,128)(2,1)S(1)}, bf16[32,2048]{1,0:T(8,128)(2,1)S(1)}, u32[]{:S(2)}, u32[]{:S(2)}) collective-permute-start(bf16[32,2048]{1,0:T(8,128)(2,1)S(1)} %get-tuple-element.145), channel_id=1, source_target_pairs={{0,2},{1,3},{2,0},{3,1},{4,6},{5,7},{6,4},{7,5},{8,10},{9,11},{10,... | collective-permute-start | bytes 393224 | tf_op jit(solution)/shard_map/ppermute | solution.py:47
  128.3 1.2 collective-permute-start.39
  129.4 3.3 %collective-permute-done.40.refs_5_ = bf16[64,2048]{1,0:T(8,128)(2,1)S(1)} collective-permute-done((bf16[64,2048]{1,0:T(8,128)(2,1)S(1)}, bf16[64,2048]{1,0:T(8,128)(2,1)S(1)}, u32[]{:S(2)}, u32[]{:S(2)}) %collective-permute-start.40) | collective-permute-done | bytes 262176 | tf_op jit(solution)/shard_map/ppermute | solution.py:37
  132.7 1.8 %collective-permute-done.38.refs_3_ = bf16[32,2048]{1,0:T(8,128)(2,1)S(1)} collective-permute-done((bf16[32,2048]{1,0:T(8,128)(2,1)S(1)}, bf16[32,2048]{1,0:T(8,128)(2,1)S(1)}, u32[]{:S(2)}, u32[]{:S(2)}) %collective-permute-start.38) | collective-permute-done | bytes 131104 | tf_op jit(solution)/shard_map/ppermute | solution.py:47
  134.8 1.7 %collective-permute-start.45 = (bf16[64,2048]{1,0:T(8,128)(2,1)S(1)}, bf16[64,2048]{1,0:T(8,128)(2,1)S(1)}, u32[]{:S(2)}, u32[]{:S(2)}) collective-permute-start(bf16[64,2048]{1,0:T(8,128)(2,1)S(1)} %collect.5.refs_0_), channel_id=1, source_target_pairs={{0,4},{1,5},{2,6},{3,7},{4,12},{5,13},{6,14},{7,15},{8,0},{9,1},{1... | collective-permute-start | bytes 786440 | tf_op jit(solution)/shard_map/ppermute | solution.py:37
  136.6 1.3 collective-permute-start.42
  137.8 1.0 collective-permute-start.43
  138.9 1.3 collective-permute-start.44
  140.1 2.6 %collective-permute-done.42.refs_4_ = bf16[32,2048]{1,0:T(8,128)(2,1)S(1)} collective-permute-done((bf16[32,2048]{1,0:T(8,128)(2,1)S(1)}, bf16[32,2048]{1,0:T(8,128)(2,1)S(1)}, u32[]{:S(2)}, u32[]{:S(2)}) %collective-permute-start.42) | collective-permute-done | bytes 131104 | tf_op jit(solution)/shard_map/ppermute | solution.py:47
  143.0 1.7 %collective-permute-done.44.refs_6_ = bf16[32,2048]{1,0:T(8,128)(2,1)S(1)} collective-permute-done((bf16[32,2048]{1,0:T(8,128)(2,1)S(1)}, bf16[32,2048]{1,0:T(8,128)(2,1)S(1)}, u32[]{:S(2)}, u32[]{:S(2)}) %collective-permute-start.44) | collective-permute-done | bytes 131104 | tf_op jit(solution)/shard_map/ppermute | solution.py:47
  144.7 1.0 conclude.1
  145.7 1.5 %collective-permute-done.46 = bf16[64,2048]{1,0:T(8,128)(2,1)S(1)} collective-permute-done((bf16[64,2048]{1,0:T(8,128)(2,1)S(1)}, bf16[64,2048]{1,0:T(8,128)(2,1)S(1)}, u32[]{:S(2)}, u32[]{:S(2)}) %collective-permute-start.46) | collective-permute-done | bytes 262176 | tf_op jit(solution)/shard_map/ppermute | solution.py:52
  147.6 1.8 %convolution_convert_fusion.1 = bf16[128,1536]{1,0:T(8,128)(2,1)} fusion(bf16[128,2048]{1,0:T(8,128)(2,1)S(1)} %convolution_convert_fusion, bf16[2048,1536]{1,0:T(8,128)(2,1)S(1)} %bitcast.35), kind=kOutput, calls=%fused_computation.1 | convolution fusion | flops 805502976 | bytes 7208960 | tf_op jit(solution)/shard_map/dot_general | solution.py:70
  149.4 1.1 convolution_convert_fusion.3
  (109 shorter events, 12.5 us)
Async XLA Ops:
  0.6 148.7 %copy-start = (bf16[2048,288]{0,1:T(8,128)(2,1)S(1)}, bf16[2048,288]{0,1:T(8,128)(2,1)}, u32[]{:S(2)}) copy-start(bf16[2048,288]{0,1:T(8,128)(2,1)} %param.37) | copy-start | bytes 3538948
  2.6 13.1 %collective-permute-start = (bf16[128,640]{1,0:T(8,128)(2,1)}, bf16[128,640]{1,0:T(8,128)(2,1)S(1)}, u32[]{:S(2)}, u32[]{:S(2)}) collective-permute-start(bf16[128,640]{1,0:T(8,128)(2,1)} %get-tuple-element.79.refs_0_), channel_id=1, source_target_pairs={{0,4},{1,5},{2,6},{3,7},{4,8},{5,9},{6,10},{7,11},{8,12},{9,13},{1... | collective-permute-start | bytes 491528 | tf_op jit(solution)/shard_map/ppermute | solution.py:42
  5.6 10.0 %collective-permute-start.1 = (bf16[64,640]{1,0:T(8,128)(2,1)}, bf16[64,640]{1,0:T(8,128)(2,1)S(1)}, u32[]{:S(2)}, u32[]{:S(2)}) collective-permute-start(bf16[64,640]{1,0:T(8,128)(2,1)} %get-tuple-element.83), channel_id=1, source_target_pairs={{0,8},{1,9},{2,10},{3,11},{4,12},{5,13},{6,14},{7,15},{8,0},{9,1},... | collective-permute-start | bytes 245768 | tf_op jit(solution)/shard_map/ppermute | solution.py:42
  8.2 7.5 %collective-permute-start.2 = (bf16[64,640]{1,0:T(8,128)(2,1)}, bf16[64,640]{1,0:T(8,128)(2,1)S(1)}, u32[]{:S(2)}, u32[]{:S(2)}) collective-permute-start(bf16[64,640]{1,0:T(8,128)(2,1)} %get-tuple-element.83), channel_id=1, source_target_pairs={{0,12},{1,13},{2,14},{3,15},{4,0},{5,1},{6,2},{7,3},{8,4},{9,5},{1... | collective-permute-start | bytes 245768 | tf_op jit(solution)/shard_map/ppermute | solution.py:42
  15.6 0.9 copy-start.8
  16.7 5.1 %copy-start.12 = (bf16[384,640]{1,0:T(8,128)(2,1)}, bf16[384,640]{1,0:T(8,128)(2,1)S(1)}, u32[]{:S(2)}) copy-start(bf16[384,640]{1,0:T(8,128)(2,1)S(1)} %get-tuple-element.84.refs_0_.refs_6_) | copy-start | bytes 1474564
  16.7 5.1 %collective-permute-start.3 = (bf16[384,640]{1,0:T(8,128)(2,1)S(1)}, bf16[384,640]{1,0:T(8,128)(2,1)S(1)}, u32[]{:S(2)}, u32[]{:S(2)}) collective-permute-start(bf16[384,640]{1,0:T(8,128)(2,1)S(1)} %get-tuple-element.84.refs_0_.refs_6_), channel_id=1, source_target_pairs={{0,16},{16,0},{1,17},{17,1},{2,18},{18,2},{3,19},{19,3},{4,20},{20... | collective-permute-start | bytes 1474568 | tf_op jit(solution)/shard_map/ppermute | solution.py:52
  16.8 12.5 %collective-permute-start.4 = (bf16[320,640]{1,0:T(8,128)(2,1)S(1)}, bf16[320,640]{1,0:T(8,128)(2,1)S(1)}, u32[]{:S(2)}, u32[]{:S(2)}) collective-permute-start(bf16[320,640]{1,0:T(8,128)(2,1)S(1)} %get-tuple-element.92), channel_id=1, source_target_pairs={{0,1},{1,0},{2,3},{3,2},{4,5},{5,4},{6,7},{7,6},{8,9},{9,8},{10,11... | collective-permute-start | bytes 1228808 | tf_op jit(solution)/shard_map/ppermute | solution.py:47
  18.3 11.5 %collective-permute-start.5 = (bf16[320,640]{1,0:T(8,128)(2,1)S(1)}, bf16[320,640]{1,0:T(8,128)(2,1)S(1)}, u32[]{:S(2)}, u32[]{:S(2)}) collective-permute-start(bf16[320,640]{1,0:T(8,128)(2,1)S(1)} %get-tuple-element.93), channel_id=1, source_target_pairs={{0,2},{1,3},{2,0},{3,1},{4,6},{5,7},{6,4},{7,5},{8,10},{9,11},{10,... | collective-permute-start | bytes 1228808 | tf_op jit(solution)/shard_map/ppermute | solution.py:47
  30.6 2.3 %copy-start.6 = (bf16[320,640]{1,0:T(8,128)(2,1)}, bf16[320,640]{1,0:T(8,128)(2,1)S(1)}, u32[]{:S(2)}) copy-start(bf16[320,640]{1,0:T(8,128)(2,1)S(1)} %get-tuple-element.94.refs_0_) | copy-start | bytes 1228804
  30.6 2.3 %copy-start.7 = (bf16[320,640]{1,0:T(8,128)(2,1)}, bf16[320,640]{1,0:T(8,128)(2,1)S(1)}, u32[]{:S(2)}) copy-start(bf16[320,640]{1,0:T(8,128)(2,1)S(1)} %get-tuple-element.95.refs_1_) | copy-start | bytes 1228804
  30.6 2.0 %collective-permute-start.6 = (bf16[320,640]{1,0:T(8,128)(2,1)S(1)}, bf16[320,640]{1,0:T(8,128)(2,1)S(1)}, u32[]{:S(2)}, u32[]{:S(2)}) collective-permute-start(bf16[320,640]{1,0:T(8,128)(2,1)S(1)} %get-tuple-element.94.refs_0_), channel_id=1, source_target_pairs={{0,16},{16,0},{1,17},{17,1},{2,18},{18,2},{3,19},{19,3},{4,20},{20... | collective-permute-start | bytes 1228808 | tf_op jit(solution)/shard_map/ppermute | solution.py:52
  30.6 2.3 %collective-permute-start.7 = (bf16[320,640]{1,0:T(8,128)(2,1)S(1)}, bf16[320,640]{1,0:T(8,128)(2,1)S(1)}, u32[]{:S(2)}, u32[]{:S(2)}) collective-permute-start(bf16[320,640]{1,0:T(8,128)(2,1)S(1)} %get-tuple-element.95.refs_1_), channel_id=1, source_target_pairs={{0,16},{16,0},{1,17},{17,1},{2,18},{18,2},{3,19},{19,3},{4,20},{20... | collective-permute-start | bytes 1228808 | tf_op jit(solution)/shard_map/ppermute | solution.py:52
  31.1 12.3 %collective-permute-start.8 = (bf16[320,640]{1,0:T(8,128)(2,1)S(1)}, bf16[320,640]{1,0:T(8,128)(2,1)S(1)}, u32[]{:S(2)}, u32[]{:S(2)}) collective-permute-start(bf16[320,640]{1,0:T(8,128)(2,1)S(1)} %get-tuple-element.100), channel_id=1, source_target_pairs={{0,3},{1,2},{2,1},{3,0},{4,7},{5,6},{6,5},{7,4},{8,11},{9,10},{10,... | collective-permute-start | bytes 1228808 | tf_op jit(solution)/shard_map/ppermute | solution.py:47
  44.1 1.8 %copy-start.4 = (bf16[320,640]{1,0:T(8,128)(2,1)}, bf16[320,640]{1,0:T(8,128)(2,1)S(1)}, u32[]{:S(2)}) copy-start(bf16[320,640]{1,0:T(8,128)(2,1)S(1)} %pass_on.6.refs_0_) | copy-start | bytes 1228804
  44.1 1.7 %collective-permute-start.9 = (bf16[320,640]{1,0:T(8,128)(2,1)S(1)}, bf16[320,640]{1,0:T(8,128)(2,1)S(1)}, u32[]{:S(2)}, u32[]{:S(2)}) collective-permute-start(bf16[320,640]{1,0:T(8,128)(2,1)S(1)} %pass_on.6.refs_0_), channel_id=1, source_target_pairs={{0,16},{16,0},{1,17},{17,1},{2,18},{18,2},{3,19},{19,3},{4,20},{20... | collective-permute-start | bytes 1228808 | tf_op jit(solution)/shard_map/ppermute | solution.py:52
  46.6 9.6 %copy-start.16 = (bf16[2048]{0:T(1024)(128)(2,1)S(1)}, bf16[2048]{0:T(1024)(128)(2,1)}, u32[]{:S(2)}) copy-start(bf16[2048]{0:T(1024)(128)(2,1)} %param.30) | copy-start | bytes 12292
  46.6 9.6 %copy-start.13 = (bf16[128,2048]{1,0:T(8,128)(2,1)S(1)}, bf16[128,2048]{1,0:T(8,128)(2,1)}, u32[]{:S(2)}) copy-start(bf16[128,2048]{1,0:T(8,128)(2,1)} %param.23) | copy-start | bytes 1572868
  46.6 9.6 %copy-start.15 = (bf16[128,128]{1,0:T(8,128)(2,1)S(1)}, bf16[128,128]{1,0:T(8,128)(2,1)}, u32[]{:S(2)}) copy-start(bf16[128,128]{1,0:T(8,128)(2,1)} %get-tuple-element.80.refs_3_) | copy-start | bytes 98308
  46.6 11.2 %copy-start.5 = (bf16[2048,16]{0,1:T(8,128)(2,1)S(1)}, bf16[2048,16]{0,1:T(8,128)(2,1)}, u32[]{:S(2)}) copy-start(bf16[2048,16]{0,1:T(8,128)(2,1)} %param.31) | copy-start | bytes 196612
  56.0 1.7 %collective-permute-start.10 = (bf16[64,2048]{1,0:T(8,128)(2,1)}, bf16[64,2048]{1,0:T(8,128)(2,1)S(1)}, u32[]{:S(2)}, u32[]{:S(2)}) collective-permute-start(bf16[64,2048]{1,0:T(8,128)(2,1)} %get-tuple-element.102), channel_id=1, source_target_pairs={{0,16},{16,0},{1,17},{17,1},{2,18},{18,2},{3,19},{19,3},{4,20},{20... | collective-permute-start | bytes 786440 | tf_op jit(solution)/shard_map/ppermute | solution.py:52
  57.8 1.0 copy-start.11
  58.8 17.9 %copy-start.1 = (bf16[1,2048,704]{1,2,0:T(8,128)(2,1)S(1)}, bf16[1,2048,704]{1,2,0:T(8,128)(2,1)}, u32[]{:S(2)}) copy-start(bf16[1,2048,704]{1,2,0:T(8,128)(2,1)} %param.32) | copy-start | bytes 8650756
  58.8 17.9 %copy-start.2 = (bf16[1,2048,704]{1,2,0:T(8,128)(2,1)S(1)}, bf16[1,2048,704]{1,2,0:T(8,128)(2,1)}, u32[]{:S(2)}) copy-start(bf16[1,2048,704]{1,2,0:T(8,128)(2,1)} %param.33) | copy-start | bytes 8650756
  58.8 17.9 %copy-start.3 = (bf16[1,704,2048]{2,1,0:T(8,128)(2,1)S(1)}, bf16[1,704,2048]{2,1,0:T(8,128)(2,1)}, u32[]{:S(2)}) copy-start(bf16[1,704,2048]{2,1,0:T(8,128)(2,1)} %param.34) | copy-start | bytes 8650756
  59.4 11.3 %collective-permute-start.11 = (bf16[64,2048]{1,0:T(8,128)(2,1)S(1)}, bf16[64,2048]{1,0:T(8,128)(2,1)S(1)}, u32[]{:S(2)}, u32[]{:S(2)}) collective-permute-start(bf16[64,2048]{1,0:T(8,128)(2,1)S(1)} %get-tuple-element.106), channel_id=1, source_target_pairs={{0,4},{1,5},{2,6},{3,7},{4,12},{5,13},{6,14},{7,15},{8,0},{9,1},{1... | collective-permute-start | bytes 786440 | tf_op jit(solution)/shard_map/ppermute | solution.py:37
  61.7 6.4 %collective-permute-start.12 = (bf16[32,2048]{1,0:T(8,128)(2,1)S(1)}, bf16[32,2048]{1,0:T(8,128)(2,1)S(1)}, u32[]{:S(2)}, u32[]{:S(2)}) collective-permute-start(bf16[32,2048]{1,0:T(8,128)(2,1)S(1)} %get-tuple-element.108), channel_id=1, source_target_pairs={{0,1},{1,0},{2,3},{3,2},{4,5},{5,4},{6,7},{7,6},{8,9},{9,8},{10,11... | collective-permute-start | bytes 393224 | tf_op jit(solution)/shard_map/ppermute | solution.py:47
  62.2 6.9 %collective-permute-start.13 = (bf16[32,2048]{1,0:T(8,128)(2,1)S(1)}, bf16[32,2048]{1,0:T(8,128)(2,1)S(1)}, u32[]{:S(2)}, u32[]{:S(2)}) collective-permute-start(bf16[32,2048]{1,0:T(8,128)(2,1)S(1)} %get-tuple-element.109), channel_id=1, source_target_pairs={{0,2},{1,3},{2,0},{3,1},{4,6},{5,7},{6,4},{7,5},{8,10},{9,11},{10,... | collective-permute-start | bytes 393224 | tf_op jit(solution)/shard_map/ppermute | solution.py:47
  63.7 7.0 %collective-permute-start.14 = (bf16[32,2048]{1,0:T(8,128)(2,1)S(1)}, bf16[32,2048]{1,0:T(8,128)(2,1)S(1)}, u32[]{:S(2)}, u32[]{:S(2)}) collective-permute-start(bf16[32,2048]{1,0:T(8,128)(2,1)S(1)} %get-tuple-element.110), channel_id=1, source_target_pairs={{0,3},{1,2},{2,1},{3,0},{4,7},{5,6},{6,5},{7,4},{8,11},{9,10},{10,... | collective-permute-start | bytes 393224 | tf_op jit(solution)/shard_map/ppermute | solution.py:47
  71.3 5.4 %collective-permute-start.15 = (bf16[128,2048]{1,0:T(8,128)(2,1)S(1)}, bf16[128,2048]{1,0:T(8,128)(2,1)S(1)}, u32[]{:S(2)}, u32[]{:S(2)}) collective-permute-start(bf16[128,2048]{1,0:T(8,128)(2,1)S(1)} %get-tuple-element.111.refs_0_), channel_id=1, source_target_pairs={{0,16},{16,0},{1,17},{17,1},{2,18},{18,2},{3,19},{19,3},{4,20},{20... | collective-permute-start | bytes 1572872 | tf_op jit(solution)/shard_map/ppermute | solution.py:52
  71.4 10.6 %collective-permute-start.16 = (bf16[64,2048]{1,0:T(8,128)(2,1)S(1)}, bf16[64,2048]{1,0:T(8,128)(2,1)S(1)}, u32[]{:S(2)}, u32[]{:S(2)}) collective-permute-start(bf16[64,2048]{1,0:T(8,128)(2,1)S(1)} %collective-permute-done.11.refs_0_), channel_id=1, source_target_pairs={{0,4},{1,5},{2,6},{3,7},{4,12},{5,13},{6,14},{7,15},{8,0},{9,1},{1... | collective-permute-start | bytes 786440 | tf_op jit(solution)/shard_map/ppermute | solution.py:37
  73.2 8.1 %collective-permute-start.17 = (bf16[32,2048]{1,0:T(8,128)(2,1)S(1)}, bf16[32,2048]{1,0:T(8,128)(2,1)S(1)}, u32[]{:S(2)}, u32[]{:S(2)}) collective-permute-start(bf16[32,2048]{1,0:T(8,128)(2,1)S(1)} %get-tuple-element.114), channel_id=1, source_target_pairs={{0,1},{1,0},{2,3},{3,2},{4,5},{5,4},{6,7},{7,6},{8,9},{9,8},{10,11... | collective-permute-start | bytes 393224 | tf_op jit(solution)/shard_map/ppermute | solution.py:47
  74.0 7.9 %collective-permute-start.18 = (bf16[32,2048]{1,0:T(8,128)(2,1)S(1)}, bf16[32,2048]{1,0:T(8,128)(2,1)S(1)}, u32[]{:S(2)}, u32[]{:S(2)}) collective-permute-start(bf16[32,2048]{1,0:T(8,128)(2,1)S(1)} %get-tuple-element.115), channel_id=1, source_target_pairs={{0,2},{1,3},{2,0},{3,1},{4,6},{5,7},{6,4},{7,5},{8,10},{9,11},{10,... | collective-permute-start | bytes 393224 | tf_op jit(solution)/shard_map/ppermute | solution.py:47
  75.5 6.4 %collective-permute-start.19 = (bf16[32,2048]{1,0:T(8,128)(2,1)S(1)}, bf16[32,2048]{1,0:T(8,128)(2,1)S(1)}, u32[]{:S(2)}, u32[]{:S(2)}) collective-permute-start(bf16[32,2048]{1,0:T(8,128)(2,1)S(1)} %get-tuple-element.116), channel_id=1, source_target_pairs={{0,3},{1,2},{2,1},{3,0},{4,7},{5,6},{6,5},{7,4},{8,11},{9,10},{10,... | collective-permute-start | bytes 393224 | tf_op jit(solution)/shard_map/ppermute | solution.py:47
  82.5 4.3 %collective-permute-start.20 = (bf16[128,2048]{1,0:T(8,128)(2,1)S(1)}, bf16[128,2048]{1,0:T(8,128)(2,1)S(1)}, u32[]{:S(2)}, u32[]{:S(2)}) collective-permute-start(bf16[128,2048]{1,0:T(8,128)(2,1)S(1)} %get-tuple-element.117.refs_0_), channel_id=1, source_target_pairs={{0,16},{16,0},{1,17},{17,1},{2,18},{18,2},{3,19},{19,3},{4,20},{20... | collective-permute-start | bytes 1572872 | tf_op jit(solution)/shard_map/ppermute | solution.py:52
  82.6 9.6 %collective-permute-start.21 = (bf16[64,2048]{1,0:T(8,128)(2,1)S(1)}, bf16[64,2048]{1,0:T(8,128)(2,1)S(1)}, u32[]{:S(2)}, u32[]{:S(2)}) collective-permute-start(bf16[64,2048]{1,0:T(8,128)(2,1)S(1)} %collective-permute-done.16.refs_1_), channel_id=1, source_target_pairs={{0,4},{1,5},{2,6},{3,7},{4,12},{5,13},{6,14},{7,15},{8,0},{9,1},{1... | collective-permute-start | bytes 786440 | tf_op jit(solution)/shard_map/ppermute | solution.py:37
  83.3 8.9 %collective-permute-start.22 = (bf16[32,2048]{1,0:T(8,128)(2,1)S(1)}, bf16[32,2048]{1,0:T(8,128)(2,1)S(1)}, u32[]{:S(2)}, u32[]{:S(2)}) collective-permute-start(bf16[32,2048]{1,0:T(8,128)(2,1)S(1)} %get-tuple-element.120), channel_id=1, source_target_pairs={{0,1},{1,0},{2,3},{3,2},{4,5},{5,4},{6,7},{7,6},{8,9},{9,8},{10,11... | collective-permute-start | bytes 393224 | tf_op jit(solution)/shard_map/ppermute | solution.py:47
  84.2 8.0 %collective-permute-start.23 = (bf16[32,2048]{1,0:T(8,128)(2,1)S(1)}, bf16[32,2048]{1,0:T(8,128)(2,1)S(1)}, u32[]{:S(2)}, u32[]{:S(2)}) collective-permute-start(bf16[32,2048]{1,0:T(8,128)(2,1)S(1)} %get-tuple-element.121), channel_id=1, source_target_pairs={{0,2},{1,3},{2,0},{3,1},{4,6},{5,7},{6,4},{7,5},{8,10},{9,11},{10,... | collective-permute-start | bytes 393224 | tf_op jit(solution)/shard_map/ppermute | solution.py:47
  85.6 6.7 %collective-permute-start.24 = (bf16[32,2048]{1,0:T(8,128)(2,1)S(1)}, bf16[32,2048]{1,0:T(8,128)(2,1)S(1)}, u32[]{:S(2)}, u32[]{:S(2)}) collective-permute-start(bf16[32,2048]{1,0:T(8,128)(2,1)S(1)} %get-tuple-element.122), channel_id=1, source_target_pairs={{0,3},{1,2},{2,1},{3,0},{4,7},{5,6},{6,5},{7,4},{8,11},{9,10},{10,... | collective-permute-start | bytes 393224 | tf_op jit(solution)/shard_map/ppermute | solution.py:47
  92.3 1.9 %collective-permute-start.25 = (bf16[128,2048]{1,0:T(8,128)(2,1)S(1)}, bf16[128,2048]{1,0:T(8,128)(2,1)S(1)}, u32[]{:S(2)}, u32[]{:S(2)}) collective-permute-start(bf16[128,2048]{1,0:T(8,128)(2,1)S(1)} %pass_on.7), channel_id=1, source_target_pairs={{0,16},{16,0},{1,17},{17,1},{2,18},{18,2},{3,19},{19,3},{4,20},{20... | collective-permute-start | bytes 1572872 | tf_op jit(solution)/shard_map/ppermute | solution.py:52
  95.0 3.7 %collective-permute-start.26 = (bf16[128,2048]{1,0:T(8,128)(2,1)S(1)}, bf16[128,2048]{1,0:T(8,128)(2,1)S(1)}, u32[]{:S(2)}, u32[]{:S(2)}) collective-permute-start(bf16[128,2048]{1,0:T(8,128)(2,1)S(1)} %get-tuple-element.127.refs_0_), channel_id=1, source_target_pairs={{0,16},{16,0},{1,17},{17,1},{2,18},{18,2},{3,19},{19,3},{4,20},{20... | collective-permute-start | bytes 1572872 | tf_op jit(solution)/shard_map/ppermute | solution.py:52
  95.2 9.1 %collective-permute-start.27 = (bf16[64,2048]{1,0:T(8,128)(2,1)S(1)}, bf16[64,2048]{1,0:T(8,128)(2,1)S(1)}, u32[]{:S(2)}, u32[]{:S(2)}) collective-permute-start(bf16[64,2048]{1,0:T(8,128)(2,1)S(1)} %get-tuple-element.130), channel_id=1, source_target_pairs={{0,1},{1,0},{2,3},{3,2},{4,5},{5,4},{6,7},{7,6},{8,9},{9,8},{10,11... | collective-permute-start | bytes 786440 | tf_op jit(solution)/shard_map/ppermute | solution.py:47
  96.4 12.6 %collective-permute-start.28 = (bf16[64,2048]{1,0:T(8,128)(2,1)S(1)}, bf16[64,2048]{1,0:T(8,128)(2,1)S(1)}, u32[]{:S(2)}, u32[]{:S(2)}) collective-permute-start(bf16[64,2048]{1,0:T(8,128)(2,1)S(1)} %get-tuple-element.131), channel_id=1, source_target_pairs={{0,2},{1,3},{2,0},{3,1},{4,6},{5,7},{6,4},{7,5},{8,10},{9,11},{10,... | collective-permute-start | bytes 786440 | tf_op jit(solution)/shard_map/ppermute | solution.py:47
  97.5 12.8 %collective-permute-start.29 = (bf16[64,2048]{1,0:T(8,128)(2,1)S(1)}, bf16[64,2048]{1,0:T(8,128)(2,1)S(1)}, u32[]{:S(2)}, u32[]{:S(2)}) collective-permute-start(bf16[64,2048]{1,0:T(8,128)(2,1)S(1)} %get-tuple-element.132), channel_id=1, source_target_pairs={{0,3},{1,2},{2,1},{3,0},{4,7},{5,6},{6,5},{7,4},{8,11},{9,10},{10,... | collective-permute-start | bytes 786440 | tf_op jit(solution)/shard_map/ppermute | solution.py:47
  110.3 1.9 %collective-permute-start.30 = (bf16[128,2048]{1,0:T(8,128)(2,1)S(1)}, bf16[128,2048]{1,0:T(8,128)(2,1)S(1)}, u32[]{:S(2)}, u32[]{:S(2)}) collective-permute-start(bf16[128,2048]{1,0:T(8,128)(2,1)S(1)} %pass_on.8), channel_id=1, source_target_pairs={{0,16},{16,0},{1,17},{17,1},{2,18},{18,2},{3,19},{19,3},{4,20},{20... | collective-permute-start | bytes 1572872 | tf_op jit(solution)/shard_map/ppermute | solution.py:52
  112.4 4.3 %collective-permute-start.35 = (bf16[128,2048]{1,0:T(8,128)(2,1)S(1)}, bf16[128,2048]{1,0:T(8,128)(2,1)S(1)}, u32[]{:S(2)}, u32[]{:S(2)}) collective-permute-start(bf16[128,2048]{1,0:T(8,128)(2,1)S(1)} %get-tuple-element.140.refs_0_), channel_id=1, source_target_pairs={{0,16},{16,0},{1,17},{17,1},{2,18},{18,2},{3,19},{19,3},{4,20},{20... | collective-permute-start | bytes 1572872 | tf_op jit(solution)/shard_map/ppermute | solution.py:52
  112.8 9.5 %collective-permute-start.34 = (bf16[64,2048]{1,0:T(8,128)(2,1)S(1)}, bf16[64,2048]{1,0:T(8,128)(2,1)S(1)}, u32[]{:S(2)}, u32[]{:S(2)}) collective-permute-start(bf16[64,2048]{1,0:T(8,128)(2,1)S(1)} %collect.3), channel_id=1, source_target_pairs={{0,4},{1,5},{2,6},{3,7},{4,12},{5,13},{6,14},{7,15},{8,0},{9,1},{1... | collective-permute-start | bytes 786440 | tf_op jit(solution)/shard_map/ppermute | solution.py:37
  113.2 9.2 %collective-permute-start.31 = (bf16[32,2048]{1,0:T(8,128)(2,1)S(1)}, bf16[32,2048]{1,0:T(8,128)(2,1)S(1)}, u32[]{:S(2)}, u32[]{:S(2)}) collective-permute-start(bf16[32,2048]{1,0:T(8,128)(2,1)S(1)} %get-tuple-element.136), channel_id=1, source_target_pairs={{0,1},{1,0},{2,3},{3,2},{4,5},{5,4},{6,7},{7,6},{8,9},{9,8},{10,11... | collective-permute-start | bytes 393224 | tf_op jit(solution)/shard_map/ppermute | solution.py:47
  114.5 7.9 %collective-permute-start.32 = (bf16[32,2048]{1,0:T(8,128)(2,1)S(1)}, bf16[32,2048]{1,0:T(8,128)(2,1)S(1)}, u32[]{:S(2)}, u32[]{:S(2)}) collective-permute-start(bf16[32,2048]{1,0:T(8,128)(2,1)S(1)} %get-tuple-element.137), channel_id=1, source_target_pairs={{0,2},{1,3},{2,0},{3,1},{4,6},{5,7},{6,4},{7,5},{8,10},{9,11},{10,... | collective-permute-start | bytes 393224 | tf_op jit(solution)/shard_map/ppermute | solution.py:47
  115.5 7.0 %collective-permute-start.33 = (bf16[32,2048]{1,0:T(8,128)(2,1)S(1)}, bf16[32,2048]{1,0:T(8,128)(2,1)S(1)}, u32[]{:S(2)}, u32[]{:S(2)}) collective-permute-start(bf16[32,2048]{1,0:T(8,128)(2,1)S(1)} %get-tuple-element.138), channel_id=1, source_target_pairs={{0,3},{1,2},{2,1},{3,0},{4,7},{5,6},{6,5},{7,4},{8,11},{9,10},{10,... | collective-permute-start | bytes 393224 | tf_op jit(solution)/shard_map/ppermute | solution.py:47
  116.7 30.8 %slice-start = ((s8[6291456]{0:T(1024)(128)(4,1)}), s8[2097152]{0:T(1024)(128)(4,1)S(1)}, s32[]{:S(2)}) async-start(s8[6291456]{0:T(1024)(128)(4,1)} %bitcast.34), calls=%async_computation | async-start | bytes 4194304
  122.5 25.1 %slice-start.1 = ((s8[6291456]{0:T(1024)(128)(4,1)}), s8[4194304]{0:T(1024)(128)(4,1)S(1)}, s32[]{:S(2)}) async-start(s8[6291456]{0:T(1024)(128)(4,1)} %bitcast.34), calls=%async_computation.1 | async-start | bytes 8388608
  122.5 3.3 %collective-permute-start.36 = (bf16[128,2048]{1,0:T(8,128)(2,1)S(1)}, bf16[128,2048]{1,0:T(8,128)(2,1)S(1)}, u32[]{:S(2)}, u32[]{:S(2)}) collective-permute-start(bf16[128,2048]{1,0:T(8,128)(2,1)S(1)} %pass_on.9), channel_id=1, source_target_pairs={{0,16},{16,0},{1,17},{17,1},{2,18},{18,2},{3,19},{19,3},{4,20},{20... | collective-permute-start | bytes 1572872 | tf_op jit(solution)/shard_map/ppermute | solution.py:52
  122.5 13.9 %collective-permute-start.41 = (bf16[128,2048]{1,0:T(8,128)(2,1)S(1)}, bf16[128,2048]{1,0:T(8,128)(2,1)S(1)}, u32[]{:S(2)}, u32[]{:S(2)}) collective-permute-start(bf16[128,2048]{1,0:T(8,128)(2,1)S(1)} %get-tuple-element.148), channel_id=1, source_target_pairs={{0,16},{16,0},{1,17},{17,1},{2,18},{18,2},{3,19},{19,3},{4,20},{20... | collective-permute-start | bytes 1572872 | tf_op jit(solution)/shard_map/ppermute | solution.py:52
  123.0 17.1 %copy-start.17 = (bf16[2048]{0:T(1024)(128)(2,1)S(1)}, bf16[2048]{0:T(1024)(128)(2,1)}, u32[]{:S(2)}) copy-start(bf16[2048]{0:T(1024)(128)(2,1)} %param.35) | copy-start | bytes 12292
  123.3 9.4 %collective-permute-start.40 = (bf16[64,2048]{1,0:T(8,128)(2,1)S(1)}, bf16[64,2048]{1,0:T(8,128)(2,1)S(1)}, u32[]{:S(2)}, u32[]{:S(2)}) collective-permute-start(bf16[64,2048]{1,0:T(8,128)(2,1)S(1)} %collect.4.refs_0_), channel_id=1, source_target_pairs={{0,4},{1,5},{2,6},{3,7},{4,12},{5,13},{6,14},{7,15},{8,0},{9,1},{1... | collective-permute-start | bytes 786440 | tf_op jit(solution)/shard_map/ppermute | solution.py:37
  125.9 6.9 %collective-permute-start.37 = (bf16[32,2048]{1,0:T(8,128)(2,1)S(1)}, bf16[32,2048]{1,0:T(8,128)(2,1)S(1)}, u32[]{:S(2)}, u32[]{:S(2)}) collective-permute-start(bf16[32,2048]{1,0:T(8,128)(2,1)S(1)} %get-tuple-element.144), channel_id=1, source_target_pairs={{0,1},{1,0},{2,3},{3,2},{4,5},{5,4},{6,7},{7,6},{8,9},{9,8},{10,11... | collective-permute-start | bytes 393224 | tf_op jit(solution)/shard_map/ppermute | solution.py:47
  126.7 7.8 %collective-permute-start.38 = (bf16[32,2048]{1,0:T(8,128)(2,1)S(1)}, bf16[32,2048]{1,0:T(8,128)(2,1)S(1)}, u32[]{:S(2)}, u32[]{:S(2)}) collective-permute-start(bf16[32,2048]{1,0:T(8,128)(2,1)S(1)} %get-tuple-element.145), channel_id=1, source_target_pairs={{0,2},{1,3},{2,0},{3,1},{4,6},{5,7},{6,4},{7,5},{8,10},{9,11},{10,... | collective-permute-start | bytes 393224 | tf_op jit(solution)/shard_map/ppermute | solution.py:47
  128.3 6.3 %collective-permute-start.39 = (bf16[32,2048]{1,0:T(8,128)(2,1)S(1)}, bf16[32,2048]{1,0:T(8,128)(2,1)S(1)}, u32[]{:S(2)}, u32[]{:S(2)}) collective-permute-start(bf16[32,2048]{1,0:T(8,128)(2,1)S(1)} %get-tuple-element.146), channel_id=1, source_target_pairs={{0,3},{1,2},{2,1},{3,0},{4,7},{5,6},{6,5},{7,4},{8,11},{9,10},{10,... | collective-permute-start | bytes 393224 | tf_op jit(solution)/shard_map/ppermute | solution.py:47
  134.8 10.0 %collective-permute-start.45 = (bf16[64,2048]{1,0:T(8,128)(2,1)S(1)}, bf16[64,2048]{1,0:T(8,128)(2,1)S(1)}, u32[]{:S(2)}, u32[]{:S(2)}) collective-permute-start(bf16[64,2048]{1,0:T(8,128)(2,1)S(1)} %collect.5.refs_0_), channel_id=1, source_target_pairs={{0,4},{1,5},{2,6},{3,7},{4,12},{5,13},{6,14},{7,15},{8,0},{9,1},{1... | collective-permute-start | bytes 786440 | tf_op jit(solution)/shard_map/ppermute | solution.py:37
  136.6 6.2 %collective-permute-start.42 = (bf16[32,2048]{1,0:T(8,128)(2,1)S(1)}, bf16[32,2048]{1,0:T(8,128)(2,1)S(1)}, u32[]{:S(2)}, u32[]{:S(2)}) collective-permute-start(bf16[32,2048]{1,0:T(8,128)(2,1)S(1)} %get-tuple-element.150), channel_id=1, source_target_pairs={{0,1},{1,0},{2,3},{3,2},{4,5},{5,4},{6,7},{7,6},{8,9},{9,8},{10,11... | collective-permute-start | bytes 393224 | tf_op jit(solution)/shard_map/ppermute | solution.py:47
  137.8 5.1 %collective-permute-start.43 = (bf16[32,2048]{1,0:T(8,128)(2,1)S(1)}, bf16[32,2048]{1,0:T(8,128)(2,1)S(1)}, u32[]{:S(2)}, u32[]{:S(2)}) collective-permute-start(bf16[32,2048]{1,0:T(8,128)(2,1)S(1)} %get-tuple-element.151), channel_id=1, source_target_pairs={{0,2},{1,3},{2,0},{3,1},{4,6},{5,7},{6,4},{7,5},{8,10},{9,11},{10,... | collective-permute-start | bytes 393224 | tf_op jit(solution)/shard_map/ppermute | solution.py:47
  138.9 5.9 %collective-permute-start.44 = (bf16[32,2048]{1,0:T(8,128)(2,1)S(1)}, bf16[32,2048]{1,0:T(8,128)(2,1)S(1)}, u32[]{:S(2)}, u32[]{:S(2)}) collective-permute-start(bf16[32,2048]{1,0:T(8,128)(2,1)S(1)} %get-tuple-element.152), channel_id=1, source_target_pairs={{0,3},{1,2},{2,1},{3,0},{4,7},{5,6},{6,5},{7,4},{8,11},{9,10},{10,... | collective-permute-start | bytes 393224 | tf_op jit(solution)/shard_map/ppermute | solution.py:47
  145.7 1.5 %collective-permute-start.46 = (bf16[64,2048]{1,0:T(8,128)(2,1)S(1)}, bf16[64,2048]{1,0:T(8,128)(2,1)S(1)}, u32[]{:S(2)}, u32[]{:S(2)}) collective-permute-start(bf16[64,2048]{1,0:T(8,128)(2,1)S(1)} %get-tuple-element.154), channel_id=1, source_target_pairs={{0,16},{16,0},{1,17},{17,1},{2,18},{18,2},{3,19},{19,3},{4,20},{20... | collective-permute-start | bytes 786440 | tf_op jit(solution)/shard_map/ppermute | solution.py:52
  (6 other events, 4.4 us)

commit v4 on v3

--- a/solution.py
+++ b/solution.py
@@ -47,6 +47,11 @@
     return lax.ppermute(block, "tensor", [(i, i ^ distance) for i in devices])
 
 
+def send_pieces(pieces):
+    sent = {d: send_plane(pieces[d], d) for d in reversed(range(1, PLANE))}
+    return [pieces[0]] + [sent[d] for d in range(1, PLANE)]
+
+
 def send_group(block, distance):
     devices = range(lax.axis_size("group"))
     return lax.ppermute(block, "group", [(i, i ^ distance) for i in devices])
@@ -81,18 +86,31 @@
     return inner
 
 
+def resident(arrays):
+    return [pl.BlockSpec(memory_space=pltpu.VMEM) for _ in arrays]
+
+
 def unread(arrays):
     return [pl.BlockSpec(memory_space=pl.ANY) for _ in arrays]
 
 
-def call(kernel, name, inputs, outputs, flops, limit=12, ready=()):
+def call(kernel, name, inputs, outputs, flops, limit=12, ready=(), streamed=False):
     shapes = [jax.ShapeDtypeStruct(shape, dtype) for shape, dtype in outputs]
     moved = sum(a.size * a.dtype.itemsize for a in list(inputs) + shapes)
+    if streamed:
+        places = {
+            "grid": (1,),
+            "in_specs": unread(ready) + [whole(a) for a in inputs],
+            "out_specs": [whole(shape) for shape in shapes],
+        }
+    else:
+        places = {
+            "in_specs": unread(ready) + resident(inputs),
+            "out_specs": resident(shapes),
+        }
     return pl.pallas_call(
         after(kernel, len(ready)),
-        grid=(1,),
-        in_specs=unread(ready) + [whole(a) for a in inputs],
-        out_specs=[whole(s) for s in shapes],
+        **places,
         out_shape=shapes,
         compiler_params=pltpu.CompilerParams(vmem_limit_bytes=limit * 1024 * 1024),
         cost_estimate=pl.CostEstimate(flops=flops, bytes_accessed=moved, transcendentals=0),
@@ -132,10 +150,10 @@
 
     outputs = [((size, WIDE), piece.dtype) for size in (rows + tok_quarter, rows)]
     inputs = [piece, suffix_columns, routes_columns]
-    return call(kernel, "join_share", inputs, outputs, 10_000_000, limit=58)
-
-
-def join_column(blocks, rows, share):
+    return call(kernel, "join_share", inputs, outputs, 10_000_000, limit=58, streamed=True)
+
+
+def join_column(blocks, rows, share, ready):
     count = len(blocks)
 
     def kernel(*refs):
@@ -150,18 +168,29 @@
         here = block_refs[0][rows:, :].astype(jnp.float32)
         before = block_refs[1][rows:, :].astype(jnp.float32)
         for d, far_ref in enumerate(far_refs):
-            for i, ref in enumerate(block_refs):
-                far_ref[i * rows : (i + 1) * rows, :] = ref[:rows, :]
+            if d < PLANE - 2:
+                for i, ref in enumerate(block_refs):
+                    far_ref[i * rows : (i + 1) * rows, :] = ref[:rows, :]
             later = plane_index < lax.bitwise_xor(plane_index, d + 1)
             part = jnp.where(later, here, before).astype(jnp.bfloat16)
-            far_ref[count * rows :, :] = part
+            far_ref[far_ref.shape[0] - share :, :] = part
 
     dtype = blocks[0].dtype
     outputs = [((count * rows + 2 * share, WIDE), dtype)]
-    outputs += [((count * rows + share, WIDE), dtype)] * (PLANE - 1)
+    outputs += [((count * rows + share, WIDE), dtype)] * (PLANE - 2)
+    outputs.append(((share, WIDE), dtype))
     outputs.append(((count, ROUTE_ROWS, WIDE - LAT), dtype))
-    near, *far, routes = call(kernel, "join_column", blocks, outputs, 0)
+    near, *far, routes = call(kernel, "join_column", blocks, outputs, 0, ready=ready)
     return near, far, routes
+
+
+def halves(by_y, by_x, rows):
+    def kernel(by_y_ref, by_x_ref, first_ref, second_ref):
+        first_ref[...] = by_y_ref[:rows, :]
+        second_ref[...] = by_x_ref[rows : 2 * rows, :]
+
+    outputs = [((rows, WIDE), by_y.dtype)] * 2
+    return call(kernel, "halves", [by_y, by_x], outputs, 0)
 
 
 def pass_on(blocks, ready):
@@ -184,10 +213,10 @@
 LATER = 1 << 20
 
 
-def key_table(groups, planes, segments):
+def key_table(groups, sides):
     rows = []
     for j in range(groups):
-        for d in planes:
+        for d, segments in sides:
             for k, count, real, suffix in segments:
                 rows += [(j, d, k, r, suffix, r < real) for r in range(count)]
     table = np.zeros((8, len(rows)), np.int32)
@@ -307,91 +336,82 @@
     return (scores.reshape(pair, rows // pair, count) + bias[...][None]).reshape(rows, count)
 
 
-def near_kernel(
-    block_count, token_ref, spot_ref, order_ref, query_ref, key_up_ref, *refs
-):
+def near_kernel(block_count, pair, token_ref, spot_ref, order_ref, query_ref, key_up_ref, *refs):
     key_refs = refs[:block_count]
     wide_ref, best_ref, sum_ref, acc_ref, flag_ref, keys, bias = refs[block_count:]
     flag_ref[...] = jnp.zeros_like(flag_ref)
     tokens = query_ref.shape[0]
-    pair = key_up_ref.shape[0]
-
-    @pl.when(pl.program_id(0) == 0)
-    def prepare():
-        place_keys(key_refs, spot_ref, token_ref, keys, bias)
-
+    place_keys(key_refs, spot_ref, token_ref, keys, bias)
     queries = dot_f(order_ref[...], query_ref[...]).astype(jnp.bfloat16)
     size = NOPE + ROPE
-    wide = []
     empty = jnp.zeros((tokens, WIDE - LAT - ROPE), jnp.bfloat16)
-    for h in range(pair):
-        part = queries[:, h * size : (h + 1) * size]
-        content = dot_f(part[:, :NOPE], key_up_ref[h]).astype(jnp.bfloat16)
-        wide.append(jnp.concatenate([content, part[:, NOPE:], empty], axis=1))
-    wide = jnp.concatenate(wide, axis=0)
-    wide_ref[...] = wide
-    masked = score_rows(wide, keys, bias, pair)
-    best = jnp.max(masked, axis=-1, keepdims=True)
-    weights = jnp.exp2((masked - best) * SCORE_FACTOR)
-    best_ref[...] = best
-    sum_ref[...] = jnp.sum(weights, axis=-1, keepdims=True)
-    acc_ref[...] = dot_f(weights.astype(jnp.bfloat16), keys[:, :LAT])
-
-
-def attend_near(tokens_info, spots, order, queries, key_up, blocks, ready):
+    for first in range(0, key_up_ref.shape[0], pair):
+        wide = []
+        for h in range(first, first + pair):
+            part = queries[:, h * size : (h + 1) * size]
+            content = dot_f(part[:, :NOPE], key_up_ref[h]).astype(jnp.bfloat16)
+            wide.append(jnp.concatenate([content, part[:, NOPE:], empty], axis=1))
+        wide = jnp.concatenate(wide, axis=0)
+        here = pl.ds(first * tokens, pair * tokens)
+        wide_ref[here, :] = wide
+        masked = score_rows(wide, keys, bias, pair)
+        best = jnp.max(masked, axis=-1, keepdims=True)
+        weights = jnp.exp2((masked - best) * SCORE_FACTOR)
+        best_ref[here, :] = best
+        sum_ref[here, :] = jnp.sum(weights, axis=-1, keepdims=True)
+        acc_ref[here, :] = dot_f(weights.astype(jnp.bfloat16), keys[:, :LAT])
+
+
+def attend_call(kernel, name, inputs, outputs, scratch, work, limit=24):
+    shapes = [jax.ShapeDtypeStruct(shape, dtype) for shape, dtype in outputs]
+    return pl.pallas_call(
+        kernel,
+        in_specs=resident(inputs),
+        out_specs=resident(shapes),
+        out_shape=shapes,
+        scratch_shapes=scratch,
+        compiler_params=pltpu.CompilerParams(vmem_limit_bytes=limit * 1024 * 1024),
+        cost_estimate=pl.CostEstimate(
+            flops=work, bytes_accessed=8_000_000, transcendentals=work // 2176
+        ),
+        name=name,
+    )(*inputs)
+
+
+def key_scratch(tokens, blocks):
+    count = sum(block.shape[0] for block in blocks)
+    return [pltpu.VMEM((count, WIDE), jnp.bfloat16), pltpu.VMEM((tokens, count), jnp.float32)]
+
+
+def attend_near(tokens_info, spots, order, queries, key_up, blocks):
     tokens = queries.shape[0]
     heads = key_up.shape[0]
-    pair = min(4, heads)
-    count = sum(block.shape[0] for block in blocks)
-    size = NOPE + ROPE
-
-    def per_step(columns):
-        return pl.BlockSpec((pair * tokens, columns), lambda i: (i, 0))
-
     rows = heads * tokens
-    return pl.pallas_call(
-        after(functools.partial(near_kernel, len(blocks)), len(ready)),
-        grid=(heads // pair,),
-        in_specs=unread(ready)
-        + [
-            whole(tokens_info),
-            whole(spots),
-            whole(order),
-            pl.BlockSpec((tokens, pair * size), lambda i: (0, i)),
-            pl.BlockSpec((pair, NOPE, LAT), lambda i: (i, 0, 0)),
-        ]
-        + [whole(block) for block in blocks],
-        out_specs=[per_step(WIDE), per_step(1), per_step(1), per_step(LAT)]
-        + [pl.BlockSpec((8, 128), lambda i: (0, 0))],
-        out_shape=[
-            jax.ShapeDtypeStruct((rows, WIDE), jnp.bfloat16),
-            jax.ShapeDtypeStruct((rows, 1), jnp.float32),
-            jax.ShapeDtypeStruct((rows, 1), jnp.float32),
-            jax.ShapeDtypeStruct((rows, LAT), jnp.float32),
-            jax.ShapeDtypeStruct((8, 128), jnp.float32),
-        ],
-        scratch_shapes=[
-            pltpu.VMEM((count, WIDE), jnp.bfloat16),
-            pltpu.VMEM((tokens, count), jnp.float32),
-        ],
-        compiler_params=pltpu.CompilerParams(vmem_limit_bytes=58 * 1024 * 1024),
-        cost_estimate=pl.CostEstimate(
-            flops=2 * rows * count * (LAT + ROPE + LAT),
-            bytes_accessed=8_000_000,
-            transcendentals=rows * count,
-        ),
-        name="attend_near",
-    )(*ready, tokens_info, spots, order, queries, key_up, *blocks)
-
-
-def add_keys(wide_ref, best_ref, sum_ref, acc_ref, keys, bias, pair):
-    masked = score_rows(wide_ref[...], keys, bias, pair)
-    before = best_ref[...]
+    outputs = [
+        ((rows, WIDE), jnp.bfloat16),
+        ((rows, 1), jnp.float32),
+        ((rows, 1), jnp.float32),
+        ((rows, LAT), jnp.float32),
+        ((8, 128), jnp.float32),
+    ]
+    return attend_call(
+        functools.partial(near_kernel, len(blocks), min(4, heads)),
+        "attend_near",
+        [tokens_info, spots, order, queries, key_up, *blocks],
+        outputs,
+        key_scratch(tokens, blocks),
+        2 * rows * spots.shape[1] * (LAT + ROPE + LAT),
+    )
+
+
+def add_keys(here, wide_ref, best_ref, sum_ref, acc_ref, keys, bias, pair):
+    masked = score_rows(wide_ref[here, :], keys, bias, pair)
+    before = best_ref[here, :]
     best = jnp.maximum(before, jnp.max(masked, axis=-1, keepdims=True))
     factor = jnp.exp2((before - best) * SCORE_FACTOR)
     weights = jnp.exp2((masked - best) * SCORE_FACTOR)
-    weight_sum = sum_ref[...] * factor + jnp.sum(weights, axis=-1, keepdims=True)
-    attended = acc_ref[...] * factor + dot_f(weights.astype(jnp.bfloat16), keys[:, :LAT])
+    weight_sum = sum_ref[here, :] * factor + jnp.sum(weights, axis=-1, keepdims=True)
+    attended = acc_ref[here, :] * factor + dot_f(weights.astype(jnp.bfloat16), keys[:, :LAT])
     return best, weight_sum, attended
 
 
@@ -399,57 +419,37 @@
     key_refs = refs[:block_count]
     new_best_ref, new_sum_ref, new_acc_ref, flag_ref, keys, bias = refs[block_count:]
     flag_ref[...] = jnp.zeros_like(flag_ref)
-
-    @pl.when(pl.program_id(0) == 0)
-    def prepare():
-        place_keys(key_refs, spot_ref, token_ref, keys, bias)
-
-    new_best_ref[...], new_sum_ref[...], new_acc_ref[...] = add_keys(
-        wide_ref, best_ref, sum_ref, acc_ref, keys, bias, pair
-    )
+    place_keys(key_refs, spot_ref, token_ref, keys, bias)
+    rows = pair * token_ref.shape[0]
+    for first in range(0, wide_ref.shape[0], rows):
+        here = pl.ds(first, rows)
+        new_best_ref[here, :], new_sum_ref[here, :], new_acc_ref[here, :] = add_keys(
+            here, wide_ref, best_ref, sum_ref, acc_ref, keys, bias, pair
+        )
 
 
 def attend_mid(tokens_info, spots, near, blocks):
     tokens = tokens_info.shape[0]
     rows = near[0].shape[0]
-    heads = rows // tokens
-    pair = min(4, heads)
-    count = sum(block.shape[0] for block in blocks)
-
-    def per_step(columns):
-        return pl.BlockSpec((pair * tokens, columns), lambda i: (i, 0))
-
-    return pl.pallas_call(
-        functools.partial(mid_kernel, len(blocks), pair),
-        grid=(heads // pair,),
-        in_specs=[whole(tokens_info), whole(spots)]
-        + [per_step(WIDE), per_step(1), per_step(1), per_step(LAT)]
-        + [whole(block) for block in blocks],
-        out_specs=[per_step(1), per_step(1), per_step(LAT)]
-        + [pl.BlockSpec((8, 128), lambda i: (0, 0))],
-        out_shape=[
-            jax.ShapeDtypeStruct((rows, 1), jnp.float32),
-            jax.ShapeDtypeStruct((rows, 1), jnp.float32),
-            jax.ShapeDtypeStruct((rows, LAT), jnp.float32),
-            jax.ShapeDtypeStruct((8, 128), jnp.float32),
-        ],
-        scratch_shapes=[
-            pltpu.VMEM((count, WIDE), jnp.bfloat16),
-            pltpu.VMEM((tokens, count), jnp.float32),
-        ],
-        compiler_params=pltpu.CompilerParams(vmem_limit_bytes=58 * 1024 * 1024),
-        cost_estimate=pl.CostEstimate(
-            flops=2 * rows * count * (LAT + ROPE + LAT),
-            bytes_accessed=8_000_000,
-            transcendentals=rows * count,
-        ),
-        name="attend_mid",
-    )(tokens_info, spots, *near, *blocks)
+    outputs = [
+        ((rows, 1), jnp.float32),
+        ((rows, 1), jnp.float32),
+        ((rows, LAT), jnp.float32),
+        ((8, 128), jnp.float32),
+    ]
+    return attend_call(
+        functools.partial(mid_kernel, len(blocks), min(4, rows // tokens)),
+        "attend_mid",
+        [tokens_info, spots, *near, *blocks],
+        outputs,
+        key_scratch(tokens, blocks),
+        2 * rows * spots.shape[1] * (LAT + ROPE + LAT),
+    )
 
 
 def far_kernel(
     block_count,
-    tok_quarter,
+    pair,
     token_ref,
     spot_ref,
     wide_ref,
@@ -461,76 +461,42 @@
     *refs,
 ):
     key_refs = refs[:block_count]
-    own_ref, other_ref, keys, bias, total = refs[block_count:]
-    step = pl.program_id(0)
-    pair = value_up_ref.shape[0]
-    tokens = wide_ref.shape[0] // pair
-
-    @pl.when(step == 0)
-    def prepare():
-        place_keys(key_refs, spot_ref, token_ref, keys, bias)
-        total[...] = jnp.zeros_like(total)
-
-    _, weight_sum, attended = add_keys(wide_ref, best_ref, sum_ref, acc_ref, keys, bias, pair)
-    attended = (attended / weight_sum).astype(jnp.bfloat16)
-    heads = [
-        dot_f(attended[h * tokens : (h + 1) * tokens], value_up_ref[h]).astype(jnp.bfloat16)
-        for h in range(pair)
-    ]
-    total[...] += dot_f(jnp.concatenate(heads, axis=1), output_ref[...])
-
-    @pl.when(step == pl.num_programs(0) - 1)
-    def finish():
-        own_ref[...] = total[:tok_quarter, :]
-        other_ref[...] = total[tok_quarter:, :].astype(jnp.bfloat16)
+    own_ref, other_ref, keys, bias = refs[block_count:]
+    tokens = token_ref.shape[0]
+    rows = pair * tokens
+    place_keys(key_refs, spot_ref, token_ref, keys, bias)
+    heads = []
+    for first in range(0, wide_ref.shape[0], rows):
+        _, weight_sum, attended = add_keys(
+            pl.ds(first, rows), wide_ref, best_ref, sum_ref, acc_ref, keys, bias, pair
+        )
+        attended = (attended / weight_sum).astype(jnp.bfloat16)
+        for h in range(pair):
+            part = attended[h * tokens : (h + 1) * tokens]
+            value = value_up_ref[first // tokens + h]
+            heads.append(dot_f(part, value).astype(jnp.bfloat16))
+    total = dot_f(jnp.concatenate(heads, axis=1), output_ref[...])
+    mine = own_ref.shape[0]
+    own_ref[...] = total[:mine]
+    other_ref[...] = total[mine:].astype(jnp.bfloat16)
 
 
 def attend_far(tokens_info, spots, near, value_up, output_weight, blocks, tok_quarter):
     tokens = tokens_info.shape[0]
     heads = value_up.shape[0]
     width = output_weight.shape[1]
-    pair = min(4, heads)
-    count = sum(block.shape[0] for block in blocks)
-    rows = heads * tokens
-
-    def per_step(columns):
-        return pl.BlockSpec((pair * tokens, columns), lambda i: (i, 0))
-
-    return pl.pallas_call(
-        functools.partial(far_kernel, len(blocks), tok_quarter),
-        grid=(heads // pair,),
-        in_specs=[
-            whole(tokens_info),
-            whole(spots),
-            per_step(WIDE),
-            per_step(1),
-            per_step(1),
-            per_step(LAT),
-            pl.BlockSpec((pair, LAT, value_up.shape[2]), lambda i: (i, 0, 0)),
-            pl.BlockSpec((pair * value_up.shape[2], width), lambda i: (i, 0)),
-        ]
-        + [whole(block) for block in blocks],
-        out_specs=[
-            pl.BlockSpec((tok_quarter, width), lambda i: (0, 0)),
-            pl.BlockSpec((tokens - tok_quarter, width), lambda i: (0, 0)),
-        ],
-        out_shape=[
-            jax.ShapeDtypeStruct((tok_quarter, width), jnp.float32),
-            jax.ShapeDtypeStruct((tokens - tok_quarter, width), jnp.bfloat16),
-        ],
-        scratch_shapes=[
-            pltpu.VMEM((count, WIDE), jnp.bfloat16),
-            pltpu.VMEM((tokens, count), jnp.float32),
-            pltpu.VMEM((tokens, width), jnp.float32),
-        ],
-        compiler_params=pltpu.CompilerParams(vmem_limit_bytes=58 * 1024 * 1024),
-        cost_estimate=pl.CostEstimate(
-            flops=2 * rows * count * (LAT + ROPE + LAT),
-            bytes_accessed=12_000_000,
-            transcendentals=rows * count,
-        ),
-        name="attend_far",
-    )(tokens_info, spots, *near, value_up, output_weight, *blocks)
+    outputs = [
+        ((tok_quarter, width), jnp.float32),
+        ((tokens - tok_quarter, width), jnp.bfloat16),
+    ]
+    return attend_call(
+        functools.partial(far_kernel, len(blocks), min(4, heads)),
+        "attend_far",
+        [tokens_info, spots, *near, value_up, output_weight, *blocks],
+        outputs,
+        key_scratch(tokens, blocks),
+        2 * heads * tokens * spots.shape[1] * (LAT + ROPE + LAT),
+    )
 
 
 def pick_rows(turn, ring, top, block, routes_ref, router_ref, scaled_ref, outs):
@@ -652,86 +618,29 @@
     return scaled, joined, found
 
 
-def expert_kernel(count, kept, depth_steps, *refs):
-    row_refs = refs[:count]
-    gate_ref, up_ref, down_ref, own_ref, other_ref, flag_ref, *scratch = refs[count:]
-    rows, gate_sum, up_sum, hidden = scratch
-    flag_ref[...] = jnp.zeros_like(flag_ref)
-    step = pl.program_id(0)
-    depth = gate_ref.shape[1]
-
-    @pl.when(step == 0)
-    def prepare():
-        at = 0
-        for ref in row_refs:
-            size = ref.shape[0]
-            for i in range(depth_steps):
-                rows[i, at : at + size, :] = ref[:, i * depth : (i + 1) * depth]
-            at += size
-
-    @pl.when(step < depth_steps)
-    def widen():
-        part = rows[jnp.minimum(step, depth_steps - 1)]
-        gate_part = dot_t(part, gate_ref[...])
-        up_part = dot_t(part, up_ref[...])
-
-        @pl.when(step == 0)
-        def first():
-            gate_sum[...] = gate_part
-            up_sum[...] = up_part
-
-        @pl.when(step > 0)
-        def later():
-            gate_sum[...] += gate_part
-            up_sum[...] += up_part
-
-    @pl.when(step == depth_steps - 1)
-    def activate():
-        hidden[...] = (jax.nn.silu(gate_sum[...]) * up_sum[...]).astype(jnp.bfloat16)
-
-    @pl.when(step >= depth_steps)
-    def narrow():
-        own_ref[...] = dot_f(hidden[:kept, :], down_ref[...])
-        other_ref[...] = dot_f(hidden[kept:, :], down_ref[...]).astype(jnp.bfloat16)
-
-
-def expert_apply(pieces, kept, gate_part, up_part, down_part, ready):
-    steps = 2
+def expert_apply(pieces, kept, gate_part, up_part, down_part):
     total = sum(piece.shape[0] for piece in pieces)
     units, width = gate_part.shape
-    depth = width // steps
-    return pl.pallas_call(
-        after(functools.partial(expert_kernel, len(pieces), kept, steps), len(ready)),
-        grid=(2 * steps,),
-        in_specs=unread(ready)
-        + [whole(piece) for piece in pieces]
-        + [
-            pl.BlockSpec((units, depth), lambda i: (0, jnp.minimum(i, steps - 1))),
-            pl.BlockSpec((units, depth), lambda i: (0, jnp.minimum(i, steps - 1))),
-            pl.BlockSpec((units, depth), lambda i: (0, jnp.maximum(i - steps, 0))),
-        ],
-        out_specs=[
-            pl.BlockSpec((kept, depth), lambda i: (0, jnp.maximum(i - steps, 0))),
-            pl.BlockSpec((total - kept, depth), lambda i: (0, jnp.maximum(i - steps, 0))),
-            pl.BlockSpec((8, 128), lambda i: (0, 0)),
-        ],
-        out_shape=[
-            jax.ShapeDtypeStruct((kept, width), jnp.float32),
-            jax.ShapeDtypeStruct((total - kept, width), jnp.bfloat16),
-            jax.ShapeDtypeStruct((8, 128), jnp.float32),
-        ],
-        scratch_shapes=[
-            pltpu.VMEM((steps, total, depth), jnp.bfloat16),
-            pltpu.VMEM((total, units), jnp.float32),
-            pltpu.VMEM((total, units), jnp.float32),
-            pltpu.VMEM((total, units), jnp.bfloat16),
-        ],
-        compiler_params=pltpu.CompilerParams(vmem_limit_bytes=24 * 1024 * 1024),
-        cost_estimate=pl.CostEstimate(
-            flops=6 * total * width * units, bytes_accessed=10_000_000, transcendentals=0
-        ),
-        name="experts",
-    )(*ready, *pieces, gate_part, up_part, down_part)
+
+    def kernel(*refs):
+        row_refs = refs[: len(pieces)]
+        gate_ref, up_ref, down_ref, own_ref, other_ref, flag_ref = refs[len(pieces) :]
+        flag_ref[...] = jnp.zeros_like(flag_ref)
+        rows = jnp.concatenate([ref[...] for ref in row_refs], axis=0)
+        gate_vals = dot_t(rows, gate_ref[...])
+        up_vals = dot_t(rows, up_ref[...])
+        hidden = (jax.nn.silu(gate_vals) * up_vals).astype(jnp.bfloat16)
+        partial = dot_f(hidden, down_ref[...])
+        own_ref[...] = partial[:kept]
+        other_ref[...] = partial[kept:].astype(jnp.bfloat16)
+
+    outputs = [
+        ((kept, width), jnp.float32),
+        ((total - kept, width), jnp.bfloat16),
+        ((8, 128), jnp.float32),
+    ]
+    inputs = [*pieces, gate_part, up_part, down_part]
+    return call(kernel, "experts", inputs, outputs, 6 * total * width * units, limit=20)
 
 
 def scatter_sum(scaled_ref, piece_refs, running_ref):
@@ -771,6 +680,26 @@
 
     inputs = [residual, gain, scaled, *pieces, *extra]
     return call(kernel, "conclude", inputs, [(residual.shape, jnp.bfloat16)] * 2, 35_000_000)
+
+
+def project(shares, order, query_weight, latent_rows):
+    def kernel(order_ref, query_ref, latent_ref, *refs):
+        share_refs = refs[: len(shares)]
+        queries_ref, latents_ref = refs[len(shares) :]
+        rows = jnp.concatenate([ref[...] for ref in share_refs], axis=0)
+        rows = lax.dot_general(
+            order_ref[...], rows, (((0,), (0,)), ((), ())), preferred_element_type=jnp.float32
+        ).astype(jnp.bfloat16)
+        latents_ref[...] = dot_t(latent_ref[...], rows).astype(jnp.bfloat16)
+        queries_ref[...] = dot_f(rows, query_ref[...]).astype(jnp.bfloat16)
+
+    tokens = order.shape[0]
+    outputs = [
+        ((tokens, query_weight.shape[1]), jnp.bfloat16),
+        ((latent_rows.shape[0], tokens), jnp.bfloat16),
+    ]
+    inputs = [order, query_weight, latent_rows, *shares]
+    return call(kernel, "project", inputs, outputs, 1_000_000_000, limit=16)
 
 
 def per_device(
@@ -812,10 +741,6 @@
     routes_columns = jnp.transpose(routes, (2, 0, 1))
     full, lite = join_share(piece, suffix_latent.T, routes_columns, tok_quarter)
     along = [send_round(full, PLANE)] + [send_round(lite, PLANE * k) for k in range(2, ring)]
-    column, plane, routes_ring = join_column([full, *along], piece_rows, tok_quarter)
-    plane = [send_plane(part, d + 1) for d, part in enumerate(plane)]
-    near_blocks = [send_group(column, j) if j else column for j in range(groups)]
-
     near_segments = []
     far_segments = []
     for k in range(ring):
@@ -825,11 +750,11 @@
             near_segments.append((k, tok_quarter, 0, 1))
     far_segments.append((0, tok_quarter, 0, 2))
     sides = (
-        ((0,), near_segments),
-        (range(1, PLANE - 1), far_segments),
-        ((PLANE - 1,), far_segments),
-    )
-    tables = [jnp.asarray(key_table(groups, side, parts)) for side, parts in sides]
+        [(0, near_segments)],
+        [(1, far_segments), (2, far_segments)],
+        [(3, far_segments)],
+    )
+    tables = [jnp.asarray(key_table(groups, side)) for side in sides]
     tokens_info, permutation, near_spots, mid_spots, far_spots = make_plan(
         tables,
         suffix_lengths,
@@ -842,15 +767,23 @@
         [full],
     )
 
+    column, plane, routes_ring = join_column(
+        [full, *along], piece_rows, tok_quarter, [near_spots]
+    )
+    plane = send_pieces([column, *plane])[1:]
+    near_blocks = [send_group(column, j) if j else column for j in range(groups)]
+
     *near, near_flag = attend_near(
-        tokens_info, near_spots, permutation, queries, key_up, near_blocks, [column]
-    )
-    beside = pass_on(plane[:-1], [near_flag])
+        tokens_info, near_spots, permutation, queries, key_up, near_blocks
+    )
+    beside = pass_on(plane[:2], [near_flag])
+    first, second = halves(beside[1], beside[0], ring * piece_rows // 2)
+    across = [send_plane(first, 1), send_plane(second, 2)]
     mid_blocks = [send_group(block, j) if j else block for j in range(groups) for block in beside]
     *mid, mid_flag = attend_mid(tokens_info, mid_spots, near, mid_blocks)
     near = [near[0], *mid]
-    across = pass_on(plane[-1:], [mid_flag])[0]
-    far_blocks = [send_group(across, j) if j else across for j in range(groups)]
+    across = pass_on([*across, plane[2]], [mid_flag])
+    far_blocks = [send_group(block, j) if j else block for j in range(groups) for block in across]
     attend_own, attend_other = attend_far(
         tokens_info, far_spots, near, value_up, output_weight, far_blocks, tok_quarter
     )
@@ -881,9 +814,9 @@
     running = None
     payload = pieces
     for step in range(1, ring + 4):
-        arrived = [send_plane(piece, d) if d else piece for d, piece in enumerate(payload)]
         if step <= ring - 1:
             block = send_ring(block, ring)
+        arrived = send_pieces(payload)
         if 4 <= step:
             k = step - 3
             if k < ring:
@@ -917,21 +850,16 @@
             scales.append(scaled)
         if joined is not None:
             rows = [send_group(joined, j) if j else joined for j in range(groups)]
-            results.append(expert_apply(rows, kept, gate_part, up_part, down_part, []))
+            results.append(expert_apply(rows, kept, gate_part, up_part, down_part))
     layer_rows, normed_next = conclude(
         scales[0], arrived, running, residual, next_gain[None, :]
     )
 
     shares = [send_group(normed_next, j) if j else normed_next for j in range(groups)]
-    gathered = lax.dot_general(
-        permutation,
-        jnp.concatenate(shares, axis=0),
-        (((0,), (0,)), ((), ())),
-        preferred_element_type=jnp.float32,
-    ).astype(jnp.bfloat16)
-    next_queries = dot_f(gathered, next_query_weight).astype(jnp.bfloat16)
-    next_latent = dot_f(gathered, next_latent_weight).astype(jnp.bfloat16)
-    return (layer_rows[:, None, :], next_queries, next_latent)
+    next_queries, next_latent = project(
+        shares, permutation, next_query_weight, next_latent_weight.T
+    )
+    return (layer_rows[:, None, :], next_queries, next_latent.T)
 
 
 def solution(mesh):

time: 151 us -> 138 us (0.914)
  Pallas kernels: 52.2 us -> 36.6 us
  waiting for transfers between devices: 41 us -> 49.3 us
  matrix products: 3.42 us -> 0.22 us
  local copies, waits for them, and re-layouts: 5.68 us -> 3.04 us
    pallas_call x20 -> x22, Pallas kernels: 50.2 us -> 34.5 us  [the longest x19 19.9 us: call(): pl.pallas_call(after(kernel, len(ready)), **places, out_shape=shapes, com...]
    ppermute x24 -> x26, waiting for transfers between devices: 21.4 us -> 28.3 us  [send_plane(): return lax.ppermute(block, 'tensor', [(i, i ^ distance) for i in devices])]
    ppermute x6, waiting for transfers between devices: 4.69 us -> 8.08 us  [send_ring(): return lax.ppermute(block, 'tensor', route)]
    dot_general x3 -> x1, matrix products: 3.1 us -> 0.22 us  [dot_f(): return jnp.dot(left, right, preferred_element_type=jnp.float32)]
    unnamed x46 -> x44, local copies, waits for them, and re-layouts: 5.67 us -> 3.02 us
    ppermute x24 -> x26, starting transfers between devices: 29.1 us -> 31.2 us  [send_plane(): return lax.ppermute(block, 'tensor', [(i, i ^ distance) for i in devices])]
    ppermute x14 -> x16, waiting for transfers between devices: 8.78 us -> 7.96 us  [send_group(): return lax.ppermute(block, 'group', [(i, i ^ distance) for i in devices])]
  transfers between devices with their start and end apart: 47 -> 51, of which waited for: 25 -> 28; matrix products, arithmetic and copies ran while one was open for 0% -> 0% of each run, Pallas kernels for 25% -> 17%
where the time goes in v4:
time: 138 us
  waiting for transfers between devices  49.3 us (36%)
  starting transfers between devices  47.9 us (35%)
  Pallas kernels  36.6 us (27%)
  local copies, waits for them, and re-layouts  3.04 us (2%)
    ppermute x26, starting transfers between devices, send_plane(): return lax.ppermute(block, 'tensor', [(i, i ^ distance) for i in devices])  31.2 us
    ppermute x26, waiting for transfers between devices, send_plane(): return lax.ppermute(block, 'tensor', [(i, i ^ distance) for i in devices])  28.3 us
    pallas_call x19, Pallas kernels, call(): pl.pallas_call(after(kernel, len(ready)), **places, out_shape=shapes, com...  19.9 us
    pallas_call x3, Pallas kernels, attend_call(): pl.pallas_call(kernel, in_specs=resident(inputs), out_specs=resident(shap...  14.6 us
    ppermute x6, starting transfers between devices, send_ring(): return lax.ppermute(block, 'tensor', route)  8.09 us
    ppermute x6, waiting for transfers between devices, send_ring(): return lax.ppermute(block, 'tensor', route)  8.08 us
    ppermute x16, waiting for transfers between devices, send_group(): return lax.ppermute(block, 'group', [(i, i ^ distance) for i in devices])  7.96 us
    ppermute x3, starting transfers between devices, send_round(): lax.ppermute(block, 'tensor', [(i, (i + distance) % count) for i in range...  6.06 us
  transfers between devices with their start and end apart: 51, of which 28 were waited for; matrix products, arithmetic and copies ran while one was open for 0% of the time, Pallas kernels for 17%

profile of v4, /device:TPU:0, one launch (start us, length us, event | category | flops | bytes accessed | tf_op | source)
XLA Modules:
  0.0 138.1 jit_solution(6810504789193755944)
XLA Ops:
  0.6 1.9 %join_share.1 = (bf16[128,640]{1,0:T(8,128)(2,1)}, bf16[64,640]{1,0:T(8,128)(2,1)}) custom-call(bf16[64,576]{1,0:T(8,128)(2,1)} %refs_0_.1, bf16[576,128]{1,0:T(8,128)(2,1)} %bitcast.34, s32[6,2,64]{2,1,0:T(2,128)} %bitcast.35), custom_call_target="tpu_custom_call" | custom-call | flops 10000000 | bytes 470016 | tf_op jit(solution)/shard_map/join_share/pallas_call | solution.py:111
  2.5 4.0 %collective-permute-start.1 = (bf16[64,640]{1,0:T(8,128)(2,1)}, bf16[64,640]{1,0:T(8,128)(2,1)S(1)}, u32[]{:S(2)}, u32[]{:S(2)}) collective-permute-start(bf16[64,640]{1,0:T(8,128)(2,1)} %get-tuple-element.91), channel_id=1, source_target_pairs={{0,8},{1,9},{2,10},{3,11},{4,12},{5,13},{6,14},{7,15},{8,0},{9,1},... | collective-permute-start | bytes 245768 | tf_op jit(solution)/shard_map/ppermute | solution.py:42
  6.5 1.3 collective-permute-start.2
  8.6 2.1 %make_plan.1 = (s32[128,4]{1,0:T(8,128)}, bf16[128,128]{1,0:T(8,128)(2,1)}, s32[1,768]{1,0:T(1,128)}, s32[1,1280]{1,0:T(1,128)}, s32[1,640]{1,0:T(1,128)}) custom-call(bf16[128,640]{1,0:T(8,128)(2,1)} %get-tuple-element.86.refs_0_.refs_1_, s32[8]{0:T(128)} %refs_1_.2, s32[8]{0:T(128)} %refs_2_.1, s32[4]{0:T(128)} %refs_3_.1, s32[1,256]{1,0:T(1,128)} %bitcast.38, ...), custom_call_target="tpu_custom_call" | custom-call | flops 4000000000 | bytes 1000000 | tf_op jit(solution)/shard_map/make_plan/pallas_call | solution.py:303
  11.5 4.2 %collective-permute-done.refs_2_ = bf16[128,640]{1,0:T(8,128)(2,1)S(1)} collective-permute-done((bf16[128,640]{1,0:T(8,128)(2,1)}, bf16[128,640]{1,0:T(8,128)(2,1)S(1)}, u32[]{:S(2)}, u32[]{:S(2)}) %collective-permute-start) | collective-permute-done | bytes 163872 | tf_op jit(solution)/shard_map/ppermute | solution.py:42
  16.5 1.6 %collective-permute-start.4 = (bf16[320,640]{1,0:T(8,128)(2,1)S(1)}, bf16[320,640]{1,0:T(8,128)(2,1)S(1)}, u32[]{:S(2)}, u32[]{:S(2)}) collective-permute-start(bf16[320,640]{1,0:T(8,128)(2,1)S(1)} %get-tuple-element.99), channel_id=1, source_target_pairs={{0,1},{1,0},{2,3},{3,2},{4,5},{5,4},{6,7},{7,6},{8,9},{9,8},{10,11... | collective-permute-start | bytes 1228808 | tf_op jit(solution)/shard_map/ppermute | solution.py:47
  18.1 1.5 %collective-permute-start.5 = (bf16[320,640]{1,0:T(8,128)(2,1)S(1)}, bf16[320,640]{1,0:T(8,128)(2,1)S(1)}, u32[]{:S(2)}, u32[]{:S(2)}) collective-permute-start(bf16[320,640]{1,0:T(8,128)(2,1)S(1)} %get-tuple-element.100), channel_id=1, source_target_pairs={{0,2},{1,3},{2,0},{3,1},{4,6},{5,7},{6,4},{7,5},{8,10},{9,11},{10,... | collective-permute-start | bytes 1228808 | tf_op jit(solution)/shard_map/ppermute | solution.py:47
  20.4 0.8 copy-done.11
  21.9 4.0 %attend_near.1 = (bf16[1024,640]{1,0:T(8,128)(2,1)S(1)}, f32[1024,1]{1,0:T(8,128)S(1)}, f32[1024,1]{1,0:T(8,128)S(1)}, f32[1024,512]{1,0:T(8,128)S(1)}, f32[8,128]{1,0:T(8,128)S(1)}) custom-call(s32[128,4]{1,0:T(8,128)S(1)} %copy-done.11, s32[1,768]{1,0:T(1,128)S(1)} %copy-done.13, bf16[128,128]{1,0:T(8,128)(2,1)S(1)} %copy-done.9, ...), custom_call_target="tpu_custom_call" | custom-call | flops 1711276032 | bytes 8000000 | tf_op jit(solution)/shard_map/attend_near/pallas_call | solution.py:367
  25.8 2.6 %collective-permute-done.4.refs_1_ = bf16[320,640]{1,0:T(8,128)(2,1)S(1)} collective-permute-done((bf16[320,640]{1,0:T(8,128)(2,1)S(1)}, bf16[320,640]{1,0:T(8,128)(2,1)S(1)}, u32[]{:S(2)}, u32[]{:S(2)}) %collective-permute-start.4) | collective-permute-done | bytes 409632 | tf_op jit(solution)/shard_map/ppermute | solution.py:47
  28.4 1.2 collective-permute-done.5.refs_2_
  30.1 1.5 %collective-permute-start.10 = (bf16[64,640]{1,0:T(8,128)(2,1)S(1)}, bf16[64,640]{1,0:T(8,128)(2,1)S(1)}, u32[]{:S(2)}, u32[]{:S(2)}) collective-permute-start(bf16[64,640]{1,0:T(8,128)(2,1)S(1)} %get-tuple-element.109), channel_id=1, source_target_pairs={{0,3},{1,2},{2,1},{3,0},{4,7},{5,6},{6,5},{7,4},{8,11},{9,10},{10,... | collective-permute-start | bytes 245768 | tf_op jit(solution)/shard_map/ppermute | solution.py:47
  31.6 1.6 %collective-permute-start.8 = (bf16[128,640]{1,0:T(8,128)(2,1)S(1)}, bf16[128,640]{1,0:T(8,128)(2,1)S(1)}, u32[]{:S(2)}, u32[]{:S(2)}) collective-permute-start(bf16[128,640]{1,0:T(8,128)(2,1)S(1)} %get-tuple-element.107), channel_id=1, source_target_pairs={{0,1},{1,0},{2,3},{3,2},{4,5},{5,4},{6,7},{7,6},{8,9},{9,8},{10,11... | collective-permute-start | bytes 491528 | tf_op jit(solution)/shard_map/ppermute | solution.py:47
  33.8 5.7 %attend_mid.1 = (f32[1024,1]{1,0:T(8,128)S(1)}, f32[1024,1]{1,0:T(8,128)S(1)}, f32[1024,512]{1,0:T(8,128)S(1)}, f32[8,128]{1,0:T(8,128)S(1)}) custom-call(s32[128,4]{1,0:T(8,128)S(1)} %copy-done.11, s32[1,1280]{1,0:T(1,128)S(1)} %copy-done.17, bf16[1024,640]{1,0:T(8,128)(2,1)S(1)} %get-tuple-element.93.wide_ref, f32[1024,1]{1,0:T(8,128)S(1)} %get-tuple-element.95.best_ref, ...), custom_call_target="tpu_custom_call" | custom-call | flops 2852126720 | bytes 8000000 | tf_op jit(solution)/shard_map/attend_mid/pallas_call | solution.py:367
  40.2 1.2 collective-permute-done.13.refs_5_
  41.4 4.9 %attend_far.1 = (f32[64,2048]{1,0:T(8,128)S(1)}, bf16[64,2048]{1,0:T(8,128)(2,1)S(1)}) custom-call(s32[128,4]{1,0:T(8,128)S(1)} %copy-done.11, s32[1,640]{1,0:T(1,128)S(1)} %copy-done.14, bf16[1024,640]{1,0:T(8,128)(2,1)S(1)} %get-tuple-element.93.wide_ref, f32[1024,1]{1,0:T(8,128)S(1)} %get-tuple-element.103.best_ref, ...), custom_call_target="tpu_custom_call" | custom-call | flops 1426063360 | bytes 8000000 | tf_op jit(solution)/shard_map/attend_far/pallas_call | solution.py:367
  46.9 1.0 collective-permute-done.14.refs_2_
  48.6 1.5 %collective-permute-start.15 = (bf16[64,2048]{1,0:T(8,128)(2,1)S(1)}, bf16[64,2048]{1,0:T(8,128)(2,1)S(1)}, u32[]{:S(2)}, u32[]{:S(2)}) collective-permute-start(bf16[64,2048]{1,0:T(8,128)(2,1)S(1)} %get-tuple-element.118), channel_id=1, source_target_pairs={{0,4},{1,5},{2,6},{3,7},{4,12},{5,13},{6,14},{7,15},{8,0},{9,1},{1... | collective-permute-start | bytes 786440 | tf_op jit(solution)/shard_map/ppermute | solution.py:37
  50.6 1.5 %collective-permute-start.17 = (bf16[32,2048]{1,0:T(8,128)(2,1)S(1)}, bf16[32,2048]{1,0:T(8,128)(2,1)S(1)}, u32[]{:S(2)}, u32[]{:S(2)}) collective-permute-start(bf16[32,2048]{1,0:T(8,128)(2,1)S(1)} %get-tuple-element.121), channel_id=1, source_target_pairs={{0,2},{1,3},{2,0},{3,1},{4,6},{5,7},{6,4},{7,5},{8,10},{9,11},{10,... | collective-permute-start | bytes 393224 | tf_op jit(solution)/shard_map/ppermute | solution.py:47
  52.1 1.4 %collective-permute-start.18 = (bf16[32,2048]{1,0:T(8,128)(2,1)S(1)}, bf16[32,2048]{1,0:T(8,128)(2,1)S(1)}, u32[]{:S(2)}, u32[]{:S(2)}) collective-permute-start(bf16[32,2048]{1,0:T(8,128)(2,1)S(1)} %get-tuple-element.122), channel_id=1, source_target_pairs={{0,3},{1,2},{2,1},{3,0},{4,7},{5,6},{6,5},{7,4},{8,11},{9,10},{10,... | collective-permute-start | bytes 393224 | tf_op jit(solution)/shard_map/ppermute | solution.py:47
  53.5 2.9 %collective-permute-done.16.refs_4_ = bf16[32,2048]{1,0:T(8,128)(2,1)S(1)} collective-permute-done((bf16[32,2048]{1,0:T(8,128)(2,1)S(1)}, bf16[32,2048]{1,0:T(8,128)(2,1)S(1)}, u32[]{:S(2)}, u32[]{:S(2)}) %collective-permute-start.16) | collective-permute-done | bytes 131104 | tf_op jit(solution)/shard_map/ppermute | solution.py:47
  56.4 1.1 collective-permute-done.17.refs_5_
  57.5 1.6 %collective-permute-done.18.refs_6_ = bf16[32,2048]{1,0:T(8,128)(2,1)S(1)} collective-permute-done((bf16[32,2048]{1,0:T(8,128)(2,1)S(1)}, bf16[32,2048]{1,0:T(8,128)(2,1)S(1)}, u32[]{:S(2)}, u32[]{:S(2)}) %collective-permute-start.18) | collective-permute-done | bytes 131104 | tf_op jit(solution)/shard_map/ppermute | solution.py:47
  59.8 1.9 %collective-permute-start.20 = (bf16[64,2048]{1,0:T(8,128)(2,1)S(1)}, bf16[64,2048]{1,0:T(8,128)(2,1)S(1)}, u32[]{:S(2)}, u32[]{:S(2)}) collective-permute-start(bf16[64,2048]{1,0:T(8,128)(2,1)S(1)} %collective-permute-done.15.refs_0_), channel_id=1, source_target_pairs={{0,4},{1,5},{2,6},{3,7},{4,12},{5,13},{6,14},{7,15},{8,0},{9,1},{1... | collective-permute-start | bytes 786440 | tf_op jit(solution)/shard_map/ppermute | solution.py:37
  62.5 1.5 %collective-permute-start.22 = (bf16[32,2048]{1,0:T(8,128)(2,1)S(1)}, bf16[32,2048]{1,0:T(8,128)(2,1)S(1)}, u32[]{:S(2)}, u32[]{:S(2)}) collective-permute-start(bf16[32,2048]{1,0:T(8,128)(2,1)S(1)} %get-tuple-element.127), channel_id=1, source_target_pairs={{0,2},{1,3},{2,0},{3,1},{4,6},{5,7},{6,4},{7,5},{8,10},{9,11},{10,... | collective-permute-start | bytes 393224 | tf_op jit(solution)/shard_map/ppermute | solution.py:47
  64.1 1.2 collective-permute-start.23
  65.3 2.7 %experts.4 = (f32[128,2048]{1,0:T(8,128)S(1)}, bf16[128,2048]{1,0:T(8,128)(2,1)S(1)}, f32[8,128]{1,0:T(8,128)S(1)}) custom-call(bf16[128,2048]{1,0:T(8,128)(2,1)S(1)} %get-tuple-element.123.refs_0_, bf16[128,2048]{1,0:T(8,128)(2,1)S(1)} %collective-permute-done.19.refs_1_, bf16[704,2048]{1,0:T(8,128)(2,1)S(1)} %bitcast.15, bf16[704,2048]{1,0:T(8,128)(2,1)S(1)} %bitcast.19, ...), custom_call_target="tpu_custom_call" | custom-call | flops 2214592512 | bytes 11276288 | tf_op jit(solution)/shard_map/experts/pallas_call | solution.py:111
  68.1 2.5 %collective-permute-done.22.refs_6_ = bf16[32,2048]{1,0:T(8,128)(2,1)S(1)} collective-permute-done((bf16[32,2048]{1,0:T(8,128)(2,1)S(1)}, bf16[32,2048]{1,0:T(8,128)(2,1)S(1)}, u32[]{:S(2)}, u32[]{:S(2)}) %collective-permute-start.22) | collective-permute-done | bytes 131104 | tf_op jit(solution)/shard_map/ppermute | solution.py:47
  71.3 2.0 %collective-permute-start.25 = (bf16[64,2048]{1,0:T(8,128)(2,1)S(1)}, bf16[64,2048]{1,0:T(8,128)(2,1)S(1)}, u32[]{:S(2)}, u32[]{:S(2)}) collective-permute-start(bf16[64,2048]{1,0:T(8,128)(2,1)S(1)} %collective-permute-done.20.refs_1_), channel_id=1, source_target_pairs={{0,4},{1,5},{2,6},{3,7},{4,12},{5,13},{6,14},{7,15},{8,0},{9,1},{1... | collective-permute-start | bytes 786440 | tf_op jit(solution)/shard_map/ppermute | solution.py:37
  73.3 1.2 collective-permute-start.26
  74.5 0.8 collective-permute-start.27
  75.3 1.4 %collective-permute-start.28 = (bf16[32,2048]{1,0:T(8,128)(2,1)S(1)}, bf16[32,2048]{1,0:T(8,128)(2,1)S(1)}, u32[]{:S(2)}, u32[]{:S(2)}) collective-permute-start(bf16[32,2048]{1,0:T(8,128)(2,1)S(1)} %get-tuple-element.134), channel_id=1, source_target_pairs={{0,3},{1,2},{2,1},{3,0},{4,7},{5,6},{6,5},{7,4},{8,11},{9,10},{10,... | collective-permute-start | bytes 393224 | tf_op jit(solution)/shard_map/ppermute | solution.py:47
  76.8 2.7 %experts.5 = (f32[128,2048]{1,0:T(8,128)S(1)}, bf16[128,2048]{1,0:T(8,128)(2,1)S(1)}, f32[8,128]{1,0:T(8,128)S(1)}) custom-call(bf16[128,2048]{1,0:T(8,128)(2,1)S(1)} %get-tuple-element.129.refs_0_, bf16[128,2048]{1,0:T(8,128)(2,1)S(1)} %collective-permute-done.24.refs_1_, bf16[704,2048]{1,0:T(8,128)(2,1)S(1)} %bitcast.16, bf16[704,2048]{1,0:T(8,128)(2,1)S(1)} %bitcast.20, ...), custom_call_target="tpu_custom_call" | custom-call | flops 2214592512 | bytes 11276288 | tf_op jit(solution)/shard_map/experts/pallas_call | solution.py:111
  79.4 1.4 %collective-permute-done.25.refs_3_.refs_1_ = bf16[64,2048]{1,0:T(8,128)(2,1)S(1)} collective-permute-done((bf16[64,2048]{1,0:T(8,128)(2,1)S(1)}, bf16[64,2048]{1,0:T(8,128)(2,1)S(1)}, u32[]{:S(2)}, u32[]{:S(2)}) %collective-permute-start.25) | collective-permute-done | bytes 262176 | tf_op jit(solution)/shard_map/ppermute | solution.py:37
  81.0 1.6 %collective-permute-done.28.refs_2_.refs_9_ = bf16[32,2048]{1,0:T(8,128)(2,1)S(1)} collective-permute-done((bf16[32,2048]{1,0:T(8,128)(2,1)S(1)}, bf16[32,2048]{1,0:T(8,128)(2,1)S(1)}, u32[]{:S(2)}, u32[]{:S(2)}) %collective-permute-start.28) | collective-permute-done | bytes 131104 | tf_op jit(solution)/shard_map/ppermute | solution.py:47
  82.6 1.9 %collective-permute-done.29.refs_5_ = bf16[128,2048]{1,0:T(8,128)(2,1)S(1)} collective-permute-done((bf16[128,2048]{1,0:T(8,128)(2,1)S(1)}, bf16[128,2048]{1,0:T(8,128)(2,1)S(1)}, u32[]{:S(2)}, u32[]{:S(2)}) %collective-permute-start.29) | collective-permute-done | bytes 524320 | tf_op jit(solution)/shard_map/ppermute | solution.py:57
  85.5 0.8 collective-permute-start.31
  86.3 1.5 %collective-permute-start.32 = (bf16[64,2048]{1,0:T(8,128)(2,1)S(1)}, bf16[64,2048]{1,0:T(8,128)(2,1)S(1)}, u32[]{:S(2)}, u32[]{:S(2)}) collective-permute-start(bf16[64,2048]{1,0:T(8,128)(2,1)S(1)} %get-tuple-element.143), channel_id=1, source_target_pairs={{0,2},{1,3},{2,0},{3,1},{4,6},{5,7},{6,4},{7,5},{8,10},{9,11},{10,... | collective-permute-start | bytes 786440 | tf_op jit(solution)/shard_map/ppermute | solution.py:47
  87.8 1.2 collective-permute-start.33
  89.0 2.7 %experts.6 = (f32[128,2048]{1,0:T(8,128)S(1)}, bf16[128,2048]{1,0:T(8,128)(2,1)S(1)}, f32[8,128]{1,0:T(8,128)S(1)}) custom-call(bf16[128,2048]{1,0:T(8,128)(2,1)S(1)} %get-tuple-element.139.refs_0_, bf16[128,2048]{1,0:T(8,128)(2,1)S(1)} %collective-permute-done.30.refs_1_, bf16[704,2048]{1,0:T(8,128)(2,1)S(1)} %bitcast.17, bf16[704,2048]{1,0:T(8,128)(2,1)S(1)} %bitcast.21, ...), custom_call_target="tpu_custom_call" | custom-call | flops 2214592512 | bytes 11276288 | tf_op jit(solution)/shard_map/experts/pallas_call | solution.py:111
  91.7 2.9 %collective-permute-done.31.refs_0_.refs_4_.refs_2_ = bf16[64,2048]{1,0:T(8,128)(2,1)S(1)} collective-permute-done((bf16[64,2048]{1,0:T(8,128)(2,1)S(1)}, bf16[64,2048]{1,0:T(8,128)(2,1)S(1)}, u32[]{:S(2)}, u32[]{:S(2)}) %collective-permute-start.31) | collective-permute-done | bytes 262176 | tf_op jit(solution)/shard_map/ppermute | solution.py:47
  94.6 5.6 %collective-permute-done.32.refs_1_.refs_5_.refs_3_ = bf16[64,2048]{1,0:T(8,128)(2,1)S(1)} collective-permute-done((bf16[64,2048]{1,0:T(8,128)(2,1)S(1)}, bf16[64,2048]{1,0:T(8,128)(2,1)S(1)}, u32[]{:S(2)}, u32[]{:S(2)}) %collective-permute-start.32) | collective-permute-done | bytes 262176 | tf_op jit(solution)/shard_map/ppermute | solution.py:47
  100.2 1.9 %collective-permute-done.34.refs_2_ = bf16[128,2048]{1,0:T(8,128)(2,1)S(1)} collective-permute-done((bf16[128,2048]{1,0:T(8,128)(2,1)S(1)}, bf16[128,2048]{1,0:T(8,128)(2,1)S(1)}, u32[]{:S(2)}, u32[]{:S(2)}) %collective-permute-start.34) | collective-permute-done | bytes 524320 | tf_op jit(solution)/shard_map/ppermute | solution.py:57
  102.7 0.9 collective-permute-start.38
  103.7 0.9 collective-permute-start.35
  104.6 1.4 collective-permute-start.36
  106.0 1.2 collective-permute-start.37
  107.2 3.1 %experts.7 = (f32[128,2048]{1,0:T(8,128)S(1)}, bf16[128,2048]{1,0:T(8,128)(2,1)S(1)}, f32[8,128]{1,0:T(8,128)}) custom-call(bf16[128,2048]{1,0:T(8,128)(2,1)S(1)} %get-tuple-element.152.refs_0_, bf16[128,2048]{1,0:T(8,128)(2,1)S(1)} %collective-permute-done.39.refs_1_, bf16[704,2048]{1,0:T(8,128)(2,1)S(1)} %bitcast.18, bf16[704,2048]{1,0:T(8,128)(2,1)S(1)} %bitcast.22, ...), custom_call_target="tpu_custom_call" | custom-call | flops 2214592512 | bytes 11276288 | tf_op jit(solution)/shard_map/experts/pallas_call | solution.py:111
  110.3 2.2 %collective-permute-done.38.refs_5_.refs_3_ = bf16[64,2048]{1,0:T(8,128)(2,1)S(1)} collective-permute-done((bf16[64,2048]{1,0:T(8,128)(2,1)S(1)}, bf16[64,2048]{1,0:T(8,128)(2,1)S(1)}, u32[]{:S(2)}, u32[]{:S(2)}) %collective-permute-start.38) | collective-permute-done | bytes 262176 | tf_op jit(solution)/shard_map/ppermute | solution.py:37
  113.4 0.8 collective-permute-start.44
  114.7 1.2 collective-permute-start.41
  115.9 1.1 collective-permute-start.42
  117.0 1.2 collective-permute-start.43
  118.2 4.4 %collective-permute-done.44.refs_5_ = bf16[64,2048]{1,0:T(8,128)(2,1)S(1)} collective-permute-done((bf16[64,2048]{1,0:T(8,128)(2,1)S(1)}, bf16[64,2048]{1,0:T(8,128)(2,1)S(1)}, u32[]{:S(2)}, u32[]{:S(2)}) %collective-permute-start.44) | collective-permute-done | bytes 262176 | tf_op jit(solution)/shard_map/ppermute | solution.py:37
  122.7 1.3 collective-permute-done.43.refs_4_
  124.2 0.9 collective-permute-start.49
  125.3 1.3 collective-permute-start.46
  126.6 0.8 collective-permute-start.47
  127.4 1.4 %collective-permute-start.48 = (bf16[32,2048]{1,0:T(8,128)(2,1)S(1)}, bf16[32,2048]{1,0:T(8,128)(2,1)S(1)}, u32[]{:S(2)}, u32[]{:S(2)}) collective-permute-start(bf16[32,2048]{1,0:T(8,128)(2,1)S(1)} %get-tuple-element.164), channel_id=1, source_target_pairs={{0,3},{1,2},{2,1},{3,0},{4,7},{5,6},{6,5},{7,4},{8,11},{9,10},{10,... | collective-permute-start | bytes 393224 | tf_op jit(solution)/shard_map/ppermute | solution.py:47
  128.8 2.6 %collective-permute-done.46.refs_4_ = bf16[32,2048]{1,0:T(8,128)(2,1)S(1)} collective-permute-done((bf16[32,2048]{1,0:T(8,128)(2,1)S(1)}, bf16[32,2048]{1,0:T(8,128)(2,1)S(1)}, u32[]{:S(2)}, u32[]{:S(2)}) %collective-permute-start.46) | collective-permute-done | bytes 131104 | tf_op jit(solution)/shard_map/ppermute | solution.py:47
  131.7 1.6 %collective-permute-done.48.refs_6_ = bf16[32,2048]{1,0:T(8,128)(2,1)S(1)} collective-permute-done((bf16[32,2048]{1,0:T(8,128)(2,1)S(1)}, bf16[32,2048]{1,0:T(8,128)(2,1)S(1)}, u32[]{:S(2)}, u32[]{:S(2)}) %collective-permute-start.48) | collective-permute-done | bytes 131104 | tf_op jit(solution)/shard_map/ppermute | solution.py:47
  133.3 1.0 conclude.1
  134.2 1.5 %collective-permute-done.50.refs_4_ = bf16[64,2048]{1,0:T(8,128)(2,1)S(1)} collective-permute-done((bf16[64,2048]{1,0:T(8,128)(2,1)S(1)}, bf16[64,2048]{1,0:T(8,128)(2,1)S(1)}, u32[]{:S(2)}, u32[]{:S(2)}) %collective-permute-start.50) | collective-permute-done | bytes 262176 | tf_op jit(solution)/shard_map/ppermute | solution.py:57
  135.8 2.3 %project.1 = (bf16[128,1536]{1,0:T(8,128)(2,1)}, bf16[288,128]{1,0:T(8,128)(2,1)}) custom-call(bf16[128,128]{1,0:T(8,128)(2,1)S(1)} %copy-done.10, bf16[2048,1536]{1,0:T(8,128)(2,1)S(1)} %bitcast.28, bf16[288,2048]{1,0:T(8,128)(2,1)S(1)} %bitcast.29, bf16[64,2048]{1,0:T(8,128)(2,1)S(1)} %get-tuple-element.166.refs_3_, ...), custom_call_target="tpu_custom_call" | custom-call | flops 1000000000 | bytes 8495104 | tf_op jit(solution)/shard_map/project/pallas_call | solution.py:111
  (114 shorter events, 13.0 us)
Async XLA Ops:
  0.6 46.1 %copy-start = (bf16[128,2048]{1,0:T(8,128)(2,1)S(1)}, bf16[128,2048]{1,0:T(8,128)(2,1)}, u32[]{:S(2)}) copy-start(bf16[128,2048]{1,0:T(8,128)(2,1)} %param.23) | copy-start | bytes 1572868
  2.5 8.7 %collective-permute-start.1 = (bf16[64,640]{1,0:T(8,128)(2,1)}, bf16[64,640]{1,0:T(8,128)(2,1)S(1)}, u32[]{:S(2)}, u32[]{:S(2)}) collective-permute-start(bf16[64,640]{1,0:T(8,128)(2,1)} %get-tuple-element.91), channel_id=1, source_target_pairs={{0,8},{1,9},{2,10},{3,11},{4,12},{5,13},{6,14},{7,15},{8,0},{9,1},... | collective-permute-start | bytes 245768 | tf_op jit(solution)/shard_map/ppermute | solution.py:42
  6.5 4.9 %collective-permute-start.2 = (bf16[64,640]{1,0:T(8,128)(2,1)}, bf16[64,640]{1,0:T(8,128)(2,1)S(1)}, u32[]{:S(2)}, u32[]{:S(2)}) collective-permute-start(bf16[64,640]{1,0:T(8,128)(2,1)} %get-tuple-element.91), channel_id=1, source_target_pairs={{0,12},{1,13},{2,14},{3,15},{4,0},{5,1},{6,2},{7,3},{8,4},{9,5},{1... | collective-permute-start | bytes 245768 | tf_op jit(solution)/shard_map/ppermute | solution.py:42
  7.9 7.7 %collective-permute-start = (bf16[128,640]{1,0:T(8,128)(2,1)}, bf16[128,640]{1,0:T(8,128)(2,1)S(1)}, u32[]{:S(2)}, u32[]{:S(2)}) collective-permute-start(bf16[128,640]{1,0:T(8,128)(2,1)} %get-tuple-element.86.refs_0_.refs_1_), channel_id=1, source_target_pairs={{0,4},{1,5},{2,6},{3,7},{4,8},{5,9},{6,10},{7,11},{8,12},{9,13},{1... | collective-permute-start | bytes 491528 | tf_op jit(solution)/shard_map/ppermute | solution.py:42
  8.6 11.0 %copy-start.15 = (bf16[8,128,512]{2,1,0:T(8,128)(2,1)S(1)}, bf16[8,128,512]{2,1,0:T(8,128)(2,1)}, u32[]{:S(2)}) copy-start(bf16[8,128,512]{2,1,0:T(8,128)(2,1)} %key_up_ref.1) | copy-start | bytes 3145732
  8.6 11.0 %copy-start.16 = (bf16[128,1536]{1,0:T(8,128)(2,1)S(1)}, bf16[128,1536]{1,0:T(8,128)(2,1)}, u32[]{:S(2)}) copy-start(bf16[128,1536]{1,0:T(8,128)(2,1)} %query_ref.1) | copy-start | bytes 1179652
  16.4 3.2 %collective-permute-start.3 = (bf16[384,640]{1,0:T(8,128)(2,1)S(1)}, bf16[384,640]{1,0:T(8,128)(2,1)S(1)}, u32[]{:S(2)}, u32[]{:S(2)}) collective-permute-start(bf16[384,640]{1,0:T(8,128)(2,1)S(1)} %get-tuple-element.92.refs_0_), channel_id=1, source_target_pairs={{0,16},{16,0},{1,17},{17,1},{2,18},{18,2},{3,19},{19,3},{4,20},{20... | collective-permute-start | bytes 1474568 | tf_op jit(solution)/shard_map/ppermute | solution.py:57
  16.5 11.9 %collective-permute-start.4 = (bf16[320,640]{1,0:T(8,128)(2,1)S(1)}, bf16[320,640]{1,0:T(8,128)(2,1)S(1)}, u32[]{:S(2)}, u32[]{:S(2)}) collective-permute-start(bf16[320,640]{1,0:T(8,128)(2,1)S(1)} %get-tuple-element.99), channel_id=1, source_target_pairs={{0,1},{1,0},{2,3},{3,2},{4,5},{5,4},{6,7},{7,6},{8,9},{9,8},{10,11... | collective-permute-start | bytes 1228808 | tf_op jit(solution)/shard_map/ppermute | solution.py:47
  18.1 11.5 %collective-permute-start.5 = (bf16[320,640]{1,0:T(8,128)(2,1)S(1)}, bf16[320,640]{1,0:T(8,128)(2,1)S(1)}, u32[]{:S(2)}, u32[]{:S(2)}) collective-permute-start(bf16[320,640]{1,0:T(8,128)(2,1)S(1)} %get-tuple-element.100), channel_id=1, source_target_pairs={{0,2},{1,3},{2,0},{3,1},{4,6},{5,7},{6,4},{7,5},{8,10},{9,11},{10,... | collective-permute-start | bytes 1228808 | tf_op jit(solution)/shard_map/ppermute | solution.py:47
  21.9 11.8 %copy-start.17 = (s32[1,1280]{1,0:T(1,128)S(1)}, s32[1,1280]{1,0:T(1,128)}, u32[]{:S(2)}) copy-start(s32[1,1280]{1,0:T(1,128)} %get-tuple-element.94.spot_ref) | copy-start | bytes 15364
  29.6 4.1 %collective-permute-start.6 = (bf16[320,640]{1,0:T(8,128)(2,1)S(1)}, bf16[320,640]{1,0:T(8,128)(2,1)S(1)}, u32[]{:S(2)}, u32[]{:S(2)}) collective-permute-start(bf16[320,640]{1,0:T(8,128)(2,1)S(1)} %get-tuple-element.101.refs_0_.refs_1_), channel_id=1, source_target_pairs={{0,16},{16,0},{1,17},{17,1},{2,18},{18,2},{3,19},{19,3},{4,20},{20... | collective-permute-start | bytes 1228808 | tf_op jit(solution)/shard_map/ppermute | solution.py:57
  29.6 4.1 %collective-permute-start.7 = (bf16[320,640]{1,0:T(8,128)(2,1)S(1)}, bf16[320,640]{1,0:T(8,128)(2,1)S(1)}, u32[]{:S(2)}, u32[]{:S(2)}) collective-permute-start(bf16[320,640]{1,0:T(8,128)(2,1)S(1)} %get-tuple-element.102.refs_1_.refs_0_), channel_id=1, source_target_pairs={{0,16},{16,0},{1,17},{17,1},{2,18},{18,2},{3,19},{19,3},{4,20},{20... | collective-permute-start | bytes 1228808 | tf_op jit(solution)/shard_map/ppermute | solution.py:57
  30.1 9.4 %collective-permute-start.10 = (bf16[64,640]{1,0:T(8,128)(2,1)S(1)}, bf16[64,640]{1,0:T(8,128)(2,1)S(1)}, u32[]{:S(2)}, u32[]{:S(2)}) collective-permute-start(bf16[64,640]{1,0:T(8,128)(2,1)S(1)} %get-tuple-element.109), channel_id=1, source_target_pairs={{0,3},{1,2},{2,1},{3,0},{4,7},{5,6},{6,5},{7,4},{8,11},{9,10},{10,... | collective-permute-start | bytes 245768 | tf_op jit(solution)/shard_map/ppermute | solution.py:47
  31.6 7.9 %collective-permute-start.8 = (bf16[128,640]{1,0:T(8,128)(2,1)S(1)}, bf16[128,640]{1,0:T(8,128)(2,1)S(1)}, u32[]{:S(2)}, u32[]{:S(2)}) collective-permute-start(bf16[128,640]{1,0:T(8,128)(2,1)S(1)} %get-tuple-element.107), channel_id=1, source_target_pairs={{0,1},{1,0},{2,3},{3,2},{4,5},{5,4},{6,7},{7,6},{8,9},{9,8},{10,11... | collective-permute-start | bytes 491528 | tf_op jit(solution)/shard_map/ppermute | solution.py:47
  33.2 6.3 %collective-permute-start.9 = (bf16[128,640]{1,0:T(8,128)(2,1)S(1)}, bf16[128,640]{1,0:T(8,128)(2,1)S(1)}, u32[]{:S(2)}, u32[]{:S(2)}) collective-permute-start(bf16[128,640]{1,0:T(8,128)(2,1)S(1)} %get-tuple-element.108), channel_id=1, source_target_pairs={{0,2},{1,3},{2,0},{3,1},{4,6},{5,7},{6,4},{7,5},{8,10},{9,11},{10,... | collective-permute-start | bytes 491528 | tf_op jit(solution)/shard_map/ppermute | solution.py:47
  33.7 7.7 %copy-start.4 = (bf16[1024,2048]{1,0:T(8,128)(2,1)S(1)}, bf16[1024,2048]{1,0:T(8,128)(2,1)}, u32[]{:S(2)}) copy-start(bf16[1024,2048]{1,0:T(8,128)(2,1)} %output_ref.1) | copy-start | bytes 12582916
  33.7 7.7 %copy-start.6 = (bf16[8,512,128]{2,1,0:T(8,128)(2,1)S(1)}, bf16[8,512,128]{2,1,0:T(8,128)(2,1)}, u32[]{:S(2)}) copy-start(bf16[8,512,128]{2,1,0:T(8,128)(2,1)} %value_up_ref.1) | copy-start | bytes 3145732
  39.5 1.9 %collective-permute-start.11 = (bf16[128,640]{1,0:T(8,128)(2,1)S(1)}, bf16[128,640]{1,0:T(8,128)(2,1)S(1)}, u32[]{:S(2)}, u32[]{:S(2)}) collective-permute-start(bf16[128,640]{1,0:T(8,128)(2,1)S(1)} %get-tuple-element.110.refs_0_), channel_id=1, source_target_pairs={{0,16},{16,0},{1,17},{17,1},{2,18},{18,2},{3,19},{19,3},{4,20},{20... | collective-permute-start | bytes 491528 | tf_op jit(solution)/shard_map/ppermute | solution.py:57
  39.6 1.8 %collective-permute-start.12 = (bf16[128,640]{1,0:T(8,128)(2,1)S(1)}, bf16[128,640]{1,0:T(8,128)(2,1)S(1)}, u32[]{:S(2)}, u32[]{:S(2)}) collective-permute-start(bf16[128,640]{1,0:T(8,128)(2,1)S(1)} %get-tuple-element.111.refs_1_), channel_id=1, source_target_pairs={{0,16},{16,0},{1,17},{17,1},{2,18},{18,2},{3,19},{19,3},{4,20},{20... | collective-permute-start | bytes 491528 | tf_op jit(solution)/shard_map/ppermute | solution.py:57
  40.1 1.3 collective-permute-start.13
  46.4 1.6 %collective-permute-start.14 = (bf16[64,2048]{1,0:T(8,128)(2,1)S(1)}, bf16[64,2048]{1,0:T(8,128)(2,1)S(1)}, u32[]{:S(2)}, u32[]{:S(2)}) collective-permute-start(bf16[64,2048]{1,0:T(8,128)(2,1)S(1)} %get-tuple-element.114), channel_id=1, source_target_pairs={{0,16},{16,0},{1,17},{17,1},{2,18},{18,2},{3,19},{19,3},{4,20},{20... | collective-permute-start | bytes 786440 | tf_op jit(solution)/shard_map/ppermute | solution.py:57
  48.0 17.3 %copy-start.1 = (bf16[1,2048,704]{1,2,0:T(8,128)(2,1)S(1)}, bf16[1,2048,704]{1,2,0:T(8,128)(2,1)}, u32[]{:S(2)}) copy-start(bf16[1,2048,704]{1,2,0:T(8,128)(2,1)} %param.32) | copy-start | bytes 8650756
  48.0 17.3 %copy-start.2 = (bf16[1,2048,704]{1,2,0:T(8,128)(2,1)S(1)}, bf16[1,2048,704]{1,2,0:T(8,128)(2,1)}, u32[]{:S(2)}) copy-start(bf16[1,2048,704]{1,2,0:T(8,128)(2,1)} %param.33) | copy-start | bytes 8650756
  48.0 17.3 %copy-start.3 = (bf16[1,704,2048]{2,1,0:T(8,128)(2,1)S(1)}, bf16[1,704,2048]{2,1,0:T(8,128)(2,1)}, u32[]{:S(2)}) copy-start(bf16[1,704,2048]{2,1,0:T(8,128)(2,1)} %param.34) | copy-start | bytes 8650756
  48.6 10.6 %collective-permute-start.15 = (bf16[64,2048]{1,0:T(8,128)(2,1)S(1)}, bf16[64,2048]{1,0:T(8,128)(2,1)S(1)}, u32[]{:S(2)}, u32[]{:S(2)}) collective-permute-start(bf16[64,2048]{1,0:T(8,128)(2,1)S(1)} %get-tuple-element.118), channel_id=1, source_target_pairs={{0,4},{1,5},{2,6},{3,7},{4,12},{5,13},{6,14},{7,15},{8,0},{9,1},{1... | collective-permute-start | bytes 786440 | tf_op jit(solution)/shard_map/ppermute | solution.py:37
  50.0 6.4 %collective-permute-start.16 = (bf16[32,2048]{1,0:T(8,128)(2,1)S(1)}, bf16[32,2048]{1,0:T(8,128)(2,1)S(1)}, u32[]{:S(2)}, u32[]{:S(2)}) collective-permute-start(bf16[32,2048]{1,0:T(8,128)(2,1)S(1)} %get-tuple-element.120), channel_id=1, source_target_pairs={{0,1},{1,0},{2,3},{3,2},{4,5},{5,4},{6,7},{7,6},{8,9},{9,8},{10,11... | collective-permute-start | bytes 393224 | tf_op jit(solution)/shard_map/ppermute | solution.py:47
  50.6 6.9 %collective-permute-start.17 = (bf16[32,2048]{1,0:T(8,128)(2,1)S(1)}, bf16[32,2048]{1,0:T(8,128)(2,1)S(1)}, u32[]{:S(2)}, u32[]{:S(2)}) collective-permute-start(bf16[32,2048]{1,0:T(8,128)(2,1)S(1)} %get-tuple-element.121), channel_id=1, source_target_pairs={{0,2},{1,3},{2,0},{3,1},{4,6},{5,7},{6,4},{7,5},{8,10},{9,11},{10,... | collective-permute-start | bytes 393224 | tf_op jit(solution)/shard_map/ppermute | solution.py:47
  52.1 7.1 %collective-permute-start.18 = (bf16[32,2048]{1,0:T(8,128)(2,1)S(1)}, bf16[32,2048]{1,0:T(8,128)(2,1)S(1)}, u32[]{:S(2)}, u32[]{:S(2)}) collective-permute-start(bf16[32,2048]{1,0:T(8,128)(2,1)S(1)} %get-tuple-element.122), channel_id=1, source_target_pairs={{0,3},{1,2},{2,1},{3,0},{4,7},{5,6},{6,5},{7,4},{8,11},{9,10},{10,... | collective-permute-start | bytes 393224 | tf_op jit(solution)/shard_map/ppermute | solution.py:47
  59.7 5.5 %collective-permute-start.19 = (bf16[128,2048]{1,0:T(8,128)(2,1)S(1)}, bf16[128,2048]{1,0:T(8,128)(2,1)S(1)}, u32[]{:S(2)}, u32[]{:S(2)}) collective-permute-start(bf16[128,2048]{1,0:T(8,128)(2,1)S(1)} %get-tuple-element.123.refs_0_), channel_id=1, source_target_pairs={{0,16},{16,0},{1,17},{17,1},{2,18},{18,2},{3,19},{19,3},{4,20},{20... | collective-permute-start | bytes 1572872 | tf_op jit(solution)/shard_map/ppermute | solution.py:57
  59.8 10.8 %collective-permute-start.20 = (bf16[64,2048]{1,0:T(8,128)(2,1)S(1)}, bf16[64,2048]{1,0:T(8,128)(2,1)S(1)}, u32[]{:S(2)}, u32[]{:S(2)}) collective-permute-start(bf16[64,2048]{1,0:T(8,128)(2,1)S(1)} %collective-permute-done.15.refs_0_), channel_id=1, source_target_pairs={{0,4},{1,5},{2,6},{3,7},{4,12},{5,13},{6,14},{7,15},{8,0},{9,1},{1... | collective-permute-start | bytes 786440 | tf_op jit(solution)/shard_map/ppermute | solution.py:37
  61.7 6.3 %collective-permute-start.21 = (bf16[32,2048]{1,0:T(8,128)(2,1)S(1)}, bf16[32,2048]{1,0:T(8,128)(2,1)S(1)}, u32[]{:S(2)}, u32[]{:S(2)}) collective-permute-start(bf16[32,2048]{1,0:T(8,128)(2,1)S(1)} %get-tuple-element.126), channel_id=1, source_target_pairs={{0,1},{1,0},{2,3},{3,2},{4,5},{5,4},{6,7},{7,6},{8,9},{9,8},{10,11... | collective-permute-start | bytes 393224 | tf_op jit(solution)/shard_map/ppermute | solution.py:47
  62.5 8.1 %collective-permute-start.22 = (bf16[32,2048]{1,0:T(8,128)(2,1)S(1)}, bf16[32,2048]{1,0:T(8,128)(2,1)S(1)}, u32[]{:S(2)}, u32[]{:S(2)}) collective-permute-start(bf16[32,2048]{1,0:T(8,128)(2,1)S(1)} %get-tuple-element.127), channel_id=1, source_target_pairs={{0,2},{1,3},{2,0},{3,1},{4,6},{5,7},{6,4},{7,5},{8,10},{9,11},{10,... | collective-permute-start | bytes 393224 | tf_op jit(solution)/shard_map/ppermute | solution.py:47
  64.1 6.6 %collective-permute-start.23 = (bf16[32,2048]{1,0:T(8,128)(2,1)S(1)}, bf16[32,2048]{1,0:T(8,128)(2,1)S(1)}, u32[]{:S(2)}, u32[]{:S(2)}) collective-permute-start(bf16[32,2048]{1,0:T(8,128)(2,1)S(1)} %get-tuple-element.128), channel_id=1, source_target_pairs={{0,3},{1,2},{2,1},{3,0},{4,7},{5,6},{6,5},{7,4},{8,11},{9,10},{10,... | collective-permute-start | bytes 393224 | tf_op jit(solution)/shard_map/ppermute | solution.py:47
  71.2 5.6 %collective-permute-start.24 = (bf16[128,2048]{1,0:T(8,128)(2,1)S(1)}, bf16[128,2048]{1,0:T(8,128)(2,1)S(1)}, u32[]{:S(2)}, u32[]{:S(2)}) collective-permute-start(bf16[128,2048]{1,0:T(8,128)(2,1)S(1)} %get-tuple-element.129.refs_0_), channel_id=1, source_target_pairs={{0,16},{16,0},{1,17},{17,1},{2,18},{18,2},{3,19},{19,3},{4,20},{20... | collective-permute-start | bytes 1572872 | tf_op jit(solution)/shard_map/ppermute | solution.py:57
  71.3 9.6 %collective-permute-start.25 = (bf16[64,2048]{1,0:T(8,128)(2,1)S(1)}, bf16[64,2048]{1,0:T(8,128)(2,1)S(1)}, u32[]{:S(2)}, u32[]{:S(2)}) collective-permute-start(bf16[64,2048]{1,0:T(8,128)(2,1)S(1)} %collective-permute-done.20.refs_1_), channel_id=1, source_target_pairs={{0,4},{1,5},{2,6},{3,7},{4,12},{5,13},{6,14},{7,15},{8,0},{9,1},{1... | collective-permute-start | bytes 786440 | tf_op jit(solution)/shard_map/ppermute | solution.py:37
  73.3 7.6 %collective-permute-start.26 = (bf16[32,2048]{1,0:T(8,128)(2,1)S(1)}, bf16[32,2048]{1,0:T(8,128)(2,1)S(1)}, u32[]{:S(2)}, u32[]{:S(2)}) collective-permute-start(bf16[32,2048]{1,0:T(8,128)(2,1)S(1)} %get-tuple-element.132), channel_id=1, source_target_pairs={{0,1},{1,0},{2,3},{3,2},{4,5},{5,4},{6,7},{7,6},{8,9},{9,8},{10,11... | collective-permute-start | bytes 393224 | tf_op jit(solution)/shard_map/ppermute | solution.py:47
  74.5 6.5 %collective-permute-start.27 = (bf16[32,2048]{1,0:T(8,128)(2,1)S(1)}, bf16[32,2048]{1,0:T(8,128)(2,1)S(1)}, u32[]{:S(2)}, u32[]{:S(2)}) collective-permute-start(bf16[32,2048]{1,0:T(8,128)(2,1)S(1)} %get-tuple-element.133), channel_id=1, source_target_pairs={{0,2},{1,3},{2,0},{3,1},{4,6},{5,7},{6,4},{7,5},{8,10},{9,11},{10,... | collective-permute-start | bytes 393224 | tf_op jit(solution)/shard_map/ppermute | solution.py:47
  75.3 7.3 %collective-permute-start.28 = (bf16[32,2048]{1,0:T(8,128)(2,1)S(1)}, bf16[32,2048]{1,0:T(8,128)(2,1)S(1)}, u32[]{:S(2)}, u32[]{:S(2)}) collective-permute-start(bf16[32,2048]{1,0:T(8,128)(2,1)S(1)} %get-tuple-element.134), channel_id=1, source_target_pairs={{0,3},{1,2},{2,1},{3,0},{4,7},{5,6},{6,5},{7,4},{8,11},{9,10},{10,... | collective-permute-start | bytes 393224 | tf_op jit(solution)/shard_map/ppermute | solution.py:47
  82.6 1.9 %collective-permute-start.29 = (bf16[128,2048]{1,0:T(8,128)(2,1)S(1)}, bf16[128,2048]{1,0:T(8,128)(2,1)S(1)}, u32[]{:S(2)}, u32[]{:S(2)}) collective-permute-start(bf16[128,2048]{1,0:T(8,128)(2,1)S(1)} %pass_on.7), channel_id=1, source_target_pairs={{0,16},{16,0},{1,17},{17,1},{2,18},{18,2},{3,19},{19,3},{4,20},{20... | collective-permute-start | bytes 1572872 | tf_op jit(solution)/shard_map/ppermute | solution.py:57
  85.3 3.7 %collective-permute-start.30 = (bf16[128,2048]{1,0:T(8,128)(2,1)S(1)}, bf16[128,2048]{1,0:T(8,128)(2,1)S(1)}, u32[]{:S(2)}, u32[]{:S(2)}) collective-permute-start(bf16[128,2048]{1,0:T(8,128)(2,1)S(1)} %get-tuple-element.139.refs_0_), channel_id=1, source_target_pairs={{0,16},{16,0},{1,17},{17,1},{2,18},{18,2},{3,19},{19,3},{4,20},{20... | collective-permute-start | bytes 1572872 | tf_op jit(solution)/shard_map/ppermute | solution.py:57
  85.5 9.1 %collective-permute-start.31 = (bf16[64,2048]{1,0:T(8,128)(2,1)S(1)}, bf16[64,2048]{1,0:T(8,128)(2,1)S(1)}, u32[]{:S(2)}, u32[]{:S(2)}) collective-permute-start(bf16[64,2048]{1,0:T(8,128)(2,1)S(1)} %get-tuple-element.142), channel_id=1, source_target_pairs={{0,1},{1,0},{2,3},{3,2},{4,5},{5,4},{6,7},{7,6},{8,9},{9,8},{10,11... | collective-permute-start | bytes 786440 | tf_op jit(solution)/shard_map/ppermute | solution.py:47
  86.3 13.9 %collective-permute-start.32 = (bf16[64,2048]{1,0:T(8,128)(2,1)S(1)}, bf16[64,2048]{1,0:T(8,128)(2,1)S(1)}, u32[]{:S(2)}, u32[]{:S(2)}) collective-permute-start(bf16[64,2048]{1,0:T(8,128)(2,1)S(1)} %get-tuple-element.143), channel_id=1, source_target_pairs={{0,2},{1,3},{2,0},{3,1},{4,6},{5,7},{6,4},{7,5},{8,10},{9,11},{10,... | collective-permute-start | bytes 786440 | tf_op jit(solution)/shard_map/ppermute | solution.py:47
  87.8 12.4 %collective-permute-start.33 = (bf16[64,2048]{1,0:T(8,128)(2,1)S(1)}, bf16[64,2048]{1,0:T(8,128)(2,1)S(1)}, u32[]{:S(2)}, u32[]{:S(2)}) collective-permute-start(bf16[64,2048]{1,0:T(8,128)(2,1)S(1)} %get-tuple-element.144), channel_id=1, source_target_pairs={{0,3},{1,2},{2,1},{3,0},{4,7},{5,6},{6,5},{7,4},{8,11},{9,10},{10,... | collective-permute-start | bytes 786440 | tf_op jit(solution)/shard_map/ppermute | solution.py:47
  100.2 1.9 %collective-permute-start.34 = (bf16[128,2048]{1,0:T(8,128)(2,1)S(1)}, bf16[128,2048]{1,0:T(8,128)(2,1)S(1)}, u32[]{:S(2)}, u32[]{:S(2)}) collective-permute-start(bf16[128,2048]{1,0:T(8,128)(2,1)S(1)} %pass_on.8), channel_id=1, source_target_pairs={{0,16},{16,0},{1,17},{17,1},{2,18},{18,2},{3,19},{19,3},{4,20},{20... | collective-permute-start | bytes 1572872 | tf_op jit(solution)/shard_map/ppermute | solution.py:57
  102.3 4.9 %collective-permute-start.39 = (bf16[128,2048]{1,0:T(8,128)(2,1)S(1)}, bf16[128,2048]{1,0:T(8,128)(2,1)S(1)}, u32[]{:S(2)}, u32[]{:S(2)}) collective-permute-start(bf16[128,2048]{1,0:T(8,128)(2,1)S(1)} %get-tuple-element.152.refs_0_), channel_id=1, source_target_pairs={{0,16},{16,0},{1,17},{17,1},{2,18},{18,2},{3,19},{19,3},{4,20},{20... | collective-permute-start | bytes 1572872 | tf_op jit(solution)/shard_map/ppermute | solution.py:57
  102.7 9.8 %collective-permute-start.38 = (bf16[64,2048]{1,0:T(8,128)(2,1)S(1)}, bf16[64,2048]{1,0:T(8,128)(2,1)S(1)}, u32[]{:S(2)}, u32[]{:S(2)}) collective-permute-start(bf16[64,2048]{1,0:T(8,128)(2,1)S(1)} %collect.3), channel_id=1, source_target_pairs={{0,4},{1,5},{2,6},{3,7},{4,12},{5,13},{6,14},{7,15},{8,0},{9,1},{1... | collective-permute-start | bytes 786440 | tf_op jit(solution)/shard_map/ppermute | solution.py:37
  103.7 8.8 %collective-permute-start.35 = (bf16[32,2048]{1,0:T(8,128)(2,1)S(1)}, bf16[32,2048]{1,0:T(8,128)(2,1)S(1)}, u32[]{:S(2)}, u32[]{:S(2)}) collective-permute-start(bf16[32,2048]{1,0:T(8,128)(2,1)S(1)} %get-tuple-element.148), channel_id=1, source_target_pairs={{0,1},{1,0},{2,3},{3,2},{4,5},{5,4},{6,7},{7,6},{8,9},{9,8},{10,11... | collective-permute-start | bytes 393224 | tf_op jit(solution)/shard_map/ppermute | solution.py:47
  104.6 7.9 %collective-permute-start.36 = (bf16[32,2048]{1,0:T(8,128)(2,1)S(1)}, bf16[32,2048]{1,0:T(8,128)(2,1)S(1)}, u32[]{:S(2)}, u32[]{:S(2)}) collective-permute-start(bf16[32,2048]{1,0:T(8,128)(2,1)S(1)} %get-tuple-element.149), channel_id=1, source_target_pairs={{0,2},{1,3},{2,0},{3,1},{4,6},{5,7},{6,4},{7,5},{8,10},{9,11},{10,... | collective-permute-start | bytes 393224 | tf_op jit(solution)/shard_map/ppermute | solution.py:47
  106.0 29.8 %slice-start = ((s8[6291456]{0:T(1024)(128)(4,1)}), s8[4194304]{0:T(1024)(128)(4,1)S(1)}, s32[]{:S(2)}) async-start(s8[6291456]{0:T(1024)(128)(4,1)} %bitcast.27), calls=%async_computation | async-start | bytes 8388608
  106.0 29.8 %slice-start.1 = ((s8[6291456]{0:T(1024)(128)(4,1)}), s8[2097152]{0:T(1024)(128)(4,1)S(1)}, s32[]{:S(2)}) async-start(s8[6291456]{0:T(1024)(128)(4,1)} %bitcast.27), calls=%async_computation.1 | async-start | bytes 4194304
  106.0 6.6 %collective-permute-start.37 = (bf16[32,2048]{1,0:T(8,128)(2,1)S(1)}, bf16[32,2048]{1,0:T(8,128)(2,1)S(1)}, u32[]{:S(2)}, u32[]{:S(2)}) collective-permute-start(bf16[32,2048]{1,0:T(8,128)(2,1)S(1)} %get-tuple-element.150), channel_id=1, source_target_pairs={{0,3},{1,2},{2,1},{3,0},{4,7},{5,6},{6,5},{7,4},{8,11},{9,10},{10,... | collective-permute-start | bytes 393224 | tf_op jit(solution)/shard_map/ppermute | solution.py:47
  112.6 1.9 %collective-permute-start.40 = (bf16[128,2048]{1,0:T(8,128)(2,1)S(1)}, bf16[128,2048]{1,0:T(8,128)(2,1)S(1)}, u32[]{:S(2)}, u32[]{:S(2)}) collective-permute-start(bf16[128,2048]{1,0:T(8,128)(2,1)S(1)} %pass_on.9), channel_id=1, source_target_pairs={{0,16},{16,0},{1,17},{17,1},{2,18},{18,2},{3,19},{19,3},{4,20},{20... | collective-permute-start | bytes 1572872 | tf_op jit(solution)/shard_map/ppermute | solution.py:57
  112.7 12.5 %collective-permute-start.45 = (bf16[128,2048]{1,0:T(8,128)(2,1)S(1)}, bf16[128,2048]{1,0:T(8,128)(2,1)S(1)}, u32[]{:S(2)}, u32[]{:S(2)}) collective-permute-start(bf16[128,2048]{1,0:T(8,128)(2,1)S(1)} %get-tuple-element.160), channel_id=1, source_target_pairs={{0,16},{16,0},{1,17},{17,1},{2,18},{18,2},{3,19},{19,3},{4,20},{20... | collective-permute-start | bytes 1572872 | tf_op jit(solution)/shard_map/ppermute | solution.py:57
  113.2 15.7 %copy-start.19 = (bf16[2048]{0:T(1024)(128)(2,1)S(1)}, bf16[2048]{0:T(1024)(128)(2,1)}, u32[]{:S(2)}) copy-start(bf16[2048]{0:T(1024)(128)(2,1)} %param.35) | copy-start | bytes 12292
  113.4 9.2 %collective-permute-start.44 = (bf16[64,2048]{1,0:T(8,128)(2,1)S(1)}, bf16[64,2048]{1,0:T(8,128)(2,1)S(1)}, u32[]{:S(2)}, u32[]{:S(2)}) collective-permute-start(bf16[64,2048]{1,0:T(8,128)(2,1)S(1)} %collect.4.refs_0_), channel_id=1, source_target_pairs={{0,4},{1,5},{2,6},{3,7},{4,12},{5,13},{6,14},{7,15},{8,0},{9,1},{1... | collective-permute-start | bytes 786440 | tf_op jit(solution)/shard_map/ppermute | solution.py:37
  114.6 21.2 %copy-start.5 = (bf16[2048,288]{0,1:T(8,128)(2,1)S(1)}, bf16[2048,288]{0,1:T(8,128)(2,1)}, u32[]{:S(2)}) copy-start(bf16[2048,288]{0,1:T(8,128)(2,1)} %param.37) | copy-start | bytes 3538948
  114.7 8.0 %collective-permute-start.41 = (bf16[32,2048]{1,0:T(8,128)(2,1)S(1)}, bf16[32,2048]{1,0:T(8,128)(2,1)S(1)}, u32[]{:S(2)}, u32[]{:S(2)}) collective-permute-start(bf16[32,2048]{1,0:T(8,128)(2,1)S(1)} %get-tuple-element.156), channel_id=1, source_target_pairs={{0,1},{1,0},{2,3},{3,2},{4,5},{5,4},{6,7},{7,6},{8,9},{9,8},{10,11... | collective-permute-start | bytes 393224 | tf_op jit(solution)/shard_map/ppermute | solution.py:47
  115.9 6.8 %collective-permute-start.42 = (bf16[32,2048]{1,0:T(8,128)(2,1)S(1)}, bf16[32,2048]{1,0:T(8,128)(2,1)S(1)}, u32[]{:S(2)}, u32[]{:S(2)}) collective-permute-start(bf16[32,2048]{1,0:T(8,128)(2,1)S(1)} %get-tuple-element.157), channel_id=1, source_target_pairs={{0,2},{1,3},{2,0},{3,1},{4,6},{5,7},{6,4},{7,5},{8,10},{9,11},{10,... | collective-permute-start | bytes 393224 | tf_op jit(solution)/shard_map/ppermute | solution.py:47
  117.0 6.9 %collective-permute-start.43 = (bf16[32,2048]{1,0:T(8,128)(2,1)S(1)}, bf16[32,2048]{1,0:T(8,128)(2,1)S(1)}, u32[]{:S(2)}, u32[]{:S(2)}) collective-permute-start(bf16[32,2048]{1,0:T(8,128)(2,1)S(1)} %get-tuple-element.158), channel_id=1, source_target_pairs={{0,3},{1,2},{2,1},{3,0},{4,7},{5,6},{6,5},{7,4},{8,11},{9,10},{10,... | collective-permute-start | bytes 393224 | tf_op jit(solution)/shard_map/ppermute | solution.py:47
  124.2 9.0 %collective-permute-start.49 = (bf16[64,2048]{1,0:T(8,128)(2,1)S(1)}, bf16[64,2048]{1,0:T(8,128)(2,1)S(1)}, u32[]{:S(2)}, u32[]{:S(2)}) collective-permute-start(bf16[64,2048]{1,0:T(8,128)(2,1)S(1)} %collect.5.refs_0_), channel_id=1, source_target_pairs={{0,4},{1,5},{2,6},{3,7},{4,12},{5,13},{6,14},{7,15},{8,0},{9,1},{1... | collective-permute-start | bytes 786440 | tf_op jit(solution)/shard_map/ppermute | solution.py:37
  125.3 6.2 %collective-permute-start.46 = (bf16[32,2048]{1,0:T(8,128)(2,1)S(1)}, bf16[32,2048]{1,0:T(8,128)(2,1)S(1)}, u32[]{:S(2)}, u32[]{:S(2)}) collective-permute-start(bf16[32,2048]{1,0:T(8,128)(2,1)S(1)} %get-tuple-element.162), channel_id=1, source_target_pairs={{0,1},{1,0},{2,3},{3,2},{4,5},{5,4},{6,7},{7,6},{8,9},{9,8},{10,11... | collective-permute-start | bytes 393224 | tf_op jit(solution)/shard_map/ppermute | solution.py:47
  126.6 5.1 %collective-permute-start.47 = (bf16[32,2048]{1,0:T(8,128)(2,1)S(1)}, bf16[32,2048]{1,0:T(8,128)(2,1)S(1)}, u32[]{:S(2)}, u32[]{:S(2)}) collective-permute-start(bf16[32,2048]{1,0:T(8,128)(2,1)S(1)} %get-tuple-element.163), channel_id=1, source_target_pairs={{0,2},{1,3},{2,0},{3,1},{4,6},{5,7},{6,4},{7,5},{8,10},{9,11},{10,... | collective-permute-start | bytes 393224 | tf_op jit(solution)/shard_map/ppermute | solution.py:47
  127.4 5.9 %collective-permute-start.48 = (bf16[32,2048]{1,0:T(8,128)(2,1)S(1)}, bf16[32,2048]{1,0:T(8,128)(2,1)S(1)}, u32[]{:S(2)}, u32[]{:S(2)}) collective-permute-start(bf16[32,2048]{1,0:T(8,128)(2,1)S(1)} %get-tuple-element.164), channel_id=1, source_target_pairs={{0,3},{1,2},{2,1},{3,0},{4,7},{5,6},{6,5},{7,4},{8,11},{9,10},{10,... | collective-permute-start | bytes 393224 | tf_op jit(solution)/shard_map/ppermute | solution.py:47
  134.2 1.5 %collective-permute-start.50 = (bf16[64,2048]{1,0:T(8,128)(2,1)S(1)}, bf16[64,2048]{1,0:T(8,128)(2,1)S(1)}, u32[]{:S(2)}, u32[]{:S(2)}) collective-permute-start(bf16[64,2048]{1,0:T(8,128)(2,1)S(1)} %get-tuple-element.166.refs_3_), channel_id=1, source_target_pairs={{0,16},{16,0},{1,17},{17,1},{2,18},{18,2},{3,19},{19,3},{4,20},{20... | collective-permute-start | bytes 786440 | tf_op jit(solution)/shard_map/ppermute | solution.py:57
  (9 other events, 34.8 us)

commit v5 on v4

--- a/solution.py
+++ b/solution.py
@@ -168,9 +168,8 @@
         here = block_refs[0][rows:, :].astype(jnp.float32)
         before = block_refs[1][rows:, :].astype(jnp.float32)
         for d, far_ref in enumerate(far_refs):
-            if d < PLANE - 2:
-                for i, ref in enumerate(block_refs):
-                    far_ref[i * rows : (i + 1) * rows, :] = ref[:rows, :]
+            for i, ref in enumerate(block_refs):
+                far_ref[i * rows : (i + 1) * rows, :] = ref[:rows, :]
             later = plane_index < lax.bitwise_xor(plane_index, d + 1)
             part = jnp.where(later, here, before).astype(jnp.bfloat16)
             far_ref[far_ref.shape[0] - share :, :] = part
@@ -178,18 +177,20 @@
     dtype = blocks[0].dtype
     outputs = [((count * rows + 2 * share, WIDE), dtype)]
     outputs += [((count * rows + share, WIDE), dtype)] * (PLANE - 2)
-    outputs.append(((share, WIDE), dtype))
     outputs.append(((count, ROUTE_ROWS, WIDE - LAT), dtype))
     near, *far, routes = call(kernel, "join_column", blocks, outputs, 0, ready=ready)
     return near, far, routes
 
 
-def halves(by_y, by_x, rows):
+def halves(by_y, by_x, first, prefix):
+    share = by_y.shape[0] - prefix
+
     def kernel(by_y_ref, by_x_ref, first_ref, second_ref):
-        first_ref[...] = by_y_ref[:rows, :]
-        second_ref[...] = by_x_ref[rows : 2 * rows, :]
-
-    outputs = [((rows, WIDE), by_y.dtype)] * 2
+        first_ref[:first, :] = by_y_ref[:first, :]
+        first_ref[first:, :] = by_y_ref[prefix:, :]
+        second_ref[...] = by_x_ref[first:prefix, :]
+
+    outputs = [((first + share, WIDE), by_y.dtype), ((prefix - first, WIDE), by_y.dtype)]
     return call(kernel, "halves", [by_y, by_x], outputs, 0)
 
 
@@ -213,12 +214,12 @@
 LATER = 1 << 20
 
 
-def key_table(groups, sides):
-    rows = []
-    for j in range(groups):
-        for d, segments in sides:
-            for k, count, real, suffix in segments:
-                rows += [(j, d, k, r, suffix, r < real) for r in range(count)]
+def segment_rows(d, segments):
+    return [(d, k, r, s, r < real) for k, count, real, s in segments for r in range(count)]
+
+
+def key_table(groups, side):
+    rows = [(j, *row) for j in range(groups) for row in side]
     table = np.zeros((8, len(rows)), np.int32)
     table[:6] = np.array(rows, np.int32).T
     table[6] = table[3] // PAGE
@@ -226,15 +227,15 @@
     return table
 
 
-def make_plan(tables, lengths, tenants, tenant_lengths, page_table, ring, piece_rows, sizes, ready):
+def make_plan(table, counts, lengths, tenants, tenant_lengths, page_table, ring, piece_rows, sizes, ready):
     tok_slice, tok_quarter, groups = sizes
     requests = lengths.shape[0]
     tenant_count = tenant_lengths.shape[0]
     pages = page_table.shape[1]
     piece_pages = piece_rows // PAGE
 
-    def spots_of(table, page_row, group_index, ring_index, plane_index):
-        j, d, k, r, suffix, real, page_at, within = (table[i : i + 1, :] for i in range(8))
+    def spots_of(part, page_row, group_index, ring_index, plane_index):
+        j, d, k, r, suffix, real, page_at, within = (part[i : i + 1, :] for i in range(8))
         in_plane = lax.bitwise_xor(plane_index, d)
         k = jnp.where(suffix == 2, jnp.where(in_plane < plane_index, 0, 1), k)
         from_ring = ring_index - k
@@ -242,7 +243,7 @@
         of_group = lax.bitwise_xor(group_index, j)
         owner = (of_group * ring + from_ring) * PLANE + in_plane
         index = owner * piece_pages + page_at
-        count = table.shape[1]
+        count = part.shape[1]
         page = lax.broadcasted_iota(jnp.int32, (pages, count), 0)
         hit = jnp.where(page == index, 1.0, 0.0).astype(jnp.bfloat16)
         found = dot_f(page_row, hit)[:1].astype(jnp.int32)
@@ -250,19 +251,19 @@
         token = (from_ring * PLANE + in_plane) * tok_slice + of_group * tok_quarter + r
         return jnp.where(suffix > 0, token + LATER, logical)
 
-    def kernel(lengths_ref, tenants_ref, tenant_lengths_ref, page_ref, *refs):
-        table_refs = refs[: len(tables)]
-        info_ref, order_ref, *spot_refs = refs[len(tables) :]
+    def kernel(lengths_ref, tenants_ref, tenant_lengths_ref, page_ref, table_ref, *refs):
+        info_ref, order_ref, *spot_refs = refs
         group_index = jnp.full((1, 1), lax.axis_index("group"), jnp.int32)
         tensor_index = lax.axis_index("tensor")
         ring_index = jnp.full((1, 1), lax.div(tensor_index, PLANE), jnp.int32)
         plane_index = jnp.full((1, 1), lax.rem(tensor_index, PLANE), jnp.int32)
         page_row = page_ref[...].astype(jnp.float32).astype(jnp.bfloat16)
         page_row = jnp.broadcast_to(page_row, (16, pages))
-        for table_ref, spot_ref in zip(table_refs, spot_refs):
-            spot_ref[...] = spots_of(
-                table_ref[...], page_row, group_index, ring_index, plane_index
-            )
+        at = 0
+        for count, spot_ref in zip(counts, spot_refs):
+            part = table_ref[:, at : at + count]
+            spot_ref[...] = spots_of(part, page_row, group_index, ring_index, plane_index)
+            at += count
         row = lax.broadcasted_iota(jnp.int32, (tok_slice, 1), 0)
         share = jnp.zeros((tok_slice, 1), jnp.int32)
         for j in range(1, groups):
@@ -297,16 +298,15 @@
     shapes = [
         jax.ShapeDtypeStruct((tok_slice, 4), jnp.int32),
         jax.ShapeDtypeStruct((tok_slice, tok_slice), jnp.bfloat16),
-    ] + [jax.ShapeDtypeStruct((1, table.shape[1]), jnp.int32) for table in tables]
+    ] + [jax.ShapeDtypeStruct((1, count), jnp.int32) for count in counts]
     scalar = pl.BlockSpec(memory_space=pltpu.SMEM)
-    arrays = [page_table, *tables]
+    arrays = [page_table, table]
     return pl.pallas_call(
         after(kernel, len(ready)),
-        grid=(1,),
-        in_specs=unread(ready) + [scalar, scalar, scalar] + [whole(a) for a in arrays],
-        out_specs=[whole(shape) for shape in shapes],
+        in_specs=unread(ready) + [scalar, scalar, scalar] + resident(arrays),
+        out_specs=resident(shapes),
         out_shape=shapes,
-        compiler_params=pltpu.CompilerParams(vmem_limit_bytes=58 * 1024 * 1024),
+        compiler_params=pltpu.CompilerParams(vmem_limit_bytes=20 * 1024 * 1024),
         cost_estimate=pl.CostEstimate(
             flops=4_000_000_000, bytes_accessed=1_000_000, transcendentals=0
         ),
@@ -567,55 +567,52 @@
     return residual, normed, scaled, pieces
 
 
-def turn(step, block, arrived, results, routes, router, sizes, ready):
+def turn(step, block, arrived, routes, router, sizes, ready):
     ring, top, capacity = sizes
-    inputs = []
-    outputs = []
     width = arrived[0].shape[1]
-    rows = 0
+    inputs = [*arrived]
+    outputs = [((PLANE * capacity, width), jnp.bfloat16)]
     if block is not None:
         inputs += [block, routes, router]
         outputs.append(((PLANE * capacity, block.shape[0]), jnp.bfloat16))
-        rows += capacity
-    if results is not None:
-        inputs += results
-        rows += capacity
-    joining = step <= ring
-    if joining:
-        inputs += arrived
-        outputs.append(((PLANE * capacity, width), jnp.bfloat16))
-    count = len(inputs)
-    outputs += [((rows, width), jnp.bfloat16)] * PLANE
+        outputs += [((capacity, width), jnp.bfloat16)] * PLANE
 
     def kernel(*refs):
-        taken = list(refs[:count])
-        given = list(refs[count:])
-        outs = given[-PLANE:]
-        at = 0
+        row_refs = refs[:PLANE]
+        joined_ref = refs[len(inputs)]
+        for d, ref in enumerate(row_refs):
+            joined_ref[d * capacity : (d + 1) * capacity, :] = ref[:capacity, :]
         if block is not None:
-            block_ref, routes_ref, router_ref = taken[:3]
-            taken = taken[3:]
-            parts = [out.at[pl.ds(0, capacity), :] for out in outs]
-            values = block_ref[...]
-            pick_rows(step, ring, top, values, routes_ref, router_ref, given.pop(0), parts)
-            at = capacity
-        if results is not None:
-            total = taken[0][...]
-            for ref in taken[1 : len(results)]:
-                total = total + ref[...].astype(jnp.float32)
-            taken = taken[len(results) :]
-            total = total.astype(jnp.bfloat16)
-            for d, out in enumerate(outs):
-                out[at : at + capacity, :] = total[d * capacity : (d + 1) * capacity]
-        if joining:
-            joined_ref = given.pop(0)
-            for d, ref in enumerate(taken):
-                joined_ref[d * capacity : (d + 1) * capacity, :] = ref[:capacity, :]
-
-    found = list(call(kernel, "turn", inputs, outputs, 70_000_000, ready=ready))
-    scaled = found.pop(0) if block is not None else None
-    joined = found.pop(0) if joining else None
-    return scaled, joined, found
+            block_ref, routes_ref, router_ref = refs[PLANE : len(inputs)]
+            scaled_ref, *outs = refs[len(inputs) + 1 :]
+            pick_rows(
+                step, ring, top, block_ref[...], routes_ref, router_ref, scaled_ref, outs
+            )
+
+    joined, *found = call(kernel, "turn", inputs, outputs, 70_000_000, ready=ready)
+    if block is None:
+        return joined, None, []
+    return joined, found[0], found[1:]
+
+
+def blend(own, others, pieces, ready):
+    capacity = own.shape[0] // PLANE
+    first = pieces[0].shape[0] if pieces else 0
+    inputs = [own, *others, *pieces]
+
+    def kernel(*refs):
+        outs = refs[len(inputs) :]
+        total = refs[0][...]
+        for ref in refs[1 : 1 + len(others)]:
+            total = total + ref[...].astype(jnp.float32)
+        total = total.astype(jnp.bfloat16)
+        for d, out in enumerate(outs):
+            if pieces:
+                out[:first, :] = refs[1 + len(others) + d][...]
+            out[first:, :] = total[d * capacity : (d + 1) * capacity]
+
+    outputs = [((first + capacity, own.shape[1]), jnp.bfloat16)] * PLANE
+    return call(kernel, "blend", inputs, outputs, 1_000_000, ready=ready)
 
 
 def expert_apply(pieces, kept, gate_part, up_part, down_part):
@@ -749,14 +746,18 @@
         if k < 2:
             near_segments.append((k, tok_quarter, 0, 1))
     far_segments.append((0, tok_quarter, 0, 2))
+    prefix_rows = ring * piece_rows
+    first_rows = (prefix_rows - tok_quarter) // 2
+    diagonal = segment_rows(3, far_segments)
     sides = (
-        [(0, near_segments)],
-        [(1, far_segments), (2, far_segments)],
-        [(3, far_segments)],
-    )
-    tables = [jnp.asarray(key_table(groups, side)) for side in sides]
+        segment_rows(0, near_segments),
+        segment_rows(1, far_segments) + segment_rows(2, far_segments),
+        diagonal[:first_rows] + diagonal[prefix_rows:] + diagonal[first_rows:prefix_rows],
+    )
+    tables = [key_table(groups, side) for side in sides]
     tokens_info, permutation, near_spots, mid_spots, far_spots = make_plan(
-        tables,
+        jnp.asarray(np.concatenate(tables, axis=1)),
+        [part.shape[1] for part in tables],
         suffix_lengths,
         request_tenant,
         tenant_lengths,
@@ -770,19 +771,19 @@
     column, plane, routes_ring = join_column(
         [full, *along], piece_rows, tok_quarter, [near_spots]
     )
-    plane = send_pieces([column, *plane])[1:]
+    plane = [send_plane(part, d + 1) for d, part in enumerate(plane)]
     near_blocks = [send_group(column, j) if j else column for j in range(groups)]
 
     *near, near_flag = attend_near(
         tokens_info, near_spots, permutation, queries, key_up, near_blocks
     )
-    beside = pass_on(plane[:2], [near_flag])
-    first, second = halves(beside[1], beside[0], ring * piece_rows // 2)
+    beside = pass_on(plane, [near_flag])
+    first, second = halves(beside[1], beside[0], first_rows, prefix_rows)
     across = [send_plane(first, 1), send_plane(second, 2)]
     mid_blocks = [send_group(block, j) if j else block for j in range(groups) for block in beside]
     *mid, mid_flag = attend_mid(tokens_info, mid_spots, near, mid_blocks)
     near = [near[0], *mid]
-    across = pass_on([*across, plane[2]], [mid_flag])
+    across = pass_on(across, [mid_flag])
     far_blocks = [send_group(block, j) if j else block for j in range(groups) for block in across]
     attend_own, attend_other = attend_far(
         tokens_info, far_spots, near, value_up, output_weight, far_blocks, tok_quarter
@@ -825,32 +826,31 @@
                 running = send_ring(total, ring)
             else:
                 break
+        payload = []
         back = step - 2 if step - 2 < ring else 0
-        given = None
         if step >= 3:
             own, other, _ = results[back]
             if back:
                 along_z = [block] if step <= ring - 1 else [landed] if step > 4 else []
                 other = pass_on([other], arrived[1:] + along_z)[0]
-            given = [own] + [
+            others = [
                 send_group(other[(j - 1) * kept : j * kept], j) for j in range(1, groups)
             ]
-        ready = [results[step - 2][2]] if 2 <= step <= ring else []
-        scaled, joined, payload = turn(
-            step,
-            block if step <= ring - 1 else None,
-            arrived,
-            given,
-            routes_ring,
-            experts_columns,
-            sizes,
-            ready if step <= ring else [total],
-        )
-        if scaled is not None:
+        if step <= ring:
+            joined, scaled, payload = turn(
+                step,
+                block if step <= ring - 1 else None,
+                arrived,
+                routes_ring,
+                experts_columns,
+                sizes,
+                [results[step - 2][2]] if step >= 2 else [],
+            )
             scales.append(scaled)
-        if joined is not None:
             rows = [send_group(joined, j) if j else joined for j in range(groups)]
             results.append(expert_apply(rows, kept, gate_part, up_part, down_part))
+        if step >= 3:
+            payload = blend(own, others, payload, [] if back else [total])
     layer_rows, normed_next = conclude(
         scales[0], arrived, running, residual, next_gain[None, :]
     )

time: 138 us -> 134 us (0.971)
  waiting for transfers between devices: 49.3 us -> 45.4 us
  local copies, waits for them, and re-layouts: 3.04 us -> 4.56 us
    ppermute x3, waiting for transfers between devices: 4.99 us -> 1.47 us  [send_round(): lax.ppermute(block, 'tensor', [(i, (i + distance) % count) for i in range...]
    ppermute x26 -> x25, waiting for transfers between devices: 28.3 us -> 31.2 us  [send_plane(): return lax.ppermute(block, 'tensor', [(i, i ^ distance) for i in devices])]
    ppermute x16 -> x15, waiting for transfers between devices: 7.96 us -> 5.36 us  [send_group(): return lax.ppermute(block, 'group', [(i, i ^ distance) for i in devices])]
    unnamed x44 -> x40, local copies, waits for them, and re-layouts: 3.02 us -> 4.54 us
    ppermute x26 -> x25, starting transfers between devices: 31.2 us -> 29.9 us  [send_plane(): return lax.ppermute(block, 'tensor', [(i, i ^ distance) for i in devices])]
    ppermute x16 -> x15, starting transfers between devices: 2.58 us -> 3.22 us  [send_group(): return lax.ppermute(block, 'group', [(i, i ^ distance) for i in devices])]
    pallas_call x19 -> x21, Pallas kernels: 19.9 us -> 19.7 us  [call(): pl.pallas_call(after(kernel, len(ready)), **places, out_shape=shapes, com...]
  transfers between devices with their start and end apart: 51 -> 49, of which waited for: 28 -> 25; matrix products, arithmetic and copies ran while one was open for 0% -> 0% of each run, Pallas kernels for 17% -> 18%
where the time goes in v5:
time: 134 us
  starting transfers between devices  47.1 us (35%)
  waiting for transfers between devices  45.4 us (34%)
  Pallas kernels  35.4 us (26%)
  local copies, waits for them, and re-layouts  4.56 us (3%)
    ppermute x25, waiting for transfers between devices, send_plane(): return lax.ppermute(block, 'tensor', [(i, i ^ distance) for i in devices])  31.2 us
    ppermute x25, starting transfers between devices, send_plane(): return lax.ppermute(block, 'tensor', [(i, i ^ distance) for i in devices])  29.9 us
    pallas_call x21, Pallas kernels, call(): pl.pallas_call(after(kernel, len(ready)), **places, out_shape=shapes, com...  19.7 us
    pallas_call x3, Pallas kernels, attend_call(): pl.pallas_call(kernel, in_specs=resident(inputs), out_specs=resident(shap...  14.6 us
    ppermute x6, starting transfers between devices, send_ring(): return lax.ppermute(block, 'tensor', route)  7.96 us
    ppermute x6, waiting for transfers between devices, send_ring(): return lax.ppermute(block, 'tensor', route)  7.42 us
    ppermute x3, starting transfers between devices, send_round(): lax.ppermute(block, 'tensor', [(i, (i + distance) % count) for i in range...  6.06 us
    ppermute x15, waiting for transfers between devices, send_group(): return lax.ppermute(block, 'group', [(i, i ^ distance) for i in devices])  5.36 us
  transfers between devices with their start and end apart: 49, of which 25 were waited for; matrix products, arithmetic and copies ran while one was open for 0% of the time, Pallas kernels for 18%

profile of v5, /device:TPU:0, one launch (start us, length us, event | category | flops | bytes accessed | tf_op | source)
XLA Modules:
  0.0 133.7 jit_solution(12397499113789224589)
XLA Ops:
  0.6 1.9 %join_share.1 = (bf16[128,640]{1,0:T(8,128)(2,1)}, bf16[64,640]{1,0:T(8,128)(2,1)}) custom-call(bf16[64,576]{1,0:T(8,128)(2,1)} %refs_0_.1, bf16[576,128]{1,0:T(8,128)(2,1)} %bitcast.35, s32[6,2,64]{2,1,0:T(2,128)} %bitcast.36), custom_call_target="tpu_custom_call" | custom-call | flops 10000000 | bytes 470016 | tf_op jit(solution)/shard_map/join_share/pallas_call | solution.py:111
  2.5 4.0 %collective-permute-start.1 = (bf16[64,640]{1,0:T(8,128)(2,1)}, bf16[64,640]{1,0:T(8,128)(2,1)S(1)}, u32[]{:S(2)}, u32[]{:S(2)}) collective-permute-start(bf16[64,640]{1,0:T(8,128)(2,1)} %get-tuple-element.92), channel_id=1, source_target_pairs={{0,8},{1,9},{2,10},{3,11},{4,12},{5,13},{6,14},{7,15},{8,0},{9,1},... | collective-permute-start | bytes 245768 | tf_op jit(solution)/shard_map/ppermute | solution.py:42
  6.5 1.3 %collective-permute-start.2 = (bf16[64,640]{1,0:T(8,128)(2,1)}, bf16[64,640]{1,0:T(8,128)(2,1)S(1)}, u32[]{:S(2)}, u32[]{:S(2)}) collective-permute-start(bf16[64,640]{1,0:T(8,128)(2,1)} %get-tuple-element.92), channel_id=1, source_target_pairs={{0,12},{1,13},{2,14},{3,15},{4,0},{5,1},{6,2},{7,3},{8,4},{9,5},{1... | collective-permute-start | bytes 245768 | tf_op jit(solution)/shard_map/ppermute | solution.py:42
  7.9 0.7 collective-permute-start
  8.6 0.9 copy-done.8
  9.5 0.7 copy-done.11
  12.2 0.9 copy-done.15
  13.1 1.1 make_plan.1
  14.2 1.5 %collective-permute-done.refs_2_ = bf16[128,640]{1,0:T(8,128)(2,1)S(1)} collective-permute-done((bf16[128,640]{1,0:T(8,128)(2,1)}, bf16[128,640]{1,0:T(8,128)(2,1)S(1)}, u32[]{:S(2)}, u32[]{:S(2)}) %collective-permute-start) | collective-permute-done | bytes 163872 | tf_op jit(solution)/shard_map/ppermute | solution.py:42
  15.8 1.6 %collective-permute-start.4 = (bf16[320,640]{1,0:T(8,128)(2,1)S(1)}, bf16[320,640]{1,0:T(8,128)(2,1)S(1)}, u32[]{:S(2)}, u32[]{:S(2)}) collective-permute-start(bf16[320,640]{1,0:T(8,128)(2,1)S(1)} %get-tuple-element.100), channel_id=1, source_target_pairs={{0,1},{1,0},{2,3},{3,2},{4,5},{5,4},{6,7},{7,6},{8,9},{9,8},{10,11... | collective-permute-start | bytes 1228808 | tf_op jit(solution)/shard_map/ppermute | solution.py:47
  17.4 1.5 %collective-permute-start.5 = (bf16[320,640]{1,0:T(8,128)(2,1)S(1)}, bf16[320,640]{1,0:T(8,128)(2,1)S(1)}, u32[]{:S(2)}, u32[]{:S(2)}) collective-permute-start(bf16[320,640]{1,0:T(8,128)(2,1)S(1)} %get-tuple-element.101), channel_id=1, source_target_pairs={{0,2},{1,3},{2,0},{3,1},{4,6},{5,7},{6,4},{7,5},{8,10},{9,11},{10,... | collective-permute-start | bytes 1228808 | tf_op jit(solution)/shard_map/ppermute | solution.py:47
  18.9 4.0 %attend_near.1 = (bf16[1024,640]{1,0:T(8,128)(2,1)S(1)}, f32[1024,1]{1,0:T(8,128)S(1)}, f32[1024,1]{1,0:T(8,128)S(1)}, f32[1024,512]{1,0:T(8,128)S(1)}, f32[8,128]{1,0:T(8,128)S(1)}) custom-call(s32[128,4]{1,0:T(8,128)S(1)} %get-tuple-element.89.token_ref, s32[1,768]{1,0:T(1,128)S(1)} %get-tuple-element.91.refs_0_.spot_ref, ...), custom_call_target="tpu_custom_call" | custom-call | flops 1711276032 | bytes 8000000 | tf_op jit(solution)/shard_map/attend_near/pallas_call | solution.py:367
  22.9 4.8 %collective-permute-done.4.refs_1_ = bf16[320,640]{1,0:T(8,128)(2,1)S(1)} collective-permute-done((bf16[320,640]{1,0:T(8,128)(2,1)S(1)}, bf16[320,640]{1,0:T(8,128)(2,1)S(1)}, u32[]{:S(2)}, u32[]{:S(2)}) %collective-permute-start.4) | collective-permute-done | bytes 409632 | tf_op jit(solution)/shard_map/ppermute | solution.py:47
  27.7 1.2 collective-permute-done.5.refs_2_
  30.1 1.5 %collective-permute-start.9 = (bf16[160,640]{1,0:T(8,128)(2,1)S(1)}, bf16[160,640]{1,0:T(8,128)(2,1)S(1)}, u32[]{:S(2)}, u32[]{:S(2)}) collective-permute-start(bf16[160,640]{1,0:T(8,128)(2,1)S(1)} %get-tuple-element.109), channel_id=1, source_target_pairs={{0,2},{1,3},{2,0},{3,1},{4,6},{5,7},{6,4},{7,5},{8,10},{9,11},{10,... | collective-permute-start | bytes 614408 | tf_op jit(solution)/shard_map/ppermute | solution.py:47
  31.6 5.7 %attend_mid.1 = (f32[1024,1]{1,0:T(8,128)S(1)}, f32[1024,1]{1,0:T(8,128)S(1)}, f32[1024,512]{1,0:T(8,128)S(1)}, f32[8,128]{1,0:T(8,128)S(1)}) custom-call(s32[128,4]{1,0:T(8,128)S(1)} %get-tuple-element.89.token_ref, s32[1,1280]{1,0:T(1,128)S(1)} %get-tuple-element.95.spot_ref, bf16[1024,640]{1,0:T(8,128)(2,1)S(1)} %get-tuple-element.94.wide_ref, ...), custom_call_target="tpu_custom_call" | custom-call | flops 2852126720 | bytes 8000000 | tf_op jit(solution)/shard_map/attend_mid/pallas_call | solution.py:367
  38.0 0.9 collective-permute-done.10.refs_2_
  39.2 4.9 %attend_far.1 = (f32[64,2048]{1,0:T(8,128)S(1)}, bf16[64,2048]{1,0:T(8,128)(2,1)S(1)}) custom-call(s32[128,4]{1,0:T(8,128)S(1)} %get-tuple-element.89.token_ref, s32[1,640]{1,0:T(1,128)S(1)} %get-tuple-element.90.spot_ref, bf16[1024,640]{1,0:T(8,128)(2,1)S(1)} %get-tuple-element.94.wide_ref, f32[1024,1]{1,0:T(8,128)S(1)} %get-tuple-element.104.best_ref, ...), custom_call_target="tpu_custom_call" | custom-call | flops 1426063360 | bytes 8000000 | tf_op jit(solution)/shard_map/attend_far/pallas_call | solution.py:367
  44.7 1.1 collective-permute-done.12.refs_2_
  46.3 1.5 %collective-permute-start.16 = (bf16[64,2048]{1,0:T(8,128)(2,1)S(1)}, bf16[64,2048]{1,0:T(8,128)(2,1)S(1)}, u32[]{:S(2)}, u32[]{:S(2)}) collective-permute-start(bf16[64,2048]{1,0:T(8,128)(2,1)S(1)} %get-tuple-element.121), channel_id=1, source_target_pairs={{0,4},{1,5},{2,6},{3,7},{4,12},{5,13},{6,14},{7,15},{8,0},{9,1},{1... | collective-permute-start | bytes 786440 | tf_op jit(solution)/shard_map/ppermute | solution.py:37
  47.8 1.5 %collective-permute-start.13 = (bf16[32,2048]{1,0:T(8,128)(2,1)S(1)}, bf16[32,2048]{1,0:T(8,128)(2,1)S(1)}, u32[]{:S(2)}, u32[]{:S(2)}) collective-permute-start(bf16[32,2048]{1,0:T(8,128)(2,1)S(1)} %get-tuple-element.118), channel_id=1, source_target_pairs={{0,1},{1,0},{2,3},{3,2},{4,5},{5,4},{6,7},{7,6},{8,9},{9,8},{10,11... | collective-permute-start | bytes 393224 | tf_op jit(solution)/shard_map/ppermute | solution.py:47
  49.3 0.8 collective-permute-start.14
  50.1 1.2 collective-permute-start.15
  51.3 2.2 %collective-permute-done.13.refs_1_ = bf16[32,2048]{1,0:T(8,128)(2,1)S(1)} collective-permute-done((bf16[32,2048]{1,0:T(8,128)(2,1)S(1)}, bf16[32,2048]{1,0:T(8,128)(2,1)S(1)}, u32[]{:S(2)}, u32[]{:S(2)}) %collective-permute-start.13) | collective-permute-done | bytes 131104 | tf_op jit(solution)/shard_map/ppermute | solution.py:47
  53.5 3.7 %collective-permute-done.14.refs_2_ = bf16[32,2048]{1,0:T(8,128)(2,1)S(1)} collective-permute-done((bf16[32,2048]{1,0:T(8,128)(2,1)S(1)}, bf16[32,2048]{1,0:T(8,128)(2,1)S(1)}, u32[]{:S(2)}, u32[]{:S(2)}) %collective-permute-start.14) | collective-permute-done | bytes 131104 | tf_op jit(solution)/shard_map/ppermute | solution.py:47
  57.8 1.9 %collective-permute-start.21 = (bf16[64,2048]{1,0:T(8,128)(2,1)S(1)}, bf16[64,2048]{1,0:T(8,128)(2,1)S(1)}, u32[]{:S(2)}, u32[]{:S(2)}) collective-permute-start(bf16[64,2048]{1,0:T(8,128)(2,1)S(1)} %collective-permute-done.16.refs_4_), channel_id=1, source_target_pairs={{0,4},{1,5},{2,6},{3,7},{4,12},{5,13},{6,14},{7,15},{8,0},{9,1},{1... | collective-permute-start | bytes 786440 | tf_op jit(solution)/shard_map/ppermute | solution.py:37
  60.3 1.2 collective-permute-start.19
  61.5 1.7 %collective-permute-start.20 = (bf16[32,2048]{1,0:T(8,128)(2,1)S(1)}, bf16[32,2048]{1,0:T(8,128)(2,1)S(1)}, u32[]{:S(2)}, u32[]{:S(2)}) collective-permute-start(bf16[32,2048]{1,0:T(8,128)(2,1)S(1)} %get-tuple-element.127), channel_id=1, source_target_pairs={{0,3},{1,2},{2,1},{3,0},{4,7},{5,6},{6,5},{7,4},{8,11},{9,10},{10,... | collective-permute-start | bytes 393224 | tf_op jit(solution)/shard_map/ppermute | solution.py:47
  63.3 2.6 %experts.4 = (f32[128,2048]{1,0:T(8,128)S(1)}, bf16[128,2048]{1,0:T(8,128)(2,1)S(1)}, f32[8,128]{1,0:T(8,128)S(1)}) custom-call(bf16[128,2048]{1,0:T(8,128)(2,1)S(1)} %get-tuple-element.122.refs_0_, bf16[128,2048]{1,0:T(8,128)(2,1)S(1)} %collective-permute-done.17.refs_1_, bf16[704,2048]{1,0:T(8,128)(2,1)S(1)} %bitcast.15, bf16[704,2048]{1,0:T(8,128)(2,1)S(1)} %bitcast.19, ...), custom_call_target="tpu_custom_call" | custom-call | flops 2214592512 | bytes 11276288 | tf_op jit(solution)/shard_map/experts/pallas_call | solution.py:111
  66.4 2.0 %collective-permute-done.20.refs_4_ = bf16[32,2048]{1,0:T(8,128)(2,1)S(1)} collective-permute-done((bf16[32,2048]{1,0:T(8,128)(2,1)S(1)}, bf16[32,2048]{1,0:T(8,128)(2,1)S(1)}, u32[]{:S(2)}, u32[]{:S(2)}) %collective-permute-start.20) | collective-permute-done | bytes 131104 | tf_op jit(solution)/shard_map/ppermute | solution.py:47
  69.0 2.0 %collective-permute-start.26 = (bf16[64,2048]{1,0:T(8,128)(2,1)S(1)}, bf16[64,2048]{1,0:T(8,128)(2,1)S(1)}, u32[]{:S(2)}, u32[]{:S(2)}) collective-permute-start(bf16[64,2048]{1,0:T(8,128)(2,1)S(1)} %collective-permute-done.21.refs_5_), channel_id=1, source_target_pairs={{0,4},{1,5},{2,6},{3,7},{4,12},{5,13},{6,14},{7,15},{8,0},{9,1},{1... | collective-permute-start | bytes 786440 | tf_op jit(solution)/shard_map/ppermute | solution.py:37
  71.0 1.5 %collective-permute-start.23 = (bf16[32,2048]{1,0:T(8,128)(2,1)S(1)}, bf16[32,2048]{1,0:T(8,128)(2,1)S(1)}, u32[]{:S(2)}, u32[]{:S(2)}) collective-permute-start(bf16[32,2048]{1,0:T(8,128)(2,1)S(1)} %get-tuple-element.131), channel_id=1, source_target_pairs={{0,1},{1,0},{2,3},{3,2},{4,5},{5,4},{6,7},{7,6},{8,9},{9,8},{10,11... | collective-permute-start | bytes 393224 | tf_op jit(solution)/shard_map/ppermute | solution.py:47
  72.5 0.8 collective-permute-start.24
  73.4 1.2 collective-permute-start.25
  74.5 2.6 %experts.5 = (f32[128,2048]{1,0:T(8,128)S(1)}, bf16[128,2048]{1,0:T(8,128)(2,1)S(1)}, f32[8,128]{1,0:T(8,128)S(1)}) custom-call(bf16[128,2048]{1,0:T(8,128)(2,1)S(1)} %get-tuple-element.128.refs_0_, bf16[128,2048]{1,0:T(8,128)(2,1)S(1)} %collective-permute-done.22.refs_1_, bf16[704,2048]{1,0:T(8,128)(2,1)S(1)} %bitcast.16, bf16[704,2048]{1,0:T(8,128)(2,1)S(1)} %bitcast.20, ...), custom_call_target="tpu_custom_call" | custom-call | flops 2214592512 | bytes 11276288 | tf_op jit(solution)/shard_map/experts/pallas_call | solution.py:111
  77.2 1.5 %collective-permute-done.26.refs_5_.refs_3_ = bf16[64,2048]{1,0:T(8,128)(2,1)S(1)} collective-permute-done((bf16[64,2048]{1,0:T(8,128)(2,1)S(1)}, bf16[64,2048]{1,0:T(8,128)(2,1)S(1)}, u32[]{:S(2)}, u32[]{:S(2)}) %collective-permute-start.26) | collective-permute-done | bytes 262176 | tf_op jit(solution)/shard_map/ppermute | solution.py:37
  78.7 2.0 %collective-permute-done.24.refs_3_.refs_1_ = bf16[32,2048]{1,0:T(8,128)(2,1)S(1)} collective-permute-done((bf16[32,2048]{1,0:T(8,128)(2,1)S(1)}, bf16[32,2048]{1,0:T(8,128)(2,1)S(1)}, u32[]{:S(2)}, u32[]{:S(2)}) %collective-permute-start.24) | collective-permute-done | bytes 131104 | tf_op jit(solution)/shard_map/ppermute | solution.py:47
  81.8 0.8 collective-permute-done.28.refs_1_
  83.3 1.2 collective-permute-start.30
  84.5 1.8 %collective-permute-start.31 = (bf16[64,2048]{1,0:T(8,128)(2,1)S(1)}, bf16[64,2048]{1,0:T(8,128)(2,1)S(1)}, u32[]{:S(2)}, u32[]{:S(2)}) collective-permute-start(bf16[64,2048]{1,0:T(8,128)(2,1)S(1)} %get-tuple-element.146), channel_id=1, source_target_pairs={{0,3},{1,2},{2,1},{3,0},{4,7},{5,6},{6,5},{7,4},{8,11},{9,10},{10,... | collective-permute-start | bytes 786440 | tf_op jit(solution)/shard_map/ppermute | solution.py:47
  86.2 2.6 %experts.6 = (f32[128,2048]{1,0:T(8,128)S(1)}, bf16[128,2048]{1,0:T(8,128)(2,1)S(1)}, f32[8,128]{1,0:T(8,128)S(1)}) custom-call(bf16[128,2048]{1,0:T(8,128)(2,1)S(1)} %get-tuple-element.135.refs_0_, bf16[128,2048]{1,0:T(8,128)(2,1)S(1)} %collective-permute-done.27.refs_1_, bf16[704,2048]{1,0:T(8,128)(2,1)S(1)} %bitcast.17, bf16[704,2048]{1,0:T(8,128)(2,1)S(1)} %bitcast.21, ...), custom_call_target="tpu_custom_call" | custom-call | flops 2214592512 | bytes 11276288 | tf_op jit(solution)/shard_map/experts/pallas_call | solution.py:111
  88.9 3.0 %collective-permute-done.29.refs_2_.refs_0_ = bf16[64,2048]{1,0:T(8,128)(2,1)S(1)} collective-permute-done((bf16[64,2048]{1,0:T(8,128)(2,1)S(1)}, bf16[64,2048]{1,0:T(8,128)(2,1)S(1)}, u32[]{:S(2)}, u32[]{:S(2)}) %collective-permute-start.29) | collective-permute-done | bytes 262176 | tf_op jit(solution)/shard_map/ppermute | solution.py:47
  92.1 4.8 %collective-permute-done.31.refs_4_.refs_2_ = bf16[64,2048]{1,0:T(8,128)(2,1)S(1)} collective-permute-done((bf16[64,2048]{1,0:T(8,128)(2,1)S(1)}, bf16[64,2048]{1,0:T(8,128)(2,1)S(1)}, u32[]{:S(2)}, u32[]{:S(2)}) %collective-permute-start.31) | collective-permute-done | bytes 262176 | tf_op jit(solution)/shard_map/ppermute | solution.py:47
  97.8 1.2 collective-permute-start.37
  99.1 1.4 %collective-permute-start.34 = (bf16[32,2048]{1,0:T(8,128)(2,1)S(1)}, bf16[32,2048]{1,0:T(8,128)(2,1)S(1)}, u32[]{:S(2)}, u32[]{:S(2)}) collective-permute-start(bf16[32,2048]{1,0:T(8,128)(2,1)S(1)} %get-tuple-element.150), channel_id=1, source_target_pairs={{0,1},{1,0},{2,3},{3,2},{4,5},{5,4},{6,7},{7,6},{8,9},{9,8},{10,11... | collective-permute-start | bytes 393224 | tf_op jit(solution)/shard_map/ppermute | solution.py:47
  100.5 0.8 collective-permute-start.35
  101.3 1.3 collective-permute-start.36
  102.7 3.1 %experts.7 = (f32[128,2048]{1,0:T(8,128)S(1)}, bf16[128,2048]{1,0:T(8,128)(2,1)S(1)}, f32[8,128]{1,0:T(8,128)}) custom-call(bf16[128,2048]{1,0:T(8,128)(2,1)S(1)} %turn.7.refs_0_, bf16[128,2048]{1,0:T(8,128)(2,1)S(1)} %collective-permute-done.32.refs_1_, bf16[704,2048]{1,0:T(8,128)(2,1)S(1)} %bitcast.18, bf16[704,2048]{1,0:T(8,128)(2,1)S(1)} %bitcast.22, ...), custom_call_target="tpu_custom_call" | custom-call | flops 2214592512 | bytes 11276288 | tf_op jit(solution)/shard_map/experts/pallas_call | solution.py:111
  105.7 1.5 %collective-permute-done.37.refs_3_.refs_5_ = bf16[64,2048]{1,0:T(8,128)(2,1)S(1)} collective-permute-done((bf16[64,2048]{1,0:T(8,128)(2,1)S(1)}, bf16[64,2048]{1,0:T(8,128)(2,1)S(1)}, u32[]{:S(2)}, u32[]{:S(2)}) %collective-permute-start.37) | collective-permute-done | bytes 262176 | tf_op jit(solution)/shard_map/ppermute | solution.py:37
  107.2 1.3 %collective-permute-done.35.refs_1_.refs_3_ = bf16[32,2048]{1,0:T(8,128)(2,1)S(1)} collective-permute-done((bf16[32,2048]{1,0:T(8,128)(2,1)S(1)}, bf16[32,2048]{1,0:T(8,128)(2,1)S(1)}, u32[]{:S(2)}, u32[]{:S(2)}) %collective-permute-start.35) | collective-permute-done | bytes 131104 | tf_op jit(solution)/shard_map/ppermute | solution.py:47
  109.8 0.7 collective-permute-done.38.refs_1_
  111.2 1.2 collective-permute-start.40
  112.4 1.8 %collective-permute-start.41 = (bf16[32,2048]{1,0:T(8,128)(2,1)S(1)}, bf16[32,2048]{1,0:T(8,128)(2,1)S(1)}, u32[]{:S(2)}, u32[]{:S(2)}) collective-permute-start(bf16[32,2048]{1,0:T(8,128)(2,1)S(1)} %get-tuple-element.158), channel_id=1, source_target_pairs={{0,3},{1,2},{2,1},{3,0},{4,7},{5,6},{6,5},{7,4},{8,11},{9,10},{10,... | collective-permute-start | bytes 393224 | tf_op jit(solution)/shard_map/ppermute | solution.py:47
  114.1 4.5 %collective-permute-done.42.refs_5_ = bf16[64,2048]{1,0:T(8,128)(2,1)S(1)} collective-permute-done((bf16[64,2048]{1,0:T(8,128)(2,1)S(1)}, bf16[64,2048]{1,0:T(8,128)(2,1)S(1)}, u32[]{:S(2)}, u32[]{:S(2)}) %collective-permute-start.42) | collective-permute-done | bytes 262176 | tf_op jit(solution)/shard_map/ppermute | solution.py:37
  118.6 0.7 collective-permute-done.41.refs_4_
  119.5 1.0 collective-permute-start.47
  120.6 1.2 collective-permute-start.44
  121.7 0.9 collective-permute-start.45
  122.6 1.5 %collective-permute-start.46 = (bf16[32,2048]{1,0:T(8,128)(2,1)S(1)}, bf16[32,2048]{1,0:T(8,128)(2,1)S(1)}, u32[]{:S(2)}, u32[]{:S(2)}) collective-permute-start(bf16[32,2048]{1,0:T(8,128)(2,1)S(1)} %get-tuple-element.166), channel_id=1, source_target_pairs={{0,3},{1,2},{2,1},{3,0},{4,7},{5,6},{6,5},{7,4},{8,11},{9,10},{10,... | collective-permute-start | bytes 393224 | tf_op jit(solution)/shard_map/ppermute | solution.py:47
  124.1 2.2 %collective-permute-done.44.refs_4_ = bf16[32,2048]{1,0:T(8,128)(2,1)S(1)} collective-permute-done((bf16[32,2048]{1,0:T(8,128)(2,1)S(1)}, bf16[32,2048]{1,0:T(8,128)(2,1)S(1)}, u32[]{:S(2)}, u32[]{:S(2)}) %collective-permute-start.44) | collective-permute-done | bytes 131104 | tf_op jit(solution)/shard_map/ppermute | solution.py:47
  126.4 2.5 %collective-permute-done.45.refs_5_ = bf16[32,2048]{1,0:T(8,128)(2,1)S(1)} collective-permute-done((bf16[32,2048]{1,0:T(8,128)(2,1)S(1)}, bf16[32,2048]{1,0:T(8,128)(2,1)S(1)}, u32[]{:S(2)}, u32[]{:S(2)}) %collective-permute-start.45) | collective-permute-done | bytes 131104 | tf_op jit(solution)/shard_map/ppermute | solution.py:47
  128.9 1.0 conclude.1
  129.8 1.5 %collective-permute-done.48.refs_4_ = bf16[64,2048]{1,0:T(8,128)(2,1)S(1)} collective-permute-done((bf16[64,2048]{1,0:T(8,128)(2,1)S(1)}, bf16[64,2048]{1,0:T(8,128)(2,1)S(1)}, u32[]{:S(2)}, u32[]{:S(2)}) %collective-permute-start.48) | collective-permute-done | bytes 262176 | tf_op jit(solution)/shard_map/ppermute | solution.py:57
  131.4 2.3 %project.1 = (bf16[128,1536]{1,0:T(8,128)(2,1)}, bf16[288,128]{1,0:T(8,128)(2,1)}) custom-call(bf16[128,128]{1,0:T(8,128)(2,1)S(1)} %get-tuple-element.88.order_ref.refs_0_, bf16[2048,1536]{1,0:T(8,128)(2,1)S(1)} %bitcast.28, bf16[288,2048]{1,0:T(8,128)(2,1)S(1)} %bitcast.29, bf16[64,2048]{1,0:T(8,128)(2,1)S(1)} %get-tuple-element.168.refs_3_, ...), custom_call_target="tpu_custom_call" | custom-call | flops 1000000000 | bytes 8495104 | tf_op jit(solution)/shard_map/project/pallas_call | solution.py:111
  (108 shorter events, 12.9 us)
Async XLA Ops:
  0.6 43.8 %copy-start = (bf16[128,2048]{1,0:T(8,128)(2,1)S(1)}, bf16[128,2048]{1,0:T(8,128)(2,1)}, u32[]{:S(2)}) copy-start(bf16[128,2048]{1,0:T(8,128)(2,1)} %param.21) | copy-start | bytes 1572868
  2.5 11.6 %collective-permute-start.1 = (bf16[64,640]{1,0:T(8,128)(2,1)}, bf16[64,640]{1,0:T(8,128)(2,1)S(1)}, u32[]{:S(2)}, u32[]{:S(2)}) collective-permute-start(bf16[64,640]{1,0:T(8,128)(2,1)} %get-tuple-element.92), channel_id=1, source_target_pairs={{0,8},{1,9},{2,10},{3,11},{4,12},{5,13},{6,14},{7,15},{8,0},{9,1},... | collective-permute-start | bytes 245768 | tf_op jit(solution)/shard_map/ppermute | solution.py:42
  6.5 7.6 %collective-permute-start.2 = (bf16[64,640]{1,0:T(8,128)(2,1)}, bf16[64,640]{1,0:T(8,128)(2,1)S(1)}, u32[]{:S(2)}, u32[]{:S(2)}) collective-permute-start(bf16[64,640]{1,0:T(8,128)(2,1)} %get-tuple-element.92), channel_id=1, source_target_pairs={{0,12},{1,13},{2,14},{3,15},{4,0},{5,1},{6,2},{7,3},{8,4},{9,5},{1... | collective-permute-start | bytes 245768 | tf_op jit(solution)/shard_map/ppermute | solution.py:42
  7.9 7.7 %collective-permute-start = (bf16[128,640]{1,0:T(8,128)(2,1)}, bf16[128,640]{1,0:T(8,128)(2,1)S(1)}, u32[]{:S(2)}, u32[]{:S(2)}) collective-permute-start(bf16[128,640]{1,0:T(8,128)(2,1)} %get-tuple-element.87.refs_0_.refs_1_), channel_id=1, source_target_pairs={{0,4},{1,5},{2,6},{3,7},{4,8},{5,9},{6,10},{7,11},{8,12},{9,13},{1... | collective-permute-start | bytes 491528 | tf_op jit(solution)/shard_map/ppermute | solution.py:42
  8.6 0.9 copy-start.8
  13.1 5.8 %copy-start.9 = (bf16[8,128,512]{2,1,0:T(8,128)(2,1)S(1)}, bf16[8,128,512]{2,1,0:T(8,128)(2,1)}, u32[]{:S(2)}) copy-start(bf16[8,128,512]{2,1,0:T(8,128)(2,1)} %key_up_ref.1) | copy-start | bytes 3145732
  13.1 5.8 %copy-start.10 = (bf16[128,1536]{1,0:T(8,128)(2,1)S(1)}, bf16[128,1536]{1,0:T(8,128)(2,1)}, u32[]{:S(2)}) copy-start(bf16[128,1536]{1,0:T(8,128)(2,1)} %query_ref.1) | copy-start | bytes 1179652
  15.8 3.2 %collective-permute-start.3 = (bf16[384,640]{1,0:T(8,128)(2,1)S(1)}, bf16[384,640]{1,0:T(8,128)(2,1)S(1)}, u32[]{:S(2)}, u32[]{:S(2)}) collective-permute-start(bf16[384,640]{1,0:T(8,128)(2,1)S(1)} %get-tuple-element.93.refs_0_), channel_id=1, source_target_pairs={{0,16},{16,0},{1,17},{17,1},{2,18},{18,2},{3,19},{19,3},{4,20},{20... | collective-permute-start | bytes 1474568 | tf_op jit(solution)/shard_map/ppermute | solution.py:57
  15.8 11.9 %collective-permute-start.4 = (bf16[320,640]{1,0:T(8,128)(2,1)S(1)}, bf16[320,640]{1,0:T(8,128)(2,1)S(1)}, u32[]{:S(2)}, u32[]{:S(2)}) collective-permute-start(bf16[320,640]{1,0:T(8,128)(2,1)S(1)} %get-tuple-element.100), channel_id=1, source_target_pairs={{0,1},{1,0},{2,3},{3,2},{4,5},{5,4},{6,7},{7,6},{8,9},{9,8},{10,11... | collective-permute-start | bytes 1228808 | tf_op jit(solution)/shard_map/ppermute | solution.py:47
  17.4 11.5 %collective-permute-start.5 = (bf16[320,640]{1,0:T(8,128)(2,1)S(1)}, bf16[320,640]{1,0:T(8,128)(2,1)S(1)}, u32[]{:S(2)}, u32[]{:S(2)}) collective-permute-start(bf16[320,640]{1,0:T(8,128)(2,1)S(1)} %get-tuple-element.101), channel_id=1, source_target_pairs={{0,2},{1,3},{2,0},{3,1},{4,6},{5,7},{6,4},{7,5},{8,10},{9,11},{10,... | collective-permute-start | bytes 1228808 | tf_op jit(solution)/shard_map/ppermute | solution.py:47
  28.9 2.7 %collective-permute-start.6 = (bf16[320,640]{1,0:T(8,128)(2,1)S(1)}, bf16[320,640]{1,0:T(8,128)(2,1)S(1)}, u32[]{:S(2)}, u32[]{:S(2)}) collective-permute-start(bf16[320,640]{1,0:T(8,128)(2,1)S(1)} %get-tuple-element.102.refs_0_.refs_1_), channel_id=1, source_target_pairs={{0,16},{16,0},{1,17},{17,1},{2,18},{18,2},{3,19},{19,3},{4,20},{20... | collective-permute-start | bytes 1228808 | tf_op jit(solution)/shard_map/ppermute | solution.py:57
  28.9 2.7 %collective-permute-start.7 = (bf16[320,640]{1,0:T(8,128)(2,1)S(1)}, bf16[320,640]{1,0:T(8,128)(2,1)S(1)}, u32[]{:S(2)}, u32[]{:S(2)}) collective-permute-start(bf16[320,640]{1,0:T(8,128)(2,1)S(1)} %get-tuple-element.103.refs_1_.refs_0_), channel_id=1, source_target_pairs={{0,16},{16,0},{1,17},{17,1},{2,18},{18,2},{3,19},{19,3},{4,20},{20... | collective-permute-start | bytes 1228808 | tf_op jit(solution)/shard_map/ppermute | solution.py:57
  29.5 7.9 %collective-permute-start.8 = (bf16[160,640]{1,0:T(8,128)(2,1)S(1)}, bf16[160,640]{1,0:T(8,128)(2,1)S(1)}, u32[]{:S(2)}, u32[]{:S(2)}) collective-permute-start(bf16[160,640]{1,0:T(8,128)(2,1)S(1)} %get-tuple-element.108), channel_id=1, source_target_pairs={{0,1},{1,0},{2,3},{3,2},{4,5},{5,4},{6,7},{7,6},{8,9},{9,8},{10,11... | collective-permute-start | bytes 614408 | tf_op jit(solution)/shard_map/ppermute | solution.py:47
  30.1 7.3 %collective-permute-start.9 = (bf16[160,640]{1,0:T(8,128)(2,1)S(1)}, bf16[160,640]{1,0:T(8,128)(2,1)S(1)}, u32[]{:S(2)}, u32[]{:S(2)}) collective-permute-start(bf16[160,640]{1,0:T(8,128)(2,1)S(1)} %get-tuple-element.109), channel_id=1, source_target_pairs={{0,2},{1,3},{2,0},{3,1},{4,6},{5,7},{6,4},{7,5},{8,10},{9,11},{10,... | collective-permute-start | bytes 614408 | tf_op jit(solution)/shard_map/ppermute | solution.py:47
  31.6 7.6 %copy-start.4 = (bf16[1024,2048]{1,0:T(8,128)(2,1)S(1)}, bf16[1024,2048]{1,0:T(8,128)(2,1)}, u32[]{:S(2)}) copy-start(bf16[1024,2048]{1,0:T(8,128)(2,1)} %output_ref.1) | copy-start | bytes 12582916
  31.6 7.6 %copy-start.6 = (bf16[8,512,128]{2,1,0:T(8,128)(2,1)S(1)}, bf16[8,512,128]{2,1,0:T(8,128)(2,1)}, u32[]{:S(2)}) copy-start(bf16[8,512,128]{2,1,0:T(8,128)(2,1)} %value_up_ref.1) | copy-start | bytes 3145732
  37.4 1.5 %collective-permute-start.10 = (bf16[160,640]{1,0:T(8,128)(2,1)S(1)}, bf16[160,640]{1,0:T(8,128)(2,1)S(1)}, u32[]{:S(2)}, u32[]{:S(2)}) collective-permute-start(bf16[160,640]{1,0:T(8,128)(2,1)S(1)} %get-tuple-element.110.refs_0_), channel_id=1, source_target_pairs={{0,16},{16,0},{1,17},{17,1},{2,18},{18,2},{3,19},{19,3},{4,20},{20... | collective-permute-start | bytes 614408 | tf_op jit(solution)/shard_map/ppermute | solution.py:57
  37.5 1.7 %collective-permute-start.11 = (bf16[160,640]{1,0:T(8,128)(2,1)S(1)}, bf16[160,640]{1,0:T(8,128)(2,1)S(1)}, u32[]{:S(2)}, u32[]{:S(2)}) collective-permute-start(bf16[160,640]{1,0:T(8,128)(2,1)S(1)} %get-tuple-element.111.refs_1_), channel_id=1, source_target_pairs={{0,16},{16,0},{1,17},{17,1},{2,18},{18,2},{3,19},{19,3},{4,20},{20... | collective-permute-start | bytes 614408 | tf_op jit(solution)/shard_map/ppermute | solution.py:57
  39.2 5.2 %copy-start.16 = (bf16[2048]{0:T(1024)(128)(2,1)S(1)}, bf16[2048]{0:T(1024)(128)(2,1)}, u32[]{:S(2)}) copy-start(bf16[2048]{0:T(1024)(128)(2,1)} %param.28) | copy-start | bytes 12292
  39.2 6.5 %copy-start.7 = (bf16[2048,16]{0,1:T(8,128)(2,1)S(1)}, bf16[2048,16]{0,1:T(8,128)(2,1)}, u32[]{:S(2)}) copy-start(bf16[2048,16]{0,1:T(8,128)(2,1)} %param.29) | copy-start | bytes 196612
  44.1 1.6 %collective-permute-start.12 = (bf16[64,2048]{1,0:T(8,128)(2,1)S(1)}, bf16[64,2048]{1,0:T(8,128)(2,1)S(1)}, u32[]{:S(2)}, u32[]{:S(2)}) collective-permute-start(bf16[64,2048]{1,0:T(8,128)(2,1)S(1)} %get-tuple-element.113), channel_id=1, source_target_pairs={{0,16},{16,0},{1,17},{17,1},{2,18},{18,2},{3,19},{19,3},{4,20},{20... | collective-permute-start | bytes 786440 | tf_op jit(solution)/shard_map/ppermute | solution.py:57
  45.8 17.5 %copy-start.1 = (bf16[1,2048,704]{1,2,0:T(8,128)(2,1)S(1)}, bf16[1,2048,704]{1,2,0:T(8,128)(2,1)}, u32[]{:S(2)}) copy-start(bf16[1,2048,704]{1,2,0:T(8,128)(2,1)} %param.30) | copy-start | bytes 8650756
  45.8 17.5 %copy-start.2 = (bf16[1,2048,704]{1,2,0:T(8,128)(2,1)S(1)}, bf16[1,2048,704]{1,2,0:T(8,128)(2,1)}, u32[]{:S(2)}) copy-start(bf16[1,2048,704]{1,2,0:T(8,128)(2,1)} %param.31) | copy-start | bytes 8650756
  45.8 17.5 %copy-start.3 = (bf16[1,704,2048]{2,1,0:T(8,128)(2,1)S(1)}, bf16[1,704,2048]{2,1,0:T(8,128)(2,1)}, u32[]{:S(2)}) copy-start(bf16[1,704,2048]{2,1,0:T(8,128)(2,1)} %param.32) | copy-start | bytes 8650756
  46.3 10.8 %collective-permute-start.16 = (bf16[64,2048]{1,0:T(8,128)(2,1)S(1)}, bf16[64,2048]{1,0:T(8,128)(2,1)S(1)}, u32[]{:S(2)}, u32[]{:S(2)}) collective-permute-start(bf16[64,2048]{1,0:T(8,128)(2,1)S(1)} %get-tuple-element.121), channel_id=1, source_target_pairs={{0,4},{1,5},{2,6},{3,7},{4,12},{5,13},{6,14},{7,15},{8,0},{9,1},{1... | collective-permute-start | bytes 786440 | tf_op jit(solution)/shard_map/ppermute | solution.py:37
  47.8 5.7 %collective-permute-start.13 = (bf16[32,2048]{1,0:T(8,128)(2,1)S(1)}, bf16[32,2048]{1,0:T(8,128)(2,1)S(1)}, u32[]{:S(2)}, u32[]{:S(2)}) collective-permute-start(bf16[32,2048]{1,0:T(8,128)(2,1)S(1)} %get-tuple-element.118), channel_id=1, source_target_pairs={{0,1},{1,0},{2,3},{3,2},{4,5},{5,4},{6,7},{7,6},{8,9},{9,8},{10,11... | collective-permute-start | bytes 393224 | tf_op jit(solution)/shard_map/ppermute | solution.py:47
  49.3 7.9 %collective-permute-start.14 = (bf16[32,2048]{1,0:T(8,128)(2,1)S(1)}, bf16[32,2048]{1,0:T(8,128)(2,1)S(1)}, u32[]{:S(2)}, u32[]{:S(2)}) collective-permute-start(bf16[32,2048]{1,0:T(8,128)(2,1)S(1)} %get-tuple-element.119), channel_id=1, source_target_pairs={{0,2},{1,3},{2,0},{3,1},{4,6},{5,7},{6,4},{7,5},{8,10},{9,11},{10,... | collective-permute-start | bytes 393224 | tf_op jit(solution)/shard_map/ppermute | solution.py:47
  50.1 7.0 %collective-permute-start.15 = (bf16[32,2048]{1,0:T(8,128)(2,1)S(1)}, bf16[32,2048]{1,0:T(8,128)(2,1)S(1)}, u32[]{:S(2)}, u32[]{:S(2)}) collective-permute-start(bf16[32,2048]{1,0:T(8,128)(2,1)S(1)} %get-tuple-element.120), channel_id=1, source_target_pairs={{0,3},{1,2},{2,1},{3,0},{4,7},{5,6},{6,5},{7,4},{8,11},{9,10},{10,... | collective-permute-start | bytes 393224 | tf_op jit(solution)/shard_map/ppermute | solution.py:47
  57.7 5.5 %collective-permute-start.17 = (bf16[128,2048]{1,0:T(8,128)(2,1)S(1)}, bf16[128,2048]{1,0:T(8,128)(2,1)S(1)}, u32[]{:S(2)}, u32[]{:S(2)}) collective-permute-start(bf16[128,2048]{1,0:T(8,128)(2,1)S(1)} %get-tuple-element.122.refs_0_), channel_id=1, source_target_pairs={{0,16},{16,0},{1,17},{17,1},{2,18},{18,2},{3,19},{19,3},{4,20},{20... | collective-permute-start | bytes 1572872 | tf_op jit(solution)/shard_map/ppermute | solution.py:57
  57.8 10.6 %collective-permute-start.21 = (bf16[64,2048]{1,0:T(8,128)(2,1)S(1)}, bf16[64,2048]{1,0:T(8,128)(2,1)S(1)}, u32[]{:S(2)}, u32[]{:S(2)}) collective-permute-start(bf16[64,2048]{1,0:T(8,128)(2,1)S(1)} %collective-permute-done.16.refs_4_), channel_id=1, source_target_pairs={{0,4},{1,5},{2,6},{3,7},{4,12},{5,13},{6,14},{7,15},{8,0},{9,1},{1... | collective-permute-start | bytes 786440 | tf_op jit(solution)/shard_map/ppermute | solution.py:37
  59.7 6.3 %collective-permute-start.18 = (bf16[32,2048]{1,0:T(8,128)(2,1)S(1)}, bf16[32,2048]{1,0:T(8,128)(2,1)S(1)}, u32[]{:S(2)}, u32[]{:S(2)}) collective-permute-start(bf16[32,2048]{1,0:T(8,128)(2,1)S(1)} %get-tuple-element.125), channel_id=1, source_target_pairs={{0,1},{1,0},{2,3},{3,2},{4,5},{5,4},{6,7},{7,6},{8,9},{9,8},{10,11... | collective-permute-start | bytes 393224 | tf_op jit(solution)/shard_map/ppermute | solution.py:47
  60.3 6.1 %collective-permute-start.19 = (bf16[32,2048]{1,0:T(8,128)(2,1)S(1)}, bf16[32,2048]{1,0:T(8,128)(2,1)S(1)}, u32[]{:S(2)}, u32[]{:S(2)}) collective-permute-start(bf16[32,2048]{1,0:T(8,128)(2,1)S(1)} %get-tuple-element.126), channel_id=1, source_target_pairs={{0,2},{1,3},{2,0},{3,1},{4,6},{5,7},{6,4},{7,5},{8,10},{9,11},{10,... | collective-permute-start | bytes 393224 | tf_op jit(solution)/shard_map/ppermute | solution.py:47
  61.5 6.9 %collective-permute-start.20 = (bf16[32,2048]{1,0:T(8,128)(2,1)S(1)}, bf16[32,2048]{1,0:T(8,128)(2,1)S(1)}, u32[]{:S(2)}, u32[]{:S(2)}) collective-permute-start(bf16[32,2048]{1,0:T(8,128)(2,1)S(1)} %get-tuple-element.127), channel_id=1, source_target_pairs={{0,3},{1,2},{2,1},{3,0},{4,7},{5,6},{6,5},{7,4},{8,11},{9,10},{10,... | collective-permute-start | bytes 393224 | tf_op jit(solution)/shard_map/ppermute | solution.py:47
  69.0 5.6 %collective-permute-start.22 = (bf16[128,2048]{1,0:T(8,128)(2,1)S(1)}, bf16[128,2048]{1,0:T(8,128)(2,1)S(1)}, u32[]{:S(2)}, u32[]{:S(2)}) collective-permute-start(bf16[128,2048]{1,0:T(8,128)(2,1)S(1)} %get-tuple-element.128.refs_0_), channel_id=1, source_target_pairs={{0,16},{16,0},{1,17},{17,1},{2,18},{18,2},{3,19},{19,3},{4,20},{20... | collective-permute-start | bytes 1572872 | tf_op jit(solution)/shard_map/ppermute | solution.py:57
  69.0 9.6 %collective-permute-start.26 = (bf16[64,2048]{1,0:T(8,128)(2,1)S(1)}, bf16[64,2048]{1,0:T(8,128)(2,1)S(1)}, u32[]{:S(2)}, u32[]{:S(2)}) collective-permute-start(bf16[64,2048]{1,0:T(8,128)(2,1)S(1)} %collective-permute-done.21.refs_5_), channel_id=1, source_target_pairs={{0,4},{1,5},{2,6},{3,7},{4,12},{5,13},{6,14},{7,15},{8,0},{9,1},{1... | collective-permute-start | bytes 786440 | tf_op jit(solution)/shard_map/ppermute | solution.py:37
  71.0 7.6 %collective-permute-start.23 = (bf16[32,2048]{1,0:T(8,128)(2,1)S(1)}, bf16[32,2048]{1,0:T(8,128)(2,1)S(1)}, u32[]{:S(2)}, u32[]{:S(2)}) collective-permute-start(bf16[32,2048]{1,0:T(8,128)(2,1)S(1)} %get-tuple-element.131), channel_id=1, source_target_pairs={{0,1},{1,0},{2,3},{3,2},{4,5},{5,4},{6,7},{7,6},{8,9},{9,8},{10,11... | collective-permute-start | bytes 393224 | tf_op jit(solution)/shard_map/ppermute | solution.py:47
  72.5 8.1 %collective-permute-start.24 = (bf16[32,2048]{1,0:T(8,128)(2,1)S(1)}, bf16[32,2048]{1,0:T(8,128)(2,1)S(1)}, u32[]{:S(2)}, u32[]{:S(2)}) collective-permute-start(bf16[32,2048]{1,0:T(8,128)(2,1)S(1)} %get-tuple-element.132), channel_id=1, source_target_pairs={{0,2},{1,3},{2,0},{3,1},{4,6},{5,7},{6,4},{7,5},{8,10},{9,11},{10,... | collective-permute-start | bytes 393224 | tf_op jit(solution)/shard_map/ppermute | solution.py:47
  73.4 7.3 %collective-permute-start.25 = (bf16[32,2048]{1,0:T(8,128)(2,1)S(1)}, bf16[32,2048]{1,0:T(8,128)(2,1)S(1)}, u32[]{:S(2)}, u32[]{:S(2)}) collective-permute-start(bf16[32,2048]{1,0:T(8,128)(2,1)S(1)} %get-tuple-element.133), channel_id=1, source_target_pairs={{0,3},{1,2},{2,1},{3,0},{4,7},{5,6},{6,5},{7,4},{8,11},{9,10},{10,... | collective-permute-start | bytes 393224 | tf_op jit(solution)/shard_map/ppermute | solution.py:47
  80.6 1.9 %collective-permute-start.28 = (bf16[128,2048]{1,0:T(8,128)(2,1)S(1)}, bf16[128,2048]{1,0:T(8,128)(2,1)S(1)}, u32[]{:S(2)}, u32[]{:S(2)}) collective-permute-start(bf16[128,2048]{1,0:T(8,128)(2,1)S(1)} %pass_on.7), channel_id=1, source_target_pairs={{0,16},{16,0},{1,17},{17,1},{2,18},{18,2},{3,19},{19,3},{4,20},{20... | collective-permute-start | bytes 1572872 | tf_op jit(solution)/shard_map/ppermute | solution.py:57
  81.2 5.0 %collective-permute-start.27 = (bf16[128,2048]{1,0:T(8,128)(2,1)S(1)}, bf16[128,2048]{1,0:T(8,128)(2,1)S(1)}, u32[]{:S(2)}, u32[]{:S(2)}) collective-permute-start(bf16[128,2048]{1,0:T(8,128)(2,1)S(1)} %get-tuple-element.135.refs_0_), channel_id=1, source_target_pairs={{0,16},{16,0},{1,17},{17,1},{2,18},{18,2},{3,19},{19,3},{4,20},{20... | collective-permute-start | bytes 1572872 | tf_op jit(solution)/shard_map/ppermute | solution.py:57
  82.6 9.2 %collective-permute-start.29 = (bf16[64,2048]{1,0:T(8,128)(2,1)S(1)}, bf16[64,2048]{1,0:T(8,128)(2,1)S(1)}, u32[]{:S(2)}, u32[]{:S(2)}) collective-permute-start(bf16[64,2048]{1,0:T(8,128)(2,1)S(1)} %get-tuple-element.144), channel_id=1, source_target_pairs={{0,1},{1,0},{2,3},{3,2},{4,5},{5,4},{6,7},{7,6},{8,9},{9,8},{10,11... | collective-permute-start | bytes 786440 | tf_op jit(solution)/shard_map/ppermute | solution.py:47
  83.3 8.9 %collective-permute-start.30 = (bf16[64,2048]{1,0:T(8,128)(2,1)S(1)}, bf16[64,2048]{1,0:T(8,128)(2,1)S(1)}, u32[]{:S(2)}, u32[]{:S(2)}) collective-permute-start(bf16[64,2048]{1,0:T(8,128)(2,1)S(1)} %get-tuple-element.145), channel_id=1, source_target_pairs={{0,2},{1,3},{2,0},{3,1},{4,6},{5,7},{6,4},{7,5},{8,10},{9,11},{10,... | collective-permute-start | bytes 786440 | tf_op jit(solution)/shard_map/ppermute | solution.py:47
  84.5 12.5 %collective-permute-start.31 = (bf16[64,2048]{1,0:T(8,128)(2,1)S(1)}, bf16[64,2048]{1,0:T(8,128)(2,1)S(1)}, u32[]{:S(2)}, u32[]{:S(2)}) collective-permute-start(bf16[64,2048]{1,0:T(8,128)(2,1)S(1)} %get-tuple-element.146), channel_id=1, source_target_pairs={{0,3},{1,2},{2,1},{3,0},{4,7},{5,6},{6,5},{7,4},{8,11},{9,10},{10,... | collective-permute-start | bytes 786440 | tf_op jit(solution)/shard_map/ppermute | solution.py:47
  97.0 2.1 %collective-permute-start.33 = (bf16[128,2048]{1,0:T(8,128)(2,1)S(1)}, bf16[128,2048]{1,0:T(8,128)(2,1)S(1)}, u32[]{:S(2)}, u32[]{:S(2)}) collective-permute-start(bf16[128,2048]{1,0:T(8,128)(2,1)S(1)} %pass_on.8), channel_id=1, source_target_pairs={{0,16},{16,0},{1,17},{17,1},{2,18},{18,2},{3,19},{19,3},{4,20},{20... | collective-permute-start | bytes 1572872 | tf_op jit(solution)/shard_map/ppermute | solution.py:57
  97.0 5.7 %collective-permute-start.32 = (bf16[128,2048]{1,0:T(8,128)(2,1)S(1)}, bf16[128,2048]{1,0:T(8,128)(2,1)S(1)}, u32[]{:S(2)}, u32[]{:S(2)}) collective-permute-start(bf16[128,2048]{1,0:T(8,128)(2,1)S(1)} %turn.7.refs_0_), channel_id=1, source_target_pairs={{0,16},{16,0},{1,17},{17,1},{2,18},{18,2},{3,19},{19,3},{4,20},{20... | collective-permute-start | bytes 1572872 | tf_op jit(solution)/shard_map/ppermute | solution.py:57
  97.8 9.4 %collective-permute-start.37 = (bf16[64,2048]{1,0:T(8,128)(2,1)S(1)}, bf16[64,2048]{1,0:T(8,128)(2,1)S(1)}, u32[]{:S(2)}, u32[]{:S(2)}) collective-permute-start(bf16[64,2048]{1,0:T(8,128)(2,1)S(1)} %collect.3), channel_id=1, source_target_pairs={{0,4},{1,5},{2,6},{3,7},{4,12},{5,13},{6,14},{7,15},{8,0},{9,1},{1... | collective-permute-start | bytes 786440 | tf_op jit(solution)/shard_map/ppermute | solution.py:37
  99.1 8.1 %collective-permute-start.34 = (bf16[32,2048]{1,0:T(8,128)(2,1)S(1)}, bf16[32,2048]{1,0:T(8,128)(2,1)S(1)}, u32[]{:S(2)}, u32[]{:S(2)}) collective-permute-start(bf16[32,2048]{1,0:T(8,128)(2,1)S(1)} %get-tuple-element.150), channel_id=1, source_target_pairs={{0,1},{1,0},{2,3},{3,2},{4,5},{5,4},{6,7},{7,6},{8,9},{9,8},{10,11... | collective-permute-start | bytes 393224 | tf_op jit(solution)/shard_map/ppermute | solution.py:47
  100.5 8.1 %collective-permute-start.35 = (bf16[32,2048]{1,0:T(8,128)(2,1)S(1)}, bf16[32,2048]{1,0:T(8,128)(2,1)S(1)}, u32[]{:S(2)}, u32[]{:S(2)}) collective-permute-start(bf16[32,2048]{1,0:T(8,128)(2,1)S(1)} %get-tuple-element.151), channel_id=1, source_target_pairs={{0,2},{1,3},{2,0},{3,1},{4,6},{5,7},{6,4},{7,5},{8,10},{9,11},{10,... | collective-permute-start | bytes 393224 | tf_op jit(solution)/shard_map/ppermute | solution.py:47
  101.3 30.0 %slice-start = ((s8[6291456]{0:T(1024)(128)(4,1)}), s8[4194304]{0:T(1024)(128)(4,1)S(1)}, s32[]{:S(2)}) async-start(s8[6291456]{0:T(1024)(128)(4,1)} %bitcast.27), calls=%async_computation | async-start | bytes 8388608
  101.3 30.0 %slice-start.1 = ((s8[6291456]{0:T(1024)(128)(4,1)}), s8[2097152]{0:T(1024)(128)(4,1)S(1)}, s32[]{:S(2)}) async-start(s8[6291456]{0:T(1024)(128)(4,1)} %bitcast.27), calls=%async_computation.1 | async-start | bytes 4194304
  101.3 7.2 %collective-permute-start.36 = (bf16[32,2048]{1,0:T(8,128)(2,1)S(1)}, bf16[32,2048]{1,0:T(8,128)(2,1)S(1)}, u32[]{:S(2)}, u32[]{:S(2)}) collective-permute-start(bf16[32,2048]{1,0:T(8,128)(2,1)S(1)} %get-tuple-element.152), channel_id=1, source_target_pairs={{0,3},{1,2},{2,1},{3,0},{4,7},{5,6},{6,5},{7,4},{8,11},{9,10},{10,... | collective-permute-start | bytes 393224 | tf_op jit(solution)/shard_map/ppermute | solution.py:47
  108.6 15.6 %copy-start.17 = (bf16[2048]{0:T(1024)(128)(2,1)S(1)}, bf16[2048]{0:T(1024)(128)(2,1)}, u32[]{:S(2)}) copy-start(bf16[2048]{0:T(1024)(128)(2,1)} %param.33) | copy-start | bytes 12292
  108.6 1.9 %collective-permute-start.38 = (bf16[128,2048]{1,0:T(8,128)(2,1)S(1)}, bf16[128,2048]{1,0:T(8,128)(2,1)S(1)}, u32[]{:S(2)}, u32[]{:S(2)}) collective-permute-start(bf16[128,2048]{1,0:T(8,128)(2,1)S(1)} %pass_on.9), channel_id=1, source_target_pairs={{0,16},{16,0},{1,17},{17,1},{2,18},{18,2},{3,19},{19,3},{4,20},{20... | collective-permute-start | bytes 1572872 | tf_op jit(solution)/shard_map/ppermute | solution.py:57
  108.6 11.9 %collective-permute-start.43 = (bf16[128,2048]{1,0:T(8,128)(2,1)S(1)}, bf16[128,2048]{1,0:T(8,128)(2,1)S(1)}, u32[]{:S(2)}, u32[]{:S(2)}) collective-permute-start(bf16[128,2048]{1,0:T(8,128)(2,1)S(1)} %get-tuple-element.162), channel_id=1, source_target_pairs={{0,16},{16,0},{1,17},{17,1},{2,18},{18,2},{3,19},{19,3},{4,20},{20... | collective-permute-start | bytes 1572872 | tf_op jit(solution)/shard_map/ppermute | solution.py:57
  109.3 22.0 %copy-start.5 = (bf16[2048,288]{0,1:T(8,128)(2,1)S(1)}, bf16[2048,288]{0,1:T(8,128)(2,1)}, u32[]{:S(2)}) copy-start(bf16[2048,288]{0,1:T(8,128)(2,1)} %param.35) | copy-start | bytes 3538948
  109.4 9.2 %collective-permute-start.42 = (bf16[64,2048]{1,0:T(8,128)(2,1)S(1)}, bf16[64,2048]{1,0:T(8,128)(2,1)S(1)}, u32[]{:S(2)}, u32[]{:S(2)}) collective-permute-start(bf16[64,2048]{1,0:T(8,128)(2,1)S(1)} %collect.4), channel_id=1, source_target_pairs={{0,4},{1,5},{2,6},{3,7},{4,12},{5,13},{6,14},{7,15},{8,0},{9,1},{1... | collective-permute-start | bytes 786440 | tf_op jit(solution)/shard_map/ppermute | solution.py:37
  110.6 8.0 %collective-permute-start.39 = (bf16[32,2048]{1,0:T(8,128)(2,1)S(1)}, bf16[32,2048]{1,0:T(8,128)(2,1)S(1)}, u32[]{:S(2)}, u32[]{:S(2)}) collective-permute-start(bf16[32,2048]{1,0:T(8,128)(2,1)S(1)} %get-tuple-element.156), channel_id=1, source_target_pairs={{0,1},{1,0},{2,3},{3,2},{4,5},{5,4},{6,7},{7,6},{8,9},{9,8},{10,11... | collective-permute-start | bytes 393224 | tf_op jit(solution)/shard_map/ppermute | solution.py:47
  111.2 7.4 %collective-permute-start.40 = (bf16[32,2048]{1,0:T(8,128)(2,1)S(1)}, bf16[32,2048]{1,0:T(8,128)(2,1)S(1)}, u32[]{:S(2)}, u32[]{:S(2)}) collective-permute-start(bf16[32,2048]{1,0:T(8,128)(2,1)S(1)} %get-tuple-element.157), channel_id=1, source_target_pairs={{0,2},{1,3},{2,0},{3,1},{4,6},{5,7},{6,4},{7,5},{8,10},{9,11},{10,... | collective-permute-start | bytes 393224 | tf_op jit(solution)/shard_map/ppermute | solution.py:47
  112.4 6.9 %collective-permute-start.41 = (bf16[32,2048]{1,0:T(8,128)(2,1)S(1)}, bf16[32,2048]{1,0:T(8,128)(2,1)S(1)}, u32[]{:S(2)}, u32[]{:S(2)}) collective-permute-start(bf16[32,2048]{1,0:T(8,128)(2,1)S(1)} %get-tuple-element.158), channel_id=1, source_target_pairs={{0,3},{1,2},{2,1},{3,0},{4,7},{5,6},{6,5},{7,4},{8,11},{9,10},{10,... | collective-permute-start | bytes 393224 | tf_op jit(solution)/shard_map/ppermute | solution.py:47
  119.5 9.3 %collective-permute-start.47 = (bf16[64,2048]{1,0:T(8,128)(2,1)S(1)}, bf16[64,2048]{1,0:T(8,128)(2,1)S(1)}, u32[]{:S(2)}, u32[]{:S(2)}) collective-permute-start(bf16[64,2048]{1,0:T(8,128)(2,1)S(1)} %collect.5.refs_0_), channel_id=1, source_target_pairs={{0,4},{1,5},{2,6},{3,7},{4,12},{5,13},{6,14},{7,15},{8,0},{9,1},{1... | collective-permute-start | bytes 786440 | tf_op jit(solution)/shard_map/ppermute | solution.py:37
  120.6 5.8 %collective-permute-start.44 = (bf16[32,2048]{1,0:T(8,128)(2,1)S(1)}, bf16[32,2048]{1,0:T(8,128)(2,1)S(1)}, u32[]{:S(2)}, u32[]{:S(2)}) collective-permute-start(bf16[32,2048]{1,0:T(8,128)(2,1)S(1)} %get-tuple-element.164), channel_id=1, source_target_pairs={{0,1},{1,0},{2,3},{3,2},{4,5},{5,4},{6,7},{7,6},{8,9},{9,8},{10,11... | collective-permute-start | bytes 393224 | tf_op jit(solution)/shard_map/ppermute | solution.py:47
  121.7 7.1 %collective-permute-start.45 = (bf16[32,2048]{1,0:T(8,128)(2,1)S(1)}, bf16[32,2048]{1,0:T(8,128)(2,1)S(1)}, u32[]{:S(2)}, u32[]{:S(2)}) collective-permute-start(bf16[32,2048]{1,0:T(8,128)(2,1)S(1)} %get-tuple-element.165), channel_id=1, source_target_pairs={{0,2},{1,3},{2,0},{3,1},{4,6},{5,7},{6,4},{7,5},{8,10},{9,11},{10,... | collective-permute-start | bytes 393224 | tf_op jit(solution)/shard_map/ppermute | solution.py:47
  122.6 6.2 %collective-permute-start.46 = (bf16[32,2048]{1,0:T(8,128)(2,1)S(1)}, bf16[32,2048]{1,0:T(8,128)(2,1)S(1)}, u32[]{:S(2)}, u32[]{:S(2)}) collective-permute-start(bf16[32,2048]{1,0:T(8,128)(2,1)S(1)} %get-tuple-element.166), channel_id=1, source_target_pairs={{0,3},{1,2},{2,1},{3,0},{4,7},{5,6},{6,5},{7,4},{8,11},{9,10},{10,... | collective-permute-start | bytes 393224 | tf_op jit(solution)/shard_map/ppermute | solution.py:47
  129.8 1.5 %collective-permute-start.48 = (bf16[64,2048]{1,0:T(8,128)(2,1)S(1)}, bf16[64,2048]{1,0:T(8,128)(2,1)S(1)}, u32[]{:S(2)}, u32[]{:S(2)}) collective-permute-start(bf16[64,2048]{1,0:T(8,128)(2,1)S(1)} %get-tuple-element.168.refs_3_), channel_id=1, source_target_pairs={{0,16},{16,0},{1,17},{17,1},{2,18},{18,2},{3,19},{19,3},{4,20},{20... | collective-permute-start | bytes 786440 | tf_op jit(solution)/shard_map/ppermute | solution.py:57
  (5 other events, 3.5 us)

commit v6 on v5

--- a/solution.py
+++ b/solution.py
@@ -567,32 +567,28 @@
     return residual, normed, scaled, pieces
 
 
-def turn(step, block, arrived, routes, router, sizes, ready):
+def choose(step, block, routes, router, sizes, ready):
     ring, top, capacity = sizes
-    width = arrived[0].shape[1]
-    inputs = [*arrived]
-    outputs = [((PLANE * capacity, width), jnp.bfloat16)]
-    if block is not None:
-        inputs += [block, routes, router]
-        outputs.append(((PLANE * capacity, block.shape[0]), jnp.bfloat16))
-        outputs += [((capacity, width), jnp.bfloat16)] * PLANE
-
+    width = block.shape[1]
+
+    def kernel(block_ref, routes_ref, router_ref, scaled_ref, *outs):
+        pick_rows(step, ring, top, block_ref[...], routes_ref, router_ref, scaled_ref, outs)
+
+    outputs = [((PLANE * capacity, block.shape[0]), jnp.bfloat16)]
+    outputs += [((capacity, width), jnp.bfloat16)] * PLANE
+    inputs = [block, routes, router]
+    scaled, *pieces = call(kernel, "choose", inputs, outputs, 70_000_000, ready=ready)
+    return scaled, pieces
+
+
+def join_arrived(arrived, capacity, ready):
     def kernel(*refs):
-        row_refs = refs[:PLANE]
-        joined_ref = refs[len(inputs)]
-        for d, ref in enumerate(row_refs):
+        joined_ref = refs[PLANE]
+        for d, ref in enumerate(refs[:PLANE]):
             joined_ref[d * capacity : (d + 1) * capacity, :] = ref[:capacity, :]
-        if block is not None:
-            block_ref, routes_ref, router_ref = refs[PLANE : len(inputs)]
-            scaled_ref, *outs = refs[len(inputs) + 1 :]
-            pick_rows(
-                step, ring, top, block_ref[...], routes_ref, router_ref, scaled_ref, outs
-            )
-
-    joined, *found = call(kernel, "turn", inputs, outputs, 70_000_000, ready=ready)
-    if block is None:
-        return joined, None, []
-    return joined, found[0], found[1:]
+
+    outputs = [((PLANE * capacity, arrived[0].shape[1]), jnp.bfloat16)]
+    return call(kernel, "join_arrived", arrived, outputs, 0, ready=ready)[0]
 
 
 def blend(own, others, pieces, ready):
@@ -679,10 +675,11 @@
     return call(kernel, "conclude", inputs, [(residual.shape, jnp.bfloat16)] * 2, 35_000_000)
 
 
-def project(shares, order, query_weight, latent_rows):
-    def kernel(order_ref, query_ref, latent_ref, *refs):
+def project(shares, order, query_weight, latent_rows, layer_rows):
+    def kernel(order_ref, query_ref, latent_ref, layer_ref, *refs):
         share_refs = refs[: len(shares)]
-        queries_ref, latents_ref = refs[len(shares) :]
+        queries_ref, latents_ref, copy_ref = refs[len(shares) :]
+        copy_ref[...] = layer_ref[...]
         rows = jnp.concatenate([ref[...] for ref in share_refs], axis=0)
         rows = lax.dot_general(
             order_ref[...], rows, (((0,), (0,)), ((), ())), preferred_element_type=jnp.float32
@@ -694,8 +691,9 @@
     outputs = [
         ((tokens, query_weight.shape[1]), jnp.bfloat16),
         ((latent_rows.shape[0], tokens), jnp.bfloat16),
+        (layer_rows.shape, jnp.bfloat16),
     ]
-    inputs = [order, query_weight, latent_rows, *shares]
+    inputs = [order, query_weight, latent_rows, layer_rows, *shares]
     return call(kernel, "project", inputs, outputs, 1_000_000_000, limit=16)
 
 
@@ -837,16 +835,14 @@
                 send_group(other[(j - 1) * kept : j * kept], j) for j in range(1, groups)
             ]
         if step <= ring:
-            joined, scaled, payload = turn(
-                step,
-                block if step <= ring - 1 else None,
-                arrived,
-                routes_ring,
-                experts_columns,
-                sizes,
-                [results[step - 2][2]] if step >= 2 else [],
-            )
-            scales.append(scaled)
+            ready = [results[step - 2][2]] if step >= 2 else []
+            if step <= ring - 1:
+                scaled, payload = choose(
+                    step, block, routes_ring, experts_columns, sizes, ready
+                )
+                scales.append(scaled)
+                ready = [scaled]
+            joined = join_arrived(arrived, capacity, ready)
             rows = [send_group(joined, j) if j else joined for j in range(groups)]
             results.append(expert_apply(rows, kept, gate_part, up_part, down_part))
         if step >= 3:
@@ -856,8 +852,8 @@
     )
 
     shares = [send_group(normed_next, j) if j else normed_next for j in range(groups)]
-    next_queries, next_latent = project(
-        shares, permutation, next_query_weight, next_latent_weight.T
+    next_queries, next_latent, layer_rows = project(
+        shares, permutation, next_query_weight, next_latent_weight.T, layer_rows
     )
     return (layer_rows[:, None, :], next_queries, next_latent.T)
 

time: 134 us -> 133 us (level)
  waiting for transfers between devices: 45.4 us -> 43.6 us
    ppermute x25, waiting for transfers between devices: 31.2 us -> 23.8 us  [send_plane(): return lax.ppermute(block, 'tensor', [(i, i ^ distance) for i in devices])]
    ppermute x6, waiting for transfers between devices: 7.42 us -> 13.3 us  [send_ring(): return lax.ppermute(block, 'tensor', route)]
    pallas_call x21 -> x24, Pallas kernels: 19.7 us -> 19.3 us  [call(): pl.pallas_call(after(kernel, len(ready)), **places, out_shape=shapes, com...]
  transfers between devices with their start and end apart: 49 -> 49, of which waited for: 25 -> 24; matrix products, arithmetic and copies ran while one was open for 0% -> 0% of each run, Pallas kernels for 18% -> 19%
where the time goes in v6:
time: 133 us
  starting transfers between devices  48.2 us (36%)
  waiting for transfers between devices  43.6 us (33%)
  Pallas kernels  35 us (26%)
  local copies, waits for them, and re-layouts  4.56 us (3%)
    ppermute x25, starting transfers between devices, send_plane(): return lax.ppermute(block, 'tensor', [(i, i ^ distance) for i in devices])  29.9 us
    ppermute x25, waiting for transfers between devices, send_plane(): return lax.ppermute(block, 'tensor', [(i, i ^ distance) for i in devices])  23.8 us
    pallas_call x24, Pallas kernels, call(): pl.pallas_call(after(kernel, len(ready)), **places, out_shape=shapes, com...  19.3 us
    pallas_call x3, Pallas kernels, attend_call(): pl.pallas_call(kernel, in_specs=resident(inputs), out_specs=resident(shap...  14.6 us
    ppermute x6, waiting for transfers between devices, send_ring(): return lax.ppermute(block, 'tensor', route)  13.3 us
    ppermute x6, starting transfers between devices, send_ring(): return lax.ppermute(block, 'tensor', route)  8.95 us
    ppermute x3, starting transfers between devices, send_round(): lax.ppermute(block, 'tensor', [(i, (i + distance) % count) for i in range...  6.06 us
    ppermute x15, waiting for transfers between devices, send_group(): return lax.ppermute(block, 'group', [(i, i ^ distance) for i in devices])  5.06 us
  transfers between devices with their start and end apart: 49, of which 24 were waited for; matrix products, arithmetic and copies ran while one was open for 0% of the time, Pallas kernels for 19%

profile of v6, /device:TPU:0, one launch (start us, length us, event | category | flops | bytes accessed | tf_op | source)
XLA Modules:
  0.0 132.6 jit_solution(15611549186331255994)
XLA Ops:
  0.6 1.9 %join_share.1 = (bf16[128,640]{1,0:T(8,128)(2,1)}, bf16[64,640]{1,0:T(8,128)(2,1)}) custom-call(bf16[64,576]{1,0:T(8,128)(2,1)} %refs_0_.1, bf16[576,128]{1,0:T(8,128)(2,1)} %bitcast.35, s32[6,2,64]{2,1,0:T(2,128)} %bitcast.36), custom_call_target="tpu_custom_call" | custom-call | flops 10000000 | bytes 470016 | tf_op jit(solution)/shard_map/join_share/pallas_call | solution.py:111
  2.5 4.0 %collective-permute-start.1 = (bf16[64,640]{1,0:T(8,128)(2,1)}, bf16[64,640]{1,0:T(8,128)(2,1)S(1)}, u32[]{:S(2)}, u32[]{:S(2)}) collective-permute-start(bf16[64,640]{1,0:T(8,128)(2,1)} %get-tuple-element.90), channel_id=1, source_target_pairs={{0,8},{1,9},{2,10},{3,11},{4,12},{5,13},{6,14},{7,15},{8,0},{9,1},... | collective-permute-start | bytes 245768 | tf_op jit(solution)/shard_map/ppermute | solution.py:42
  6.5 1.3 %collective-permute-start.2 = (bf16[64,640]{1,0:T(8,128)(2,1)}, bf16[64,640]{1,0:T(8,128)(2,1)S(1)}, u32[]{:S(2)}, u32[]{:S(2)}) collective-permute-start(bf16[64,640]{1,0:T(8,128)(2,1)} %get-tuple-element.90), channel_id=1, source_target_pairs={{0,12},{1,13},{2,14},{3,15},{4,0},{5,1},{6,2},{7,3},{8,4},{9,5},{1... | collective-permute-start | bytes 245768 | tf_op jit(solution)/shard_map/ppermute | solution.py:42
  7.9 0.7 collective-permute-start
  8.6 0.9 copy-done.8
  9.5 0.7 copy-done.11
  10.2 0.7 copy-done.12
  10.9 0.7 copy-done.13
  11.5 0.7 copy-done.14
  12.2 0.9 copy-done.15
  13.1 1.1 make_plan.1
  14.2 1.5 %collective-permute-done.refs_2_ = bf16[128,640]{1,0:T(8,128)(2,1)S(1)} collective-permute-done((bf16[128,640]{1,0:T(8,128)(2,1)}, bf16[128,640]{1,0:T(8,128)(2,1)S(1)}, u32[]{:S(2)}, u32[]{:S(2)}) %collective-permute-start) | collective-permute-done | bytes 163872 | tf_op jit(solution)/shard_map/ppermute | solution.py:42
  15.8 1.6 %collective-permute-start.4 = (bf16[320,640]{1,0:T(8,128)(2,1)S(1)}, bf16[320,640]{1,0:T(8,128)(2,1)S(1)}, u32[]{:S(2)}, u32[]{:S(2)}) collective-permute-start(bf16[320,640]{1,0:T(8,128)(2,1)S(1)} %get-tuple-element.98), channel_id=1, source_target_pairs={{0,1},{1,0},{2,3},{3,2},{4,5},{5,4},{6,7},{7,6},{8,9},{9,8},{10,11... | collective-permute-start | bytes 1228808 | tf_op jit(solution)/shard_map/ppermute | solution.py:47
  17.4 1.5 %collective-permute-start.5 = (bf16[320,640]{1,0:T(8,128)(2,1)S(1)}, bf16[320,640]{1,0:T(8,128)(2,1)S(1)}, u32[]{:S(2)}, u32[]{:S(2)}) collective-permute-start(bf16[320,640]{1,0:T(8,128)(2,1)S(1)} %get-tuple-element.99), channel_id=1, source_target_pairs={{0,2},{1,3},{2,0},{3,1},{4,6},{5,7},{6,4},{7,5},{8,10},{9,11},{10,... | collective-permute-start | bytes 1228808 | tf_op jit(solution)/shard_map/ppermute | solution.py:47
  18.9 4.0 %attend_near.1 = (bf16[1024,640]{1,0:T(8,128)(2,1)S(1)}, f32[1024,1]{1,0:T(8,128)S(1)}, f32[1024,1]{1,0:T(8,128)S(1)}, f32[1024,512]{1,0:T(8,128)S(1)}, f32[8,128]{1,0:T(8,128)S(1)}) custom-call(s32[128,4]{1,0:T(8,128)S(1)} %get-tuple-element.87.token_ref, s32[1,768]{1,0:T(1,128)S(1)} %get-tuple-element.89.refs_0_.spot_ref, ...), custom_call_target="tpu_custom_call" | custom-call | flops 1711276032 | bytes 8000000 | tf_op jit(solution)/shard_map/attend_near/pallas_call | solution.py:367
  22.9 4.8 %collective-permute-done.4.refs_1_ = bf16[320,640]{1,0:T(8,128)(2,1)S(1)} collective-permute-done((bf16[320,640]{1,0:T(8,128)(2,1)S(1)}, bf16[320,640]{1,0:T(8,128)(2,1)S(1)}, u32[]{:S(2)}, u32[]{:S(2)}) %collective-permute-start.4) | collective-permute-done | bytes 409632 | tf_op jit(solution)/shard_map/ppermute | solution.py:47
  27.7 1.2 collective-permute-done.5.refs_2_
  30.1 1.5 %collective-permute-start.9 = (bf16[160,640]{1,0:T(8,128)(2,1)S(1)}, bf16[160,640]{1,0:T(8,128)(2,1)S(1)}, u32[]{:S(2)}, u32[]{:S(2)}) collective-permute-start(bf16[160,640]{1,0:T(8,128)(2,1)S(1)} %get-tuple-element.107), channel_id=1, source_target_pairs={{0,2},{1,3},{2,0},{3,1},{4,6},{5,7},{6,4},{7,5},{8,10},{9,11},{10,... | collective-permute-start | bytes 614408 | tf_op jit(solution)/shard_map/ppermute | solution.py:47
  31.6 5.7 %attend_mid.1 = (f32[1024,1]{1,0:T(8,128)S(1)}, f32[1024,1]{1,0:T(8,128)S(1)}, f32[1024,512]{1,0:T(8,128)S(1)}, f32[8,128]{1,0:T(8,128)S(1)}) custom-call(s32[128,4]{1,0:T(8,128)S(1)} %get-tuple-element.87.token_ref, s32[1,1280]{1,0:T(1,128)S(1)} %get-tuple-element.93.spot_ref, bf16[1024,640]{1,0:T(8,128)(2,1)S(1)} %get-tuple-element.92.wide_ref, ...), custom_call_target="tpu_custom_call" | custom-call | flops 2852126720 | bytes 8000000 | tf_op jit(solution)/shard_map/attend_mid/pallas_call | solution.py:367
  38.0 0.9 collective-permute-done.10.refs_2_
  39.2 4.9 %attend_far.1 = (f32[64,2048]{1,0:T(8,128)S(1)}, bf16[64,2048]{1,0:T(8,128)(2,1)S(1)}) custom-call(s32[128,4]{1,0:T(8,128)S(1)} %get-tuple-element.87.token_ref, s32[1,640]{1,0:T(1,128)S(1)} %get-tuple-element.88.spot_ref, bf16[1024,640]{1,0:T(8,128)(2,1)S(1)} %get-tuple-element.92.wide_ref, f32[1024,1]{1,0:T(8,128)S(1)} %get-tuple-element.102.best_ref, ...), custom_call_target="tpu_custom_call" | custom-call | flops 1426063360 | bytes 8000000 | tf_op jit(solution)/shard_map/attend_far/pallas_call | solution.py:367
  44.7 1.1 collective-permute-done.12.refs_2_
  46.3 1.5 %collective-permute-start.13 = (bf16[64,2048]{1,0:T(8,128)(2,1)S(1)}, bf16[64,2048]{1,0:T(8,128)(2,1)S(1)}, u32[]{:S(2)}, u32[]{:S(2)}) collective-permute-start(bf16[64,2048]{1,0:T(8,128)(2,1)S(1)} %get-tuple-element.115), channel_id=1, source_target_pairs={{0,4},{1,5},{2,6},{3,7},{4,12},{5,13},{6,14},{7,15},{8,0},{9,1},{1... | collective-permute-start | bytes 786440 | tf_op jit(solution)/shard_map/ppermute | solution.py:37
  47.8 1.5 %collective-permute-start.14 = (bf16[32,2048]{1,0:T(8,128)(2,1)S(1)}, bf16[32,2048]{1,0:T(8,128)(2,1)S(1)}, u32[]{:S(2)}, u32[]{:S(2)}) collective-permute-start(bf16[32,2048]{1,0:T(8,128)(2,1)S(1)} %get-tuple-element.118), channel_id=1, source_target_pairs={{0,1},{1,0},{2,3},{3,2},{4,5},{5,4},{6,7},{7,6},{8,9},{9,8},{10,11... | collective-permute-start | bytes 393224 | tf_op jit(solution)/shard_map/ppermute | solution.py:47
  49.3 0.8 collective-permute-start.15
  50.1 1.2 collective-permute-start.16
  51.3 5.0 %collective-permute-done.13.refs_0_ = bf16[64,2048]{1,0:T(8,128)(2,1)S(1)} collective-permute-done((bf16[64,2048]{1,0:T(8,128)(2,1)S(1)}, bf16[64,2048]{1,0:T(8,128)(2,1)S(1)}, u32[]{:S(2)}, u32[]{:S(2)}) %collective-permute-start.13) | collective-permute-done | bytes 262176 | tf_op jit(solution)/shard_map/ppermute | solution.py:37
  57.3 1.9 %collective-permute-start.18 = (bf16[64,2048]{1,0:T(8,128)(2,1)S(1)}, bf16[64,2048]{1,0:T(8,128)(2,1)S(1)}, u32[]{:S(2)}, u32[]{:S(2)}) collective-permute-start(bf16[64,2048]{1,0:T(8,128)(2,1)S(1)} %collective-permute-done.13.refs_0_), channel_id=1, source_target_pairs={{0,4},{1,5},{2,6},{3,7},{4,12},{5,13},{6,14},{7,15},{8,0},{9,1},{1... | collective-permute-start | bytes 786440 | tf_op jit(solution)/shard_map/ppermute | solution.py:37
  59.8 1.2 collective-permute-start.20
  61.0 1.8 %collective-permute-start.21 = (bf16[32,2048]{1,0:T(8,128)(2,1)S(1)}, bf16[32,2048]{1,0:T(8,128)(2,1)S(1)}, u32[]{:S(2)}, u32[]{:S(2)}) collective-permute-start(bf16[32,2048]{1,0:T(8,128)(2,1)S(1)} %get-tuple-element.126), channel_id=1, source_target_pairs={{0,3},{1,2},{2,1},{3,0},{4,7},{5,6},{6,5},{7,4},{8,11},{9,10},{10,... | collective-permute-start | bytes 393224 | tf_op jit(solution)/shard_map/ppermute | solution.py:47
  62.7 2.6 %experts.4 = (f32[128,2048]{1,0:T(8,128)S(1)}, bf16[128,2048]{1,0:T(8,128)(2,1)S(1)}, f32[8,128]{1,0:T(8,128)S(1)}) custom-call(bf16[128,2048]{1,0:T(8,128)(2,1)S(1)} %join_arrived.4.refs_0_, bf16[128,2048]{1,0:T(8,128)(2,1)S(1)} %collective-permute-done.17.refs_1_, bf16[704,2048]{1,0:T(8,128)(2,1)S(1)} %bitcast.15, bf16[704,2048]{1,0:T(8,128)(2,1)S(1)} %bitcast.19, ...), custom_call_target="tpu_custom_call" | custom-call | flops 2214592512 | bytes 11276288 | tf_op jit(solution)/shard_map/experts/pallas_call | solution.py:111
  65.4 1.5 %collective-permute-done.18.refs_1_ = bf16[64,2048]{1,0:T(8,128)(2,1)S(1)} collective-permute-done((bf16[64,2048]{1,0:T(8,128)(2,1)S(1)}, bf16[64,2048]{1,0:T(8,128)(2,1)S(1)}, u32[]{:S(2)}, u32[]{:S(2)}) %collective-permute-start.18) | collective-permute-done | bytes 262176 | tf_op jit(solution)/shard_map/ppermute | solution.py:37
  68.0 2.0 %collective-permute-start.23 = (bf16[64,2048]{1,0:T(8,128)(2,1)S(1)}, bf16[64,2048]{1,0:T(8,128)(2,1)S(1)}, u32[]{:S(2)}, u32[]{:S(2)}) collective-permute-start(bf16[64,2048]{1,0:T(8,128)(2,1)S(1)} %collective-permute-done.18.refs_1_), channel_id=1, source_target_pairs={{0,4},{1,5},{2,6},{3,7},{4,12},{5,13},{6,14},{7,15},{8,0},{9,1},{1... | collective-permute-start | bytes 786440 | tf_op jit(solution)/shard_map/ppermute | solution.py:37
  70.0 1.5 %collective-permute-start.24 = (bf16[32,2048]{1,0:T(8,128)(2,1)S(1)}, bf16[32,2048]{1,0:T(8,128)(2,1)S(1)}, u32[]{:S(2)}, u32[]{:S(2)}) collective-permute-start(bf16[32,2048]{1,0:T(8,128)(2,1)S(1)} %get-tuple-element.130), channel_id=1, source_target_pairs={{0,1},{1,0},{2,3},{3,2},{4,5},{5,4},{6,7},{7,6},{8,9},{9,8},{10,11... | collective-permute-start | bytes 393224 | tf_op jit(solution)/shard_map/ppermute | solution.py:47
  71.5 0.8 collective-permute-start.25
  72.3 1.2 collective-permute-start.26
  73.5 2.6 %experts.5 = (f32[128,2048]{1,0:T(8,128)S(1)}, bf16[128,2048]{1,0:T(8,128)(2,1)S(1)}, f32[8,128]{1,0:T(8,128)S(1)}) custom-call(bf16[128,2048]{1,0:T(8,128)(2,1)S(1)} %join_arrived.5.refs_0_, bf16[128,2048]{1,0:T(8,128)(2,1)S(1)} %collective-permute-done.22.refs_1_, bf16[704,2048]{1,0:T(8,128)(2,1)S(1)} %bitcast.16, bf16[704,2048]{1,0:T(8,128)(2,1)S(1)} %bitcast.20, ...), custom_call_target="tpu_custom_call" | custom-call | flops 2214592512 | bytes 11276288 | tf_op jit(solution)/shard_map/experts/pallas_call | solution.py:111
  76.1 1.4 %collective-permute-done.23.refs_1_.refs_3_ = bf16[64,2048]{1,0:T(8,128)(2,1)S(1)} collective-permute-done((bf16[64,2048]{1,0:T(8,128)(2,1)S(1)}, bf16[64,2048]{1,0:T(8,128)(2,1)S(1)}, u32[]{:S(2)}, u32[]{:S(2)}) %collective-permute-start.23) | collective-permute-done | bytes 262176 | tf_op jit(solution)/shard_map/ppermute | solution.py:37
  77.6 2.0 %collective-permute-done.25.refs_3_.refs_1_ = bf16[32,2048]{1,0:T(8,128)(2,1)S(1)} collective-permute-done((bf16[32,2048]{1,0:T(8,128)(2,1)S(1)}, bf16[32,2048]{1,0:T(8,128)(2,1)S(1)}, u32[]{:S(2)}, u32[]{:S(2)}) %collective-permute-start.25) | collective-permute-done | bytes 131104 | tf_op jit(solution)/shard_map/ppermute | solution.py:47
  80.8 0.7 collective-permute-done.28.refs_1_
  82.2 1.2 collective-permute-start.30
  83.4 1.8 %collective-permute-start.31 = (bf16[64,2048]{1,0:T(8,128)(2,1)S(1)}, bf16[64,2048]{1,0:T(8,128)(2,1)S(1)}, u32[]{:S(2)}, u32[]{:S(2)}) collective-permute-start(bf16[64,2048]{1,0:T(8,128)(2,1)S(1)} %get-tuple-element.143), channel_id=1, source_target_pairs={{0,3},{1,2},{2,1},{3,0},{4,7},{5,6},{6,5},{7,4},{8,11},{9,10},{10,... | collective-permute-start | bytes 786440 | tf_op jit(solution)/shard_map/ppermute | solution.py:47
  85.2 2.6 %experts.6 = (f32[128,2048]{1,0:T(8,128)S(1)}, bf16[128,2048]{1,0:T(8,128)(2,1)S(1)}, f32[8,128]{1,0:T(8,128)S(1)}) custom-call(bf16[128,2048]{1,0:T(8,128)(2,1)S(1)} %join_arrived.6.refs_0_, bf16[128,2048]{1,0:T(8,128)(2,1)S(1)} %collective-permute-done.27.refs_1_, bf16[704,2048]{1,0:T(8,128)(2,1)S(1)} %bitcast.17, bf16[704,2048]{1,0:T(8,128)(2,1)S(1)} %bitcast.21, ...), custom_call_target="tpu_custom_call" | custom-call | flops 2214592512 | bytes 11276288 | tf_op jit(solution)/shard_map/experts/pallas_call | solution.py:111
  87.8 3.0 %collective-permute-done.29.refs_2_.refs_0_ = bf16[64,2048]{1,0:T(8,128)(2,1)S(1)} collective-permute-done((bf16[64,2048]{1,0:T(8,128)(2,1)S(1)}, bf16[64,2048]{1,0:T(8,128)(2,1)S(1)}, u32[]{:S(2)}, u32[]{:S(2)}) %collective-permute-start.29) | collective-permute-done | bytes 262176 | tf_op jit(solution)/shard_map/ppermute | solution.py:47
  91.1 4.8 %collective-permute-done.31.refs_4_.refs_2_ = bf16[64,2048]{1,0:T(8,128)(2,1)S(1)} collective-permute-done((bf16[64,2048]{1,0:T(8,128)(2,1)S(1)}, bf16[64,2048]{1,0:T(8,128)(2,1)S(1)}, u32[]{:S(2)}, u32[]{:S(2)}) %collective-permute-start.31) | collective-permute-done | bytes 262176 | tf_op jit(solution)/shard_map/ppermute | solution.py:47
  96.8 1.8 %collective-permute-start.37 = (bf16[64,2048]{1,0:T(8,128)(2,1)S(1)}, bf16[64,2048]{1,0:T(8,128)(2,1)S(1)}, u32[]{:S(2)}, u32[]{:S(2)}) collective-permute-start(bf16[64,2048]{1,0:T(8,128)(2,1)S(1)} %collect.3), channel_id=1, source_target_pairs={{0,4},{1,5},{2,6},{3,7},{4,12},{5,13},{6,14},{7,15},{8,0},{9,1},{1... | collective-permute-start | bytes 786440 | tf_op jit(solution)/shard_map/ppermute | solution.py:37
  98.7 0.8 collective-permute-start.34
  99.5 1.0 collective-permute-start.35
  100.5 1.8 %collective-permute-start.36 = (bf16[32,2048]{1,0:T(8,128)(2,1)S(1)}, bf16[32,2048]{1,0:T(8,128)(2,1)S(1)}, u32[]{:S(2)}, u32[]{:S(2)}) collective-permute-start(bf16[32,2048]{1,0:T(8,128)(2,1)S(1)} %get-tuple-element.149), channel_id=1, source_target_pairs={{0,3},{1,2},{2,1},{3,0},{4,7},{5,6},{6,5},{7,4},{8,11},{9,10},{10,... | collective-permute-start | bytes 393224 | tf_op jit(solution)/shard_map/ppermute | solution.py:47
  102.2 3.1 %experts.7 = (f32[128,2048]{1,0:T(8,128)S(1)}, bf16[128,2048]{1,0:T(8,128)(2,1)S(1)}, f32[8,128]{1,0:T(8,128)}) custom-call(bf16[128,2048]{1,0:T(8,128)(2,1)S(1)} %join_arrived.7.refs_0_, bf16[128,2048]{1,0:T(8,128)(2,1)S(1)} %collective-permute-done.32.refs_1_, bf16[704,2048]{1,0:T(8,128)(2,1)S(1)} %bitcast.18, bf16[704,2048]{1,0:T(8,128)(2,1)S(1)} %bitcast.22, ...), custom_call_target="tpu_custom_call" | custom-call | flops 2214592512 | bytes 11276288 | tf_op jit(solution)/shard_map/experts/pallas_call | solution.py:111
  105.3 0.9 collective-permute-done.37.refs_3_.refs_5_
  106.2 1.3 %collective-permute-done.35.refs_1_.refs_3_ = bf16[32,2048]{1,0:T(8,128)(2,1)S(1)} collective-permute-done((bf16[32,2048]{1,0:T(8,128)(2,1)S(1)}, bf16[32,2048]{1,0:T(8,128)(2,1)S(1)}, u32[]{:S(2)}, u32[]{:S(2)}) %collective-permute-start.35) | collective-permute-done | bytes 131104 | tf_op jit(solution)/shard_map/ppermute | solution.py:47
  109.5 1.1 collective-permute-start.39
  110.6 0.8 collective-permute-start.40
  111.4 1.6 %collective-permute-start.41 = (bf16[32,2048]{1,0:T(8,128)(2,1)S(1)}, bf16[32,2048]{1,0:T(8,128)(2,1)S(1)}, u32[]{:S(2)}, u32[]{:S(2)}) collective-permute-start(bf16[32,2048]{1,0:T(8,128)(2,1)S(1)} %get-tuple-element.154), channel_id=1, source_target_pairs={{0,3},{1,2},{2,1},{3,0},{4,7},{5,6},{6,5},{7,4},{8,11},{9,10},{10,... | collective-permute-start | bytes 393224 | tf_op jit(solution)/shard_map/ppermute | solution.py:47
  113.1 4.5 %collective-permute-done.42.refs_5_ = bf16[64,2048]{1,0:T(8,128)(2,1)S(1)} collective-permute-done((bf16[64,2048]{1,0:T(8,128)(2,1)S(1)}, bf16[64,2048]{1,0:T(8,128)(2,1)S(1)}, u32[]{:S(2)}, u32[]{:S(2)}) %collective-permute-start.42) | collective-permute-done | bytes 262176 | tf_op jit(solution)/shard_map/ppermute | solution.py:37
  117.5 1.1 collective-permute-done.40.refs_3_
  118.9 1.1 collective-permute-start.47
  120.8 1.2 collective-permute-start.45
  121.9 1.8 %collective-permute-start.46 = (bf16[32,2048]{1,0:T(8,128)(2,1)S(1)}, bf16[32,2048]{1,0:T(8,128)(2,1)S(1)}, u32[]{:S(2)}, u32[]{:S(2)}) collective-permute-start(bf16[32,2048]{1,0:T(8,128)(2,1)S(1)} %get-tuple-element.161), channel_id=1, source_target_pairs={{0,3},{1,2},{2,1},{3,0},{4,7},{5,6},{6,5},{7,4},{8,11},{9,10},{10,... | collective-permute-start | bytes 393224 | tf_op jit(solution)/shard_map/ppermute | solution.py:47
  123.7 2.4 %collective-permute-done.44.refs_4_ = bf16[32,2048]{1,0:T(8,128)(2,1)S(1)} collective-permute-done((bf16[32,2048]{1,0:T(8,128)(2,1)S(1)}, bf16[32,2048]{1,0:T(8,128)(2,1)S(1)}, u32[]{:S(2)}, u32[]{:S(2)}) %collective-permute-start.44) | collective-permute-done | bytes 131104 | tf_op jit(solution)/shard_map/ppermute | solution.py:47
  126.1 2.2 %collective-permute-done.45.refs_5_ = bf16[32,2048]{1,0:T(8,128)(2,1)S(1)} collective-permute-done((bf16[32,2048]{1,0:T(8,128)(2,1)S(1)}, bf16[32,2048]{1,0:T(8,128)(2,1)S(1)}, u32[]{:S(2)}, u32[]{:S(2)}) %collective-permute-start.45) | collective-permute-done | bytes 131104 | tf_op jit(solution)/shard_map/ppermute | solution.py:47
  128.8 1.5 %collective-permute-done.48.refs_5_ = bf16[64,2048]{1,0:T(8,128)(2,1)S(1)} collective-permute-done((bf16[64,2048]{1,0:T(8,128)(2,1)S(1)}, bf16[64,2048]{1,0:T(8,128)(2,1)S(1)}, u32[]{:S(2)}, u32[]{:S(2)}) %collective-permute-start.48) | collective-permute-done | bytes 262176 | tf_op jit(solution)/shard_map/ppermute | solution.py:57
  130.3 2.3 %project.1 = (bf16[128,1536]{1,0:T(8,128)(2,1)}, bf16[288,128]{1,0:T(8,128)(2,1)}, bf16[64,2048]{1,0:T(8,128)(2,1)}) custom-call(bf16[128,128]{1,0:T(8,128)(2,1)S(1)} %get-tuple-element.86.order_ref.refs_0_, bf16[2048,1536]{1,0:T(8,128)(2,1)S(1)} %bitcast.28, bf16[288,2048]{1,0:T(8,128)(2,1)S(1)} %bitcast.29, ...), custom_call_target="tpu_custom_call" | custom-call | flops 1000000000 | bytes 9019392 | tf_op jit(solution)/shard_map/project/pallas_call | solution.py:111
  (111 shorter events, 12.5 us)
Async XLA Ops:
  0.6 43.8 %copy-start = (bf16[128,2048]{1,0:T(8,128)(2,1)S(1)}, bf16[128,2048]{1,0:T(8,128)(2,1)}, u32[]{:S(2)}) copy-start(bf16[128,2048]{1,0:T(8,128)(2,1)} %param.21) | copy-start | bytes 1572868
  2.5 11.6 %collective-permute-start.1 = (bf16[64,640]{1,0:T(8,128)(2,1)}, bf16[64,640]{1,0:T(8,128)(2,1)S(1)}, u32[]{:S(2)}, u32[]{:S(2)}) collective-permute-start(bf16[64,640]{1,0:T(8,128)(2,1)} %get-tuple-element.90), channel_id=1, source_target_pairs={{0,8},{1,9},{2,10},{3,11},{4,12},{5,13},{6,14},{7,15},{8,0},{9,1},... | collective-permute-start | bytes 245768 | tf_op jit(solution)/shard_map/ppermute | solution.py:42
  6.5 7.6 %collective-permute-start.2 = (bf16[64,640]{1,0:T(8,128)(2,1)}, bf16[64,640]{1,0:T(8,128)(2,1)S(1)}, u32[]{:S(2)}, u32[]{:S(2)}) collective-permute-start(bf16[64,640]{1,0:T(8,128)(2,1)} %get-tuple-element.90), channel_id=1, source_target_pairs={{0,12},{1,13},{2,14},{3,15},{4,0},{5,1},{6,2},{7,3},{8,4},{9,5},{1... | collective-permute-start | bytes 245768 | tf_op jit(solution)/shard_map/ppermute | solution.py:42
  7.9 7.7 %collective-permute-start = (bf16[128,640]{1,0:T(8,128)(2,1)}, bf16[128,640]{1,0:T(8,128)(2,1)S(1)}, u32[]{:S(2)}, u32[]{:S(2)}) collective-permute-start(bf16[128,640]{1,0:T(8,128)(2,1)} %get-tuple-element.85.refs_0_.refs_1_), channel_id=1, source_target_pairs={{0,4},{1,5},{2,6},{3,7},{4,8},{5,9},{6,10},{7,11},{8,12},{9,13},{1... | collective-permute-start | bytes 491528 | tf_op jit(solution)/shard_map/ppermute | solution.py:42
  8.6 0.9 copy-start.8
  13.1 5.8 %copy-start.9 = (bf16[8,128,512]{2,1,0:T(8,128)(2,1)S(1)}, bf16[8,128,512]{2,1,0:T(8,128)(2,1)}, u32[]{:S(2)}) copy-start(bf16[8,128,512]{2,1,0:T(8,128)(2,1)} %key_up_ref.1) | copy-start | bytes 3145732
  13.1 5.8 %copy-start.10 = (bf16[128,1536]{1,0:T(8,128)(2,1)S(1)}, bf16[128,1536]{1,0:T(8,128)(2,1)}, u32[]{:S(2)}) copy-start(bf16[128,1536]{1,0:T(8,128)(2,1)} %query_ref.1) | copy-start | bytes 1179652
  15.8 3.2 %collective-permute-start.3 = (bf16[384,640]{1,0:T(8,128)(2,1)S(1)}, bf16[384,640]{1,0:T(8,128)(2,1)S(1)}, u32[]{:S(2)}, u32[]{:S(2)}) collective-permute-start(bf16[384,640]{1,0:T(8,128)(2,1)S(1)} %get-tuple-element.91.refs_0_), channel_id=1, source_target_pairs={{0,16},{16,0},{1,17},{17,1},{2,18},{18,2},{3,19},{19,3},{4,20},{20... | collective-permute-start | bytes 1474568 | tf_op jit(solution)/shard_map/ppermute | solution.py:57
  15.8 11.9 %collective-permute-start.4 = (bf16[320,640]{1,0:T(8,128)(2,1)S(1)}, bf16[320,640]{1,0:T(8,128)(2,1)S(1)}, u32[]{:S(2)}, u32[]{:S(2)}) collective-permute-start(bf16[320,640]{1,0:T(8,128)(2,1)S(1)} %get-tuple-element.98), channel_id=1, source_target_pairs={{0,1},{1,0},{2,3},{3,2},{4,5},{5,4},{6,7},{7,6},{8,9},{9,8},{10,11... | collective-permute-start | bytes 1228808 | tf_op jit(solution)/shard_map/ppermute | solution.py:47
  17.4 11.5 %collective-permute-start.5 = (bf16[320,640]{1,0:T(8,128)(2,1)S(1)}, bf16[320,640]{1,0:T(8,128)(2,1)S(1)}, u32[]{:S(2)}, u32[]{:S(2)}) collective-permute-start(bf16[320,640]{1,0:T(8,128)(2,1)S(1)} %get-tuple-element.99), channel_id=1, source_target_pairs={{0,2},{1,3},{2,0},{3,1},{4,6},{5,7},{6,4},{7,5},{8,10},{9,11},{10,... | collective-permute-start | bytes 1228808 | tf_op jit(solution)/shard_map/ppermute | solution.py:47
  28.9 2.7 %collective-permute-start.6 = (bf16[320,640]{1,0:T(8,128)(2,1)S(1)}, bf16[320,640]{1,0:T(8,128)(2,1)S(1)}, u32[]{:S(2)}, u32[]{:S(2)}) collective-permute-start(bf16[320,640]{1,0:T(8,128)(2,1)S(1)} %get-tuple-element.100.refs_0_.refs_1_), channel_id=1, source_target_pairs={{0,16},{16,0},{1,17},{17,1},{2,18},{18,2},{3,19},{19,3},{4,20},{20... | collective-permute-start | bytes 1228808 | tf_op jit(solution)/shard_map/ppermute | solution.py:57
  28.9 2.7 %collective-permute-start.7 = (bf16[320,640]{1,0:T(8,128)(2,1)S(1)}, bf16[320,640]{1,0:T(8,128)(2,1)S(1)}, u32[]{:S(2)}, u32[]{:S(2)}) collective-permute-start(bf16[320,640]{1,0:T(8,128)(2,1)S(1)} %get-tuple-element.101.refs_1_.refs_0_), channel_id=1, source_target_pairs={{0,16},{16,0},{1,17},{17,1},{2,18},{18,2},{3,19},{19,3},{4,20},{20... | collective-permute-start | bytes 1228808 | tf_op jit(solution)/shard_map/ppermute | solution.py:57
  29.5 7.9 %collective-permute-start.8 = (bf16[160,640]{1,0:T(8,128)(2,1)S(1)}, bf16[160,640]{1,0:T(8,128)(2,1)S(1)}, u32[]{:S(2)}, u32[]{:S(2)}) collective-permute-start(bf16[160,640]{1,0:T(8,128)(2,1)S(1)} %get-tuple-element.106), channel_id=1, source_target_pairs={{0,1},{1,0},{2,3},{3,2},{4,5},{5,4},{6,7},{7,6},{8,9},{9,8},{10,11... | collective-permute-start | bytes 614408 | tf_op jit(solution)/shard_map/ppermute | solution.py:47
  30.1 7.3 %collective-permute-start.9 = (bf16[160,640]{1,0:T(8,128)(2,1)S(1)}, bf16[160,640]{1,0:T(8,128)(2,1)S(1)}, u32[]{:S(2)}, u32[]{:S(2)}) collective-permute-start(bf16[160,640]{1,0:T(8,128)(2,1)S(1)} %get-tuple-element.107), channel_id=1, source_target_pairs={{0,2},{1,3},{2,0},{3,1},{4,6},{5,7},{6,4},{7,5},{8,10},{9,11},{10,... | collective-permute-start | bytes 614408 | tf_op jit(solution)/shard_map/ppermute | solution.py:47
  31.6 7.6 %copy-start.4 = (bf16[1024,2048]{1,0:T(8,128)(2,1)S(1)}, bf16[1024,2048]{1,0:T(8,128)(2,1)}, u32[]{:S(2)}) copy-start(bf16[1024,2048]{1,0:T(8,128)(2,1)} %output_ref.1) | copy-start | bytes 12582916
  31.6 7.6 %copy-start.6 = (bf16[8,512,128]{2,1,0:T(8,128)(2,1)S(1)}, bf16[8,512,128]{2,1,0:T(8,128)(2,1)}, u32[]{:S(2)}) copy-start(bf16[8,512,128]{2,1,0:T(8,128)(2,1)} %value_up_ref.1) | copy-start | bytes 3145732
  37.4 1.5 %collective-permute-start.10 = (bf16[160,640]{1,0:T(8,128)(2,1)S(1)}, bf16[160,640]{1,0:T(8,128)(2,1)S(1)}, u32[]{:S(2)}, u32[]{:S(2)}) collective-permute-start(bf16[160,640]{1,0:T(8,128)(2,1)S(1)} %get-tuple-element.108.refs_0_), channel_id=1, source_target_pairs={{0,16},{16,0},{1,17},{17,1},{2,18},{18,2},{3,19},{19,3},{4,20},{20... | collective-permute-start | bytes 614408 | tf_op jit(solution)/shard_map/ppermute | solution.py:57
  37.5 1.7 %collective-permute-start.11 = (bf16[160,640]{1,0:T(8,128)(2,1)S(1)}, bf16[160,640]{1,0:T(8,128)(2,1)S(1)}, u32[]{:S(2)}, u32[]{:S(2)}) collective-permute-start(bf16[160,640]{1,0:T(8,128)(2,1)S(1)} %get-tuple-element.109.refs_1_), channel_id=1, source_target_pairs={{0,16},{16,0},{1,17},{17,1},{2,18},{18,2},{3,19},{19,3},{4,20},{20... | collective-permute-start | bytes 614408 | tf_op jit(solution)/shard_map/ppermute | solution.py:57
  39.2 5.2 %copy-start.16 = (bf16[2048]{0:T(1024)(128)(2,1)S(1)}, bf16[2048]{0:T(1024)(128)(2,1)}, u32[]{:S(2)}) copy-start(bf16[2048]{0:T(1024)(128)(2,1)} %param.28) | copy-start | bytes 12292
  39.2 6.5 %copy-start.7 = (bf16[2048,16]{0,1:T(8,128)(2,1)S(1)}, bf16[2048,16]{0,1:T(8,128)(2,1)}, u32[]{:S(2)}) copy-start(bf16[2048,16]{0,1:T(8,128)(2,1)} %param.29) | copy-start | bytes 196612
  44.1 1.6 %collective-permute-start.12 = (bf16[64,2048]{1,0:T(8,128)(2,1)S(1)}, bf16[64,2048]{1,0:T(8,128)(2,1)S(1)}, u32[]{:S(2)}, u32[]{:S(2)}) collective-permute-start(bf16[64,2048]{1,0:T(8,128)(2,1)S(1)} %get-tuple-element.111), channel_id=1, source_target_pairs={{0,16},{16,0},{1,17},{17,1},{2,18},{18,2},{3,19},{19,3},{4,20},{20... | collective-permute-start | bytes 786440 | tf_op jit(solution)/shard_map/ppermute | solution.py:57
  45.7 17.0 %copy-start.1 = (bf16[1,2048,704]{1,2,0:T(8,128)(2,1)S(1)}, bf16[1,2048,704]{1,2,0:T(8,128)(2,1)}, u32[]{:S(2)}) copy-start(bf16[1,2048,704]{1,2,0:T(8,128)(2,1)} %param.30) | copy-start | bytes 8650756
  45.7 17.0 %copy-start.2 = (bf16[1,2048,704]{1,2,0:T(8,128)(2,1)S(1)}, bf16[1,2048,704]{1,2,0:T(8,128)(2,1)}, u32[]{:S(2)}) copy-start(bf16[1,2048,704]{1,2,0:T(8,128)(2,1)} %param.31) | copy-start | bytes 8650756
  45.7 17.0 %copy-start.3 = (bf16[1,704,2048]{2,1,0:T(8,128)(2,1)S(1)}, bf16[1,704,2048]{2,1,0:T(8,128)(2,1)}, u32[]{:S(2)}) copy-start(bf16[1,704,2048]{2,1,0:T(8,128)(2,1)} %param.32) | copy-start | bytes 8650756
  46.3 10.0 %collective-permute-start.13 = (bf16[64,2048]{1,0:T(8,128)(2,1)S(1)}, bf16[64,2048]{1,0:T(8,128)(2,1)S(1)}, u32[]{:S(2)}, u32[]{:S(2)}) collective-permute-start(bf16[64,2048]{1,0:T(8,128)(2,1)S(1)} %get-tuple-element.115), channel_id=1, source_target_pairs={{0,4},{1,5},{2,6},{3,7},{4,12},{5,13},{6,14},{7,15},{8,0},{9,1},{1... | collective-permute-start | bytes 786440 | tf_op jit(solution)/shard_map/ppermute | solution.py:37
  47.8 9.1 %collective-permute-start.14 = (bf16[32,2048]{1,0:T(8,128)(2,1)S(1)}, bf16[32,2048]{1,0:T(8,128)(2,1)S(1)}, u32[]{:S(2)}, u32[]{:S(2)}) collective-permute-start(bf16[32,2048]{1,0:T(8,128)(2,1)S(1)} %get-tuple-element.118), channel_id=1, source_target_pairs={{0,1},{1,0},{2,3},{3,2},{4,5},{5,4},{6,7},{7,6},{8,9},{9,8},{10,11... | collective-permute-start | bytes 393224 | tf_op jit(solution)/shard_map/ppermute | solution.py:47
  49.3 7.9 %collective-permute-start.15 = (bf16[32,2048]{1,0:T(8,128)(2,1)S(1)}, bf16[32,2048]{1,0:T(8,128)(2,1)S(1)}, u32[]{:S(2)}, u32[]{:S(2)}) collective-permute-start(bf16[32,2048]{1,0:T(8,128)(2,1)S(1)} %get-tuple-element.119), channel_id=1, source_target_pairs={{0,2},{1,3},{2,0},{3,1},{4,6},{5,7},{6,4},{7,5},{8,10},{9,11},{10,... | collective-permute-start | bytes 393224 | tf_op jit(solution)/shard_map/ppermute | solution.py:47
  50.1 7.0 %collective-permute-start.16 = (bf16[32,2048]{1,0:T(8,128)(2,1)S(1)}, bf16[32,2048]{1,0:T(8,128)(2,1)S(1)}, u32[]{:S(2)}, u32[]{:S(2)}) collective-permute-start(bf16[32,2048]{1,0:T(8,128)(2,1)S(1)} %get-tuple-element.120), channel_id=1, source_target_pairs={{0,3},{1,2},{2,1},{3,0},{4,7},{5,6},{6,5},{7,4},{8,11},{9,10},{10,... | collective-permute-start | bytes 393224 | tf_op jit(solution)/shard_map/ppermute | solution.py:47
  57.2 5.5 %collective-permute-start.17 = (bf16[128,2048]{1,0:T(8,128)(2,1)S(1)}, bf16[128,2048]{1,0:T(8,128)(2,1)S(1)}, u32[]{:S(2)}, u32[]{:S(2)}) collective-permute-start(bf16[128,2048]{1,0:T(8,128)(2,1)S(1)} %join_arrived.4.refs_0_), channel_id=1, source_target_pairs={{0,16},{16,0},{1,17},{17,1},{2,18},{18,2},{3,19},{19,3},{4,20},{20... | collective-permute-start | bytes 1572872 | tf_op jit(solution)/shard_map/ppermute | solution.py:57
  57.3 9.6 %collective-permute-start.18 = (bf16[64,2048]{1,0:T(8,128)(2,1)S(1)}, bf16[64,2048]{1,0:T(8,128)(2,1)S(1)}, u32[]{:S(2)}, u32[]{:S(2)}) collective-permute-start(bf16[64,2048]{1,0:T(8,128)(2,1)S(1)} %collective-permute-done.13.refs_0_), channel_id=1, source_target_pairs={{0,4},{1,5},{2,6},{3,7},{4,12},{5,13},{6,14},{7,15},{8,0},{9,1},{1... | collective-permute-start | bytes 786440 | tf_op jit(solution)/shard_map/ppermute | solution.py:37
  59.2 8.2 %collective-permute-start.19 = (bf16[32,2048]{1,0:T(8,128)(2,1)S(1)}, bf16[32,2048]{1,0:T(8,128)(2,1)S(1)}, u32[]{:S(2)}, u32[]{:S(2)}) collective-permute-start(bf16[32,2048]{1,0:T(8,128)(2,1)S(1)} %get-tuple-element.124), channel_id=1, source_target_pairs={{0,1},{1,0},{2,3},{3,2},{4,5},{5,4},{6,7},{7,6},{8,9},{9,8},{10,11... | collective-permute-start | bytes 393224 | tf_op jit(solution)/shard_map/ppermute | solution.py:47
  59.8 7.7 %collective-permute-start.20 = (bf16[32,2048]{1,0:T(8,128)(2,1)S(1)}, bf16[32,2048]{1,0:T(8,128)(2,1)S(1)}, u32[]{:S(2)}, u32[]{:S(2)}) collective-permute-start(bf16[32,2048]{1,0:T(8,128)(2,1)S(1)} %get-tuple-element.125), channel_id=1, source_target_pairs={{0,2},{1,3},{2,0},{3,1},{4,6},{5,7},{6,4},{7,5},{8,10},{9,11},{10,... | collective-permute-start | bytes 393224 | tf_op jit(solution)/shard_map/ppermute | solution.py:47
  61.0 6.9 %collective-permute-start.21 = (bf16[32,2048]{1,0:T(8,128)(2,1)S(1)}, bf16[32,2048]{1,0:T(8,128)(2,1)S(1)}, u32[]{:S(2)}, u32[]{:S(2)}) collective-permute-start(bf16[32,2048]{1,0:T(8,128)(2,1)S(1)} %get-tuple-element.126), channel_id=1, source_target_pairs={{0,3},{1,2},{2,1},{3,0},{4,7},{5,6},{6,5},{7,4},{8,11},{9,10},{10,... | collective-permute-start | bytes 393224 | tf_op jit(solution)/shard_map/ppermute | solution.py:47
  67.9 5.6 %collective-permute-start.22 = (bf16[128,2048]{1,0:T(8,128)(2,1)S(1)}, bf16[128,2048]{1,0:T(8,128)(2,1)S(1)}, u32[]{:S(2)}, u32[]{:S(2)}) collective-permute-start(bf16[128,2048]{1,0:T(8,128)(2,1)S(1)} %join_arrived.5.refs_0_), channel_id=1, source_target_pairs={{0,16},{16,0},{1,17},{17,1},{2,18},{18,2},{3,19},{19,3},{4,20},{20... | collective-permute-start | bytes 1572872 | tf_op jit(solution)/shard_map/ppermute | solution.py:57
  68.0 9.6 %collective-permute-start.23 = (bf16[64,2048]{1,0:T(8,128)(2,1)S(1)}, bf16[64,2048]{1,0:T(8,128)(2,1)S(1)}, u32[]{:S(2)}, u32[]{:S(2)}) collective-permute-start(bf16[64,2048]{1,0:T(8,128)(2,1)S(1)} %collective-permute-done.18.refs_1_), channel_id=1, source_target_pairs={{0,4},{1,5},{2,6},{3,7},{4,12},{5,13},{6,14},{7,15},{8,0},{9,1},{1... | collective-permute-start | bytes 786440 | tf_op jit(solution)/shard_map/ppermute | solution.py:37
  70.0 7.6 %collective-permute-start.24 = (bf16[32,2048]{1,0:T(8,128)(2,1)S(1)}, bf16[32,2048]{1,0:T(8,128)(2,1)S(1)}, u32[]{:S(2)}, u32[]{:S(2)}) collective-permute-start(bf16[32,2048]{1,0:T(8,128)(2,1)S(1)} %get-tuple-element.130), channel_id=1, source_target_pairs={{0,1},{1,0},{2,3},{3,2},{4,5},{5,4},{6,7},{7,6},{8,9},{9,8},{10,11... | collective-permute-start | bytes 393224 | tf_op jit(solution)/shard_map/ppermute | solution.py:47
  71.5 8.1 %collective-permute-start.25 = (bf16[32,2048]{1,0:T(8,128)(2,1)S(1)}, bf16[32,2048]{1,0:T(8,128)(2,1)S(1)}, u32[]{:S(2)}, u32[]{:S(2)}) collective-permute-start(bf16[32,2048]{1,0:T(8,128)(2,1)S(1)} %get-tuple-element.131), channel_id=1, source_target_pairs={{0,2},{1,3},{2,0},{3,1},{4,6},{5,7},{6,4},{7,5},{8,10},{9,11},{10,... | collective-permute-start | bytes 393224 | tf_op jit(solution)/shard_map/ppermute | solution.py:47
  72.3 7.3 %collective-permute-start.26 = (bf16[32,2048]{1,0:T(8,128)(2,1)S(1)}, bf16[32,2048]{1,0:T(8,128)(2,1)S(1)}, u32[]{:S(2)}, u32[]{:S(2)}) collective-permute-start(bf16[32,2048]{1,0:T(8,128)(2,1)S(1)} %get-tuple-element.132), channel_id=1, source_target_pairs={{0,3},{1,2},{2,1},{3,0},{4,7},{5,6},{6,5},{7,4},{8,11},{9,10},{10,... | collective-permute-start | bytes 393224 | tf_op jit(solution)/shard_map/ppermute | solution.py:47
  79.6 1.9 %collective-permute-start.28 = (bf16[128,2048]{1,0:T(8,128)(2,1)S(1)}, bf16[128,2048]{1,0:T(8,128)(2,1)S(1)}, u32[]{:S(2)}, u32[]{:S(2)}) collective-permute-start(bf16[128,2048]{1,0:T(8,128)(2,1)S(1)} %pass_on.7), channel_id=1, source_target_pairs={{0,16},{16,0},{1,17},{17,1},{2,18},{18,2},{3,19},{19,3},{4,20},{20... | collective-permute-start | bytes 1572872 | tf_op jit(solution)/shard_map/ppermute | solution.py:57
  80.2 5.0 %collective-permute-start.27 = (bf16[128,2048]{1,0:T(8,128)(2,1)S(1)}, bf16[128,2048]{1,0:T(8,128)(2,1)S(1)}, u32[]{:S(2)}, u32[]{:S(2)}) collective-permute-start(bf16[128,2048]{1,0:T(8,128)(2,1)S(1)} %join_arrived.6.refs_0_), channel_id=1, source_target_pairs={{0,16},{16,0},{1,17},{17,1},{2,18},{18,2},{3,19},{19,3},{4,20},{20... | collective-permute-start | bytes 1572872 | tf_op jit(solution)/shard_map/ppermute | solution.py:57
  81.6 9.2 %collective-permute-start.29 = (bf16[64,2048]{1,0:T(8,128)(2,1)S(1)}, bf16[64,2048]{1,0:T(8,128)(2,1)S(1)}, u32[]{:S(2)}, u32[]{:S(2)}) collective-permute-start(bf16[64,2048]{1,0:T(8,128)(2,1)S(1)} %get-tuple-element.141), channel_id=1, source_target_pairs={{0,1},{1,0},{2,3},{3,2},{4,5},{5,4},{6,7},{7,6},{8,9},{9,8},{10,11... | collective-permute-start | bytes 786440 | tf_op jit(solution)/shard_map/ppermute | solution.py:47
  82.2 8.9 %collective-permute-start.30 = (bf16[64,2048]{1,0:T(8,128)(2,1)S(1)}, bf16[64,2048]{1,0:T(8,128)(2,1)S(1)}, u32[]{:S(2)}, u32[]{:S(2)}) collective-permute-start(bf16[64,2048]{1,0:T(8,128)(2,1)S(1)} %get-tuple-element.142), channel_id=1, source_target_pairs={{0,2},{1,3},{2,0},{3,1},{4,6},{5,7},{6,4},{7,5},{8,10},{9,11},{10,... | collective-permute-start | bytes 786440 | tf_op jit(solution)/shard_map/ppermute | solution.py:47
  83.4 12.5 %collective-permute-start.31 = (bf16[64,2048]{1,0:T(8,128)(2,1)S(1)}, bf16[64,2048]{1,0:T(8,128)(2,1)S(1)}, u32[]{:S(2)}, u32[]{:S(2)}) collective-permute-start(bf16[64,2048]{1,0:T(8,128)(2,1)S(1)} %get-tuple-element.143), channel_id=1, source_target_pairs={{0,3},{1,2},{2,1},{3,0},{4,7},{5,6},{6,5},{7,4},{8,11},{9,10},{10,... | collective-permute-start | bytes 786440 | tf_op jit(solution)/shard_map/ppermute | solution.py:47
  95.9 2.6 %collective-permute-start.33 = (bf16[128,2048]{1,0:T(8,128)(2,1)S(1)}, bf16[128,2048]{1,0:T(8,128)(2,1)S(1)}, u32[]{:S(2)}, u32[]{:S(2)}) collective-permute-start(bf16[128,2048]{1,0:T(8,128)(2,1)S(1)} %pass_on.8), channel_id=1, source_target_pairs={{0,16},{16,0},{1,17},{17,1},{2,18},{18,2},{3,19},{19,3},{4,20},{20... | collective-permute-start | bytes 1572872 | tf_op jit(solution)/shard_map/ppermute | solution.py:57
  96.0 6.3 %collective-permute-start.32 = (bf16[128,2048]{1,0:T(8,128)(2,1)S(1)}, bf16[128,2048]{1,0:T(8,128)(2,1)S(1)}, u32[]{:S(2)}, u32[]{:S(2)}) collective-permute-start(bf16[128,2048]{1,0:T(8,128)(2,1)S(1)} %join_arrived.7.refs_0_), channel_id=1, source_target_pairs={{0,16},{16,0},{1,17},{17,1},{2,18},{18,2},{3,19},{19,3},{4,20},{20... | collective-permute-start | bytes 1572872 | tf_op jit(solution)/shard_map/ppermute | solution.py:57
  96.8 9.4 %collective-permute-start.37 = (bf16[64,2048]{1,0:T(8,128)(2,1)S(1)}, bf16[64,2048]{1,0:T(8,128)(2,1)S(1)}, u32[]{:S(2)}, u32[]{:S(2)}) collective-permute-start(bf16[64,2048]{1,0:T(8,128)(2,1)S(1)} %collect.3), channel_id=1, source_target_pairs={{0,4},{1,5},{2,6},{3,7},{4,12},{5,13},{6,14},{7,15},{8,0},{9,1},{1... | collective-permute-start | bytes 786440 | tf_op jit(solution)/shard_map/ppermute | solution.py:37
  98.7 7.5 %collective-permute-start.34 = (bf16[32,2048]{1,0:T(8,128)(2,1)S(1)}, bf16[32,2048]{1,0:T(8,128)(2,1)S(1)}, u32[]{:S(2)}, u32[]{:S(2)}) collective-permute-start(bf16[32,2048]{1,0:T(8,128)(2,1)S(1)} %get-tuple-element.147), channel_id=1, source_target_pairs={{0,1},{1,0},{2,3},{3,2},{4,5},{5,4},{6,7},{7,6},{8,9},{9,8},{10,11... | collective-permute-start | bytes 393224 | tf_op jit(solution)/shard_map/ppermute | solution.py:47
  99.5 8.1 %collective-permute-start.35 = (bf16[32,2048]{1,0:T(8,128)(2,1)S(1)}, bf16[32,2048]{1,0:T(8,128)(2,1)S(1)}, u32[]{:S(2)}, u32[]{:S(2)}) collective-permute-start(bf16[32,2048]{1,0:T(8,128)(2,1)S(1)} %get-tuple-element.148), channel_id=1, source_target_pairs={{0,2},{1,3},{2,0},{3,1},{4,6},{5,7},{6,4},{7,5},{8,10},{9,11},{10,... | collective-permute-start | bytes 393224 | tf_op jit(solution)/shard_map/ppermute | solution.py:47
  100.5 29.8 %slice-start = ((s8[6291456]{0:T(1024)(128)(4,1)}), s8[4194304]{0:T(1024)(128)(4,1)S(1)}, s32[]{:S(2)}) async-start(s8[6291456]{0:T(1024)(128)(4,1)} %bitcast.27), calls=%async_computation | async-start | bytes 8388608
  100.5 29.8 %slice-start.1 = ((s8[6291456]{0:T(1024)(128)(4,1)}), s8[2097152]{0:T(1024)(128)(4,1)S(1)}, s32[]{:S(2)}) async-start(s8[6291456]{0:T(1024)(128)(4,1)} %bitcast.27), calls=%async_computation.1 | async-start | bytes 4194304
  100.5 7.1 %collective-permute-start.36 = (bf16[32,2048]{1,0:T(8,128)(2,1)S(1)}, bf16[32,2048]{1,0:T(8,128)(2,1)S(1)}, u32[]{:S(2)}, u32[]{:S(2)}) collective-permute-start(bf16[32,2048]{1,0:T(8,128)(2,1)S(1)} %get-tuple-element.149), channel_id=1, source_target_pairs={{0,3},{1,2},{2,1},{3,0},{4,7},{5,6},{6,5},{7,4},{8,11},{9,10},{10,... | collective-permute-start | bytes 393224 | tf_op jit(solution)/shard_map/ppermute | solution.py:47
  107.5 16.2 %copy-start.17 = (bf16[2048]{0:T(1024)(128)(2,1)S(1)}, bf16[2048]{0:T(1024)(128)(2,1)}, u32[]{:S(2)}) copy-start(bf16[2048]{0:T(1024)(128)(2,1)} %param.33) | copy-start | bytes 12292
  107.5 1.9 %collective-permute-start.38 = (bf16[128,2048]{1,0:T(8,128)(2,1)S(1)}, bf16[128,2048]{1,0:T(8,128)(2,1)S(1)}, u32[]{:S(2)}, u32[]{:S(2)}) collective-permute-start(bf16[128,2048]{1,0:T(8,128)(2,1)S(1)} %pass_on.9), channel_id=1, source_target_pairs={{0,16},{16,0},{1,17},{17,1},{2,18},{18,2},{3,19},{19,3},{4,20},{20... | collective-permute-start | bytes 1572872 | tf_op jit(solution)/shard_map/ppermute | solution.py:57
  107.5 12.5 %collective-permute-start.43 = (bf16[128,2048]{1,0:T(8,128)(2,1)S(1)}, bf16[128,2048]{1,0:T(8,128)(2,1)S(1)}, u32[]{:S(2)}, u32[]{:S(2)}) collective-permute-start(bf16[128,2048]{1,0:T(8,128)(2,1)S(1)} %get-tuple-element.157), channel_id=1, source_target_pairs={{0,16},{16,0},{1,17},{17,1},{2,18},{18,2},{3,19},{19,3},{4,20},{20... | collective-permute-start | bytes 1572872 | tf_op jit(solution)/shard_map/ppermute | solution.py:57
  108.3 22.0 %copy-start.5 = (bf16[2048,288]{0,1:T(8,128)(2,1)S(1)}, bf16[2048,288]{0,1:T(8,128)(2,1)}, u32[]{:S(2)}) copy-start(bf16[2048,288]{0,1:T(8,128)(2,1)} %param.35) | copy-start | bytes 3538948
  108.3 9.2 %collective-permute-start.42 = (bf16[64,2048]{1,0:T(8,128)(2,1)S(1)}, bf16[64,2048]{1,0:T(8,128)(2,1)S(1)}, u32[]{:S(2)}, u32[]{:S(2)}) collective-permute-start(bf16[64,2048]{1,0:T(8,128)(2,1)S(1)} %collect.4), channel_id=1, source_target_pairs={{0,4},{1,5},{2,6},{3,7},{4,12},{5,13},{6,14},{7,15},{8,0},{9,1},{1... | collective-permute-start | bytes 786440 | tf_op jit(solution)/shard_map/ppermute | solution.py:37
  109.5 8.0 %collective-permute-start.39 = (bf16[32,2048]{1,0:T(8,128)(2,1)S(1)}, bf16[32,2048]{1,0:T(8,128)(2,1)S(1)}, u32[]{:S(2)}, u32[]{:S(2)}) collective-permute-start(bf16[32,2048]{1,0:T(8,128)(2,1)S(1)} %get-tuple-element.152), channel_id=1, source_target_pairs={{0,1},{1,0},{2,3},{3,2},{4,5},{5,4},{6,7},{7,6},{8,9},{9,8},{10,11... | collective-permute-start | bytes 393224 | tf_op jit(solution)/shard_map/ppermute | solution.py:47
  110.6 8.1 %collective-permute-start.40 = (bf16[32,2048]{1,0:T(8,128)(2,1)S(1)}, bf16[32,2048]{1,0:T(8,128)(2,1)S(1)}, u32[]{:S(2)}, u32[]{:S(2)}) collective-permute-start(bf16[32,2048]{1,0:T(8,128)(2,1)S(1)} %get-tuple-element.153), channel_id=1, source_target_pairs={{0,2},{1,3},{2,0},{3,1},{4,6},{5,7},{6,4},{7,5},{8,10},{9,11},{10,... | collective-permute-start | bytes 393224 | tf_op jit(solution)/shard_map/ppermute | solution.py:47
  111.4 7.2 %collective-permute-start.41 = (bf16[32,2048]{1,0:T(8,128)(2,1)S(1)}, bf16[32,2048]{1,0:T(8,128)(2,1)S(1)}, u32[]{:S(2)}, u32[]{:S(2)}) collective-permute-start(bf16[32,2048]{1,0:T(8,128)(2,1)S(1)} %get-tuple-element.154), channel_id=1, source_target_pairs={{0,3},{1,2},{2,1},{3,0},{4,7},{5,6},{6,5},{7,4},{8,11},{9,10},{10,... | collective-permute-start | bytes 393224 | tf_op jit(solution)/shard_map/ppermute | solution.py:47
  118.9 9.3 %collective-permute-start.47 = (bf16[64,2048]{1,0:T(8,128)(2,1)S(1)}, bf16[64,2048]{1,0:T(8,128)(2,1)S(1)}, u32[]{:S(2)}, u32[]{:S(2)}) collective-permute-start(bf16[64,2048]{1,0:T(8,128)(2,1)S(1)} %collect.5.refs_0_), channel_id=1, source_target_pairs={{0,4},{1,5},{2,6},{3,7},{4,12},{5,13},{6,14},{7,15},{8,0},{9,1},{1... | collective-permute-start | bytes 786440 | tf_op jit(solution)/shard_map/ppermute | solution.py:37
  120.1 6.0 %collective-permute-start.44 = (bf16[32,2048]{1,0:T(8,128)(2,1)S(1)}, bf16[32,2048]{1,0:T(8,128)(2,1)S(1)}, u32[]{:S(2)}, u32[]{:S(2)}) collective-permute-start(bf16[32,2048]{1,0:T(8,128)(2,1)S(1)} %get-tuple-element.159), channel_id=1, source_target_pairs={{0,1},{1,0},{2,3},{3,2},{4,5},{5,4},{6,7},{7,6},{8,9},{9,8},{10,11... | collective-permute-start | bytes 393224 | tf_op jit(solution)/shard_map/ppermute | solution.py:47
  120.8 7.5 %collective-permute-start.45 = (bf16[32,2048]{1,0:T(8,128)(2,1)S(1)}, bf16[32,2048]{1,0:T(8,128)(2,1)S(1)}, u32[]{:S(2)}, u32[]{:S(2)}) collective-permute-start(bf16[32,2048]{1,0:T(8,128)(2,1)S(1)} %get-tuple-element.160), channel_id=1, source_target_pairs={{0,2},{1,3},{2,0},{3,1},{4,6},{5,7},{6,4},{7,5},{8,10},{9,11},{10,... | collective-permute-start | bytes 393224 | tf_op jit(solution)/shard_map/ppermute | solution.py:47
  121.9 6.3 %collective-permute-start.46 = (bf16[32,2048]{1,0:T(8,128)(2,1)S(1)}, bf16[32,2048]{1,0:T(8,128)(2,1)S(1)}, u32[]{:S(2)}, u32[]{:S(2)}) collective-permute-start(bf16[32,2048]{1,0:T(8,128)(2,1)S(1)} %get-tuple-element.161), channel_id=1, source_target_pairs={{0,3},{1,2},{2,1},{3,0},{4,7},{5,6},{6,5},{7,4},{8,11},{9,10},{10,... | collective-permute-start | bytes 393224 | tf_op jit(solution)/shard_map/ppermute | solution.py:47
  128.7 1.6 %collective-permute-start.48 = (bf16[64,2048]{1,0:T(8,128)(2,1)S(1)}, bf16[64,2048]{1,0:T(8,128)(2,1)S(1)}, u32[]{:S(2)}, u32[]{:S(2)}) collective-permute-start(bf16[64,2048]{1,0:T(8,128)(2,1)S(1)} %get-tuple-element.163.refs_4_), channel_id=1, source_target_pairs={{0,16},{16,0},{1,17},{17,1},{2,18},{18,2},{3,19},{19,3},{4,20},{20... | collective-permute-start | bytes 786440 | tf_op jit(solution)/shard_map/ppermute | solution.py:57
  (5 other events, 3.5 us)

commit v7 on v6

--- a/solution.py
+++ b/solution.py
@@ -828,7 +828,7 @@
         back = step - 2 if step - 2 < ring else 0
         if step >= 3:
             own, other, _ = results[back]
-            if back:
+            if back in (1, ring - 1):
                 along_z = [block] if step <= ring - 1 else [landed] if step > 4 else []
                 other = pass_on([other], arrived[1:] + along_z)[0]
             others = [

time: 133 us -> 132 us (level)
  no operation moved by 1% of the time
where the time goes in v7:
time: 132 us
  starting transfers between devices  47.4 us (36%)
  waiting for transfers between devices  43.8 us (33%)
  Pallas kernels  35 us (27%)
  local copies, waits for them, and re-layouts  4.56 us (3%)
    ppermute x25, starting transfers between devices, send_plane(): return lax.ppermute(block, 'tensor', [(i, i ^ distance) for i in devices])  29.9 us
    ppermute x25, waiting for transfers between devices, send_plane(): return lax.ppermute(block, 'tensor', [(i, i ^ distance) for i in devices])  24 us
    pallas_call x24, Pallas kernels, call(): pl.pallas_call(after(kernel, len(ready)), **places, out_shape=shapes, com...  19.3 us
    pallas_call x3, Pallas kernels, attend_call(): pl.pallas_call(kernel, in_specs=resident(inputs), out_specs=resident(shap...  14.6 us
    ppermute x6, waiting for transfers between devices, send_ring(): return lax.ppermute(block, 'tensor', route)  13.7 us
    ppermute x6, starting transfers between devices, send_ring(): return lax.ppermute(block, 'tensor', route)  8.59 us
    ppermute x3, starting transfers between devices, send_round(): lax.ppermute(block, 'tensor', [(i, (i + distance) % count) for i in range...  6.06 us
    ppermute x15, waiting for transfers between devices, send_group(): return lax.ppermute(block, 'group', [(i, i ^ distance) for i in devices])  4.66 us
  transfers between devices with their start and end apart: 49, of which 24 were waited for; matrix products, arithmetic and copies ran while one was open for 0% of the time, Pallas kernels for 19%

profile of v7, /device:TPU:0, one launch (start us, length us, event | category | flops | bytes accessed | tf_op | source)
XLA Modules:
  0.0 132.0 jit_solution(5537832200585146248)
XLA Ops:
  0.6 1.9 %join_share.1 = (bf16[128,640]{1,0:T(8,128)(2,1)}, bf16[64,640]{1,0:T(8,128)(2,1)}) custom-call(bf16[64,576]{1,0:T(8,128)(2,1)} %refs_0_.1, bf16[576,128]{1,0:T(8,128)(2,1)} %bitcast.35, s32[6,2,64]{2,1,0:T(2,128)} %bitcast.36), custom_call_target="tpu_custom_call" | custom-call | flops 10000000 | bytes 470016 | tf_op jit(solution)/shard_map/join_share/pallas_call | solution.py:111
  2.5 4.0 %collective-permute-start.1 = (bf16[64,640]{1,0:T(8,128)(2,1)}, bf16[64,640]{1,0:T(8,128)(2,1)S(1)}, u32[]{:S(2)}, u32[]{:S(2)}) collective-permute-start(bf16[64,640]{1,0:T(8,128)(2,1)} %get-tuple-element.90), channel_id=1, source_target_pairs={{0,8},{1,9},{2,10},{3,11},{4,12},{5,13},{6,14},{7,15},{8,0},{9,1},... | collective-permute-start | bytes 245768 | tf_op jit(solution)/shard_map/ppermute | solution.py:42
  6.5 1.3 %collective-permute-start.2 = (bf16[64,640]{1,0:T(8,128)(2,1)}, bf16[64,640]{1,0:T(8,128)(2,1)S(1)}, u32[]{:S(2)}, u32[]{:S(2)}) collective-permute-start(bf16[64,640]{1,0:T(8,128)(2,1)} %get-tuple-element.90), channel_id=1, source_target_pairs={{0,12},{1,13},{2,14},{3,15},{4,0},{5,1},{6,2},{7,3},{8,4},{9,5},{1... | collective-permute-start | bytes 245768 | tf_op jit(solution)/shard_map/ppermute | solution.py:42
  7.9 0.7 collective-permute-start
  8.6 0.9 copy-done.8
  9.5 0.7 copy-done.11
  10.2 0.7 copy-done.12
  10.9 0.7 copy-done.13
  11.5 0.7 copy-done.14
  12.2 0.9 copy-done.15
  13.1 1.1 make_plan.1
  14.2 1.5 %collective-permute-done.refs_2_ = bf16[128,640]{1,0:T(8,128)(2,1)S(1)} collective-permute-done((bf16[128,640]{1,0:T(8,128)(2,1)}, bf16[128,640]{1,0:T(8,128)(2,1)S(1)}, u32[]{:S(2)}, u32[]{:S(2)}) %collective-permute-start) | collective-permute-done | bytes 163872 | tf_op jit(solution)/shard_map/ppermute | solution.py:42
  15.8 1.6 %collective-permute-start.4 = (bf16[320,640]{1,0:T(8,128)(2,1)S(1)}, bf16[320,640]{1,0:T(8,128)(2,1)S(1)}, u32[]{:S(2)}, u32[]{:S(2)}) collective-permute-start(bf16[320,640]{1,0:T(8,128)(2,1)S(1)} %get-tuple-element.98), channel_id=1, source_target_pairs={{0,1},{1,0},{2,3},{3,2},{4,5},{5,4},{6,7},{7,6},{8,9},{9,8},{10,11... | collective-permute-start | bytes 1228808 | tf_op jit(solution)/shard_map/ppermute | solution.py:47
  17.4 1.5 %collective-permute-start.5 = (bf16[320,640]{1,0:T(8,128)(2,1)S(1)}, bf16[320,640]{1,0:T(8,128)(2,1)S(1)}, u32[]{:S(2)}, u32[]{:S(2)}) collective-permute-start(bf16[320,640]{1,0:T(8,128)(2,1)S(1)} %get-tuple-element.99), channel_id=1, source_target_pairs={{0,2},{1,3},{2,0},{3,1},{4,6},{5,7},{6,4},{7,5},{8,10},{9,11},{10,... | collective-permute-start | bytes 1228808 | tf_op jit(solution)/shard_map/ppermute | solution.py:47
  18.9 4.0 %attend_near.1 = (bf16[1024,640]{1,0:T(8,128)(2,1)S(1)}, f32[1024,1]{1,0:T(8,128)S(1)}, f32[1024,1]{1,0:T(8,128)S(1)}, f32[1024,512]{1,0:T(8,128)S(1)}, f32[8,128]{1,0:T(8,128)S(1)}) custom-call(s32[128,4]{1,0:T(8,128)S(1)} %get-tuple-element.87.token_ref, s32[1,768]{1,0:T(1,128)S(1)} %get-tuple-element.89.refs_0_.spot_ref, ...), custom_call_target="tpu_custom_call" | custom-call | flops 1711276032 | bytes 8000000 | tf_op jit(solution)/shard_map/attend_near/pallas_call | solution.py:367
  22.9 4.8 %collective-permute-done.4.refs_1_ = bf16[320,640]{1,0:T(8,128)(2,1)S(1)} collective-permute-done((bf16[320,640]{1,0:T(8,128)(2,1)S(1)}, bf16[320,640]{1,0:T(8,128)(2,1)S(1)}, u32[]{:S(2)}, u32[]{:S(2)}) %collective-permute-start.4) | collective-permute-done | bytes 409632 | tf_op jit(solution)/shard_map/ppermute | solution.py:47
  27.7 1.2 collective-permute-done.5.refs_2_
  30.1 1.5 %collective-permute-start.9 = (bf16[160,640]{1,0:T(8,128)(2,1)S(1)}, bf16[160,640]{1,0:T(8,128)(2,1)S(1)}, u32[]{:S(2)}, u32[]{:S(2)}) collective-permute-start(bf16[160,640]{1,0:T(8,128)(2,1)S(1)} %get-tuple-element.107), channel_id=1, source_target_pairs={{0,2},{1,3},{2,0},{3,1},{4,6},{5,7},{6,4},{7,5},{8,10},{9,11},{10,... | collective-permute-start | bytes 614408 | tf_op jit(solution)/shard_map/ppermute | solution.py:47
  31.6 5.7 %attend_mid.1 = (f32[1024,1]{1,0:T(8,128)S(1)}, f32[1024,1]{1,0:T(8,128)S(1)}, f32[1024,512]{1,0:T(8,128)S(1)}, f32[8,128]{1,0:T(8,128)S(1)}) custom-call(s32[128,4]{1,0:T(8,128)S(1)} %get-tuple-element.87.token_ref, s32[1,1280]{1,0:T(1,128)S(1)} %get-tuple-element.93.spot_ref, bf16[1024,640]{1,0:T(8,128)(2,1)S(1)} %get-tuple-element.92.wide_ref, ...), custom_call_target="tpu_custom_call" | custom-call | flops 2852126720 | bytes 8000000 | tf_op jit(solution)/shard_map/attend_mid/pallas_call | solution.py:367
  38.0 0.9 collective-permute-done.10.refs_2_
  39.2 4.9 %attend_far.1 = (f32[64,2048]{1,0:T(8,128)S(1)}, bf16[64,2048]{1,0:T(8,128)(2,1)S(1)}) custom-call(s32[128,4]{1,0:T(8,128)S(1)} %get-tuple-element.87.token_ref, s32[1,640]{1,0:T(1,128)S(1)} %get-tuple-element.88.spot_ref, bf16[1024,640]{1,0:T(8,128)(2,1)S(1)} %get-tuple-element.92.wide_ref, f32[1024,1]{1,0:T(8,128)S(1)} %get-tuple-element.102.best_ref, ...), custom_call_target="tpu_custom_call" | custom-call | flops 1426063360 | bytes 8000000 | tf_op jit(solution)/shard_map/attend_far/pallas_call | solution.py:367
  44.7 1.1 collective-permute-done.12.refs_2_
  46.3 1.5 %collective-permute-start.13 = (bf16[64,2048]{1,0:T(8,128)(2,1)S(1)}, bf16[64,2048]{1,0:T(8,128)(2,1)S(1)}, u32[]{:S(2)}, u32[]{:S(2)}) collective-permute-start(bf16[64,2048]{1,0:T(8,128)(2,1)S(1)} %get-tuple-element.115), channel_id=1, source_target_pairs={{0,4},{1,5},{2,6},{3,7},{4,12},{5,13},{6,14},{7,15},{8,0},{9,1},{1... | collective-permute-start | bytes 786440 | tf_op jit(solution)/shard_map/ppermute | solution.py:37
  47.8 1.5 %collective-permute-start.14 = (bf16[32,2048]{1,0:T(8,128)(2,1)S(1)}, bf16[32,2048]{1,0:T(8,128)(2,1)S(1)}, u32[]{:S(2)}, u32[]{:S(2)}) collective-permute-start(bf16[32,2048]{1,0:T(8,128)(2,1)S(1)} %get-tuple-element.118), channel_id=1, source_target_pairs={{0,1},{1,0},{2,3},{3,2},{4,5},{5,4},{6,7},{7,6},{8,9},{9,8},{10,11... | collective-permute-start | bytes 393224 | tf_op jit(solution)/shard_map/ppermute | solution.py:47
  49.3 0.8 collective-permute-start.15
  50.1 1.2 collective-permute-start.16
  51.3 5.0 %collective-permute-done.13.refs_0_ = bf16[64,2048]{1,0:T(8,128)(2,1)S(1)} collective-permute-done((bf16[64,2048]{1,0:T(8,128)(2,1)S(1)}, bf16[64,2048]{1,0:T(8,128)(2,1)S(1)}, u32[]{:S(2)}, u32[]{:S(2)}) %collective-permute-start.13) | collective-permute-done | bytes 262176 | tf_op jit(solution)/shard_map/ppermute | solution.py:37
  57.3 1.9 %collective-permute-start.18 = (bf16[64,2048]{1,0:T(8,128)(2,1)S(1)}, bf16[64,2048]{1,0:T(8,128)(2,1)S(1)}, u32[]{:S(2)}, u32[]{:S(2)}) collective-permute-start(bf16[64,2048]{1,0:T(8,128)(2,1)S(1)} %collective-permute-done.13.refs_0_), channel_id=1, source_target_pairs={{0,4},{1,5},{2,6},{3,7},{4,12},{5,13},{6,14},{7,15},{8,0},{9,1},{1... | collective-permute-start | bytes 786440 | tf_op jit(solution)/shard_map/ppermute | solution.py:37
  59.8 1.2 collective-permute-start.20
  61.0 1.8 %collective-permute-start.21 = (bf16[32,2048]{1,0:T(8,128)(2,1)S(1)}, bf16[32,2048]{1,0:T(8,128)(2,1)S(1)}, u32[]{:S(2)}, u32[]{:S(2)}) collective-permute-start(bf16[32,2048]{1,0:T(8,128)(2,1)S(1)} %get-tuple-element.126), channel_id=1, source_target_pairs={{0,3},{1,2},{2,1},{3,0},{4,7},{5,6},{6,5},{7,4},{8,11},{9,10},{10,... | collective-permute-start | bytes 393224 | tf_op jit(solution)/shard_map/ppermute | solution.py:47
  62.8 2.6 %experts.4 = (f32[128,2048]{1,0:T(8,128)S(1)}, bf16[128,2048]{1,0:T(8,128)(2,1)S(1)}, f32[8,128]{1,0:T(8,128)S(1)}) custom-call(bf16[128,2048]{1,0:T(8,128)(2,1)S(1)} %join_arrived.4.refs_0_, bf16[128,2048]{1,0:T(8,128)(2,1)S(1)} %collective-permute-done.17.refs_1_, bf16[704,2048]{1,0:T(8,128)(2,1)S(1)} %bitcast.15, bf16[704,2048]{1,0:T(8,128)(2,1)S(1)} %bitcast.19, ...), custom_call_target="tpu_custom_call" | custom-call | flops 2214592512 | bytes 11276288 | tf_op jit(solution)/shard_map/experts/pallas_call | solution.py:111
  65.4 1.5 %collective-permute-done.18.refs_1_ = bf16[64,2048]{1,0:T(8,128)(2,1)S(1)} collective-permute-done((bf16[64,2048]{1,0:T(8,128)(2,1)S(1)}, bf16[64,2048]{1,0:T(8,128)(2,1)S(1)}, u32[]{:S(2)}, u32[]{:S(2)}) %collective-permute-start.18) | collective-permute-done | bytes 262176 | tf_op jit(solution)/shard_map/ppermute | solution.py:37
  68.0 2.0 %collective-permute-start.23 = (bf16[64,2048]{1,0:T(8,128)(2,1)S(1)}, bf16[64,2048]{1,0:T(8,128)(2,1)S(1)}, u32[]{:S(2)}, u32[]{:S(2)}) collective-permute-start(bf16[64,2048]{1,0:T(8,128)(2,1)S(1)} %collective-permute-done.18.refs_1_), channel_id=1, source_target_pairs={{0,4},{1,5},{2,6},{3,7},{4,12},{5,13},{6,14},{7,15},{8,0},{9,1},{1... | collective-permute-start | bytes 786440 | tf_op jit(solution)/shard_map/ppermute | solution.py:37
  70.0 1.5 %collective-permute-start.24 = (bf16[32,2048]{1,0:T(8,128)(2,1)S(1)}, bf16[32,2048]{1,0:T(8,128)(2,1)S(1)}, u32[]{:S(2)}, u32[]{:S(2)}) collective-permute-start(bf16[32,2048]{1,0:T(8,128)(2,1)S(1)} %get-tuple-element.130), channel_id=1, source_target_pairs={{0,1},{1,0},{2,3},{3,2},{4,5},{5,4},{6,7},{7,6},{8,9},{9,8},{10,11... | collective-permute-start | bytes 393224 | tf_op jit(solution)/shard_map/ppermute | solution.py:47
  71.5 0.8 collective-permute-start.25
  72.3 1.2 collective-permute-start.26
  73.5 2.6 %experts.5 = (f32[128,2048]{1,0:T(8,128)S(1)}, bf16[128,2048]{1,0:T(8,128)(2,1)S(1)}, f32[8,128]{1,0:T(8,128)S(1)}) custom-call(bf16[128,2048]{1,0:T(8,128)(2,1)S(1)} %join_arrived.5.refs_0_, bf16[128,2048]{1,0:T(8,128)(2,1)S(1)} %collective-permute-done.22.refs_1_, bf16[704,2048]{1,0:T(8,128)(2,1)S(1)} %bitcast.16, bf16[704,2048]{1,0:T(8,128)(2,1)S(1)} %bitcast.20, ...), custom_call_target="tpu_custom_call" | custom-call | flops 2214592512 | bytes 11276288 | tf_op jit(solution)/shard_map/experts/pallas_call | solution.py:111
  76.2 1.4 %collective-permute-done.23.refs_1_.refs_3_ = bf16[64,2048]{1,0:T(8,128)(2,1)S(1)} collective-permute-done((bf16[64,2048]{1,0:T(8,128)(2,1)S(1)}, bf16[64,2048]{1,0:T(8,128)(2,1)S(1)}, u32[]{:S(2)}, u32[]{:S(2)}) %collective-permute-start.23) | collective-permute-done | bytes 262176 | tf_op jit(solution)/shard_map/ppermute | solution.py:37
  77.6 2.0 %collective-permute-done.25.refs_3_.refs_1_ = bf16[32,2048]{1,0:T(8,128)(2,1)S(1)} collective-permute-done((bf16[32,2048]{1,0:T(8,128)(2,1)S(1)}, bf16[32,2048]{1,0:T(8,128)(2,1)S(1)}, u32[]{:S(2)}, u32[]{:S(2)}) %collective-permute-start.25) | collective-permute-done | bytes 131104 | tf_op jit(solution)/shard_map/ppermute | solution.py:47
  80.8 0.7 collective-permute-done.28.refs_1_
  82.2 1.2 collective-permute-start.30
  83.4 1.8 %collective-permute-start.31 = (bf16[64,2048]{1,0:T(8,128)(2,1)S(1)}, bf16[64,2048]{1,0:T(8,128)(2,1)S(1)}, u32[]{:S(2)}, u32[]{:S(2)}) collective-permute-start(bf16[64,2048]{1,0:T(8,128)(2,1)S(1)} %get-tuple-element.143), channel_id=1, source_target_pairs={{0,3},{1,2},{2,1},{3,0},{4,7},{5,6},{6,5},{7,4},{8,11},{9,10},{10,... | collective-permute-start | bytes 786440 | tf_op jit(solution)/shard_map/ppermute | solution.py:47
  85.2 2.6 %experts.6 = (f32[128,2048]{1,0:T(8,128)S(1)}, bf16[128,2048]{1,0:T(8,128)(2,1)S(1)}, f32[8,128]{1,0:T(8,128)S(1)}) custom-call(bf16[128,2048]{1,0:T(8,128)(2,1)S(1)} %join_arrived.6.refs_0_, bf16[128,2048]{1,0:T(8,128)(2,1)S(1)} %collective-permute-done.27.refs_1_, bf16[704,2048]{1,0:T(8,128)(2,1)S(1)} %bitcast.17, bf16[704,2048]{1,0:T(8,128)(2,1)S(1)} %bitcast.21, ...), custom_call_target="tpu_custom_call" | custom-call | flops 2214592512 | bytes 11276288 | tf_op jit(solution)/shard_map/experts/pallas_call | solution.py:111
  87.9 2.9 %collective-permute-done.29.refs_2_ = bf16[64,2048]{1,0:T(8,128)(2,1)S(1)} collective-permute-done((bf16[64,2048]{1,0:T(8,128)(2,1)S(1)}, bf16[64,2048]{1,0:T(8,128)(2,1)S(1)}, u32[]{:S(2)}, u32[]{:S(2)}) %collective-permute-start.29) | collective-permute-done | bytes 262176 | tf_op jit(solution)/shard_map/ppermute | solution.py:47
  91.1 4.8 %collective-permute-done.31.refs_4_ = bf16[64,2048]{1,0:T(8,128)(2,1)S(1)} collective-permute-done((bf16[64,2048]{1,0:T(8,128)(2,1)S(1)}, bf16[64,2048]{1,0:T(8,128)(2,1)S(1)}, u32[]{:S(2)}, u32[]{:S(2)}) %collective-permute-start.31) | collective-permute-done | bytes 262176 | tf_op jit(solution)/shard_map/ppermute | solution.py:47
  96.3 1.8 %collective-permute-start.37 = (bf16[64,2048]{1,0:T(8,128)(2,1)S(1)}, bf16[64,2048]{1,0:T(8,128)(2,1)S(1)}, u32[]{:S(2)}, u32[]{:S(2)}) collective-permute-start(bf16[64,2048]{1,0:T(8,128)(2,1)S(1)} %collect.3), channel_id=1, source_target_pairs={{0,4},{1,5},{2,6},{3,7},{4,12},{5,13},{6,14},{7,15},{8,0},{9,1},{1... | collective-permute-start | bytes 786440 | tf_op jit(solution)/shard_map/ppermute | solution.py:37
  98.8 1.2 collective-permute-start.35
  100.0 1.8 %collective-permute-start.36 = (bf16[32,2048]{1,0:T(8,128)(2,1)S(1)}, bf16[32,2048]{1,0:T(8,128)(2,1)S(1)}, u32[]{:S(2)}, u32[]{:S(2)}) collective-permute-start(bf16[32,2048]{1,0:T(8,128)(2,1)S(1)} %get-tuple-element.149), channel_id=1, source_target_pairs={{0,3},{1,2},{2,1},{3,0},{4,7},{5,6},{6,5},{7,4},{8,11},{9,10},{10,... | collective-permute-start | bytes 393224 | tf_op jit(solution)/shard_map/ppermute | solution.py:47
  101.7 3.1 %experts.7 = (f32[128,2048]{1,0:T(8,128)S(1)}, bf16[128,2048]{1,0:T(8,128)(2,1)S(1)}, f32[8,128]{1,0:T(8,128)}) custom-call(bf16[128,2048]{1,0:T(8,128)(2,1)S(1)} %join_arrived.7.refs_0_, bf16[128,2048]{1,0:T(8,128)(2,1)S(1)} %collective-permute-done.32.refs_1_, bf16[704,2048]{1,0:T(8,128)(2,1)S(1)} %bitcast.18, bf16[704,2048]{1,0:T(8,128)(2,1)S(1)} %bitcast.22, ...), custom_call_target="tpu_custom_call" | custom-call | flops 2214592512 | bytes 11276288 | tf_op jit(solution)/shard_map/experts/pallas_call | solution.py:111
  104.8 1.4 %collective-permute-done.37.refs_3_.refs_5_ = bf16[64,2048]{1,0:T(8,128)(2,1)S(1)} collective-permute-done((bf16[64,2048]{1,0:T(8,128)(2,1)S(1)}, bf16[64,2048]{1,0:T(8,128)(2,1)S(1)}, u32[]{:S(2)}, u32[]{:S(2)}) %collective-permute-start.37) | collective-permute-done | bytes 262176 | tf_op jit(solution)/shard_map/ppermute | solution.py:37
  106.2 0.8 collective-permute-done.36.refs_2_.refs_4_
  107.7 1.0 collective-permute-start.42
  108.9 1.5 %collective-permute-start.39 = (bf16[32,2048]{1,0:T(8,128)(2,1)S(1)}, bf16[32,2048]{1,0:T(8,128)(2,1)S(1)}, u32[]{:S(2)}, u32[]{:S(2)}) collective-permute-start(bf16[32,2048]{1,0:T(8,128)(2,1)S(1)} %get-tuple-element.152), channel_id=1, source_target_pairs={{0,1},{1,0},{2,3},{3,2},{4,5},{5,4},{6,7},{7,6},{8,9},{9,8},{10,11... | collective-permute-start | bytes 393224 | tf_op jit(solution)/shard_map/ppermute | solution.py:47
  110.5 0.8 collective-permute-start.40
  111.3 1.2 collective-permute-start.41
  112.5 4.4 %collective-permute-done.42.refs_5_ = bf16[64,2048]{1,0:T(8,128)(2,1)S(1)} collective-permute-done((bf16[64,2048]{1,0:T(8,128)(2,1)S(1)}, bf16[64,2048]{1,0:T(8,128)(2,1)S(1)}, u32[]{:S(2)}, u32[]{:S(2)}) %collective-permute-start.42) | collective-permute-done | bytes 262176 | tf_op jit(solution)/shard_map/ppermute | solution.py:37
  116.9 1.7 %collective-permute-done.40.refs_3_ = bf16[32,2048]{1,0:T(8,128)(2,1)S(1)} collective-permute-done((bf16[32,2048]{1,0:T(8,128)(2,1)S(1)}, bf16[32,2048]{1,0:T(8,128)(2,1)S(1)}, u32[]{:S(2)}, u32[]{:S(2)}) %collective-permute-start.40) | collective-permute-done | bytes 131104 | tf_op jit(solution)/shard_map/ppermute | solution.py:47
  119.3 1.4 %collective-permute-start.44 = (bf16[32,2048]{1,0:T(8,128)(2,1)S(1)}, bf16[32,2048]{1,0:T(8,128)(2,1)S(1)}, u32[]{:S(2)}, u32[]{:S(2)}) collective-permute-start(bf16[32,2048]{1,0:T(8,128)(2,1)S(1)} %get-tuple-element.159), channel_id=1, source_target_pairs={{0,1},{1,0},{2,3},{3,2},{4,5},{5,4},{6,7},{7,6},{8,9},{9,8},{10,11... | collective-permute-start | bytes 393224 | tf_op jit(solution)/shard_map/ppermute | solution.py:47
  120.6 0.8 collective-permute-start.45
  121.5 1.3 %collective-permute-start.46 = (bf16[32,2048]{1,0:T(8,128)(2,1)S(1)}, bf16[32,2048]{1,0:T(8,128)(2,1)S(1)}, u32[]{:S(2)}, u32[]{:S(2)}) collective-permute-start(bf16[32,2048]{1,0:T(8,128)(2,1)S(1)} %get-tuple-element.161), channel_id=1, source_target_pairs={{0,3},{1,2},{2,1},{3,0},{4,7},{5,6},{6,5},{7,4},{8,11},{9,10},{10,... | collective-permute-start | bytes 393224 | tf_op jit(solution)/shard_map/ppermute | solution.py:47
  122.8 2.4 %collective-permute-done.44.refs_4_ = bf16[32,2048]{1,0:T(8,128)(2,1)S(1)} collective-permute-done((bf16[32,2048]{1,0:T(8,128)(2,1)S(1)}, bf16[32,2048]{1,0:T(8,128)(2,1)S(1)}, u32[]{:S(2)}, u32[]{:S(2)}) %collective-permute-start.44) | collective-permute-done | bytes 131104 | tf_op jit(solution)/shard_map/ppermute | solution.py:47
  125.2 2.4 %collective-permute-done.45.refs_5_ = bf16[32,2048]{1,0:T(8,128)(2,1)S(1)} collective-permute-done((bf16[32,2048]{1,0:T(8,128)(2,1)S(1)}, bf16[32,2048]{1,0:T(8,128)(2,1)S(1)}, u32[]{:S(2)}, u32[]{:S(2)}) %collective-permute-start.45) | collective-permute-done | bytes 131104 | tf_op jit(solution)/shard_map/ppermute | solution.py:47
  128.2 1.5 %collective-permute-done.48.refs_5_ = bf16[64,2048]{1,0:T(8,128)(2,1)S(1)} collective-permute-done((bf16[64,2048]{1,0:T(8,128)(2,1)S(1)}, bf16[64,2048]{1,0:T(8,128)(2,1)S(1)}, u32[]{:S(2)}, u32[]{:S(2)}) %collective-permute-start.48) | collective-permute-done | bytes 262176 | tf_op jit(solution)/shard_map/ppermute | solution.py:57
  129.7 2.3 %project.1 = (bf16[128,1536]{1,0:T(8,128)(2,1)}, bf16[288,128]{1,0:T(8,128)(2,1)}, bf16[64,2048]{1,0:T(8,128)(2,1)}) custom-call(bf16[128,128]{1,0:T(8,128)(2,1)S(1)} %get-tuple-element.86.order_ref.refs_0_, bf16[2048,1536]{1,0:T(8,128)(2,1)S(1)} %bitcast.28, bf16[288,2048]{1,0:T(8,128)(2,1)S(1)} %bitcast.29, ...), custom_call_target="tpu_custom_call" | custom-call | flops 1000000000 | bytes 9019392 | tf_op jit(solution)/shard_map/project/pallas_call | solution.py:111
  (110 shorter events, 11.4 us)
Async XLA Ops:
  0.6 43.8 %copy-start = (bf16[128,2048]{1,0:T(8,128)(2,1)S(1)}, bf16[128,2048]{1,0:T(8,128)(2,1)}, u32[]{:S(2)}) copy-start(bf16[128,2048]{1,0:T(8,128)(2,1)} %param.21) | copy-start | bytes 1572868
  2.5 11.6 %collective-permute-start.1 = (bf16[64,640]{1,0:T(8,128)(2,1)}, bf16[64,640]{1,0:T(8,128)(2,1)S(1)}, u32[]{:S(2)}, u32[]{:S(2)}) collective-permute-start(bf16[64,640]{1,0:T(8,128)(2,1)} %get-tuple-element.90), channel_id=1, source_target_pairs={{0,8},{1,9},{2,10},{3,11},{4,12},{5,13},{6,14},{7,15},{8,0},{9,1},... | collective-permute-start | bytes 245768 | tf_op jit(solution)/shard_map/ppermute | solution.py:42
  6.5 7.6 %collective-permute-start.2 = (bf16[64,640]{1,0:T(8,128)(2,1)}, bf16[64,640]{1,0:T(8,128)(2,1)S(1)}, u32[]{:S(2)}, u32[]{:S(2)}) collective-permute-start(bf16[64,640]{1,0:T(8,128)(2,1)} %get-tuple-element.90), channel_id=1, source_target_pairs={{0,12},{1,13},{2,14},{3,15},{4,0},{5,1},{6,2},{7,3},{8,4},{9,5},{1... | collective-permute-start | bytes 245768 | tf_op jit(solution)/shard_map/ppermute | solution.py:42
  7.9 7.7 %collective-permute-start = (bf16[128,640]{1,0:T(8,128)(2,1)}, bf16[128,640]{1,0:T(8,128)(2,1)S(1)}, u32[]{:S(2)}, u32[]{:S(2)}) collective-permute-start(bf16[128,640]{1,0:T(8,128)(2,1)} %get-tuple-element.85.refs_0_.refs_1_), channel_id=1, source_target_pairs={{0,4},{1,5},{2,6},{3,7},{4,8},{5,9},{6,10},{7,11},{8,12},{9,13},{1... | collective-permute-start | bytes 491528 | tf_op jit(solution)/shard_map/ppermute | solution.py:42
  8.6 0.9 copy-start.8
  13.1 5.8 %copy-start.9 = (bf16[8,128,512]{2,1,0:T(8,128)(2,1)S(1)}, bf16[8,128,512]{2,1,0:T(8,128)(2,1)}, u32[]{:S(2)}) copy-start(bf16[8,128,512]{2,1,0:T(8,128)(2,1)} %key_up_ref.1) | copy-start | bytes 3145732
  13.1 5.8 %copy-start.10 = (bf16[128,1536]{1,0:T(8,128)(2,1)S(1)}, bf16[128,1536]{1,0:T(8,128)(2,1)}, u32[]{:S(2)}) copy-start(bf16[128,1536]{1,0:T(8,128)(2,1)} %query_ref.1) | copy-start | bytes 1179652
  15.8 3.2 %collective-permute-start.3 = (bf16[384,640]{1,0:T(8,128)(2,1)S(1)}, bf16[384,640]{1,0:T(8,128)(2,1)S(1)}, u32[]{:S(2)}, u32[]{:S(2)}) collective-permute-start(bf16[384,640]{1,0:T(8,128)(2,1)S(1)} %get-tuple-element.91.refs_0_), channel_id=1, source_target_pairs={{0,16},{16,0},{1,17},{17,1},{2,18},{18,2},{3,19},{19,3},{4,20},{20... | collective-permute-start | bytes 1474568 | tf_op jit(solution)/shard_map/ppermute | solution.py:57
  15.8 11.9 %collective-permute-start.4 = (bf16[320,640]{1,0:T(8,128)(2,1)S(1)}, bf16[320,640]{1,0:T(8,128)(2,1)S(1)}, u32[]{:S(2)}, u32[]{:S(2)}) collective-permute-start(bf16[320,640]{1,0:T(8,128)(2,1)S(1)} %get-tuple-element.98), channel_id=1, source_target_pairs={{0,1},{1,0},{2,3},{3,2},{4,5},{5,4},{6,7},{7,6},{8,9},{9,8},{10,11... | collective-permute-start | bytes 1228808 | tf_op jit(solution)/shard_map/ppermute | solution.py:47
  17.4 11.5 %collective-permute-start.5 = (bf16[320,640]{1,0:T(8,128)(2,1)S(1)}, bf16[320,640]{1,0:T(8,128)(2,1)S(1)}, u32[]{:S(2)}, u32[]{:S(2)}) collective-permute-start(bf16[320,640]{1,0:T(8,128)(2,1)S(1)} %get-tuple-element.99), channel_id=1, source_target_pairs={{0,2},{1,3},{2,0},{3,1},{4,6},{5,7},{6,4},{7,5},{8,10},{9,11},{10,... | collective-permute-start | bytes 1228808 | tf_op jit(solution)/shard_map/ppermute | solution.py:47
  28.9 2.7 %collective-permute-start.6 = (bf16[320,640]{1,0:T(8,128)(2,1)S(1)}, bf16[320,640]{1,0:T(8,128)(2,1)S(1)}, u32[]{:S(2)}, u32[]{:S(2)}) collective-permute-start(bf16[320,640]{1,0:T(8,128)(2,1)S(1)} %get-tuple-element.100.refs_0_.refs_1_), channel_id=1, source_target_pairs={{0,16},{16,0},{1,17},{17,1},{2,18},{18,2},{3,19},{19,3},{4,20},{20... | collective-permute-start | bytes 1228808 | tf_op jit(solution)/shard_map/ppermute | solution.py:57
  28.9 2.7 %collective-permute-start.7 = (bf16[320,640]{1,0:T(8,128)(2,1)S(1)}, bf16[320,640]{1,0:T(8,128)(2,1)S(1)}, u32[]{:S(2)}, u32[]{:S(2)}) collective-permute-start(bf16[320,640]{1,0:T(8,128)(2,1)S(1)} %get-tuple-element.101.refs_1_.refs_0_), channel_id=1, source_target_pairs={{0,16},{16,0},{1,17},{17,1},{2,18},{18,2},{3,19},{19,3},{4,20},{20... | collective-permute-start | bytes 1228808 | tf_op jit(solution)/shard_map/ppermute | solution.py:57
  29.5 7.9 %collective-permute-start.8 = (bf16[160,640]{1,0:T(8,128)(2,1)S(1)}, bf16[160,640]{1,0:T(8,128)(2,1)S(1)}, u32[]{:S(2)}, u32[]{:S(2)}) collective-permute-start(bf16[160,640]{1,0:T(8,128)(2,1)S(1)} %get-tuple-element.106), channel_id=1, source_target_pairs={{0,1},{1,0},{2,3},{3,2},{4,5},{5,4},{6,7},{7,6},{8,9},{9,8},{10,11... | collective-permute-start | bytes 614408 | tf_op jit(solution)/shard_map/ppermute | solution.py:47
  30.1 7.3 %collective-permute-start.9 = (bf16[160,640]{1,0:T(8,128)(2,1)S(1)}, bf16[160,640]{1,0:T(8,128)(2,1)S(1)}, u32[]{:S(2)}, u32[]{:S(2)}) collective-permute-start(bf16[160,640]{1,0:T(8,128)(2,1)S(1)} %get-tuple-element.107), channel_id=1, source_target_pairs={{0,2},{1,3},{2,0},{3,1},{4,6},{5,7},{6,4},{7,5},{8,10},{9,11},{10,... | collective-permute-start | bytes 614408 | tf_op jit(solution)/shard_map/ppermute | solution.py:47
  31.6 7.6 %copy-start.4 = (bf16[1024,2048]{1,0:T(8,128)(2,1)S(1)}, bf16[1024,2048]{1,0:T(8,128)(2,1)}, u32[]{:S(2)}) copy-start(bf16[1024,2048]{1,0:T(8,128)(2,1)} %output_ref.1) | copy-start | bytes 12582916
  31.6 7.6 %copy-start.6 = (bf16[8,512,128]{2,1,0:T(8,128)(2,1)S(1)}, bf16[8,512,128]{2,1,0:T(8,128)(2,1)}, u32[]{:S(2)}) copy-start(bf16[8,512,128]{2,1,0:T(8,128)(2,1)} %value_up_ref.1) | copy-start | bytes 3145732
  37.4 1.5 %collective-permute-start.10 = (bf16[160,640]{1,0:T(8,128)(2,1)S(1)}, bf16[160,640]{1,0:T(8,128)(2,1)S(1)}, u32[]{:S(2)}, u32[]{:S(2)}) collective-permute-start(bf16[160,640]{1,0:T(8,128)(2,1)S(1)} %get-tuple-element.108.refs_0_), channel_id=1, source_target_pairs={{0,16},{16,0},{1,17},{17,1},{2,18},{18,2},{3,19},{19,3},{4,20},{20... | collective-permute-start | bytes 614408 | tf_op jit(solution)/shard_map/ppermute | solution.py:57
  37.5 1.7 %collective-permute-start.11 = (bf16[160,640]{1,0:T(8,128)(2,1)S(1)}, bf16[160,640]{1,0:T(8,128)(2,1)S(1)}, u32[]{:S(2)}, u32[]{:S(2)}) collective-permute-start(bf16[160,640]{1,0:T(8,128)(2,1)S(1)} %get-tuple-element.109.refs_1_), channel_id=1, source_target_pairs={{0,16},{16,0},{1,17},{17,1},{2,18},{18,2},{3,19},{19,3},{4,20},{20... | collective-permute-start | bytes 614408 | tf_op jit(solution)/shard_map/ppermute | solution.py:57
  39.2 5.2 %copy-start.16 = (bf16[2048]{0:T(1024)(128)(2,1)S(1)}, bf16[2048]{0:T(1024)(128)(2,1)}, u32[]{:S(2)}) copy-start(bf16[2048]{0:T(1024)(128)(2,1)} %param.28) | copy-start | bytes 12292
  39.2 6.5 %copy-start.7 = (bf16[2048,16]{0,1:T(8,128)(2,1)S(1)}, bf16[2048,16]{0,1:T(8,128)(2,1)}, u32[]{:S(2)}) copy-start(bf16[2048,16]{0,1:T(8,128)(2,1)} %param.29) | copy-start | bytes 196612
  44.1 1.6 %collective-permute-start.12 = (bf16[64,2048]{1,0:T(8,128)(2,1)S(1)}, bf16[64,2048]{1,0:T(8,128)(2,1)S(1)}, u32[]{:S(2)}, u32[]{:S(2)}) collective-permute-start(bf16[64,2048]{1,0:T(8,128)(2,1)S(1)} %get-tuple-element.111), channel_id=1, source_target_pairs={{0,16},{16,0},{1,17},{17,1},{2,18},{18,2},{3,19},{19,3},{4,20},{20... | collective-permute-start | bytes 786440 | tf_op jit(solution)/shard_map/ppermute | solution.py:57
  45.7 17.0 %copy-start.1 = (bf16[1,2048,704]{1,2,0:T(8,128)(2,1)S(1)}, bf16[1,2048,704]{1,2,0:T(8,128)(2,1)}, u32[]{:S(2)}) copy-start(bf16[1,2048,704]{1,2,0:T(8,128)(2,1)} %param.30) | copy-start | bytes 8650756
  45.7 17.0 %copy-start.2 = (bf16[1,2048,704]{1,2,0:T(8,128)(2,1)S(1)}, bf16[1,2048,704]{1,2,0:T(8,128)(2,1)}, u32[]{:S(2)}) copy-start(bf16[1,2048,704]{1,2,0:T(8,128)(2,1)} %param.31) | copy-start | bytes 8650756
  45.7 17.0 %copy-start.3 = (bf16[1,704,2048]{2,1,0:T(8,128)(2,1)S(1)}, bf16[1,704,2048]{2,1,0:T(8,128)(2,1)}, u32[]{:S(2)}) copy-start(bf16[1,704,2048]{2,1,0:T(8,128)(2,1)} %param.32) | copy-start | bytes 8650756
  46.3 10.0 %collective-permute-start.13 = (bf16[64,2048]{1,0:T(8,128)(2,1)S(1)}, bf16[64,2048]{1,0:T(8,128)(2,1)S(1)}, u32[]{:S(2)}, u32[]{:S(2)}) collective-permute-start(bf16[64,2048]{1,0:T(8,128)(2,1)S(1)} %get-tuple-element.115), channel_id=1, source_target_pairs={{0,4},{1,5},{2,6},{3,7},{4,12},{5,13},{6,14},{7,15},{8,0},{9,1},{1... | collective-permute-start | bytes 786440 | tf_op jit(solution)/shard_map/ppermute | solution.py:37
  47.8 9.1 %collective-permute-start.14 = (bf16[32,2048]{1,0:T(8,128)(2,1)S(1)}, bf16[32,2048]{1,0:T(8,128)(2,1)S(1)}, u32[]{:S(2)}, u32[]{:S(2)}) collective-permute-start(bf16[32,2048]{1,0:T(8,128)(2,1)S(1)} %get-tuple-element.118), channel_id=1, source_target_pairs={{0,1},{1,0},{2,3},{3,2},{4,5},{5,4},{6,7},{7,6},{8,9},{9,8},{10,11... | collective-permute-start | bytes 393224 | tf_op jit(solution)/shard_map/ppermute | solution.py:47
  49.3 7.9 %collective-permute-start.15 = (bf16[32,2048]{1,0:T(8,128)(2,1)S(1)}, bf16[32,2048]{1,0:T(8,128)(2,1)S(1)}, u32[]{:S(2)}, u32[]{:S(2)}) collective-permute-start(bf16[32,2048]{1,0:T(8,128)(2,1)S(1)} %get-tuple-element.119), channel_id=1, source_target_pairs={{0,2},{1,3},{2,0},{3,1},{4,6},{5,7},{6,4},{7,5},{8,10},{9,11},{10,... | collective-permute-start | bytes 393224 | tf_op jit(solution)/shard_map/ppermute | solution.py:47
  50.1 7.0 %collective-permute-start.16 = (bf16[32,2048]{1,0:T(8,128)(2,1)S(1)}, bf16[32,2048]{1,0:T(8,128)(2,1)S(1)}, u32[]{:S(2)}, u32[]{:S(2)}) collective-permute-start(bf16[32,2048]{1,0:T(8,128)(2,1)S(1)} %get-tuple-element.120), channel_id=1, source_target_pairs={{0,3},{1,2},{2,1},{3,0},{4,7},{5,6},{6,5},{7,4},{8,11},{9,10},{10,... | collective-permute-start | bytes 393224 | tf_op jit(solution)/shard_map/ppermute | solution.py:47
  57.2 5.5 %collective-permute-start.17 = (bf16[128,2048]{1,0:T(8,128)(2,1)S(1)}, bf16[128,2048]{1,0:T(8,128)(2,1)S(1)}, u32[]{:S(2)}, u32[]{:S(2)}) collective-permute-start(bf16[128,2048]{1,0:T(8,128)(2,1)S(1)} %join_arrived.4.refs_0_), channel_id=1, source_target_pairs={{0,16},{16,0},{1,17},{17,1},{2,18},{18,2},{3,19},{19,3},{4,20},{20... | collective-permute-start | bytes 1572872 | tf_op jit(solution)/shard_map/ppermute | solution.py:57
  57.3 9.6 %collective-permute-start.18 = (bf16[64,2048]{1,0:T(8,128)(2,1)S(1)}, bf16[64,2048]{1,0:T(8,128)(2,1)S(1)}, u32[]{:S(2)}, u32[]{:S(2)}) collective-permute-start(bf16[64,2048]{1,0:T(8,128)(2,1)S(1)} %collective-permute-done.13.refs_0_), channel_id=1, source_target_pairs={{0,4},{1,5},{2,6},{3,7},{4,12},{5,13},{6,14},{7,15},{8,0},{9,1},{1... | collective-permute-start | bytes 786440 | tf_op jit(solution)/shard_map/ppermute | solution.py:37
  59.2 8.2 %collective-permute-start.19 = (bf16[32,2048]{1,0:T(8,128)(2,1)S(1)}, bf16[32,2048]{1,0:T(8,128)(2,1)S(1)}, u32[]{:S(2)}, u32[]{:S(2)}) collective-permute-start(bf16[32,2048]{1,0:T(8,128)(2,1)S(1)} %get-tuple-element.124), channel_id=1, source_target_pairs={{0,1},{1,0},{2,3},{3,2},{4,5},{5,4},{6,7},{7,6},{8,9},{9,8},{10,11... | collective-permute-start | bytes 393224 | tf_op jit(solution)/shard_map/ppermute | solution.py:47
  59.8 7.7 %collective-permute-start.20 = (bf16[32,2048]{1,0:T(8,128)(2,1)S(1)}, bf16[32,2048]{1,0:T(8,128)(2,1)S(1)}, u32[]{:S(2)}, u32[]{:S(2)}) collective-permute-start(bf16[32,2048]{1,0:T(8,128)(2,1)S(1)} %get-tuple-element.125), channel_id=1, source_target_pairs={{0,2},{1,3},{2,0},{3,1},{4,6},{5,7},{6,4},{7,5},{8,10},{9,11},{10,... | collective-permute-start | bytes 393224 | tf_op jit(solution)/shard_map/ppermute | solution.py:47
  61.0 6.9 %collective-permute-start.21 = (bf16[32,2048]{1,0:T(8,128)(2,1)S(1)}, bf16[32,2048]{1,0:T(8,128)(2,1)S(1)}, u32[]{:S(2)}, u32[]{:S(2)}) collective-permute-start(bf16[32,2048]{1,0:T(8,128)(2,1)S(1)} %get-tuple-element.126), channel_id=1, source_target_pairs={{0,3},{1,2},{2,1},{3,0},{4,7},{5,6},{6,5},{7,4},{8,11},{9,10},{10,... | collective-permute-start | bytes 393224 | tf_op jit(solution)/shard_map/ppermute | solution.py:47
  67.9 5.6 %collective-permute-start.22 = (bf16[128,2048]{1,0:T(8,128)(2,1)S(1)}, bf16[128,2048]{1,0:T(8,128)(2,1)S(1)}, u32[]{:S(2)}, u32[]{:S(2)}) collective-permute-start(bf16[128,2048]{1,0:T(8,128)(2,1)S(1)} %join_arrived.5.refs_0_), channel_id=1, source_target_pairs={{0,16},{16,0},{1,17},{17,1},{2,18},{18,2},{3,19},{19,3},{4,20},{20... | collective-permute-start | bytes 1572872 | tf_op jit(solution)/shard_map/ppermute | solution.py:57
  68.0 9.6 %collective-permute-start.23 = (bf16[64,2048]{1,0:T(8,128)(2,1)S(1)}, bf16[64,2048]{1,0:T(8,128)(2,1)S(1)}, u32[]{:S(2)}, u32[]{:S(2)}) collective-permute-start(bf16[64,2048]{1,0:T(8,128)(2,1)S(1)} %collective-permute-done.18.refs_1_), channel_id=1, source_target_pairs={{0,4},{1,5},{2,6},{3,7},{4,12},{5,13},{6,14},{7,15},{8,0},{9,1},{1... | collective-permute-start | bytes 786440 | tf_op jit(solution)/shard_map/ppermute | solution.py:37
  70.0 7.6 %collective-permute-start.24 = (bf16[32,2048]{1,0:T(8,128)(2,1)S(1)}, bf16[32,2048]{1,0:T(8,128)(2,1)S(1)}, u32[]{:S(2)}, u32[]{:S(2)}) collective-permute-start(bf16[32,2048]{1,0:T(8,128)(2,1)S(1)} %get-tuple-element.130), channel_id=1, source_target_pairs={{0,1},{1,0},{2,3},{3,2},{4,5},{5,4},{6,7},{7,6},{8,9},{9,8},{10,11... | collective-permute-start | bytes 393224 | tf_op jit(solution)/shard_map/ppermute | solution.py:47
  71.5 8.1 %collective-permute-start.25 = (bf16[32,2048]{1,0:T(8,128)(2,1)S(1)}, bf16[32,2048]{1,0:T(8,128)(2,1)S(1)}, u32[]{:S(2)}, u32[]{:S(2)}) collective-permute-start(bf16[32,2048]{1,0:T(8,128)(2,1)S(1)} %get-tuple-element.131), channel_id=1, source_target_pairs={{0,2},{1,3},{2,0},{3,1},{4,6},{5,7},{6,4},{7,5},{8,10},{9,11},{10,... | collective-permute-start | bytes 393224 | tf_op jit(solution)/shard_map/ppermute | solution.py:47
  72.3 7.3 %collective-permute-start.26 = (bf16[32,2048]{1,0:T(8,128)(2,1)S(1)}, bf16[32,2048]{1,0:T(8,128)(2,1)S(1)}, u32[]{:S(2)}, u32[]{:S(2)}) collective-permute-start(bf16[32,2048]{1,0:T(8,128)(2,1)S(1)} %get-tuple-element.132), channel_id=1, source_target_pairs={{0,3},{1,2},{2,1},{3,0},{4,7},{5,6},{6,5},{7,4},{8,11},{9,10},{10,... | collective-permute-start | bytes 393224 | tf_op jit(solution)/shard_map/ppermute | solution.py:47
  79.6 1.9 %collective-permute-start.28 = (bf16[128,2048]{1,0:T(8,128)(2,1)S(1)}, bf16[128,2048]{1,0:T(8,128)(2,1)S(1)}, u32[]{:S(2)}, u32[]{:S(2)}) collective-permute-start(bf16[128,2048]{1,0:T(8,128)(2,1)S(1)} %pass_on.6), channel_id=1, source_target_pairs={{0,16},{16,0},{1,17},{17,1},{2,18},{18,2},{3,19},{19,3},{4,20},{20... | collective-permute-start | bytes 1572872 | tf_op jit(solution)/shard_map/ppermute | solution.py:57
  80.2 5.0 %collective-permute-start.27 = (bf16[128,2048]{1,0:T(8,128)(2,1)S(1)}, bf16[128,2048]{1,0:T(8,128)(2,1)S(1)}, u32[]{:S(2)}, u32[]{:S(2)}) collective-permute-start(bf16[128,2048]{1,0:T(8,128)(2,1)S(1)} %join_arrived.6.refs_0_), channel_id=1, source_target_pairs={{0,16},{16,0},{1,17},{17,1},{2,18},{18,2},{3,19},{19,3},{4,20},{20... | collective-permute-start | bytes 1572872 | tf_op jit(solution)/shard_map/ppermute | solution.py:57
  81.6 9.2 %collective-permute-start.29 = (bf16[64,2048]{1,0:T(8,128)(2,1)S(1)}, bf16[64,2048]{1,0:T(8,128)(2,1)S(1)}, u32[]{:S(2)}, u32[]{:S(2)}) collective-permute-start(bf16[64,2048]{1,0:T(8,128)(2,1)S(1)} %get-tuple-element.141), channel_id=1, source_target_pairs={{0,1},{1,0},{2,3},{3,2},{4,5},{5,4},{6,7},{7,6},{8,9},{9,8},{10,11... | collective-permute-start | bytes 786440 | tf_op jit(solution)/shard_map/ppermute | solution.py:47
  82.2 8.9 %collective-permute-start.30 = (bf16[64,2048]{1,0:T(8,128)(2,1)S(1)}, bf16[64,2048]{1,0:T(8,128)(2,1)S(1)}, u32[]{:S(2)}, u32[]{:S(2)}) collective-permute-start(bf16[64,2048]{1,0:T(8,128)(2,1)S(1)} %get-tuple-element.142), channel_id=1, source_target_pairs={{0,2},{1,3},{2,0},{3,1},{4,6},{5,7},{6,4},{7,5},{8,10},{9,11},{10,... | collective-permute-start | bytes 786440 | tf_op jit(solution)/shard_map/ppermute | solution.py:47
  83.4 12.5 %collective-permute-start.31 = (bf16[64,2048]{1,0:T(8,128)(2,1)S(1)}, bf16[64,2048]{1,0:T(8,128)(2,1)S(1)}, u32[]{:S(2)}, u32[]{:S(2)}) collective-permute-start(bf16[64,2048]{1,0:T(8,128)(2,1)S(1)} %get-tuple-element.143), channel_id=1, source_target_pairs={{0,3},{1,2},{2,1},{3,0},{4,7},{5,6},{6,5},{7,4},{8,11},{9,10},{10,... | collective-permute-start | bytes 786440 | tf_op jit(solution)/shard_map/ppermute | solution.py:47
  87.8 10.2 %collective-permute-start.33 = (bf16[128,2048]{1,0:T(8,128)(2,1)S(1)}, bf16[128,2048]{1,0:T(8,128)(2,1)S(1)}, u32[]{:S(2)}, u32[]{:S(2)}) collective-permute-start(bf16[128,2048]{1,0:T(8,128)(2,1)S(1)} %get-tuple-element.146), channel_id=1, source_target_pairs={{0,16},{16,0},{1,17},{17,1},{2,18},{18,2},{3,19},{19,3},{4,20},{20... | collective-permute-start | bytes 1572872 | tf_op jit(solution)/shard_map/ppermute | solution.py:57
  96.0 5.8 %collective-permute-start.32 = (bf16[128,2048]{1,0:T(8,128)(2,1)S(1)}, bf16[128,2048]{1,0:T(8,128)(2,1)S(1)}, u32[]{:S(2)}, u32[]{:S(2)}) collective-permute-start(bf16[128,2048]{1,0:T(8,128)(2,1)S(1)} %join_arrived.7.refs_0_), channel_id=1, source_target_pairs={{0,16},{16,0},{1,17},{17,1},{2,18},{18,2},{3,19},{19,3},{4,20},{20... | collective-permute-start | bytes 1572872 | tf_op jit(solution)/shard_map/ppermute | solution.py:57
  96.3 9.9 %collective-permute-start.37 = (bf16[64,2048]{1,0:T(8,128)(2,1)S(1)}, bf16[64,2048]{1,0:T(8,128)(2,1)S(1)}, u32[]{:S(2)}, u32[]{:S(2)}) collective-permute-start(bf16[64,2048]{1,0:T(8,128)(2,1)S(1)} %collect.3), channel_id=1, source_target_pairs={{0,4},{1,5},{2,6},{3,7},{4,12},{5,13},{6,14},{7,15},{8,0},{9,1},{1... | collective-permute-start | bytes 786440 | tf_op jit(solution)/shard_map/ppermute | solution.py:37
  98.2 8.0 %collective-permute-start.34 = (bf16[32,2048]{1,0:T(8,128)(2,1)S(1)}, bf16[32,2048]{1,0:T(8,128)(2,1)S(1)}, u32[]{:S(2)}, u32[]{:S(2)}) collective-permute-start(bf16[32,2048]{1,0:T(8,128)(2,1)S(1)} %get-tuple-element.147), channel_id=1, source_target_pairs={{0,1},{1,0},{2,3},{3,2},{4,5},{5,4},{6,7},{7,6},{8,9},{9,8},{10,11... | collective-permute-start | bytes 393224 | tf_op jit(solution)/shard_map/ppermute | solution.py:47
  98.8 7.4 %collective-permute-start.35 = (bf16[32,2048]{1,0:T(8,128)(2,1)S(1)}, bf16[32,2048]{1,0:T(8,128)(2,1)S(1)}, u32[]{:S(2)}, u32[]{:S(2)}) collective-permute-start(bf16[32,2048]{1,0:T(8,128)(2,1)S(1)} %get-tuple-element.148), channel_id=1, source_target_pairs={{0,2},{1,3},{2,0},{3,1},{4,6},{5,7},{6,4},{7,5},{8,10},{9,11},{10,... | collective-permute-start | bytes 393224 | tf_op jit(solution)/shard_map/ppermute | solution.py:47
  100.0 29.7 %slice-start = ((s8[6291456]{0:T(1024)(128)(4,1)}), s8[4194304]{0:T(1024)(128)(4,1)S(1)}, s32[]{:S(2)}) async-start(s8[6291456]{0:T(1024)(128)(4,1)} %bitcast.27), calls=%async_computation | async-start | bytes 8388608
  100.0 29.7 %slice-start.1 = ((s8[6291456]{0:T(1024)(128)(4,1)}), s8[2097152]{0:T(1024)(128)(4,1)S(1)}, s32[]{:S(2)}) async-start(s8[6291456]{0:T(1024)(128)(4,1)} %bitcast.27), calls=%async_computation.1 | async-start | bytes 4194304
  100.0 7.0 %collective-permute-start.36 = (bf16[32,2048]{1,0:T(8,128)(2,1)S(1)}, bf16[32,2048]{1,0:T(8,128)(2,1)S(1)}, u32[]{:S(2)}, u32[]{:S(2)}) collective-permute-start(bf16[32,2048]{1,0:T(8,128)(2,1)S(1)} %get-tuple-element.149), channel_id=1, source_target_pairs={{0,3},{1,2},{2,1},{3,0},{4,7},{5,6},{6,5},{7,4},{8,11},{9,10},{10,... | collective-permute-start | bytes 393224 | tf_op jit(solution)/shard_map/ppermute | solution.py:47
  106.9 15.9 %copy-start.17 = (bf16[2048]{0:T(1024)(128)(2,1)S(1)}, bf16[2048]{0:T(1024)(128)(2,1)}, u32[]{:S(2)}) copy-start(bf16[2048]{0:T(1024)(128)(2,1)} %param.33) | copy-start | bytes 12292
  106.9 1.9 %collective-permute-start.38 = (bf16[128,2048]{1,0:T(8,128)(2,1)S(1)}, bf16[128,2048]{1,0:T(8,128)(2,1)S(1)}, u32[]{:S(2)}, u32[]{:S(2)}) collective-permute-start(bf16[128,2048]{1,0:T(8,128)(2,1)S(1)} %pass_on.7), channel_id=1, source_target_pairs={{0,16},{16,0},{1,17},{17,1},{2,18},{18,2},{3,19},{19,3},{4,20},{20... | collective-permute-start | bytes 1572872 | tf_op jit(solution)/shard_map/ppermute | solution.py:57
  106.9 12.2 %collective-permute-start.43 = (bf16[128,2048]{1,0:T(8,128)(2,1)S(1)}, bf16[128,2048]{1,0:T(8,128)(2,1)S(1)}, u32[]{:S(2)}, u32[]{:S(2)}) collective-permute-start(bf16[128,2048]{1,0:T(8,128)(2,1)S(1)} %get-tuple-element.157), channel_id=1, source_target_pairs={{0,16},{16,0},{1,17},{17,1},{2,18},{18,2},{3,19},{19,3},{4,20},{20... | collective-permute-start | bytes 1572872 | tf_op jit(solution)/shard_map/ppermute | solution.py:57
  107.7 22.0 %copy-start.5 = (bf16[2048,288]{0,1:T(8,128)(2,1)S(1)}, bf16[2048,288]{0,1:T(8,128)(2,1)}, u32[]{:S(2)}) copy-start(bf16[2048,288]{0,1:T(8,128)(2,1)} %param.35) | copy-start | bytes 3538948
  107.7 9.2 %collective-permute-start.42 = (bf16[64,2048]{1,0:T(8,128)(2,1)S(1)}, bf16[64,2048]{1,0:T(8,128)(2,1)S(1)}, u32[]{:S(2)}, u32[]{:S(2)}) collective-permute-start(bf16[64,2048]{1,0:T(8,128)(2,1)S(1)} %collect.4), channel_id=1, source_target_pairs={{0,4},{1,5},{2,6},{3,7},{4,12},{5,13},{6,14},{7,15},{8,0},{9,1},{1... | collective-permute-start | bytes 786440 | tf_op jit(solution)/shard_map/ppermute | solution.py:37
  108.9 7.9 %collective-permute-start.39 = (bf16[32,2048]{1,0:T(8,128)(2,1)S(1)}, bf16[32,2048]{1,0:T(8,128)(2,1)S(1)}, u32[]{:S(2)}, u32[]{:S(2)}) collective-permute-start(bf16[32,2048]{1,0:T(8,128)(2,1)S(1)} %get-tuple-element.152), channel_id=1, source_target_pairs={{0,1},{1,0},{2,3},{3,2},{4,5},{5,4},{6,7},{7,6},{8,9},{9,8},{10,11... | collective-permute-start | bytes 393224 | tf_op jit(solution)/shard_map/ppermute | solution.py:47
  110.5 8.1 %collective-permute-start.40 = (bf16[32,2048]{1,0:T(8,128)(2,1)S(1)}, bf16[32,2048]{1,0:T(8,128)(2,1)S(1)}, u32[]{:S(2)}, u32[]{:S(2)}) collective-permute-start(bf16[32,2048]{1,0:T(8,128)(2,1)S(1)} %get-tuple-element.153), channel_id=1, source_target_pairs={{0,2},{1,3},{2,0},{3,1},{4,6},{5,7},{6,4},{7,5},{8,10},{9,11},{10,... | collective-permute-start | bytes 393224 | tf_op jit(solution)/shard_map/ppermute | solution.py:47
  111.3 7.2 %collective-permute-start.41 = (bf16[32,2048]{1,0:T(8,128)(2,1)S(1)}, bf16[32,2048]{1,0:T(8,128)(2,1)S(1)}, u32[]{:S(2)}, u32[]{:S(2)}) collective-permute-start(bf16[32,2048]{1,0:T(8,128)(2,1)S(1)} %get-tuple-element.154), channel_id=1, source_target_pairs={{0,3},{1,2},{2,1},{3,0},{4,7},{5,6},{6,5},{7,4},{8,11},{9,10},{10,... | collective-permute-start | bytes 393224 | tf_op jit(solution)/shard_map/ppermute | solution.py:47
  118.8 8.9 %collective-permute-start.47 = (bf16[64,2048]{1,0:T(8,128)(2,1)S(1)}, bf16[64,2048]{1,0:T(8,128)(2,1)S(1)}, u32[]{:S(2)}, u32[]{:S(2)}) collective-permute-start(bf16[64,2048]{1,0:T(8,128)(2,1)S(1)} %collect.5.refs_0_), channel_id=1, source_target_pairs={{0,4},{1,5},{2,6},{3,7},{4,12},{5,13},{6,14},{7,15},{8,0},{9,1},{1... | collective-permute-start | bytes 786440 | tf_op jit(solution)/shard_map/ppermute | solution.py:37
  119.3 6.0 %collective-permute-start.44 = (bf16[32,2048]{1,0:T(8,128)(2,1)S(1)}, bf16[32,2048]{1,0:T(8,128)(2,1)S(1)}, u32[]{:S(2)}, u32[]{:S(2)}) collective-permute-start(bf16[32,2048]{1,0:T(8,128)(2,1)S(1)} %get-tuple-element.159), channel_id=1, source_target_pairs={{0,1},{1,0},{2,3},{3,2},{4,5},{5,4},{6,7},{7,6},{8,9},{9,8},{10,11... | collective-permute-start | bytes 393224 | tf_op jit(solution)/shard_map/ppermute | solution.py:47
  120.6 7.0 %collective-permute-start.45 = (bf16[32,2048]{1,0:T(8,128)(2,1)S(1)}, bf16[32,2048]{1,0:T(8,128)(2,1)S(1)}, u32[]{:S(2)}, u32[]{:S(2)}) collective-permute-start(bf16[32,2048]{1,0:T(8,128)(2,1)S(1)} %get-tuple-element.160), channel_id=1, source_target_pairs={{0,2},{1,3},{2,0},{3,1},{4,6},{5,7},{6,4},{7,5},{8,10},{9,11},{10,... | collective-permute-start | bytes 393224 | tf_op jit(solution)/shard_map/ppermute | solution.py:47
  121.5 6.2 %collective-permute-start.46 = (bf16[32,2048]{1,0:T(8,128)(2,1)S(1)}, bf16[32,2048]{1,0:T(8,128)(2,1)S(1)}, u32[]{:S(2)}, u32[]{:S(2)}) collective-permute-start(bf16[32,2048]{1,0:T(8,128)(2,1)S(1)} %get-tuple-element.161), channel_id=1, source_target_pairs={{0,3},{1,2},{2,1},{3,0},{4,7},{5,6},{6,5},{7,4},{8,11},{9,10},{10,... | collective-permute-start | bytes 393224 | tf_op jit(solution)/shard_map/ppermute | solution.py:47
  128.1 1.6 %collective-permute-start.48 = (bf16[64,2048]{1,0:T(8,128)(2,1)S(1)}, bf16[64,2048]{1,0:T(8,128)(2,1)S(1)}, u32[]{:S(2)}, u32[]{:S(2)}) collective-permute-start(bf16[64,2048]{1,0:T(8,128)(2,1)S(1)} %get-tuple-element.163.refs_4_), channel_id=1, source_target_pairs={{0,16},{16,0},{1,17},{17,1},{2,18},{18,2},{3,19},{19,3},{4,20},{20... | collective-permute-start | bytes 786440 | tf_op jit(solution)/shard_map/ppermute | solution.py:57
  (5 other events, 3.5 us)

commit v8 on v7

--- a/solution.py
+++ b/solution.py
@@ -395,7 +395,7 @@
         ((8, 128), jnp.float32),
     ]
     return attend_call(
-        functools.partial(near_kernel, len(blocks), min(4, heads)),
+        functools.partial(near_kernel, len(blocks), min(8, heads)),
         "attend_near",
         [tokens_info, spots, order, queries, key_up, *blocks],
         outputs,
@@ -438,7 +438,7 @@
         ((8, 128), jnp.float32),
     ]
     return attend_call(
-        functools.partial(mid_kernel, len(blocks), min(4, rows // tokens)),
+        functools.partial(mid_kernel, len(blocks), min(8, rows // tokens)),
         "attend_mid",
         [tokens_info, spots, *near, *blocks],
         outputs,

time: 132 us -> 132 us (level)
  waiting for transfers between devices: 43.8 us -> 45.3 us
  transfers between devices with their start and end apart: 49 -> 49, of which waited for: 24 -> 25; matrix products, arithmetic and copies ran while one was open for 0% -> 0% of each run, Pallas kernels for 19% -> 18%
where the time goes in v8:
time: 132 us
  starting transfers between devices  46.8 us (35%)
  waiting for transfers between devices  45.3 us (34%)
  Pallas kernels  33.8 us (26%)
  local copies, waits for them, and re-layouts  4.56 us (3%)
    ppermute x25, starting transfers between devices, send_plane(): return lax.ppermute(block, 'tensor', [(i, i ^ distance) for i in devices])  29.9 us
    ppermute x25, waiting for transfers between devices, send_plane(): return lax.ppermute(block, 'tensor', [(i, i ^ distance) for i in devices])  24.7 us
    pallas_call x24, Pallas kernels, call(): pl.pallas_call(after(kernel, len(ready)), **places, out_shape=shapes, com...  19.3 us
    ppermute x6, waiting for transfers between devices, send_ring(): return lax.ppermute(block, 'tensor', route)  14.1 us
    pallas_call x3, Pallas kernels, attend_call(): pl.pallas_call(kernel, in_specs=resident(inputs), out_specs=resident(shap...  13.4 us
    ppermute x6, starting transfers between devices, send_ring(): return lax.ppermute(block, 'tensor', route)  8.04 us
    ppermute x3, starting transfers between devices, send_round(): lax.ppermute(block, 'tensor', [(i, (i + distance) % count) for i in range...  6.06 us
    ppermute x15, waiting for transfers between devices, send_group(): return lax.ppermute(block, 'group', [(i, i ^ distance) for i in devices])  5.04 us
  transfers between devices with their start and end apart: 49, of which 25 were waited for; matrix products, arithmetic and copies ran while one was open for 0% of the time, Pallas kernels for 18%

profile of v8, /device:TPU:0, one launch (start us, length us, event | category | flops | bytes accessed | tf_op | source)
XLA Modules:
  0.0 131.7 jit_solution(7478020192448966212)
XLA Ops:
  0.6 1.9 %join_share.1 = (bf16[128,640]{1,0:T(8,128)(2,1)}, bf16[64,640]{1,0:T(8,128)(2,1)}) custom-call(bf16[64,576]{1,0:T(8,128)(2,1)} %refs_0_.1, bf16[576,128]{1,0:T(8,128)(2,1)} %bitcast.35, s32[6,2,64]{2,1,0:T(2,128)} %bitcast.36), custom_call_target="tpu_custom_call" | custom-call | flops 10000000 | bytes 470016 | tf_op jit(solution)/shard_map/join_share/pallas_call | solution.py:111
  2.5 4.0 %collective-permute-start.1 = (bf16[64,640]{1,0:T(8,128)(2,1)}, bf16[64,640]{1,0:T(8,128)(2,1)S(1)}, u32[]{:S(2)}, u32[]{:S(2)}) collective-permute-start(bf16[64,640]{1,0:T(8,128)(2,1)} %get-tuple-element.90), channel_id=1, source_target_pairs={{0,8},{1,9},{2,10},{3,11},{4,12},{5,13},{6,14},{7,15},{8,0},{9,1},... | collective-permute-start | bytes 245768 | tf_op jit(solution)/shard_map/ppermute | solution.py:42
  6.5 1.3 %collective-permute-start.2 = (bf16[64,640]{1,0:T(8,128)(2,1)}, bf16[64,640]{1,0:T(8,128)(2,1)S(1)}, u32[]{:S(2)}, u32[]{:S(2)}) collective-permute-start(bf16[64,640]{1,0:T(8,128)(2,1)} %get-tuple-element.90), channel_id=1, source_target_pairs={{0,12},{1,13},{2,14},{3,15},{4,0},{5,1},{6,2},{7,3},{8,4},{9,5},{1... | collective-permute-start | bytes 245768 | tf_op jit(solution)/shard_map/ppermute | solution.py:42
  7.9 0.7 collective-permute-start
  8.6 0.9 copy-done.8
  12.2 0.9 copy-done.15
  13.1 1.1 make_plan.1
  14.2 1.5 %collective-permute-done.refs_2_ = bf16[128,640]{1,0:T(8,128)(2,1)S(1)} collective-permute-done((bf16[128,640]{1,0:T(8,128)(2,1)}, bf16[128,640]{1,0:T(8,128)(2,1)S(1)}, u32[]{:S(2)}, u32[]{:S(2)}) %collective-permute-start) | collective-permute-done | bytes 163872 | tf_op jit(solution)/shard_map/ppermute | solution.py:42
  15.8 1.6 %collective-permute-start.4 = (bf16[320,640]{1,0:T(8,128)(2,1)S(1)}, bf16[320,640]{1,0:T(8,128)(2,1)S(1)}, u32[]{:S(2)}, u32[]{:S(2)}) collective-permute-start(bf16[320,640]{1,0:T(8,128)(2,1)S(1)} %get-tuple-element.98), channel_id=1, source_target_pairs={{0,1},{1,0},{2,3},{3,2},{4,5},{5,4},{6,7},{7,6},{8,9},{9,8},{10,11... | collective-permute-start | bytes 1228808 | tf_op jit(solution)/shard_map/ppermute | solution.py:47
  17.4 1.5 %collective-permute-start.5 = (bf16[320,640]{1,0:T(8,128)(2,1)S(1)}, bf16[320,640]{1,0:T(8,128)(2,1)S(1)}, u32[]{:S(2)}, u32[]{:S(2)}) collective-permute-start(bf16[320,640]{1,0:T(8,128)(2,1)S(1)} %get-tuple-element.99), channel_id=1, source_target_pairs={{0,2},{1,3},{2,0},{3,1},{4,6},{5,7},{6,4},{7,5},{8,10},{9,11},{10,... | collective-permute-start | bytes 1228808 | tf_op jit(solution)/shard_map/ppermute | solution.py:47
  18.9 3.1 %attend_near.1 = (bf16[1024,640]{1,0:T(8,128)(2,1)S(1)}, f32[1024,1]{1,0:T(8,128)S(1)}, f32[1024,1]{1,0:T(8,128)S(1)}, f32[1024,512]{1,0:T(8,128)S(1)}, f32[8,128]{1,0:T(8,128)S(1)}) custom-call(s32[128,4]{1,0:T(8,128)S(1)} %get-tuple-element.87.token_ref, s32[1,768]{1,0:T(1,128)S(1)} %get-tuple-element.89.refs_0_.spot_ref, ...), custom_call_target="tpu_custom_call" | custom-call | flops 1711276032 | bytes 8000000 | tf_op jit(solution)/shard_map/attend_near/pallas_call | solution.py:367
  22.1 5.7 %collective-permute-done.4.refs_1_ = bf16[320,640]{1,0:T(8,128)(2,1)S(1)} collective-permute-done((bf16[320,640]{1,0:T(8,128)(2,1)S(1)}, bf16[320,640]{1,0:T(8,128)(2,1)S(1)}, u32[]{:S(2)}, u32[]{:S(2)}) %collective-permute-start.4) | collective-permute-done | bytes 409632 | tf_op jit(solution)/shard_map/ppermute | solution.py:47
  27.7 1.2 collective-permute-done.5.refs_2_
  30.1 1.5 %collective-permute-start.9 = (bf16[160,640]{1,0:T(8,128)(2,1)S(1)}, bf16[160,640]{1,0:T(8,128)(2,1)S(1)}, u32[]{:S(2)}, u32[]{:S(2)}) collective-permute-start(bf16[160,640]{1,0:T(8,128)(2,1)S(1)} %get-tuple-element.107), channel_id=1, source_target_pairs={{0,2},{1,3},{2,0},{3,1},{4,6},{5,7},{6,4},{7,5},{8,10},{9,11},{10,... | collective-permute-start | bytes 614408 | tf_op jit(solution)/shard_map/ppermute | solution.py:47
  31.6 5.4 %attend_mid.1 = (f32[1024,1]{1,0:T(8,128)S(1)}, f32[1024,1]{1,0:T(8,128)S(1)}, f32[1024,512]{1,0:T(8,128)S(1)}, f32[8,128]{1,0:T(8,128)S(1)}) custom-call(s32[128,4]{1,0:T(8,128)S(1)} %get-tuple-element.87.token_ref, s32[1,1280]{1,0:T(1,128)S(1)} %get-tuple-element.93.spot_ref, bf16[1024,640]{1,0:T(8,128)(2,1)S(1)} %get-tuple-element.92.wide_ref, ...), custom_call_target="tpu_custom_call" | custom-call | flops 2852126720 | bytes 8000000 | tf_op jit(solution)/shard_map/attend_mid/pallas_call | solution.py:367
  37.6 0.9 collective-permute-done.10.refs_2_
  38.9 4.9 %attend_far.1 = (f32[64,2048]{1,0:T(8,128)S(1)}, bf16[64,2048]{1,0:T(8,128)(2,1)S(1)}) custom-call(s32[128,4]{1,0:T(8,128)S(1)} %get-tuple-element.87.token_ref, s32[1,640]{1,0:T(1,128)S(1)} %get-tuple-element.88.spot_ref, bf16[1024,640]{1,0:T(8,128)(2,1)S(1)} %get-tuple-element.92.wide_ref, f32[1024,1]{1,0:T(8,128)S(1)} %get-tuple-element.102.best_ref, ...), custom_call_target="tpu_custom_call" | custom-call | flops 1426063360 | bytes 8000000 | tf_op jit(solution)/shard_map/attend_far/pallas_call | solution.py:367
  44.3 1.1 collective-permute-done.12.refs_2_
  46.0 1.5 %collective-permute-start.13 = (bf16[64,2048]{1,0:T(8,128)(2,1)S(1)}, bf16[64,2048]{1,0:T(8,128)(2,1)S(1)}, u32[]{:S(2)}, u32[]{:S(2)}) collective-permute-start(bf16[64,2048]{1,0:T(8,128)(2,1)S(1)} %get-tuple-element.115), channel_id=1, source_target_pairs={{0,4},{1,5},{2,6},{3,7},{4,12},{5,13},{6,14},{7,15},{8,0},{9,1},{1... | collective-permute-start | bytes 786440 | tf_op jit(solution)/shard_map/ppermute | solution.py:37
  47.4 1.5 %collective-permute-start.14 = (bf16[32,2048]{1,0:T(8,128)(2,1)S(1)}, bf16[32,2048]{1,0:T(8,128)(2,1)S(1)}, u32[]{:S(2)}, u32[]{:S(2)}) collective-permute-start(bf16[32,2048]{1,0:T(8,128)(2,1)S(1)} %get-tuple-element.118), channel_id=1, source_target_pairs={{0,1},{1,0},{2,3},{3,2},{4,5},{5,4},{6,7},{7,6},{8,9},{9,8},{10,11... | collective-permute-start | bytes 393224 | tf_op jit(solution)/shard_map/ppermute | solution.py:47
  48.9 1.2 collective-permute-start.15
  50.1 0.8 collective-permute-start.16
  50.9 5.0 %collective-permute-done.13.refs_0_ = bf16[64,2048]{1,0:T(8,128)(2,1)S(1)} collective-permute-done((bf16[64,2048]{1,0:T(8,128)(2,1)S(1)}, bf16[64,2048]{1,0:T(8,128)(2,1)S(1)}, u32[]{:S(2)}, u32[]{:S(2)}) %collective-permute-start.13) | collective-permute-done | bytes 262176 | tf_op jit(solution)/shard_map/ppermute | solution.py:37
  56.9 1.9 %collective-permute-start.18 = (bf16[64,2048]{1,0:T(8,128)(2,1)S(1)}, bf16[64,2048]{1,0:T(8,128)(2,1)S(1)}, u32[]{:S(2)}, u32[]{:S(2)}) collective-permute-start(bf16[64,2048]{1,0:T(8,128)(2,1)S(1)} %collective-permute-done.13.refs_0_), channel_id=1, source_target_pairs={{0,4},{1,5},{2,6},{3,7},{4,12},{5,13},{6,14},{7,15},{8,0},{9,1},{1... | collective-permute-start | bytes 786440 | tf_op jit(solution)/shard_map/ppermute | solution.py:37
  58.9 0.9 collective-permute-start.19
  59.8 0.8 collective-permute-start.20
  60.6 1.7 %collective-permute-start.21 = (bf16[32,2048]{1,0:T(8,128)(2,1)S(1)}, bf16[32,2048]{1,0:T(8,128)(2,1)S(1)}, u32[]{:S(2)}, u32[]{:S(2)}) collective-permute-start(bf16[32,2048]{1,0:T(8,128)(2,1)S(1)} %get-tuple-element.126), channel_id=1, source_target_pairs={{0,3},{1,2},{2,1},{3,0},{4,7},{5,6},{6,5},{7,4},{8,11},{9,10},{10,... | collective-permute-start | bytes 393224 | tf_op jit(solution)/shard_map/ppermute | solution.py:47
  62.4 2.6 %experts.4 = (f32[128,2048]{1,0:T(8,128)S(1)}, bf16[128,2048]{1,0:T(8,128)(2,1)S(1)}, f32[8,128]{1,0:T(8,128)S(1)}) custom-call(bf16[128,2048]{1,0:T(8,128)(2,1)S(1)} %join_arrived.4.refs_0_, bf16[128,2048]{1,0:T(8,128)(2,1)S(1)} %collective-permute-done.17.refs_1_, bf16[704,2048]{1,0:T(8,128)(2,1)S(1)} %bitcast.15, bf16[704,2048]{1,0:T(8,128)(2,1)S(1)} %bitcast.19, ...), custom_call_target="tpu_custom_call" | custom-call | flops 2214592512 | bytes 11276288 | tf_op jit(solution)/shard_map/experts/pallas_call | solution.py:111
  65.0 1.5 %collective-permute-done.18.refs_1_ = bf16[64,2048]{1,0:T(8,128)(2,1)S(1)} collective-permute-done((bf16[64,2048]{1,0:T(8,128)(2,1)S(1)}, bf16[64,2048]{1,0:T(8,128)(2,1)S(1)}, u32[]{:S(2)}, u32[]{:S(2)}) %collective-permute-start.18) | collective-permute-done | bytes 262176 | tf_op jit(solution)/shard_map/ppermute | solution.py:37
  67.1 0.8 collective-permute-done.21.refs_4_
  68.0 2.0 %collective-permute-start.23 = (bf16[64,2048]{1,0:T(8,128)(2,1)S(1)}, bf16[64,2048]{1,0:T(8,128)(2,1)S(1)}, u32[]{:S(2)}, u32[]{:S(2)}) collective-permute-start(bf16[64,2048]{1,0:T(8,128)(2,1)S(1)} %collective-permute-done.18.refs_1_), channel_id=1, source_target_pairs={{0,4},{1,5},{2,6},{3,7},{4,12},{5,13},{6,14},{7,15},{8,0},{9,1},{1... | collective-permute-start | bytes 786440 | tf_op jit(solution)/shard_map/ppermute | solution.py:37
  70.0 1.1 collective-permute-start.24
  71.1 1.2 collective-permute-start.25
  72.3 1.2 collective-permute-start.26
  73.5 2.6 %experts.5 = (f32[128,2048]{1,0:T(8,128)S(1)}, bf16[128,2048]{1,0:T(8,128)(2,1)S(1)}, f32[8,128]{1,0:T(8,128)S(1)}) custom-call(bf16[128,2048]{1,0:T(8,128)(2,1)S(1)} %join_arrived.5.refs_0_, bf16[128,2048]{1,0:T(8,128)(2,1)S(1)} %collective-permute-done.22.refs_1_, bf16[704,2048]{1,0:T(8,128)(2,1)S(1)} %bitcast.16, bf16[704,2048]{1,0:T(8,128)(2,1)S(1)} %bitcast.20, ...), custom_call_target="tpu_custom_call" | custom-call | flops 2214592512 | bytes 11276288 | tf_op jit(solution)/shard_map/experts/pallas_call | solution.py:111
  76.2 1.4 %collective-permute-done.23.refs_1_.refs_3_ = bf16[64,2048]{1,0:T(8,128)(2,1)S(1)} collective-permute-done((bf16[64,2048]{1,0:T(8,128)(2,1)S(1)}, bf16[64,2048]{1,0:T(8,128)(2,1)S(1)}, u32[]{:S(2)}, u32[]{:S(2)}) %collective-permute-start.23) | collective-permute-done | bytes 262176 | tf_op jit(solution)/shard_map/ppermute | solution.py:37
  77.6 1.6 %collective-permute-done.25.refs_3_.refs_1_ = bf16[32,2048]{1,0:T(8,128)(2,1)S(1)} collective-permute-done((bf16[32,2048]{1,0:T(8,128)(2,1)S(1)}, bf16[32,2048]{1,0:T(8,128)(2,1)S(1)}, u32[]{:S(2)}, u32[]{:S(2)}) %collective-permute-start.25) | collective-permute-done | bytes 131104 | tf_op jit(solution)/shard_map/ppermute | solution.py:47
  80.4 0.7 collective-permute-done.28.refs_1_
  81.2 1.0 collective-permute-start.29
  82.2 0.8 collective-permute-start.30
  83.0 1.8 %collective-permute-start.31 = (bf16[64,2048]{1,0:T(8,128)(2,1)S(1)}, bf16[64,2048]{1,0:T(8,128)(2,1)S(1)}, u32[]{:S(2)}, u32[]{:S(2)}) collective-permute-start(bf16[64,2048]{1,0:T(8,128)(2,1)S(1)} %get-tuple-element.143), channel_id=1, source_target_pairs={{0,3},{1,2},{2,1},{3,0},{4,7},{5,6},{6,5},{7,4},{8,11},{9,10},{10,... | collective-permute-start | bytes 786440 | tf_op jit(solution)/shard_map/ppermute | solution.py:47
  84.8 2.6 %experts.6 = (f32[128,2048]{1,0:T(8,128)S(1)}, bf16[128,2048]{1,0:T(8,128)(2,1)S(1)}, f32[8,128]{1,0:T(8,128)S(1)}) custom-call(bf16[128,2048]{1,0:T(8,128)(2,1)S(1)} %join_arrived.6.refs_0_, bf16[128,2048]{1,0:T(8,128)(2,1)S(1)} %collective-permute-done.27.refs_1_, bf16[704,2048]{1,0:T(8,128)(2,1)S(1)} %bitcast.17, bf16[704,2048]{1,0:T(8,128)(2,1)S(1)} %bitcast.21, ...), custom_call_target="tpu_custom_call" | custom-call | flops 2214592512 | bytes 11276288 | tf_op jit(solution)/shard_map/experts/pallas_call | solution.py:111
  87.5 2.9 %collective-permute-done.29.refs_2_ = bf16[64,2048]{1,0:T(8,128)(2,1)S(1)} collective-permute-done((bf16[64,2048]{1,0:T(8,128)(2,1)S(1)}, bf16[64,2048]{1,0:T(8,128)(2,1)S(1)}, u32[]{:S(2)}, u32[]{:S(2)}) %collective-permute-start.29) | collective-permute-done | bytes 262176 | tf_op jit(solution)/shard_map/ppermute | solution.py:47
  91.1 4.8 %collective-permute-done.31.refs_4_ = bf16[64,2048]{1,0:T(8,128)(2,1)S(1)} collective-permute-done((bf16[64,2048]{1,0:T(8,128)(2,1)S(1)}, bf16[64,2048]{1,0:T(8,128)(2,1)S(1)}, u32[]{:S(2)}, u32[]{:S(2)}) %collective-permute-start.31) | collective-permute-done | bytes 262176 | tf_op jit(solution)/shard_map/ppermute | solution.py:47
  96.3 1.4 %collective-permute-start.37 = (bf16[64,2048]{1,0:T(8,128)(2,1)S(1)}, bf16[64,2048]{1,0:T(8,128)(2,1)S(1)}, u32[]{:S(2)}, u32[]{:S(2)}) collective-permute-start(bf16[64,2048]{1,0:T(8,128)(2,1)S(1)} %collect.3), channel_id=1, source_target_pairs={{0,4},{1,5},{2,6},{3,7},{4,12},{5,13},{6,14},{7,15},{8,0},{9,1},{1... | collective-permute-start | bytes 786440 | tf_op jit(solution)/shard_map/ppermute | solution.py:37
  97.8 1.0 collective-permute-start.34
  98.8 0.8 collective-permute-start.35
  99.6 1.7 %collective-permute-start.36 = (bf16[32,2048]{1,0:T(8,128)(2,1)S(1)}, bf16[32,2048]{1,0:T(8,128)(2,1)S(1)}, u32[]{:S(2)}, u32[]{:S(2)}) collective-permute-start(bf16[32,2048]{1,0:T(8,128)(2,1)S(1)} %get-tuple-element.149), channel_id=1, source_target_pairs={{0,3},{1,2},{2,1},{3,0},{4,7},{5,6},{6,5},{7,4},{8,11},{9,10},{10,... | collective-permute-start | bytes 393224 | tf_op jit(solution)/shard_map/ppermute | solution.py:47
  101.4 3.1 %experts.7 = (f32[128,2048]{1,0:T(8,128)S(1)}, bf16[128,2048]{1,0:T(8,128)(2,1)S(1)}, f32[8,128]{1,0:T(8,128)}) custom-call(bf16[128,2048]{1,0:T(8,128)(2,1)S(1)} %join_arrived.7.refs_0_, bf16[128,2048]{1,0:T(8,128)(2,1)S(1)} %collective-permute-done.32.refs_1_, bf16[704,2048]{1,0:T(8,128)(2,1)S(1)} %bitcast.18, bf16[704,2048]{1,0:T(8,128)(2,1)S(1)} %bitcast.22, ...), custom_call_target="tpu_custom_call" | custom-call | flops 2214592512 | bytes 11276288 | tf_op jit(solution)/shard_map/experts/pallas_call | solution.py:111
  104.4 1.7 %collective-permute-done.37.refs_3_.refs_5_ = bf16[64,2048]{1,0:T(8,128)(2,1)S(1)} collective-permute-done((bf16[64,2048]{1,0:T(8,128)(2,1)S(1)}, bf16[64,2048]{1,0:T(8,128)(2,1)S(1)}, u32[]{:S(2)}, u32[]{:S(2)}) %collective-permute-start.37) | collective-permute-done | bytes 262176 | tf_op jit(solution)/shard_map/ppermute | solution.py:37
  106.2 0.8 collective-permute-done.36.refs_2_.refs_4_
  108.9 1.2 collective-permute-start.39
  110.1 1.2 collective-permute-start.40
  111.3 1.2 collective-permute-start.41
  112.5 4.4 %collective-permute-done.42.refs_5_ = bf16[64,2048]{1,0:T(8,128)(2,1)S(1)} collective-permute-done((bf16[64,2048]{1,0:T(8,128)(2,1)S(1)}, bf16[64,2048]{1,0:T(8,128)(2,1)S(1)}, u32[]{:S(2)}, u32[]{:S(2)}) %collective-permute-start.42) | collective-permute-done | bytes 262176 | tf_op jit(solution)/shard_map/ppermute | solution.py:37
  116.9 1.3 collective-permute-done.40.refs_3_
  119.1 1.2 collective-permute-start.44
  120.3 1.2 collective-permute-start.45
  121.5 1.2 collective-permute-start.46
  122.7 2.6 %collective-permute-done.44.refs_4_ = bf16[32,2048]{1,0:T(8,128)(2,1)S(1)} collective-permute-done((bf16[32,2048]{1,0:T(8,128)(2,1)S(1)}, bf16[32,2048]{1,0:T(8,128)(2,1)S(1)}, u32[]{:S(2)}, u32[]{:S(2)}) %collective-permute-start.44) | collective-permute-done | bytes 131104 | tf_op jit(solution)/shard_map/ppermute | solution.py:47
  125.2 0.8 collective-permute-done.45.refs_5_
  126.1 1.3 collective-permute-done.46.refs_6_
  127.8 1.5 %collective-permute-done.48.refs_5_ = bf16[64,2048]{1,0:T(8,128)(2,1)S(1)} collective-permute-done((bf16[64,2048]{1,0:T(8,128)(2,1)S(1)}, bf16[64,2048]{1,0:T(8,128)(2,1)S(1)}, u32[]{:S(2)}, u32[]{:S(2)}) %collective-permute-start.48) | collective-permute-done | bytes 262176 | tf_op jit(solution)/shard_map/ppermute | solution.py:57
  129.4 2.3 %project.1 = (bf16[128,1536]{1,0:T(8,128)(2,1)}, bf16[288,128]{1,0:T(8,128)(2,1)}, bf16[64,2048]{1,0:T(8,128)(2,1)}) custom-call(bf16[128,128]{1,0:T(8,128)(2,1)S(1)} %get-tuple-element.86.order_ref.refs_0_, bf16[2048,1536]{1,0:T(8,128)(2,1)S(1)} %bitcast.28, bf16[288,2048]{1,0:T(8,128)(2,1)S(1)} %bitcast.29, ...), custom_call_target="tpu_custom_call" | custom-call | flops 1000000000 | bytes 9019392 | tf_op jit(solution)/shard_map/project/pallas_call | solution.py:111
  (110 shorter events, 13.5 us)
Async XLA Ops:
  0.6 43.4 %copy-start = (bf16[128,2048]{1,0:T(8,128)(2,1)S(1)}, bf16[128,2048]{1,0:T(8,128)(2,1)}, u32[]{:S(2)}) copy-start(bf16[128,2048]{1,0:T(8,128)(2,1)} %param.21) | copy-start | bytes 1572868
  2.5 11.6 %collective-permute-start.1 = (bf16[64,640]{1,0:T(8,128)(2,1)}, bf16[64,640]{1,0:T(8,128)(2,1)S(1)}, u32[]{:S(2)}, u32[]{:S(2)}) collective-permute-start(bf16[64,640]{1,0:T(8,128)(2,1)} %get-tuple-element.90), channel_id=1, source_target_pairs={{0,8},{1,9},{2,10},{3,11},{4,12},{5,13},{6,14},{7,15},{8,0},{9,1},... | collective-permute-start | bytes 245768 | tf_op jit(solution)/shard_map/ppermute | solution.py:42
  6.5 7.6 %collective-permute-start.2 = (bf16[64,640]{1,0:T(8,128)(2,1)}, bf16[64,640]{1,0:T(8,128)(2,1)S(1)}, u32[]{:S(2)}, u32[]{:S(2)}) collective-permute-start(bf16[64,640]{1,0:T(8,128)(2,1)} %get-tuple-element.90), channel_id=1, source_target_pairs={{0,12},{1,13},{2,14},{3,15},{4,0},{5,1},{6,2},{7,3},{8,4},{9,5},{1... | collective-permute-start | bytes 245768 | tf_op jit(solution)/shard_map/ppermute | solution.py:42
  7.9 7.7 %collective-permute-start = (bf16[128,640]{1,0:T(8,128)(2,1)}, bf16[128,640]{1,0:T(8,128)(2,1)S(1)}, u32[]{:S(2)}, u32[]{:S(2)}) collective-permute-start(bf16[128,640]{1,0:T(8,128)(2,1)} %get-tuple-element.85.refs_0_.refs_1_), channel_id=1, source_target_pairs={{0,4},{1,5},{2,6},{3,7},{4,8},{5,9},{6,10},{7,11},{8,12},{9,13},{1... | collective-permute-start | bytes 491528 | tf_op jit(solution)/shard_map/ppermute | solution.py:42
  8.6 0.9 copy-start.8
  13.1 5.8 %copy-start.9 = (bf16[8,128,512]{2,1,0:T(8,128)(2,1)S(1)}, bf16[8,128,512]{2,1,0:T(8,128)(2,1)}, u32[]{:S(2)}) copy-start(bf16[8,128,512]{2,1,0:T(8,128)(2,1)} %key_up_ref.1) | copy-start | bytes 3145732
  13.1 5.8 %copy-start.10 = (bf16[128,1536]{1,0:T(8,128)(2,1)S(1)}, bf16[128,1536]{1,0:T(8,128)(2,1)}, u32[]{:S(2)}) copy-start(bf16[128,1536]{1,0:T(8,128)(2,1)} %query_ref.1) | copy-start | bytes 1179652
  15.8 3.2 %collective-permute-start.3 = (bf16[384,640]{1,0:T(8,128)(2,1)S(1)}, bf16[384,640]{1,0:T(8,128)(2,1)S(1)}, u32[]{:S(2)}, u32[]{:S(2)}) collective-permute-start(bf16[384,640]{1,0:T(8,128)(2,1)S(1)} %get-tuple-element.91.refs_0_), channel_id=1, source_target_pairs={{0,16},{16,0},{1,17},{17,1},{2,18},{18,2},{3,19},{19,3},{4,20},{20... | collective-permute-start | bytes 1474568 | tf_op jit(solution)/shard_map/ppermute | solution.py:57
  15.8 11.9 %collective-permute-start.4 = (bf16[320,640]{1,0:T(8,128)(2,1)S(1)}, bf16[320,640]{1,0:T(8,128)(2,1)S(1)}, u32[]{:S(2)}, u32[]{:S(2)}) collective-permute-start(bf16[320,640]{1,0:T(8,128)(2,1)S(1)} %get-tuple-element.98), channel_id=1, source_target_pairs={{0,1},{1,0},{2,3},{3,2},{4,5},{5,4},{6,7},{7,6},{8,9},{9,8},{10,11... | collective-permute-start | bytes 1228808 | tf_op jit(solution)/shard_map/ppermute | solution.py:47
  17.4 11.5 %collective-permute-start.5 = (bf16[320,640]{1,0:T(8,128)(2,1)S(1)}, bf16[320,640]{1,0:T(8,128)(2,1)S(1)}, u32[]{:S(2)}, u32[]{:S(2)}) collective-permute-start(bf16[320,640]{1,0:T(8,128)(2,1)S(1)} %get-tuple-element.99), channel_id=1, source_target_pairs={{0,2},{1,3},{2,0},{3,1},{4,6},{5,7},{6,4},{7,5},{8,10},{9,11},{10,... | collective-permute-start | bytes 1228808 | tf_op jit(solution)/shard_map/ppermute | solution.py:47
  28.9 2.7 %collective-permute-start.6 = (bf16[320,640]{1,0:T(8,128)(2,1)S(1)}, bf16[320,640]{1,0:T(8,128)(2,1)S(1)}, u32[]{:S(2)}, u32[]{:S(2)}) collective-permute-start(bf16[320,640]{1,0:T(8,128)(2,1)S(1)} %get-tuple-element.100.refs_0_.refs_1_), channel_id=1, source_target_pairs={{0,16},{16,0},{1,17},{17,1},{2,18},{18,2},{3,19},{19,3},{4,20},{20... | collective-permute-start | bytes 1228808 | tf_op jit(solution)/shard_map/ppermute | solution.py:57
  28.9 2.7 %collective-permute-start.7 = (bf16[320,640]{1,0:T(8,128)(2,1)S(1)}, bf16[320,640]{1,0:T(8,128)(2,1)S(1)}, u32[]{:S(2)}, u32[]{:S(2)}) collective-permute-start(bf16[320,640]{1,0:T(8,128)(2,1)S(1)} %get-tuple-element.101.refs_1_.refs_0_), channel_id=1, source_target_pairs={{0,16},{16,0},{1,17},{17,1},{2,18},{18,2},{3,19},{19,3},{4,20},{20... | collective-permute-start | bytes 1228808 | tf_op jit(solution)/shard_map/ppermute | solution.py:57
  29.5 7.5 %collective-permute-start.8 = (bf16[160,640]{1,0:T(8,128)(2,1)S(1)}, bf16[160,640]{1,0:T(8,128)(2,1)S(1)}, u32[]{:S(2)}, u32[]{:S(2)}) collective-permute-start(bf16[160,640]{1,0:T(8,128)(2,1)S(1)} %get-tuple-element.106), channel_id=1, source_target_pairs={{0,1},{1,0},{2,3},{3,2},{4,5},{5,4},{6,7},{7,6},{8,9},{9,8},{10,11... | collective-permute-start | bytes 614408 | tf_op jit(solution)/shard_map/ppermute | solution.py:47
  30.1 6.9 %collective-permute-start.9 = (bf16[160,640]{1,0:T(8,128)(2,1)S(1)}, bf16[160,640]{1,0:T(8,128)(2,1)S(1)}, u32[]{:S(2)}, u32[]{:S(2)}) collective-permute-start(bf16[160,640]{1,0:T(8,128)(2,1)S(1)} %get-tuple-element.107), channel_id=1, source_target_pairs={{0,2},{1,3},{2,0},{3,1},{4,6},{5,7},{6,4},{7,5},{8,10},{9,11},{10,... | collective-permute-start | bytes 614408 | tf_op jit(solution)/shard_map/ppermute | solution.py:47
  31.6 7.2 %copy-start.4 = (bf16[1024,2048]{1,0:T(8,128)(2,1)S(1)}, bf16[1024,2048]{1,0:T(8,128)(2,1)}, u32[]{:S(2)}) copy-start(bf16[1024,2048]{1,0:T(8,128)(2,1)} %output_ref.1) | copy-start | bytes 12582916
  31.6 7.2 %copy-start.6 = (bf16[8,512,128]{2,1,0:T(8,128)(2,1)S(1)}, bf16[8,512,128]{2,1,0:T(8,128)(2,1)}, u32[]{:S(2)}) copy-start(bf16[8,512,128]{2,1,0:T(8,128)(2,1)} %value_up_ref.1) | copy-start | bytes 3145732
  37.0 1.5 %collective-permute-start.10 = (bf16[160,640]{1,0:T(8,128)(2,1)S(1)}, bf16[160,640]{1,0:T(8,128)(2,1)S(1)}, u32[]{:S(2)}, u32[]{:S(2)}) collective-permute-start(bf16[160,640]{1,0:T(8,128)(2,1)S(1)} %get-tuple-element.108.refs_0_), channel_id=1, source_target_pairs={{0,16},{16,0},{1,17},{17,1},{2,18},{18,2},{3,19},{19,3},{4,20},{20... | collective-permute-start | bytes 614408 | tf_op jit(solution)/shard_map/ppermute | solution.py:57
  37.1 1.7 %collective-permute-start.11 = (bf16[160,640]{1,0:T(8,128)(2,1)S(1)}, bf16[160,640]{1,0:T(8,128)(2,1)S(1)}, u32[]{:S(2)}, u32[]{:S(2)}) collective-permute-start(bf16[160,640]{1,0:T(8,128)(2,1)S(1)} %get-tuple-element.109.refs_1_), channel_id=1, source_target_pairs={{0,16},{16,0},{1,17},{17,1},{2,18},{18,2},{3,19},{19,3},{4,20},{20... | collective-permute-start | bytes 614408 | tf_op jit(solution)/shard_map/ppermute | solution.py:57
  38.8 5.2 %copy-start.16 = (bf16[2048]{0:T(1024)(128)(2,1)S(1)}, bf16[2048]{0:T(1024)(128)(2,1)}, u32[]{:S(2)}) copy-start(bf16[2048]{0:T(1024)(128)(2,1)} %param.28) | copy-start | bytes 12292
  38.8 6.5 %copy-start.7 = (bf16[2048,16]{0,1:T(8,128)(2,1)S(1)}, bf16[2048,16]{0,1:T(8,128)(2,1)}, u32[]{:S(2)}) copy-start(bf16[2048,16]{0,1:T(8,128)(2,1)} %param.29) | copy-start | bytes 196612
  43.8 1.6 %collective-permute-start.12 = (bf16[64,2048]{1,0:T(8,128)(2,1)S(1)}, bf16[64,2048]{1,0:T(8,128)(2,1)S(1)}, u32[]{:S(2)}, u32[]{:S(2)}) collective-permute-start(bf16[64,2048]{1,0:T(8,128)(2,1)S(1)} %get-tuple-element.111), channel_id=1, source_target_pairs={{0,16},{16,0},{1,17},{17,1},{2,18},{18,2},{3,19},{19,3},{4,20},{20... | collective-permute-start | bytes 786440 | tf_op jit(solution)/shard_map/ppermute | solution.py:57
  45.4 17.0 %copy-start.1 = (bf16[1,2048,704]{1,2,0:T(8,128)(2,1)S(1)}, bf16[1,2048,704]{1,2,0:T(8,128)(2,1)}, u32[]{:S(2)}) copy-start(bf16[1,2048,704]{1,2,0:T(8,128)(2,1)} %param.30) | copy-start | bytes 8650756
  45.4 17.0 %copy-start.2 = (bf16[1,2048,704]{1,2,0:T(8,128)(2,1)S(1)}, bf16[1,2048,704]{1,2,0:T(8,128)(2,1)}, u32[]{:S(2)}) copy-start(bf16[1,2048,704]{1,2,0:T(8,128)(2,1)} %param.31) | copy-start | bytes 8650756
  45.4 17.0 %copy-start.3 = (bf16[1,704,2048]{2,1,0:T(8,128)(2,1)S(1)}, bf16[1,704,2048]{2,1,0:T(8,128)(2,1)}, u32[]{:S(2)}) copy-start(bf16[1,704,2048]{2,1,0:T(8,128)(2,1)} %param.32) | copy-start | bytes 8650756
  46.0 10.0 %collective-permute-start.13 = (bf16[64,2048]{1,0:T(8,128)(2,1)S(1)}, bf16[64,2048]{1,0:T(8,128)(2,1)S(1)}, u32[]{:S(2)}, u32[]{:S(2)}) collective-permute-start(bf16[64,2048]{1,0:T(8,128)(2,1)S(1)} %get-tuple-element.115), channel_id=1, source_target_pairs={{0,4},{1,5},{2,6},{3,7},{4,12},{5,13},{6,14},{7,15},{8,0},{9,1},{1... | collective-permute-start | bytes 786440 | tf_op jit(solution)/shard_map/ppermute | solution.py:37
  47.4 9.1 %collective-permute-start.14 = (bf16[32,2048]{1,0:T(8,128)(2,1)S(1)}, bf16[32,2048]{1,0:T(8,128)(2,1)S(1)}, u32[]{:S(2)}, u32[]{:S(2)}) collective-permute-start(bf16[32,2048]{1,0:T(8,128)(2,1)S(1)} %get-tuple-element.118), channel_id=1, source_target_pairs={{0,1},{1,0},{2,3},{3,2},{4,5},{5,4},{6,7},{7,6},{8,9},{9,8},{10,11... | collective-permute-start | bytes 393224 | tf_op jit(solution)/shard_map/ppermute | solution.py:47
  48.9 7.9 %collective-permute-start.15 = (bf16[32,2048]{1,0:T(8,128)(2,1)S(1)}, bf16[32,2048]{1,0:T(8,128)(2,1)S(1)}, u32[]{:S(2)}, u32[]{:S(2)}) collective-permute-start(bf16[32,2048]{1,0:T(8,128)(2,1)S(1)} %get-tuple-element.119), channel_id=1, source_target_pairs={{0,2},{1,3},{2,0},{3,1},{4,6},{5,7},{6,4},{7,5},{8,10},{9,11},{10,... | collective-permute-start | bytes 393224 | tf_op jit(solution)/shard_map/ppermute | solution.py:47
  50.1 6.7 %collective-permute-start.16 = (bf16[32,2048]{1,0:T(8,128)(2,1)S(1)}, bf16[32,2048]{1,0:T(8,128)(2,1)S(1)}, u32[]{:S(2)}, u32[]{:S(2)}) collective-permute-start(bf16[32,2048]{1,0:T(8,128)(2,1)S(1)} %get-tuple-element.120), channel_id=1, source_target_pairs={{0,3},{1,2},{2,1},{3,0},{4,7},{5,6},{6,5},{7,4},{8,11},{9,10},{10,... | collective-permute-start | bytes 393224 | tf_op jit(solution)/shard_map/ppermute | solution.py:47
  56.8 5.5 %collective-permute-start.17 = (bf16[128,2048]{1,0:T(8,128)(2,1)S(1)}, bf16[128,2048]{1,0:T(8,128)(2,1)S(1)}, u32[]{:S(2)}, u32[]{:S(2)}) collective-permute-start(bf16[128,2048]{1,0:T(8,128)(2,1)S(1)} %join_arrived.4.refs_0_), channel_id=1, source_target_pairs={{0,16},{16,0},{1,17},{17,1},{2,18},{18,2},{3,19},{19,3},{4,20},{20... | collective-permute-start | bytes 1572872 | tf_op jit(solution)/shard_map/ppermute | solution.py:57
  56.9 9.6 %collective-permute-start.18 = (bf16[64,2048]{1,0:T(8,128)(2,1)S(1)}, bf16[64,2048]{1,0:T(8,128)(2,1)S(1)}, u32[]{:S(2)}, u32[]{:S(2)}) collective-permute-start(bf16[64,2048]{1,0:T(8,128)(2,1)S(1)} %collective-permute-done.13.refs_0_), channel_id=1, source_target_pairs={{0,4},{1,5},{2,6},{3,7},{4,12},{5,13},{6,14},{7,15},{8,0},{9,1},{1... | collective-permute-start | bytes 786440 | tf_op jit(solution)/shard_map/ppermute | solution.py:37
  58.9 8.2 %collective-permute-start.19 = (bf16[32,2048]{1,0:T(8,128)(2,1)S(1)}, bf16[32,2048]{1,0:T(8,128)(2,1)S(1)}, u32[]{:S(2)}, u32[]{:S(2)}) collective-permute-start(bf16[32,2048]{1,0:T(8,128)(2,1)S(1)} %get-tuple-element.124), channel_id=1, source_target_pairs={{0,1},{1,0},{2,3},{3,2},{4,5},{5,4},{6,7},{7,6},{8,9},{9,8},{10,11... | collective-permute-start | bytes 393224 | tf_op jit(solution)/shard_map/ppermute | solution.py:47
  59.8 7.3 %collective-permute-start.20 = (bf16[32,2048]{1,0:T(8,128)(2,1)S(1)}, bf16[32,2048]{1,0:T(8,128)(2,1)S(1)}, u32[]{:S(2)}, u32[]{:S(2)}) collective-permute-start(bf16[32,2048]{1,0:T(8,128)(2,1)S(1)} %get-tuple-element.125), channel_id=1, source_target_pairs={{0,2},{1,3},{2,0},{3,1},{4,6},{5,7},{6,4},{7,5},{8,10},{9,11},{10,... | collective-permute-start | bytes 393224 | tf_op jit(solution)/shard_map/ppermute | solution.py:47
  60.6 7.3 %collective-permute-start.21 = (bf16[32,2048]{1,0:T(8,128)(2,1)S(1)}, bf16[32,2048]{1,0:T(8,128)(2,1)S(1)}, u32[]{:S(2)}, u32[]{:S(2)}) collective-permute-start(bf16[32,2048]{1,0:T(8,128)(2,1)S(1)} %get-tuple-element.126), channel_id=1, source_target_pairs={{0,3},{1,2},{2,1},{3,0},{4,7},{5,6},{6,5},{7,4},{8,11},{9,10},{10,... | collective-permute-start | bytes 393224 | tf_op jit(solution)/shard_map/ppermute | solution.py:47
  67.9 5.6 %collective-permute-start.22 = (bf16[128,2048]{1,0:T(8,128)(2,1)S(1)}, bf16[128,2048]{1,0:T(8,128)(2,1)S(1)}, u32[]{:S(2)}, u32[]{:S(2)}) collective-permute-start(bf16[128,2048]{1,0:T(8,128)(2,1)S(1)} %join_arrived.5.refs_0_), channel_id=1, source_target_pairs={{0,16},{16,0},{1,17},{17,1},{2,18},{18,2},{3,19},{19,3},{4,20},{20... | collective-permute-start | bytes 1572872 | tf_op jit(solution)/shard_map/ppermute | solution.py:57
  68.0 9.6 %collective-permute-start.23 = (bf16[64,2048]{1,0:T(8,128)(2,1)S(1)}, bf16[64,2048]{1,0:T(8,128)(2,1)S(1)}, u32[]{:S(2)}, u32[]{:S(2)}) collective-permute-start(bf16[64,2048]{1,0:T(8,128)(2,1)S(1)} %collective-permute-done.18.refs_1_), channel_id=1, source_target_pairs={{0,4},{1,5},{2,6},{3,7},{4,12},{5,13},{6,14},{7,15},{8,0},{9,1},{1... | collective-permute-start | bytes 786440 | tf_op jit(solution)/shard_map/ppermute | solution.py:37
  70.0 7.6 %collective-permute-start.24 = (bf16[32,2048]{1,0:T(8,128)(2,1)S(1)}, bf16[32,2048]{1,0:T(8,128)(2,1)S(1)}, u32[]{:S(2)}, u32[]{:S(2)}) collective-permute-start(bf16[32,2048]{1,0:T(8,128)(2,1)S(1)} %get-tuple-element.130), channel_id=1, source_target_pairs={{0,1},{1,0},{2,3},{3,2},{4,5},{5,4},{6,7},{7,6},{8,9},{9,8},{10,11... | collective-permute-start | bytes 393224 | tf_op jit(solution)/shard_map/ppermute | solution.py:47
  71.1 8.1 %collective-permute-start.25 = (bf16[32,2048]{1,0:T(8,128)(2,1)S(1)}, bf16[32,2048]{1,0:T(8,128)(2,1)S(1)}, u32[]{:S(2)}, u32[]{:S(2)}) collective-permute-start(bf16[32,2048]{1,0:T(8,128)(2,1)S(1)} %get-tuple-element.131), channel_id=1, source_target_pairs={{0,2},{1,3},{2,0},{3,1},{4,6},{5,7},{6,4},{7,5},{8,10},{9,11},{10,... | collective-permute-start | bytes 393224 | tf_op jit(solution)/shard_map/ppermute | solution.py:47
  72.3 6.9 %collective-permute-start.26 = (bf16[32,2048]{1,0:T(8,128)(2,1)S(1)}, bf16[32,2048]{1,0:T(8,128)(2,1)S(1)}, u32[]{:S(2)}, u32[]{:S(2)}) collective-permute-start(bf16[32,2048]{1,0:T(8,128)(2,1)S(1)} %get-tuple-element.132), channel_id=1, source_target_pairs={{0,3},{1,2},{2,1},{3,0},{4,7},{5,6},{6,5},{7,4},{8,11},{9,10},{10,... | collective-permute-start | bytes 393224 | tf_op jit(solution)/shard_map/ppermute | solution.py:47
  79.2 1.9 %collective-permute-start.28 = (bf16[128,2048]{1,0:T(8,128)(2,1)S(1)}, bf16[128,2048]{1,0:T(8,128)(2,1)S(1)}, u32[]{:S(2)}, u32[]{:S(2)}) collective-permute-start(bf16[128,2048]{1,0:T(8,128)(2,1)S(1)} %pass_on.6), channel_id=1, source_target_pairs={{0,16},{16,0},{1,17},{17,1},{2,18},{18,2},{3,19},{19,3},{4,20},{20... | collective-permute-start | bytes 1572872 | tf_op jit(solution)/shard_map/ppermute | solution.py:57
  79.8 5.0 %collective-permute-start.27 = (bf16[128,2048]{1,0:T(8,128)(2,1)S(1)}, bf16[128,2048]{1,0:T(8,128)(2,1)S(1)}, u32[]{:S(2)}, u32[]{:S(2)}) collective-permute-start(bf16[128,2048]{1,0:T(8,128)(2,1)S(1)} %join_arrived.6.refs_0_), channel_id=1, source_target_pairs={{0,16},{16,0},{1,17},{17,1},{2,18},{18,2},{3,19},{19,3},{4,20},{20... | collective-permute-start | bytes 1572872 | tf_op jit(solution)/shard_map/ppermute | solution.py:57
  81.2 9.2 %collective-permute-start.29 = (bf16[64,2048]{1,0:T(8,128)(2,1)S(1)}, bf16[64,2048]{1,0:T(8,128)(2,1)S(1)}, u32[]{:S(2)}, u32[]{:S(2)}) collective-permute-start(bf16[64,2048]{1,0:T(8,128)(2,1)S(1)} %get-tuple-element.141), channel_id=1, source_target_pairs={{0,1},{1,0},{2,3},{3,2},{4,5},{5,4},{6,7},{7,6},{8,9},{9,8},{10,11... | collective-permute-start | bytes 786440 | tf_op jit(solution)/shard_map/ppermute | solution.py:47
  82.2 8.9 %collective-permute-start.30 = (bf16[64,2048]{1,0:T(8,128)(2,1)S(1)}, bf16[64,2048]{1,0:T(8,128)(2,1)S(1)}, u32[]{:S(2)}, u32[]{:S(2)}) collective-permute-start(bf16[64,2048]{1,0:T(8,128)(2,1)S(1)} %get-tuple-element.142), channel_id=1, source_target_pairs={{0,2},{1,3},{2,0},{3,1},{4,6},{5,7},{6,4},{7,5},{8,10},{9,11},{10,... | collective-permute-start | bytes 786440 | tf_op jit(solution)/shard_map/ppermute | solution.py:47
  83.0 12.9 %collective-permute-start.31 = (bf16[64,2048]{1,0:T(8,128)(2,1)S(1)}, bf16[64,2048]{1,0:T(8,128)(2,1)S(1)}, u32[]{:S(2)}, u32[]{:S(2)}) collective-permute-start(bf16[64,2048]{1,0:T(8,128)(2,1)S(1)} %get-tuple-element.143), channel_id=1, source_target_pairs={{0,3},{1,2},{2,1},{3,0},{4,7},{5,6},{6,5},{7,4},{8,11},{9,10},{10,... | collective-permute-start | bytes 786440 | tf_op jit(solution)/shard_map/ppermute | solution.py:47
  87.5 10.2 %collective-permute-start.33 = (bf16[128,2048]{1,0:T(8,128)(2,1)S(1)}, bf16[128,2048]{1,0:T(8,128)(2,1)S(1)}, u32[]{:S(2)}, u32[]{:S(2)}) collective-permute-start(bf16[128,2048]{1,0:T(8,128)(2,1)S(1)} %get-tuple-element.146), channel_id=1, source_target_pairs={{0,16},{16,0},{1,17},{17,1},{2,18},{18,2},{3,19},{19,3},{4,20},{20... | collective-permute-start | bytes 1572872 | tf_op jit(solution)/shard_map/ppermute | solution.py:57
  96.0 5.4 %collective-permute-start.32 = (bf16[128,2048]{1,0:T(8,128)(2,1)S(1)}, bf16[128,2048]{1,0:T(8,128)(2,1)S(1)}, u32[]{:S(2)}, u32[]{:S(2)}) collective-permute-start(bf16[128,2048]{1,0:T(8,128)(2,1)S(1)} %join_arrived.7.refs_0_), channel_id=1, source_target_pairs={{0,16},{16,0},{1,17},{17,1},{2,18},{18,2},{3,19},{19,3},{4,20},{20... | collective-permute-start | bytes 1572872 | tf_op jit(solution)/shard_map/ppermute | solution.py:57
  96.3 9.9 %collective-permute-start.37 = (bf16[64,2048]{1,0:T(8,128)(2,1)S(1)}, bf16[64,2048]{1,0:T(8,128)(2,1)S(1)}, u32[]{:S(2)}, u32[]{:S(2)}) collective-permute-start(bf16[64,2048]{1,0:T(8,128)(2,1)S(1)} %collect.3), channel_id=1, source_target_pairs={{0,4},{1,5},{2,6},{3,7},{4,12},{5,13},{6,14},{7,15},{8,0},{9,1},{1... | collective-permute-start | bytes 786440 | tf_op jit(solution)/shard_map/ppermute | solution.py:37
  97.8 8.4 %collective-permute-start.34 = (bf16[32,2048]{1,0:T(8,128)(2,1)S(1)}, bf16[32,2048]{1,0:T(8,128)(2,1)S(1)}, u32[]{:S(2)}, u32[]{:S(2)}) collective-permute-start(bf16[32,2048]{1,0:T(8,128)(2,1)S(1)} %get-tuple-element.147), channel_id=1, source_target_pairs={{0,1},{1,0},{2,3},{3,2},{4,5},{5,4},{6,7},{7,6},{8,9},{9,8},{10,11... | collective-permute-start | bytes 393224 | tf_op jit(solution)/shard_map/ppermute | solution.py:47
  98.8 7.4 %collective-permute-start.35 = (bf16[32,2048]{1,0:T(8,128)(2,1)S(1)}, bf16[32,2048]{1,0:T(8,128)(2,1)S(1)}, u32[]{:S(2)}, u32[]{:S(2)}) collective-permute-start(bf16[32,2048]{1,0:T(8,128)(2,1)S(1)} %get-tuple-element.148), channel_id=1, source_target_pairs={{0,2},{1,3},{2,0},{3,1},{4,6},{5,7},{6,4},{7,5},{8,10},{9,11},{10,... | collective-permute-start | bytes 393224 | tf_op jit(solution)/shard_map/ppermute | solution.py:47
  99.6 29.8 %slice-start = ((s8[6291456]{0:T(1024)(128)(4,1)}), s8[4194304]{0:T(1024)(128)(4,1)S(1)}, s32[]{:S(2)}) async-start(s8[6291456]{0:T(1024)(128)(4,1)} %bitcast.27), calls=%async_computation | async-start | bytes 8388608
  99.6 29.8 %slice-start.1 = ((s8[6291456]{0:T(1024)(128)(4,1)}), s8[2097152]{0:T(1024)(128)(4,1)S(1)}, s32[]{:S(2)}) async-start(s8[6291456]{0:T(1024)(128)(4,1)} %bitcast.27), calls=%async_computation.1 | async-start | bytes 4194304
  99.6 7.3 %collective-permute-start.36 = (bf16[32,2048]{1,0:T(8,128)(2,1)S(1)}, bf16[32,2048]{1,0:T(8,128)(2,1)S(1)}, u32[]{:S(2)}, u32[]{:S(2)}) collective-permute-start(bf16[32,2048]{1,0:T(8,128)(2,1)S(1)} %get-tuple-element.149), channel_id=1, source_target_pairs={{0,3},{1,2},{2,1},{3,0},{4,7},{5,6},{6,5},{7,4},{8,11},{9,10},{10,... | collective-permute-start | bytes 393224 | tf_op jit(solution)/shard_map/ppermute | solution.py:47
  106.9 15.7 %copy-start.17 = (bf16[2048]{0:T(1024)(128)(2,1)S(1)}, bf16[2048]{0:T(1024)(128)(2,1)}, u32[]{:S(2)}) copy-start(bf16[2048]{0:T(1024)(128)(2,1)} %param.33) | copy-start | bytes 12292
  106.9 1.9 %collective-permute-start.38 = (bf16[128,2048]{1,0:T(8,128)(2,1)S(1)}, bf16[128,2048]{1,0:T(8,128)(2,1)S(1)}, u32[]{:S(2)}, u32[]{:S(2)}) collective-permute-start(bf16[128,2048]{1,0:T(8,128)(2,1)S(1)} %pass_on.7), channel_id=1, source_target_pairs={{0,16},{16,0},{1,17},{17,1},{2,18},{18,2},{3,19},{19,3},{4,20},{20... | collective-permute-start | bytes 1572872 | tf_op jit(solution)/shard_map/ppermute | solution.py:57
  106.9 12.0 %collective-permute-start.43 = (bf16[128,2048]{1,0:T(8,128)(2,1)S(1)}, bf16[128,2048]{1,0:T(8,128)(2,1)S(1)}, u32[]{:S(2)}, u32[]{:S(2)}) collective-permute-start(bf16[128,2048]{1,0:T(8,128)(2,1)S(1)} %get-tuple-element.157), channel_id=1, source_target_pairs={{0,16},{16,0},{1,17},{17,1},{2,18},{18,2},{3,19},{19,3},{4,20},{20... | collective-permute-start | bytes 1572872 | tf_op jit(solution)/shard_map/ppermute | solution.py:57
  107.7 21.7 %copy-start.5 = (bf16[2048,288]{0,1:T(8,128)(2,1)S(1)}, bf16[2048,288]{0,1:T(8,128)(2,1)}, u32[]{:S(2)}) copy-start(bf16[2048,288]{0,1:T(8,128)(2,1)} %param.35) | copy-start | bytes 3538948
  107.7 9.2 %collective-permute-start.42 = (bf16[64,2048]{1,0:T(8,128)(2,1)S(1)}, bf16[64,2048]{1,0:T(8,128)(2,1)S(1)}, u32[]{:S(2)}, u32[]{:S(2)}) collective-permute-start(bf16[64,2048]{1,0:T(8,128)(2,1)S(1)} %collect.4), channel_id=1, source_target_pairs={{0,4},{1,5},{2,6},{3,7},{4,12},{5,13},{6,14},{7,15},{8,0},{9,1},{1... | collective-permute-start | bytes 786440 | tf_op jit(solution)/shard_map/ppermute | solution.py:37
  108.9 7.9 %collective-permute-start.39 = (bf16[32,2048]{1,0:T(8,128)(2,1)S(1)}, bf16[32,2048]{1,0:T(8,128)(2,1)S(1)}, u32[]{:S(2)}, u32[]{:S(2)}) collective-permute-start(bf16[32,2048]{1,0:T(8,128)(2,1)S(1)} %get-tuple-element.152), channel_id=1, source_target_pairs={{0,1},{1,0},{2,3},{3,2},{4,5},{5,4},{6,7},{7,6},{8,9},{9,8},{10,11... | collective-permute-start | bytes 393224 | tf_op jit(solution)/shard_map/ppermute | solution.py:47
  110.1 8.1 %collective-permute-start.40 = (bf16[32,2048]{1,0:T(8,128)(2,1)S(1)}, bf16[32,2048]{1,0:T(8,128)(2,1)S(1)}, u32[]{:S(2)}, u32[]{:S(2)}) collective-permute-start(bf16[32,2048]{1,0:T(8,128)(2,1)S(1)} %get-tuple-element.153), channel_id=1, source_target_pairs={{0,2},{1,3},{2,0},{3,1},{4,6},{5,7},{6,4},{7,5},{8,10},{9,11},{10,... | collective-permute-start | bytes 393224 | tf_op jit(solution)/shard_map/ppermute | solution.py:47
  111.3 6.9 %collective-permute-start.41 = (bf16[32,2048]{1,0:T(8,128)(2,1)S(1)}, bf16[32,2048]{1,0:T(8,128)(2,1)S(1)}, u32[]{:S(2)}, u32[]{:S(2)}) collective-permute-start(bf16[32,2048]{1,0:T(8,128)(2,1)S(1)} %get-tuple-element.154), channel_id=1, source_target_pairs={{0,3},{1,2},{2,1},{3,0},{4,7},{5,6},{6,5},{7,4},{8,11},{9,10},{10,... | collective-permute-start | bytes 393224 | tf_op jit(solution)/shard_map/ppermute | solution.py:47
  118.4 8.9 %collective-permute-start.47 = (bf16[64,2048]{1,0:T(8,128)(2,1)S(1)}, bf16[64,2048]{1,0:T(8,128)(2,1)S(1)}, u32[]{:S(2)}, u32[]{:S(2)}) collective-permute-start(bf16[64,2048]{1,0:T(8,128)(2,1)S(1)} %collect.5.refs_0_), channel_id=1, source_target_pairs={{0,4},{1,5},{2,6},{3,7},{4,12},{5,13},{6,14},{7,15},{8,0},{9,1},{1... | collective-permute-start | bytes 786440 | tf_op jit(solution)/shard_map/ppermute | solution.py:37
  119.1 6.1 %collective-permute-start.44 = (bf16[32,2048]{1,0:T(8,128)(2,1)S(1)}, bf16[32,2048]{1,0:T(8,128)(2,1)S(1)}, u32[]{:S(2)}, u32[]{:S(2)}) collective-permute-start(bf16[32,2048]{1,0:T(8,128)(2,1)S(1)} %get-tuple-element.159), channel_id=1, source_target_pairs={{0,1},{1,0},{2,3},{3,2},{4,5},{5,4},{6,7},{7,6},{8,9},{9,8},{10,11... | collective-permute-start | bytes 393224 | tf_op jit(solution)/shard_map/ppermute | solution.py:47
  120.3 5.8 %collective-permute-start.45 = (bf16[32,2048]{1,0:T(8,128)(2,1)S(1)}, bf16[32,2048]{1,0:T(8,128)(2,1)S(1)}, u32[]{:S(2)}, u32[]{:S(2)}) collective-permute-start(bf16[32,2048]{1,0:T(8,128)(2,1)S(1)} %get-tuple-element.160), channel_id=1, source_target_pairs={{0,2},{1,3},{2,0},{3,1},{4,6},{5,7},{6,4},{7,5},{8,10},{9,11},{10,... | collective-permute-start | bytes 393224 | tf_op jit(solution)/shard_map/ppermute | solution.py:47
  121.5 5.9 %collective-permute-start.46 = (bf16[32,2048]{1,0:T(8,128)(2,1)S(1)}, bf16[32,2048]{1,0:T(8,128)(2,1)S(1)}, u32[]{:S(2)}, u32[]{:S(2)}) collective-permute-start(bf16[32,2048]{1,0:T(8,128)(2,1)S(1)} %get-tuple-element.161), channel_id=1, source_target_pairs={{0,3},{1,2},{2,1},{3,0},{4,7},{5,6},{6,5},{7,4},{8,11},{9,10},{10,... | collective-permute-start | bytes 393224 | tf_op jit(solution)/shard_map/ppermute | solution.py:47
  127.8 1.6 %collective-permute-start.48 = (bf16[64,2048]{1,0:T(8,128)(2,1)S(1)}, bf16[64,2048]{1,0:T(8,128)(2,1)S(1)}, u32[]{:S(2)}, u32[]{:S(2)}) collective-permute-start(bf16[64,2048]{1,0:T(8,128)(2,1)S(1)} %get-tuple-element.163.refs_4_), channel_id=1, source_target_pairs={{0,16},{16,0},{1,17},{17,1},{2,18},{18,2},{3,19},{19,3},{4,20},{20... | collective-permute-start | bytes 786440 | tf_op jit(solution)/shard_map/ppermute | solution.py:57
  (5 other events, 3.5 us)
